TPU v7x, 32 devices: a whole 2x2x4 slice. The times are simulated.
32 devices in a mesh: leaf: 8 (over z, y), rhs: 4 (over x, core).
Axes of the slice: x: 2, y: 2, z: 4, core: 2. Of those that a mesh axis runs over, the one named last changes fastest.
Arguments:
- right_side: bfloat16 [64, 32768], P(None, ('leaf', 'rhs')), may hold values from -6 to 6
- point_order: int32 [32768], P('leaf'), may hold values from 0 to 4095, as said below
- leaf_inverse: bfloat16 [64, 512, 512], P('leaf', 'rhs')
- leaf_basis: bfloat16 [64, 512, 256], P('leaf', 'rhs'), may hold values from -0.25 to 0.25
- leaf_coupling: bfloat16 [64, 512, 256], P('leaf', 'rhs'), may hold values from -0.1875 to 0.1875
- node_inverse: bfloat16 [64, 512, 512], P('leaf', 'rhs')
- node_basis: bfloat16 [64, 512, 256], P('leaf', 'rhs'), may hold values from -0.25 to 0.25
- node_coupling: bfloat16 [64, 512, 256], P('leaf', 'rhs'), may hold values from -0.375 to 0.375
Outputs:
- coefficients: float32 [64, 64, 512], P('leaf', None, 'rhs')
Inputs may be any that keep to these rules, and one draw needn't show every extreme that they name: `point_order`: within each block of 4096 entries that one index of leaf holds, every number from 0 to 4095 stands once.
All inputs are finite; a program needn't handle non-finite values.
Results may differ from a plain program's by a relative error of at most 0.03.
Values may be sent and summed in bfloat16 or wider, within the bound.
No kernel may reach another device: no remote copies, remote signals or barrier semaphores. Data moves between devices by JAX's collectives and lax.ppermute only.
A program may use at most 64 MiB of HBM per device.

v0:
```python
import jax
import jax.numpy as jnp
from jax import lax
from jax.sharding import PartitionSpec as P


def from_behind(block, axis, distance):
    devices = range(lax.axis_size(axis))
    route = [(i - distance, i) for i in devices if i - distance in devices]
    return lax.ppermute(block, axis, route)


def fetch_child(values, offset_by):
    return from_behind(values, "leaf", offset_by)


def send_share(values, offset_by):
    return from_behind(values, "leaf", offset_by)


def body(
    right_side,
    point_order,
    leaf_inverse,
    leaf_basis,
    leaf_coupling,
    node_inverse,
    node_basis,
    node_coupling,
):
    devices = lax.axis_size("leaf")
    position = lax.axis_index("leaf")
    per_dev = leaf_inverse.shape[0]
    leaf_size = leaf_inverse.shape[2]
    rank_size = leaf_basis.shape[2]
    target_count = right_side.shape[0]
    local_levels = per_dev.bit_length() - 1
    cross_levels = devices.bit_length() - 1
    gathered = lax.all_gather(right_side, "rhs", axis=1, tiled=True)
    ordered = jnp.take(gathered, point_order, axis=1).reshape(target_count, per_dev, leaf_size)
    leaf_values = jnp.einsum(
        "slj,lij->lsi", ordered, leaf_inverse, preferred_element_type=jnp.float32
    )
    partial_terms = jnp.einsum(
        "lsi,lik->lsk",
        leaf_values.astype(jnp.bfloat16),
        leaf_basis,
        preferred_element_type=jnp.float32,
    )
    compressed = lax.psum(partial_terms, "rhs").astype(jnp.bfloat16)
    solved_local = []
    for height in range(1, local_levels + 1):
        node_count = per_dev >> height
        offset = per_dev - 2 * node_count
        stacked = jnp.concatenate([compressed[0::2], compressed[1::2]], axis=-1)
        solved = jnp.einsum(
            "nsj,nij->nsi",
            stacked,
            node_inverse[offset : offset + node_count],
            preferred_element_type=jnp.float32,
        )
        solved_local.append(solved)
        partial_terms = jnp.einsum(
            "nsi,nik->nsk",
            solved.astype(jnp.bfloat16),
            node_basis[offset : offset + node_count],
            preferred_element_type=jnp.float32,
        )
        compressed = lax.psum(partial_terms, "rhs").astype(jnp.bfloat16)
    own_inverse = node_inverse[per_dev - 1]
    own_basis = node_basis[per_dev - 1]
    own_coupling = node_coupling[per_dev - 1]
    current = compressed[0]
    solved_cross = []
    for height in range(1, cross_levels + 1):
        distance = 1 if height == 1 else 2 ** (height - 2)
        from_left = fetch_child(current, distance)
        from_right = current if height == 1 else fetch_child(current, -distance)
        stacked = jnp.concatenate([from_left, from_right], axis=-1)
        solved = jnp.einsum("sj,ij->si", stacked, own_inverse, preferred_element_type=jnp.float32)
        solved_cross.append(solved)
        if height < cross_levels:
            partial_terms = jnp.einsum(
                "si,ik->sk",
                solved.astype(jnp.bfloat16),
                own_basis,
                preferred_element_type=jnp.float32,
            )
            current = lax.psum(partial_terms, "rhs").astype(jnp.bfloat16)
    node_value = solved_cross[cross_levels - 1]
    incoming = current
    for height in range(cross_levels, 0, -1):
        shares = node_value.astype(jnp.bfloat16)
        shares = lax.all_gather(shares, "rhs", axis=1, tiled=True)
        distance = 1 if height == 1 else 2 ** (height - 2)
        to_left = send_share(shares[:, :rank_size], -distance)
        to_right = (
            shares[:, rank_size:] if height == 1 else send_share(shares[:, rank_size:], distance)
        )
        is_left = position // 2 ** (height - 1) % 2 == 0
        incoming = jnp.where(is_left, to_left, to_right)
        if height > 1:
            node_value = solved_cross[height - 2] - jnp.einsum(
                "sk,ik->si", incoming, own_coupling, preferred_element_type=jnp.float32
            )
    current = incoming[None]
    for height in range(local_levels, 0, -1):
        node_count = per_dev >> height
        offset = per_dev - 2 * node_count
        node_values = solved_local[height - 1] - jnp.einsum(
            "nsk,nik->nsi",
            current,
            node_coupling[offset : offset + node_count],
            preferred_element_type=jnp.float32,
        )
        shares = lax.all_gather(node_values.astype(jnp.bfloat16), "rhs", axis=2, tiled=True)
        current = jnp.stack([shares[..., :rank_size], shares[..., rank_size:]], axis=1).reshape(
            2 * node_count, target_count, rank_size
        )
    return leaf_values - jnp.einsum(
        "lsk,lik->lsi", current, leaf_coupling, preferred_element_type=jnp.float32
    )


def solution(mesh):
    placed = (
        P(None, ("leaf", "rhs")),
        P("leaf"),
        P("leaf", "rhs", None),
        P("leaf", "rhs", None),
        P("leaf", "rhs", None),
        P("leaf", "rhs", None),
        P("leaf", "rhs", None),
        P("leaf", "rhs", None),
    )
    return jax.shard_map(
        body, mesh=mesh, in_specs=placed, out_specs=P("leaf", None, "rhs"), check_vma=False
    )
```

profile of v0, /device:TPU:0, one launch (start us, length us, event | category | flops | bytes accessed | tf_op | source)
XLA Modules:
  0.0 191.9 jit_solution(3038828365875438453)
XLA Ops:
  0.0 0.8 fusion.75
  0.8 1.1 copy.11
  1.9 11.5 %all_gather.21 = bf16[64,4096]{0,1:T(8,128)(2,1)S(1)} all-gather(bf16[64,1024]{0,1:T(8,128)(2,1)S(1)} %copy.11), channel_id=1, replica_groups=mesh['leaf'=8,'rhs'=4] {'rhs'}, dimensions={1}, use_global_device_ids=true | all-gather | bytes 655360 | tf_op jit(solution)/shard_map/all_gather | solution.py:39
  13.4 12.1 %gather_fusion = bf16[4096,64]{1,0:T(8,128)(2,1)S(1)} fusion(bf16[64,4096]{0,1:T(8,128)(2,1)S(1)} %all_gather.21, s32[4096]{0:T(1024)S(1)} %fusion.75), kind=kCustom, calls=%fused_computation | custom fusion | bytes 1064960 | tf_op jit(solution)/shard_map/jit(_take)/gather | solution.py:40
  25.5 0.3 copy.12
  25.9 0.5 fusion.7
  26.4 0.6 copy-done.3
  26.9 0.2 fusion.33
  27.2 16.5 %all-reduce.3 = bf16[8,64,256]{2,1,0:T(8,128)(2,1)S(1)} all-reduce(f32[8,64,256]{2,1,0:T(8,128)S(1)} %fusion.33), channel_id=1, replica_groups=mesh['leaf'=8,'rhs'=4] {'rhs'}, use_global_device_ids=true, to_apply=%region_0.1 | all-reduce | flops 131072 | bytes 786432 | tf_op jit(solution)/shard_map/psum | solution.py:50
  43.7 1.4 fusion.5
  45.3 14.0 %all-reduce.4 = bf16[4,64,256]{2,1,0:T(8,128)(2,1)S(1)} all-reduce(f32[4,64,256]{2,1,0:T(8,128)S(1)} %fusion.16), channel_id=1, replica_groups=mesh['leaf'=8,'rhs'=4] {'rhs'}, use_global_device_ids=true, to_apply=%region_1.2 | all-reduce | flops 65536 | bytes 393216 | tf_op jit(solution)/shard_map/psum | solution.py:69
  59.3 1.2 fusion.14
  60.7 11.5 %all-reduce.5 = bf16[2,64,256]{2,1,0:T(8,128)(2,1)S(1)} all-reduce(f32[2,64,256]{2,1,0:T(8,128)S(1)} %fusion.31), channel_id=1, replica_groups=mesh['leaf'=8,'rhs'=4] {'rhs'}, use_global_device_ids=true, to_apply=%region_2.3 | all-reduce | flops 32768 | bytes 196608 | tf_op jit(solution)/shard_map/psum | solution.py:69
  72.2 1.1 fusion.27
  73.4 10.9 %psum.45 = bf16[1,64,256]{2,1,0:T(8,128)(2,1)S(1)} all-reduce(f32[1,64,256]{2,1,0:T(8,128)S(1)} %convolution_bitcast_fusion), channel_id=1, replica_groups=mesh['leaf'=8,'rhs'=4] {'rhs'}, use_global_device_ids=true, to_apply=%region_3.4 | all-reduce | flops 16384 | bytes 98304 | tf_op jit(solution)/shard_map/psum | solution.py:69
  84.3 3.4 %collective-permute-start = (bf16[64,256]{1,0:T(8,128)(2,1)S(1)}, bf16[64,256]{1,0:T(8,128)(2,1)S(1)}, u32[]{:S(2)}, u32[]{:S(2)}) collective-permute-start(bf16[64,256]{1,0:T(8,128)(2,1)S(1)} %bitcast.64), channel_id=1, source_target_pairs={{0,4},{4,8},{8,12},{12,16},{16,20},{20,24},{24,28},{1,5},{5,9},{9,... | collective-permute-start | bytes 98312 | tf_op jit(solution)/shard_map/ppermute | solution.py:10
  87.7 1.6 collective-permute-done
  89.3 1.1 fusion.25
  90.5 10.7 %psum.46 = bf16[64,256]{1,0:T(8,128)(2,1)S(1)} all-reduce(f32[64,256]{1,0:T(8,128)S(1)} %fusion.56), channel_id=1, replica_groups=mesh['leaf'=8,'rhs'=4] {'rhs'}, use_global_device_ids=true, to_apply=%region_4.5 | all-reduce | flops 16384 | bytes 98304 | tf_op jit(solution)/shard_map/psum | solution.py:89
  101.2 4.4 %collective-permute-start.1 = (bf16[64,256]{1,0:T(8,128)(2,1)S(1)}, bf16[64,256]{1,0:T(8,128)(2,1)S(1)}, u32[]{:S(2)}, u32[]{:S(2)}) collective-permute-start(bf16[64,256]{1,0:T(8,128)(2,1)S(1)} %psum.46), channel_id=1, source_target_pairs={{0,4},{4,8},{8,12},{12,16},{16,20},{20,24},{24,28},{1,5},{5,9},{9,... | collective-permute-start | bytes 98312 | tf_op jit(solution)/shard_map/ppermute | solution.py:10
  105.6 1.3 collective-permute-start.2
  106.9 0.3 collective-permute-done.1
  107.1 4.6 %collective-permute-done.2 = bf16[64,256]{1,0:T(8,128)(2,1)S(1)} collective-permute-done((bf16[64,256]{1,0:T(8,128)(2,1)S(1)}, bf16[64,256]{1,0:T(8,128)(2,1)S(1)}, u32[]{:S(2)}, u32[]{:S(2)}) %collective-permute-start.2) | collective-permute-done | bytes 32800 | tf_op jit(solution)/shard_map/ppermute | solution.py:10
  111.8 1.1 fusion.23
  113.0 10.7 %psum.47 = bf16[64,256]{1,0:T(8,128)(2,1)S(1)} all-reduce(f32[64,256]{1,0:T(8,128)S(1)} %fusion.54), channel_id=1, replica_groups=mesh['leaf'=8,'rhs'=4] {'rhs'}, use_global_device_ids=true, to_apply=%region_5.6 | all-reduce | flops 16384 | bytes 98304 | tf_op jit(solution)/shard_map/psum | solution.py:89
  123.6 3.5 %collective-permute-start.3 = (bf16[64,256]{1,0:T(8,128)(2,1)S(1)}, bf16[64,256]{1,0:T(8,128)(2,1)S(1)}, u32[]{:S(2)}, u32[]{:S(2)}) collective-permute-start(bf16[64,256]{1,0:T(8,128)(2,1)S(1)} %psum.47), channel_id=1, source_target_pairs={{0,8},{4,12},{8,16},{12,20},{16,24},{20,28},{1,9},{5,13},{9,17},{1... | collective-permute-start | bytes 98312 | tf_op jit(solution)/shard_map/ppermute | solution.py:10
  127.1 1.3 collective-permute-start.4
  128.4 0.3 collective-permute-done.3
  128.7 4.2 %collective-permute-done.4 = bf16[64,256]{1,0:T(8,128)(2,1)S(1)} collective-permute-done((bf16[64,256]{1,0:T(8,128)(2,1)S(1)}, bf16[64,256]{1,0:T(8,128)(2,1)S(1)}, u32[]{:S(2)}, u32[]{:S(2)}) %collective-permute-start.4) | collective-permute-done | bytes 32800 | tf_op jit(solution)/shard_map/ppermute | solution.py:10
  133.0 1.1 convolution_convert_fusion
  134.0 5.3 %all_gather.22 = bf16[64,512]{1,0:T(8,128)(2,1)S(1)} all-gather(bf16[64,128]{1,0:T(8,128)(2,1)S(1)} %convolution_convert_fusion), channel_id=1, replica_groups=mesh['leaf'=8,'rhs'=4] {'rhs'}, dimensions={1}, use_global_device_ids=true | all-gather | bytes 81920 | tf_op jit(solution)/shard_map/all_gather | solution.py:94
  139.3 1.3 collective-permute-start.5
  140.6 4.5 %collective-permute-start.6 = (bf16[64,256]{1,0:T(8,128)(2,1)S(1)}, bf16[64,256]{1,0:T(8,128)(2,1)S(1)}, u32[]{:S(2)}, u32[]{:S(2)}) collective-permute-start(bf16[64,256]{1,0:T(8,128)(2,1)S(1)} %get-tuple-element.17), channel_id=1, source_target_pairs={{0,8},{4,12},{8,16},{12,20},{16,24},{20,28},{1,9},{5,13},{9,17},{1... | collective-permute-start | bytes 98312 | tf_op jit(solution)/shard_map/ppermute | solution.py:10
  145.2 1.5 collective-permute-done.6
  146.8 5.3 %all_gather.23 = bf16[64,512]{1,0:T(8,128)(2,1)S(1)} all-gather(bf16[64,128]{1,0:T(8,128)(2,1)S(1)} %fusion.2), channel_id=1, replica_groups=mesh['leaf'=8,'rhs'=4] {'rhs'}, dimensions={1}, use_global_device_ids=true | all-gather | bytes 81920 | tf_op jit(solution)/shard_map/all_gather | solution.py:94
  152.1 1.3 collective-permute-start.7
  153.4 5.4 %collective-permute-start.8 = (bf16[64,256]{1,0:T(8,128)(2,1)S(1)}, bf16[64,256]{1,0:T(8,128)(2,1)S(1)}, u32[]{:S(2)}, u32[]{:S(2)}) collective-permute-start(bf16[64,256]{1,0:T(8,128)(2,1)S(1)} %get-tuple-element.15), channel_id=1, source_target_pairs={{0,4},{4,8},{8,12},{12,16},{16,20},{20,24},{24,28},{1,5},{5,9},{9,... | collective-permute-start | bytes 98312 | tf_op jit(solution)/shard_map/ppermute | solution.py:10
  158.9 1.5 collective-permute-done.8
  160.6 5.3 %all_gather.24 = bf16[64,512]{1,0:T(8,128)(2,1)S(1)} all-gather(bf16[64,128]{1,0:T(8,128)(2,1)S(1)} %fusion.3), channel_id=1, replica_groups=mesh['leaf'=8,'rhs'=4] {'rhs'}, dimensions={1}, use_global_device_ids=true | all-gather | bytes 81920 | tf_op jit(solution)/shard_map/all_gather | solution.py:94
  165.9 1.3 collective-permute-start.9
  167.2 5.4 %collective-permute-done.9 = bf16[64,256]{1,0:T(8,128)(2,1)S(1)} collective-permute-done((bf16[64,256]{1,0:T(8,128)(2,1)S(1)}, bf16[64,256]{1,0:T(8,128)(2,1)S(1)}, u32[]{:S(2)}, u32[]{:S(2)}) %collective-permute-start.9) | collective-permute-done | bytes 32800 | tf_op jit(solution)/shard_map/ppermute | solution.py:10
  172.7 5.3 %all-gather = bf16[64,512]{1,0:T(8,128)(2,1)S(1)} all-gather(bf16[64,128]{1,0:T(8,128)(2,1)S(1)} %fusion.4), channel_id=2, replica_groups=mesh['leaf'=8,'rhs'=4] {'rhs'}, dimensions={1}, use_global_device_ids=true | all-gather | bytes 81920 | tf_op jit(solution)/shard_map/all_gather | solution.py:116
  178.0 0.2 fusion.1
  178.2 5.5 %all_gather.26 = bf16[2,64,512]{2,1,0:T(8,128)(2,1)S(1)} all-gather(bf16[2,64,128]{2,1,0:T(8,128)(2,1)S(1)} %fusion.1), channel_id=1, replica_groups=mesh['leaf'=8,'rhs'=4] {'rhs'}, dimensions={2}, use_global_device_ids=true | all-gather | bytes 163840 | tf_op jit(solution)/shard_map/all_gather | solution.py:116
  183.7 0.2 fusion
  183.9 6.0 %all_gather.27 = bf16[4,64,512]{2,1,0:T(8,128)(2,1)S(1)} all-gather(bf16[4,64,128]{2,1,0:T(8,128)(2,1)S(1)} %fusion), channel_id=1, replica_groups=mesh['leaf'=8,'rhs'=4] {'rhs'}, dimensions={2}, use_global_device_ids=true | all-gather | bytes 327680 | tf_op jit(solution)/shard_map/all_gather | solution.py:116
  190.0 1.0 copy-done.4
  190.9 1.0 convolution_subtract_fusion
  (35 shorter events, 1.3 us)
Async XLA Ops:
  0.0 25.9 %copy-start = (bf16[8,128,512]{2,1,0:T(8,128)(2,1)S(1)}, bf16[8,128,512]{2,1,0:T(8,128)(2,1)}, u32[]{:S(2)}) copy-start(bf16[8,128,512]{2,1,0:T(8,128)(2,1)} %param.10) | copy-start | bytes 3145732
  0.0 0.8 copy-start.5
  25.9 1.0 copy-start.3
  43.7 1.4 copy-start.1
  84.3 5.0 %collective-permute-start = (bf16[64,256]{1,0:T(8,128)(2,1)S(1)}, bf16[64,256]{1,0:T(8,128)(2,1)S(1)}, u32[]{:S(2)}, u32[]{:S(2)}) collective-permute-start(bf16[64,256]{1,0:T(8,128)(2,1)S(1)} %bitcast.64), channel_id=1, source_target_pairs={{0,4},{4,8},{8,12},{12,16},{16,20},{20,24},{24,28},{1,5},{5,9},{9,... | collective-permute-start | bytes 98312 | tf_op jit(solution)/shard_map/ppermute | solution.py:10
  101.2 45.5 %copy-start.2 = (bf16[8,128,256]{2,1,0:T(8,128)(2,1)S(1)}, bf16[8,128,256]{2,1,0:T(8,128)(2,1)}, u32[]{:S(2)}) copy-start(bf16[8,128,256]{2,1,0:T(8,128)(2,1)} %param.15) | copy-start | bytes 1572868
  101.2 5.9 %collective-permute-start.1 = (bf16[64,256]{1,0:T(8,128)(2,1)S(1)}, bf16[64,256]{1,0:T(8,128)(2,1)S(1)}, u32[]{:S(2)}, u32[]{:S(2)}) collective-permute-start(bf16[64,256]{1,0:T(8,128)(2,1)S(1)} %psum.46), channel_id=1, source_target_pairs={{0,4},{4,8},{8,12},{12,16},{16,20},{20,24},{24,28},{1,5},{5,9},{9,... | collective-permute-start | bytes 98312 | tf_op jit(solution)/shard_map/ppermute | solution.py:10
  105.6 6.2 %collective-permute-start.2 = (bf16[64,256]{1,0:T(8,128)(2,1)S(1)}, bf16[64,256]{1,0:T(8,128)(2,1)S(1)}, u32[]{:S(2)}, u32[]{:S(2)}) collective-permute-start(bf16[64,256]{1,0:T(8,128)(2,1)S(1)} %psum.46), channel_id=1, source_target_pairs={{4,0},{8,4},{12,8},{16,12},{20,16},{24,20},{28,24},{5,1},{9,5},{13... | collective-permute-start | bytes 98312 | tf_op jit(solution)/shard_map/ppermute | solution.py:10
  123.6 5.1 %collective-permute-start.3 = (bf16[64,256]{1,0:T(8,128)(2,1)S(1)}, bf16[64,256]{1,0:T(8,128)(2,1)S(1)}, u32[]{:S(2)}, u32[]{:S(2)}) collective-permute-start(bf16[64,256]{1,0:T(8,128)(2,1)S(1)} %psum.47), channel_id=1, source_target_pairs={{0,8},{4,12},{8,16},{12,20},{16,24},{20,28},{1,9},{5,13},{9,17},{1... | collective-permute-start | bytes 98312 | tf_op jit(solution)/shard_map/ppermute | solution.py:10
  127.1 5.8 %collective-permute-start.4 = (bf16[64,256]{1,0:T(8,128)(2,1)S(1)}, bf16[64,256]{1,0:T(8,128)(2,1)S(1)}, u32[]{:S(2)}, u32[]{:S(2)}) collective-permute-start(bf16[64,256]{1,0:T(8,128)(2,1)S(1)} %psum.47), channel_id=1, source_target_pairs={{8,0},{12,4},{16,8},{20,12},{24,16},{28,20},{9,1},{13,5},{17,9},{2... | collective-permute-start | bytes 98312 | tf_op jit(solution)/shard_map/ppermute | solution.py:10
  139.3 5.9 %collective-permute-start.5 = (bf16[64,256]{1,0:T(8,128)(2,1)S(1)}, bf16[64,256]{1,0:T(8,128)(2,1)S(1)}, u32[]{:S(2)}, u32[]{:S(2)}) collective-permute-start(bf16[64,256]{1,0:T(8,128)(2,1)S(1)} %get-tuple-element.18), channel_id=1, source_target_pairs={{8,0},{12,4},{16,8},{20,12},{24,16},{28,20},{9,1},{13,5},{17,9},{2... | collective-permute-start | bytes 98312 | tf_op jit(solution)/shard_map/ppermute | solution.py:10
  140.6 6.1 %collective-permute-start.6 = (bf16[64,256]{1,0:T(8,128)(2,1)S(1)}, bf16[64,256]{1,0:T(8,128)(2,1)S(1)}, u32[]{:S(2)}, u32[]{:S(2)}) collective-permute-start(bf16[64,256]{1,0:T(8,128)(2,1)S(1)} %get-tuple-element.17), channel_id=1, source_target_pairs={{0,8},{4,12},{8,16},{12,20},{16,24},{20,28},{1,9},{5,13},{9,17},{1... | collective-permute-start | bytes 98312 | tf_op jit(solution)/shard_map/ppermute | solution.py:10
  152.1 6.8 %collective-permute-start.7 = (bf16[64,256]{1,0:T(8,128)(2,1)S(1)}, bf16[64,256]{1,0:T(8,128)(2,1)S(1)}, u32[]{:S(2)}, u32[]{:S(2)}) collective-permute-start(bf16[64,256]{1,0:T(8,128)(2,1)S(1)} %get-tuple-element.16), channel_id=1, source_target_pairs={{4,0},{8,4},{12,8},{16,12},{20,16},{24,20},{28,24},{5,1},{9,5},{13... | collective-permute-start | bytes 98312 | tf_op jit(solution)/shard_map/ppermute | solution.py:10
  153.4 7.0 %collective-permute-start.8 = (bf16[64,256]{1,0:T(8,128)(2,1)S(1)}, bf16[64,256]{1,0:T(8,128)(2,1)S(1)}, u32[]{:S(2)}, u32[]{:S(2)}) collective-permute-start(bf16[64,256]{1,0:T(8,128)(2,1)S(1)} %get-tuple-element.15), channel_id=1, source_target_pairs={{0,4},{4,8},{8,12},{12,16},{16,20},{20,24},{24,28},{1,5},{5,9},{9,... | collective-permute-start | bytes 98312 | tf_op jit(solution)/shard_map/ppermute | solution.py:10
  165.9 6.7 %collective-permute-start.9 = (bf16[64,256]{1,0:T(8,128)(2,1)S(1)}, bf16[64,256]{1,0:T(8,128)(2,1)S(1)}, u32[]{:S(2)}, u32[]{:S(2)}) collective-permute-start(bf16[64,256]{1,0:T(8,128)(2,1)S(1)} %slice.130), channel_id=1, source_target_pairs={{4,0},{8,4},{12,8},{16,12},{20,16},{24,20},{28,24},{5,1},{9,5},{13... | collective-permute-start | bytes 98312 | tf_op jit(solution)/shard_map/ppermute | solution.py:10
  189.9 1.0 copy-start.4
where the time goes:
time: 195 us; the launch traced here: 192 us
  blocking collectives  118 us (61%)
  starting transfers between devices  27.7 us (14%)
  waiting for transfers between devices  19.5 us (10%)
  local copies, waits for them, and re-layouts  15.2 us (8%)
  matrix products  9.97 us (5%)
    psum x4, blocking collectives, body(): compressed = lax.psum(partial_terms, 'rhs').astype(jnp.bfloat16)  52.9 us
    ppermute x10, starting transfers between devices, from_behind(): return lax.ppermute(block, axis, route)  27.7 us
    psum x2, blocking collectives, body(): current = lax.psum(partial_terms, 'rhs').astype(jnp.bfloat16)  21.3 us
    ppermute x10, waiting for transfers between devices, from_behind(): return lax.ppermute(block, axis, route)  19.5 us
    all_gather x3, blocking collectives, body(): lax.all_gather(node_values.astype(jnp.bfloat16), 'rhs', axis=2, tiled=True)  16.7 us
    all_gather x3, blocking collectives, body(): shares = lax.all_gather(shares, 'rhs', axis=1, tiled=True)  15.8 us
    gather x2, local copies, waits for them, and re-layouts, body(): jnp.take(gathered, point_order, axis=1)  12.5 us
    all_gather x1, blocking collectives, body(): gathered = lax.all_gather(right_side, 'rhs', axis=1, tiled=True)  11.5 us
  transfers between devices with their start and end apart: 10, of which 8 were waited for; matrix products, arithmetic and copies ran while one was open for 0% of the time, Pallas kernels for 0%

commit v1 on v0

v1 whole, which is shorter than its diff:
```python
import functools

import jax
import jax.numpy as jnp
from jax import lax
from jax.experimental import pallas as pl
from jax.experimental.pallas import tpu as pltpu
from jax.sharding import PartitionSpec as P

LANES = 256
PIECES = (0, 2, 1, 3)
CORES = 2


def params(mebibytes=12):
    return pltpu.CompilerParams(vmem_limit_bytes=mebibytes * 1024 * 1024)


def cost(flops, moved):
    return pl.CostEstimate(flops=flops // 1000, bytes_accessed=moved // 1000, transcendentals=0)


def dot_rows(left, right):
    return lax.dot_general(
        left, right, (((1,), (1,)), ((), ())), preferred_element_type=jnp.float32
    )


def half_levels(per_dev):
    levels = []
    base = 0
    for height in range(1, per_dev.bit_length() - 1):
        node_count = per_dev >> height
        levels.append((base, node_count // 2, per_dev - 2 * node_count))
        base += node_count // 2
    return levels, base


def pack_kernel(per_dev, inverse, basis, coupling, *refs):
    targets, buffers, (sems, out_sems) = refs[:4], refs[4:8], refs[8:]
    factors, couplings, keep, cross = buffers
    levels, total = half_levels(per_dev)
    high = lax.axis_index("rhs") // CORES
    node_size = inverse.shape[2]
    rank = basis.shape[2]
    parts = (
        (inverse, 0, node_size),
        (basis, node_size, rank),
        (coupling, node_size + rank, rank),
    )
    copies = []
    for source, start, width in parts:
        columns = pl.ds(start, width)
        for base, count, offset in levels:
            mine = source.at[pl.ds(offset + high * count, count)]
            other = source.at[pl.ds(offset + (1 - high) * count, count)]
            if source is coupling:
                for n in range(count):
                    sent = couplings.at[:, pl.ds((base + n) * rank, rank)]
                    copies.append((other.at[n], sent))
            else:
                copies.append((other, factors.at[pl.ds(base, count), :, columns]))
            copies.append((mine, keep.at[pl.ds(base, count), :, columns]))
        copies.append((source.at[per_dev - 2], keep.at[total, :, columns]))
        copies.append((source.at[per_dev - 1], cross.at[:, columns]))
    started = []
    for i, (source, target) in enumerate(copies):
        copy = pltpu.make_async_copy(source, target, sems.at[i])
        copy.start()
        started.append(copy)
    for copy in started:
        copy.wait()
    started = []
    for i, (buffer, target) in enumerate(zip(buffers, targets)):
        copy = pltpu.make_async_copy(buffer, target, out_sems.at[i])
        copy.start()
        started.append(copy)
    for copy in started:
        copy.wait()


def pack(inverse, basis, coupling):
    per_dev, rows, node_size = inverse.shape
    rank = basis.shape[2]
    width = node_size + 2 * rank
    levels, total = half_levels(per_dev)
    shapes = [
        (total, rows, node_size + rank),
        (rows, total * rank),
        (total + 1, rows, width),
        (rows, width),
    ]
    return pl.pallas_call(
        functools.partial(pack_kernel, per_dev),
        in_specs=[pl.BlockSpec(memory_space=pl.ANY)] * 3,
        out_specs=[pl.BlockSpec(memory_space=pl.ANY)] * 4,
        out_shape=[jax.ShapeDtypeStruct(shape, inverse.dtype) for shape in shapes],
        scratch_shapes=[pltpu.VMEM(shape, inverse.dtype) for shape in shapes]
        + [pltpu.SemaphoreType.DMA((6 + 5 * len(levels) + total,)), pltpu.SemaphoreType.DMA((4,))],
        compiler_params=params(63),
        cost_estimate=cost(0, 4 * per_dev * rows * width),
    )(inverse, basis, coupling)


def climb_kernel(level, mine_ref, other_ref, ancestor_ref, carrier_ref):
    right = (lax.axis_index("leaf") // (1 << level)) % 2 == 1
    keep = carrier_ref.shape[1]

    @pl.when(right)
    def _():
        ancestor_ref[...] = mine_ref[...]
        carrier_ref[...] = other_ref[:, :keep]

    @pl.when(jnp.logical_not(right))
    def _():
        ancestor_ref[...] = other_ref[...]
        carrier_ref[...] = mine_ref[:, :keep]


def climb(level, mine, other, keep):
    return pl.pallas_call(
        functools.partial(climb_kernel, level),
        out_shape=[
            pltpu.VMEM(mine.shape, mine.dtype),
            pltpu.VMEM((mine.shape[0], keep), mine.dtype),
        ],
        compiler_params=params(),
        cost_estimate=cost(0, 4 * mine.size),
    )(mine, other)


def join_kernel(*refs):
    *blocks, _, out_ref = refs
    start = 0
    for ref in blocks:
        width = ref.shape[1]
        out_ref[:, start : start + width] = ref[...]
        start += width


def join(blocks, anchor):
    rows = blocks[0].shape[0]
    width = sum(block.shape[1] for block in blocks)
    return pl.pallas_call(
        join_kernel,
        out_shape=pltpu.VMEM((rows, width), blocks[0].dtype),
        compiler_params=params(),
        cost_estimate=cost(0, 4 * rows * width),
    )(*blocks, anchor)


def leaf_kernel(count, side_ref, *refs):
    points, refs = refs[:count], refs[count:]
    order_ref, inverse_ref, basis_ref, values_ref, same_ref, cross_ref, *rest = refs
    targets = values_ref.shape[1]
    stacked = rest[0] if rest else points[0]
    chunks, pieces = stacked.shape[:2]

    if rest:

        @pl.when(pl.program_id(0) == 0)
        def _():
            place = lax.axis_index("rhs")
            for flip, points_ref in zip(PIECES, points):
                for w in range(pieces):
                    stacked[place ^ flip, w] = points_ref[:, w * LANES : (w + 1) * LANES]

    order = order_ref[...]
    high = order // LANES
    low = order % LANES
    rows = lax.broadcasted_iota(jnp.int32, (LANES, order.shape[1]), 0)
    pick = jnp.where(rows == low, 1.0, 0.0).astype(jnp.bfloat16)
    spread = jnp.dot(
        stacked[...].reshape(-1, LANES), pick, preferred_element_type=jnp.float32
    )
    ordered = jnp.zeros((targets, order.shape[1]), jnp.float32)
    for k in range(chunks * pieces):
        ordered = jnp.where(high == k, spread[k * targets : (k + 1) * targets, :], ordered)
    values = dot_rows(ordered.astype(jnp.bfloat16), inverse_ref[0])
    values_ref[0] = values
    partial = jnp.dot(
        values.astype(jnp.bfloat16), basis_ref[0], preferred_element_type=jnp.float32
    ).astype(jnp.bfloat16)
    share = targets // CORES
    for core in range(CORES):

        @pl.when(side_ref[1] == core)
        def _():
            same_ref[0] = partial[core * share : (core + 1) * share]
            cross_ref[0] = partial[(1 - core) * share : (2 - core) * share]


def leaf_up(side, points, point_order, leaf_inverse, leaf_basis):
    leaves, rows, leaf_size = leaf_inverse.shape
    rank = leaf_basis.shape[2]
    half = leaves // 2
    joined = points[0].ndim == 4
    if joined:
        shape = points[0].shape
    else:
        targets, width = points[0].shape
        shape = (len(points), width // LANES, targets, LANES)
    targets = shape[2]
    share = targets // CORES
    sent = jax.ShapeDtypeStruct((half, share, rank), jnp.bfloat16)
    out_specs = [
        pl.BlockSpec((1, targets, rows), lambda i, side: (i, 0, 0)),
        pl.BlockSpec((1, share, rank), lambda i, side: (i, 0, 0)),
        pl.BlockSpec((1, share, rank), lambda i, side: (i, 0, 0)),
    ]
    out_shape = [jax.ShapeDtypeStruct((half, targets, rows), jnp.float32), sent, sent]
    if not joined:
        out_specs.append(pl.BlockSpec(shape, lambda i, side: (0, 0, 0, 0)))
        out_shape.append(pltpu.VMEM(shape, jnp.bfloat16))
    point_specs = [
        pl.BlockSpec(block.shape, lambda i, side, rank=block.ndim: (0,) * rank) for block in points
    ]
    return pl.pallas_call(
        functools.partial(leaf_kernel, len(points)),
        grid_spec=pltpu.PrefetchScalarGridSpec(
            num_scalar_prefetch=1,
            grid=(half,),
            in_specs=[
                *point_specs,
                pl.BlockSpec((1, leaf_size), lambda i, side: (0, side[0] * half + i)),
                pl.BlockSpec((1, rows, leaf_size), lambda i, side: (side[0] * half + i, 0, 0)),
                pl.BlockSpec((1, rows, rank), lambda i, side: (side[0] * half + i, 0, 0)),
            ],
            out_specs=out_specs,
        ),
        out_shape=out_shape,
        compiler_params=params(),
        cost_estimate=cost(
            leaves * targets * leaf_size * (shape[0] * shape[1] * LANES + 2 * rows),
            leaves * rows * (leaf_size + rank + 3 * targets),
        ),
    )(side, *points, point_order.reshape(1, -1), leaf_inverse, leaf_basis)


def solve_node(stacked, inverses, bases, solved_ref):
    mine = lax.axis_index("rhs")
    total = None
    for flip, inverse, basis in zip(PIECES, inverses, bases):
        solved = dot_rows(stacked, inverse)
        solved_ref[mine ^ flip] = solved
        term = jnp.dot(solved.astype(jnp.bfloat16), basis, preferred_element_type=jnp.float32)
        total = term if total is None else total + term
    return total


def group_up_kernel(per_dev, *refs):
    *refs, solved_ref, out_ref = refs
    parts, packs = refs[: 2 * CORES], refs[2 * CORES :]
    levels, _ = half_levels(per_dev)
    rank = parts[0].shape[2]

    def pieces(node, start, width):
        return [ref[node, :, pl.ds(start, width)] for ref in packs]

    sums = sum(ref[...].astype(jnp.float32) for ref in parts).astype(jnp.bfloat16)
    current = [sums[i] for i in range(sums.shape[0])]
    for base, count, _ in levels:
        following = []
        for n in range(count):
            node = base + n
            compressed = solve_node(
                jnp.concatenate([current[2 * n], current[2 * n + 1]], axis=1),
                pieces(node, 0, 2 * rank),
                pieces(node, 2 * rank, rank),
                solved_ref.at[node],
            )
            following.append(compressed.astype(jnp.bfloat16))
        current = following
    out_ref[...] = current[0]


def group_up(per_dev, parts, packs):
    leaves, share, rank = parts[0].shape
    _, total = half_levels(per_dev)
    _, rows, width = packs[0].shape
    return pl.pallas_call(
        functools.partial(group_up_kernel, per_dev),
        out_shape=[
            jax.ShapeDtypeStruct((total, 2 * CORES, share, rows), jnp.float32),
            jax.ShapeDtypeStruct((share, rank), jnp.bfloat16),
        ],
        compiler_params=params(),
        cost_estimate=cost(24 * total * share * rows * rank, 8 * total * rows * width),
    )(*parts, *packs)


def order_pair(right, mine, other):
    return jnp.concatenate([jnp.where(right, other, mine), jnp.where(right, mine, other)], axis=1)


def half_up_kernel(mine_ref, other_ref, own_ref, near_ref, solved_ref, out_ref):
    rank = mine_ref.shape[1]
    place = lax.axis_index("rhs")
    stacked = order_pair(place // CORES == 1, mine_ref[...], other_ref[...])
    total = 0.0
    for flip, ref in enumerate((own_ref, near_ref)):
        solved = dot_rows(stacked, ref[0, :, : 2 * rank])
        solved_ref[(place ^ flip) % CORES] = solved
        total += jnp.dot(
            solved.astype(jnp.bfloat16),
            ref[0, :, 2 * rank : 3 * rank],
            preferred_element_type=jnp.float32,
        )
    out_ref[...] = total.astype(jnp.bfloat16)


def half_up(mine, other, own, near):
    share, rank = mine.shape
    nodes, rows, width = own.shape
    last = pl.BlockSpec((1, rows, width), lambda i: (nodes - 1, 0, 0))
    whole = pl.BlockSpec((share, rank), lambda i: (0, 0))
    return pl.pallas_call(
        half_up_kernel,
        grid=(1,),
        in_specs=[whole, whole, last, last],
        out_specs=[pl.BlockSpec((CORES, share, rows), lambda i: (0, 0, 0)), whole],
        out_shape=[
            jax.ShapeDtypeStruct((CORES, share, rows), jnp.float32),
            jax.ShapeDtypeStruct((share, rank), jnp.bfloat16),
        ],
        compiler_params=params(),
        cost_estimate=cost(12 * share * rows * rank, 4 * rows * width),
    )(mine, other, own, near)


def total_of(refs):
    if len(refs) == 1:
        return refs[0][...]
    return sum(ref[...].astype(jnp.float32) for ref in refs).astype(jnp.bfloat16)


def cross_pair(level, refs):
    half = len(refs) // 2
    is_right = (lax.axis_index("leaf") // (1 << level)) % 2 == 1
    return order_pair(is_right, total_of(refs[:half]), total_of(refs[half:]))


def cross_up_kernel(level, *refs):
    *refs, solved_ref, out_ref = refs
    inputs, packs = refs[: -2 * CORES], refs[-2 * CORES :]
    rank = out_ref.shape[1]
    compressed = solve_node(
        cross_pair(level, inputs),
        [ref[:, : 2 * rank] for ref in packs],
        [ref[:, 2 * rank : 3 * rank] for ref in packs],
        solved_ref,
    )
    out_ref[...] = compressed.astype(jnp.bfloat16)


def cross_up(level, inputs, packs):
    share, rank = inputs[0].shape[-2:]
    rows, width = packs[0].shape
    return pl.pallas_call(
        functools.partial(cross_up_kernel, level),
        out_shape=[
            jax.ShapeDtypeStruct((2 * CORES, share, rows), jnp.float32),
            jax.ShapeDtypeStruct((share, rank), jnp.bfloat16),
        ],
        compiler_params=params(),
        cost_estimate=cost(24 * share * rows * rank, 8 * rows * width),
    )(*inputs, *packs)


def down_kernel(per_dev, cross_levels, input_count, *refs):
    *refs, out_ref, value = refs
    inputs, refs = refs[:input_count], refs[input_count:]
    solved_cross, refs = refs[: cross_levels - 1], refs[cross_levels - 1 :]
    solved_top, solved_half, refs = refs[0], refs[1], refs[2:]
    count = 2 * CORES * (cross_levels - 1)
    cross_packs, (own_top, tail, near_tail, keep, keep_near) = refs[:count], refs[count:]
    levels, total = half_levels(per_dev)
    rank = out_ref.shape[2]
    node_size = 2 * rank
    place = lax.axis_index("rhs")

    def pieces(level):
        return zip(PIECES, cross_packs[2 * CORES * level : 2 * CORES * (level + 1)])

    def choose(which):
        return jnp.concatenate([value[2 * which], value[2 * which + 1]], axis=1)

    def side(level):
        return (lax.axis_index("leaf") // (1 << level)) % 2

    def columns(ref):
        width = ref.shape[-1]
        return pl.ds(width - rank, rank)

    stacked = cross_pair(cross_levels - 1, inputs)
    tops = (
        own_top[...],
        tail[:, :node_size],
        near_tail[:, :node_size],
        near_tail[:, node_size : 2 * node_size],
    )
    for flip, block in zip(PIECES, tops):
        value[place ^ flip] = dot_rows(stacked, block).astype(jnp.bfloat16)
    incoming = choose(side(cross_levels - 1))
    for level in range(cross_levels - 2, -1, -1):
        for flip, ref in pieces(level):
            piece = place ^ flip
            solved = solved_cross[level][piece]
            value[piece] = (solved - dot_rows(incoming, ref[:, columns(ref)])).astype(jnp.bfloat16)
        incoming = choose(side(level))

    for flip, ref in ((0, keep), (1, keep_near)):
        piece = (place ^ flip) % CORES
        coupling = ref[total, :, columns(ref)]
        value[piece] = (solved_top[piece] - dot_rows(incoming, coupling)).astype(jnp.bfloat16)
    current = [choose(0)]
    for base, count, _ in reversed(levels):
        following = []
        for n in range(count):
            node = base + n
            start = node_size + node * rank
            couplings = (
                keep[node, :, columns(keep)],
                tail[:, start : start + rank],
                keep_near[node, :, columns(keep)],
                near_tail[:, node_size + start : node_size + start + rank],
            )
            for flip, coupling in zip(PIECES, couplings):
                piece = place ^ flip
                value[piece] = (
                    solved_half[node, piece] - dot_rows(current[n], coupling)
                ).astype(jnp.bfloat16)
            following += [choose(0), choose(1)]
        current = following
    for i, block in enumerate(current):
        out_ref[i] = block


def way_down(per_dev, inputs, solved_cross, solved_top, solved_half, cross_packs, others):
    share, rank = inputs[0].shape[-2:]
    rows = solved_half.shape[3]
    operands = [*inputs, *solved_cross, solved_top, solved_half]
    for packs in cross_packs:
        operands += packs
    operands += others
    return pl.pallas_call(
        functools.partial(down_kernel, per_dev, len(cross_packs) + 1, len(inputs)),
        out_shape=jax.ShapeDtypeStruct((per_dev // 2, share, rank), jnp.bfloat16),
        scratch_shapes=[pltpu.VMEM((2 * CORES, share, rows), jnp.bfloat16)],
        compiler_params=params(18),
        cost_estimate=cost(8 * share * rows * rank * per_dev, 4 * 1024 * 1024),
    )(*operands)


def finish_kernel(far_ref, own_ref, incoming_ref, coupling_ref, out_ref):
    half = own_ref.shape[0]
    high = lax.axis_index("rhs") // CORES
    for values_ref, side in ((far_ref, 1 - high), (own_ref, high)):
        for i in range(half):
            leaf = side * half + i
            incoming = jnp.concatenate(
                [incoming_ref[side * CORES + core, i] for core in range(CORES)], axis=0
            )
            out_ref[leaf] = values_ref[i] - dot_rows(incoming, coupling_ref[leaf])


def finish(far, own, incoming, coupling):
    half, targets, rows = own.shape
    return pl.pallas_call(
        finish_kernel,
        out_shape=jax.ShapeDtypeStruct((2 * half, targets, rows), jnp.float32),
        compiler_params=params(),
        cost_estimate=cost(4 * half * targets * rows * coupling.shape[2], 16 * own.size),
    )(far, own, incoming, coupling)


def swap(block, axis, bit):
    return lax.ppermute(block, axis, [(i, i ^ bit) for i in range(lax.axis_size(axis))])


def far_swap(block, leaf_bit, rhs_bit):
    shares = lax.axis_size("rhs")
    flip = leaf_bit * shares + rhs_bit
    count = lax.axis_size("leaf") * shares
    return lax.ppermute(block, ("leaf", "rhs"), [(i, i ^ flip) for i in range(count)])


def after(value, anchor):
    return lax.optimization_barrier((value, anchor))[0]


def body(
    right_side,
    point_order,
    leaf_inverse,
    leaf_basis,
    leaf_coupling,
    node_inverse,
    node_basis,
    node_coupling,
):
    devices = lax.axis_size("leaf")
    per_dev = leaf_inverse.shape[0]
    node_size = node_inverse.shape[2]
    cross_levels = devices.bit_length() - 1
    place = lax.axis_index("rhs")
    high, low = place // CORES, place % CORES

    def rise(carrier, level, anchor):
        other = after(swap(carrier, "leaf", 1 << level), anchor)
        width = node_size if level >= cross_levels - 2 else carrier.shape[1]
        return climb(level, carrier, other, width)

    send, send_coupling, keep, carrier = pack(node_inverse, node_basis, node_coupling)
    across, beside = after(
        [swap(right_side, "rhs", CORES), swap(right_side, "rhs", 1)], send
    )
    points = [across, beside, swap(after(across, beside), "rhs", 1)]
    half_far = swap(send, "rhs", CORES)
    keep_near = swap(after(keep, points), "rhs", 1)
    carrier = after(carrier, points)
    points = [right_side, *points]

    leaves = (point_order, leaf_inverse, leaf_basis)
    far_values, far_same, far_cross, joined = leaf_up(
        jnp.stack([1 - high, low]), points, *leaves
    )
    keep_near = after(keep_near, far_same)
    own_values, own_same, own_cross = leaf_up(
        jnp.stack([high, low]), [after(joined, keep_near)], *leaves
    )
    ancestor, carrier = rise(carrier, 0, own_same)
    ancestors = [ancestor]
    far_same = after(swap(far_same, "rhs", CORES), own_same)
    far_cross = after(swap(far_cross, "rhs", CORES + 1), own_same)
    parts = [own_same, far_same, swap(own_cross, "rhs", 1), far_cross]
    half_far = after(half_far, (parts, carrier))
    half_near = swap(half_far, "rhs", 1)
    fars = [swap(after(ancestors[0], half_far), "rhs", CORES)]
    nears = [swap(after(ancestors[0], half_far), "rhs", 1)]

    solved_half, current = group_up(per_dev, parts, [keep, half_far, keep_near, half_near])
    other = swap(after(current, nears[0]), "rhs", CORES)
    ancestor, carrier = rise(carrier, 1, other)
    ancestors.append(ancestor)
    solved_top, current = half_up(current, other, keep, keep_near)
    fars[0] = after(fars[0], other)
    near_far = swap(fars[0], "rhs", 1)
    cross_packs = [[ancestors[0], fars[0], nears[0], near_far]]
    fars.append(swap(join([ancestors[1]], current), "rhs", CORES))
    current = after(current, near_far)
    inputs = [
        current,
        swap(current, "rhs", CORES),
        swap(current, "leaf", 1),
        far_swap(current, 1, CORES),
    ]

    solved_cross = []
    for level in range(cross_levels - 1):
        if level > 0:
            own, far = ancestors[level], fars[level]
            own_near = swap(join([own], current), "rhs", 1)
            far_near = swap(join([far], current), "rhs", 1)
            cross_packs.append([own, far, own_near, far_near])
        solved, current = cross_up(level, inputs, cross_packs[level])
        solved_cross.append(solved)
        inputs = [current, swap(current, "leaf", 2 << level)]
        if level == 0:
            for later in range(2, cross_levels):
                ancestor, carrier = rise(carrier, later, current)
                ancestors.append(ancestor)
            for later in range(2, cross_levels - 1):
                fars.append(swap(join([ancestors[later]], current), "rhs", CORES))
            tail = swap(join([ancestors[-1], send_coupling], current), "rhs", CORES)

    near_tail = swap(join([ancestors[-1], tail], inputs[1]), "rhs", 1)
    others = [ancestors[-1], tail, near_tail, keep, keep_near]
    shares = way_down(per_dev, inputs, solved_cross, solved_top, solved_half, cross_packs, others)
    incoming = lax.all_gather(shares, "rhs", axis=0)
    return finish(far_values, own_values, incoming, leaf_coupling)


def solution(mesh):
    placed = (P(None, ("leaf", "rhs")), P("leaf")) + (P("leaf", "rhs", None),) * 6
    return jax.shard_map(
        body, mesh=mesh, in_specs=placed, out_specs=P("leaf", None, "rhs"), check_vma=False
    )
```

time: 195 us -> 69.8 us (0.36); the launches traced: 192 us -> 69.6 us
  blocking collectives: 118 us -> 5.79 us
  Pallas kernels: 0 us -> 15.8 us
  local copies, waits for them, and re-layouts: 15.2 us -> 1.51 us
  matrix products: 9.97 us -> 0 us
    psum x6 -> x0, blocking collectives: 74.3 us -> none  [the longest x4 52.9 us: body(): compressed = lax.psum(partial_terms, 'rhs').astype(jnp.bfloat16)]
    all_gather x7 -> x1, blocking collectives: 44 us -> 5.79 us  [body(): incoming = lax.all_gather(shares, 'rhs', axis=0)]
    pallas_call x0 -> x17, Pallas kernels: none -> 15.8 us  [the longest x2 6.81 us: leaf_up(): pl.pallas_call(functools.partial(leaf_kernel, len(points)), grid_spec=plt...]
    gather x2 -> x0, local copies, waits for them, and re-layouts: 12.5 us -> none  [body(): jnp.take(gathered, point_order, axis=1)]
    dot_general x19 -> x0, matrix products: 9.97 us -> none  [the longest x3 3.61 us: body(): jnp.einsum('nsj,nij->nsi', stacked, node_inverse[offset:offset + node_cou...]
    ppermute x10 -> x26, starting transfers between devices: 27.7 us -> 26.2 us  [the longest x25 24.2 us: swap(): lax.ppermute(block, axis, [(i, i ^ bit) for i in range(lax.axis_size(axis...]
    ppermute x10 -> x26, waiting for transfers between devices: 19.5 us -> 20 us  [the longest x25 17.3 us: swap(): lax.ppermute(block, axis, [(i, i ^ bit) for i in range(lax.axis_size(axis...]
  transfers between devices with their start and end apart: 10 -> 26, of which waited for: 8 -> 12; matrix products, arithmetic and copies ran while one was open for 0% -> 0% of each run, Pallas kernels for 0% -> 20%
where the time goes in v1:
time: 69.8 us; the launch traced here: 69.6 us
  starting transfers between devices  26.2 us (38%)
  waiting for transfers between devices  20 us (29%)
  Pallas kernels  15.8 us (23%)
  blocking collectives  5.79 us (8%)
  local copies, waits for them, and re-layouts  1.51 us (2%)
    ppermute x25, starting transfers between devices, swap(): lax.ppermute(block, axis, [(i, i ^ bit) for i in range(lax.axis_size(axis...  24.2 us
    ppermute x25, waiting for transfers between devices, swap(): lax.ppermute(block, axis, [(i, i ^ bit) for i in range(lax.axis_size(axis...  17.3 us
    pallas_call x2, Pallas kernels, leaf_up(): pl.pallas_call(functools.partial(leaf_kernel, len(points)), grid_spec=plt...  6.81 us
    all_gather x1, blocking collectives, body(): incoming = lax.all_gather(shares, 'rhs', axis=0)  5.79 us
    pallas_call x1, Pallas kernels, pack(): pl.pallas_call(functools.partial(pack_kernel, per_dev), in_specs=[pl.Bloc...  2.99 us
    ppermute x1, waiting for transfers between devices, far_swap(): lax.ppermute(block, ('leaf', 'rhs'), [(i, i ^ flip) for i in range(count)])  2.62 us
    ppermute x1, starting transfers between devices, far_swap(): lax.ppermute(block, ('leaf', 'rhs'), [(i, i ^ flip) for i in range(count)])  1.99 us
    unnamed x16, local copies, waits for them, and re-layouts  1.51 us
  transfers between devices with their start and end apart: 26, of which 12 were waited for; matrix products, arithmetic and copies ran while one was open for 0% of the time, Pallas kernels for 20%

profile of v1, /device:TPU:0, one launch (start us, length us, event | category | flops | bytes accessed | tf_op | source)
XLA Modules:
  0.0 69.6 jit_solution(9670148923457819284)
XLA Ops:
  0.0 2.9 %collective-permute-start = (bf16[64,1024]{1,0:T(8,128)(2,1)}, bf16[64,1024]{1,0:T(8,128)(2,1)S(1)}, u32[]{:S(2)}, u32[]{:S(2)}) collective-permute-start(bf16[64,1024]{1,0:T(8,128)(2,1)} %refs_0_.1), channel_id=1, source_target_pairs={{0,2},{1,3},{2,0},{3,1},{4,6},{5,7},{6,4},{7,5},{8,10},{9,11},{10,... | collective-permute-start | bytes 393224 | tf_op jit(solution)/shard_map/ppermute | solution.py:478
  2.9 3.0 %shard_map.82 = (bf16[3,128,768]{2,1,0:T(8,128)(2,1)}, bf16[128,768]{1,0:T(8,128)(2,1)}, bf16[4,128,1024]{2,1,0:T(8,128)(2,1)}, bf16[128,1024]{1,0:T(8,128)(2,1)}) custom-call(bf16[8,128,512]{2,1,0:T(8,128)(2,1)} %inverse.1, bf16[8,128,256]{2,1,0:T(8,128)(2,1)} %basis.1, bf16[8,128,256]{2,1,0:T(8,128)(2,1)} %coupling.1), custom_call_target="tpu_custom_call" | custom-call | bytes 4194 | tf_op jit(solution)/shard_map/pallas_call | solution.py:93
  5.9 0.7 %collective-permute-done.refs_1_ = bf16[64,1024]{1,0:T(8,128)(2,1)S(1)} collective-permute-done((bf16[64,1024]{1,0:T(8,128)(2,1)}, bf16[64,1024]{1,0:T(8,128)(2,1)S(1)}, u32[]{:S(2)}, u32[]{:S(2)}) %collective-permute-start) | collective-permute-done | bytes 131104 | tf_op jit(solution)/shard_map/ppermute | solution.py:478
  6.7 1.3 %collective-permute-done.2.refs_3_ = bf16[64,1024]{1,0:T(8,128)(2,1)S(1)} collective-permute-done((bf16[64,1024]{1,0:T(8,128)(2,1)S(1)}, bf16[64,1024]{1,0:T(8,128)(2,1)S(1)}, u32[]{:S(2)}, u32[]{:S(2)}) %collective-permute-start.2) | collective-permute-done | bytes 131104 | tf_op jit(solution)/shard_map/ppermute | solution.py:478
  8.0 0.1 collective-permute-start.3
  8.1 1.8 %collective-permute-start.7 = (bf16[3,128,768]{2,1,0:T(8,128)(2,1)}, bf16[3,128,768]{2,1,0:T(8,128)(2,1)S(1)}, u32[]{:S(2)}, u32[]{:S(2)}) collective-permute-start(bf16[3,128,768]{2,1,0:T(8,128)(2,1)} %get-tuple-element.46), channel_id=1, source_target_pairs={{0,2},{1,3},{2,0},{3,1},{4,6},{5,7},{6,4},{7,5},{8,10},{9,11},{10,... | collective-permute-start | bytes 1769480 | tf_op jit(solution)/shard_map/ppermute | solution.py:478
  9.9 1.5 %collective-permute-start.8 = (bf16[128,1024]{1,0:T(8,128)(2,1)}, bf16[128,1024]{1,0:T(8,128)(2,1)S(1)}, u32[]{:S(2)}, u32[]{:S(2)}) collective-permute-start(bf16[128,1024]{1,0:T(8,128)(2,1)} %get-tuple-element.64.mine_ref), channel_id=1, source_target_pairs={{0,4},{4,0},{8,12},{12,8},{16,20},{20,16},{24,28},{28,24},{1,5},{5... | collective-permute-start | bytes 786440 | tf_op jit(solution)/shard_map/ppermute | solution.py:478
  11.4 0.1 pad_add_fusion.side_ref
  11.5 0.1 pad_add_fusion.1.side_ref
  11.6 1.2 %copy-done.1 = bf16[8,128,512]{2,1,0:T(8,128)(2,1)S(1)} copy-done((bf16[8,128,512]{2,1,0:T(8,128)(2,1)S(1)}, bf16[8,128,512]{2,1,0:T(8,128)(2,1)}, u32[]{:S(2)}) %copy-start.1) | copy-done | bytes 1048600
  12.8 3.4 %shard_map.83 = (f32[4,64,128]{2,1,0:T(8,128)S(1)}, bf16[4,32,256]{2,1,0:T(8,128)(2,1)S(1)}, bf16[4,32,256]{2,1,0:T(8,128)(2,1)S(1)}, bf16[4,4,64,256]{3,2,1,0:T(8,128)(2,1)S(1)}) custom-call(s32[2]{0:T(128)S(1)} %pad_add_fusion.side_ref, bf16[64,1024]{1,0:T(8,128)(2,1)S(1)} %copy-done.6, bf16[64,1024]{1,0:T(8,128)(2,1)S(1)} %collective-permute-done.refs_1_, ...), custom_call_target="tpu_custom_call" | custom-call | flops 1140850 | bytes 983 | tf_op jit(solution)/shard_map/pallas_call | solution.py:218
  16.2 0.1 collective-permute-start.6
  16.3 1.4 %collective-permute-start.4 = (bf16[4,32,256]{2,1,0:T(8,128)(2,1)S(1)}, bf16[4,32,256]{2,1,0:T(8,128)(2,1)S(1)}, u32[]{:S(2)}, u32[]{:S(2)}) collective-permute-start(bf16[4,32,256]{2,1,0:T(8,128)(2,1)S(1)} %get-tuple-element.54), channel_id=1, source_target_pairs={{0,2},{1,3},{2,0},{3,1},{4,6},{5,7},{6,4},{7,5},{8,10},{9,11},{10,... | collective-permute-start | bytes 196616 | tf_op jit(solution)/shard_map/ppermute | solution.py:478
  17.7 3.4 %shard_map.84 = (f32[4,64,128]{2,1,0:T(8,128)S(1)}, bf16[4,32,256]{2,1,0:T(8,128)(2,1)S(1)}, bf16[4,32,256]{2,1,0:T(8,128)(2,1)S(1)}) custom-call(s32[2]{0:T(128)S(1)} %pad_add_fusion.1.side_ref, bf16[4,4,64,256]{3,2,1,0:T(8,128)(2,1)S(1)} %get-tuple-element.56.refs_0_, s32[1,4096]{1,0:T(1,128)S(1)} %bitcast.7, bf16[8,128,512]{2,1,0:T(8,128)(2,1)S(1)} %copy-done.1, ...), custom_call_target="tpu_custom_call" | custom-call | flops 1140850 | bytes 983 | tf_op jit(solution)/shard_map/pallas_call | solution.py:218
  21.1 0.5 collective-permute-start.5
  21.7 3.5 %collective-permute-done.6.refs_3_ = bf16[4,32,256]{2,1,0:T(8,128)(2,1)S(1)} collective-permute-done((bf16[4,32,256]{2,1,0:T(8,128)(2,1)S(1)}, bf16[4,32,256]{2,1,0:T(8,128)(2,1)S(1)}, u32[]{:S(2)}, u32[]{:S(2)}) %collective-permute-start.6) | collective-permute-done | bytes 65568 | tf_op jit(solution)/shard_map/ppermute | solution.py:478
  25.2 1.6 %collective-permute-done.4.refs_1_ = bf16[4,32,256]{2,1,0:T(8,128)(2,1)S(1)} collective-permute-done((bf16[4,32,256]{2,1,0:T(8,128)(2,1)S(1)}, bf16[4,32,256]{2,1,0:T(8,128)(2,1)S(1)}, u32[]{:S(2)}, u32[]{:S(2)}) %collective-permute-start.4) | collective-permute-done | bytes 65568 | tf_op jit(solution)/shard_map/ppermute | solution.py:478
  26.8 0.5 collective-permute-start.10
  27.3 1.7 %collective-permute-start.12 = (bf16[128,1024]{1,0:T(8,128)(2,1)S(1)}, bf16[128,1024]{1,0:T(8,128)(2,1)S(1)}, u32[]{:S(2)}, u32[]{:S(2)}) collective-permute-start(bf16[128,1024]{1,0:T(8,128)(2,1)S(1)} %get-tuple-element.70.refs_4_.refs_6_), channel_id=1, source_target_pairs={{0,2},{1,3},{2,0},{3,1},{4,6},{5,7},{6,4},{7,5},{8,10},{9,11},{10,... | collective-permute-start | bytes 786440 | tf_op jit(solution)/shard_map/ppermute | solution.py:478
  29.0 1.6 %collective-permute-start.18 = (bf16[128,1024]{1,0:T(8,128)(2,1)S(1)}, bf16[128,1024]{1,0:T(8,128)(2,1)S(1)}, u32[]{:S(2)}, u32[]{:S(2)}) collective-permute-start(bf16[128,1024]{1,0:T(8,128)(2,1)S(1)} %get-tuple-element.66.mine_ref), channel_id=1, source_target_pairs={{0,8},{4,12},{8,0},{12,4},{16,24},{20,28},{24,16},{28,20},{1,9},{5... | collective-permute-start | bytes 786440 | tf_op jit(solution)/shard_map/ppermute | solution.py:478
  30.6 1.5 %shard_map.86 = (f32[3,4,32,128]{3,2,1,0:T(8,128)S(1)}, bf16[32,256]{1,0:T(8,128)(2,1)S(1)}) custom-call(bf16[4,32,256]{2,1,0:T(8,128)(2,1)S(1)} %get-tuple-element.58.refs_0_, bf16[4,32,256]{2,1,0:T(8,128)(2,1)S(1)} %collective-permute-done.4.refs_1_, bf16[4,32,256]{2,1,0:T(8,128)(2,1)S(1)} %collective-permute-done.5.refs_2_, ...), custom_call_target="tpu_custom_call" | custom-call | flops 75497 | bytes 3145 | tf_op jit(solution)/shard_map/pallas_call | solution.py:281
  32.1 0.6 collective-permute-start.11
  32.7 3.0 %collective-permute-done.12.refs_5_.refs_7_ = bf16[128,1024]{1,0:T(8,128)(2,1)S(1)} collective-permute-done((bf16[128,1024]{1,0:T(8,128)(2,1)S(1)}, bf16[128,1024]{1,0:T(8,128)(2,1)S(1)}, u32[]{:S(2)}, u32[]{:S(2)}) %collective-permute-start.12) | collective-permute-done | bytes 262176 | tf_op jit(solution)/shard_map/ppermute | solution.py:478
  35.7 0.2 collective-permute-done.11.other_ref
  35.9 0.3 shard_map.87
  36.2 0.8 %collective-permute-done.18.other_ref = bf16[128,1024]{1,0:T(8,128)(2,1)S(1)} collective-permute-done((bf16[128,1024]{1,0:T(8,128)(2,1)S(1)}, bf16[128,1024]{1,0:T(8,128)(2,1)S(1)}, u32[]{:S(2)}, u32[]{:S(2)}) %collective-permute-start.18) | collective-permute-done | bytes 262176 | tf_op jit(solution)/shard_map/ppermute | solution.py:478
  37.1 1.1 %collective-permute-start.19 = (bf16[128,1024]{1,0:T(8,128)(2,1)S(1)}, bf16[128,1024]{1,0:T(8,128)(2,1)S(1)}, u32[]{:S(2)}, u32[]{:S(2)}) collective-permute-start(bf16[128,1024]{1,0:T(8,128)(2,1)S(1)} %shard_map.90), channel_id=1, source_target_pairs={{0,2},{1,3},{2,0},{3,1},{4,6},{5,7},{6,4},{7,5},{8,10},{9,11},{10,... | collective-permute-start | bytes 786440 | tf_op jit(solution)/shard_map/ppermute | solution.py:478
  38.1 2.6 %collective-permute-start.23 = (bf16[128,512]{1,0:T(8,128)(2,1)S(1)}, bf16[128,512]{1,0:T(8,128)(2,1)S(1)}, u32[]{:S(2)}, u32[]{:S(2)}) collective-permute-start(bf16[128,512]{1,0:T(8,128)(2,1)S(1)} %get-tuple-element.83.mine_ref), channel_id=1, source_target_pairs={{0,16},{4,20},{8,24},{12,28},{16,0},{20,4},{24,8},{28,12},{1,17},{... | collective-permute-start | bytes 393224 | tf_op jit(solution)/shard_map/ppermute | solution.py:478
  40.7 2.0 %collective-permute-start.16 = (bf16[32,256]{1,0:T(8,128)(2,1)S(1)}, bf16[32,256]{1,0:T(8,128)(2,1)S(1)}, u32[]{:S(2)}, u32[]{:S(2)}) collective-permute-start(bf16[32,256]{1,0:T(8,128)(2,1)S(1)} %get-tuple-element.74.refs_0_.refs_1_), channel_id=1, source_target_pairs={{0,6},{1,7},{2,4},{3,5},{4,2},{5,3},{6,0},{7,1},{8,14},{9,15},{10,... | collective-permute-start | bytes 49160 | tf_op jit(solution)/shard_map/ppermute | solution.py:485
  42.7 0.5 collective-permute-start.15
  43.2 1.0 %collective-permute-start.14 = (bf16[32,256]{1,0:T(8,128)(2,1)S(1)}, bf16[32,256]{1,0:T(8,128)(2,1)S(1)}, u32[]{:S(2)}, u32[]{:S(2)}) collective-permute-start(bf16[32,256]{1,0:T(8,128)(2,1)S(1)} %get-tuple-element.74.refs_0_.refs_1_), channel_id=1, source_target_pairs={{0,2},{1,3},{2,0},{3,1},{4,6},{5,7},{6,4},{7,5},{8,10},{9,11},{10,... | collective-permute-start | bytes 49160 | tf_op jit(solution)/shard_map/ppermute | solution.py:478
  44.2 2.6 %collective-permute-done.16.refs_3_ = bf16[32,256]{1,0:T(8,128)(2,1)S(1)} collective-permute-done((bf16[32,256]{1,0:T(8,128)(2,1)S(1)}, bf16[32,256]{1,0:T(8,128)(2,1)S(1)}, u32[]{:S(2)}, u32[]{:S(2)}) %collective-permute-start.16) | collective-permute-done | bytes 16416 | tf_op jit(solution)/shard_map/ppermute | solution.py:485
  46.9 0.1 collective-permute-done.14.refs_1_
  47.0 0.6 shard_map.88
  47.6 0.7 %shard_map.94 = (bf16[128,512]{1,0:T(8,128)(2,1)S(1)}, bf16[128,512]{1,0:T(8,128)(2,1)}) custom-call(bf16[128,512]{1,0:T(8,128)(2,1)S(1)} %get-tuple-element.83.mine_ref, bf16[128,512]{1,0:T(8,128)(2,1)S(1)} %collective-permute-done.23.other_ref), custom_call_target="tpu_custom_call" | custom-call | bytes 262 | tf_op jit(solution)/shard_map/pallas_call | solution.py:121
  48.3 0.3 copy-done.5
  48.6 1.4 %collective-permute-start.24 = (bf16[128,1280]{1,0:T(8,128)(2,1)S(1)}, bf16[128,1280]{1,0:T(8,128)(2,1)S(1)}, u32[]{:S(2)}, u32[]{:S(2)}) collective-permute-start(bf16[128,1280]{1,0:T(8,128)(2,1)S(1)} %shard_map.95), channel_id=1, source_target_pairs={{0,2},{1,3},{2,0},{3,1},{4,6},{5,7},{6,4},{7,5},{8,10},{9,11},{10,... | collective-permute-start | bytes 983048 | tf_op jit(solution)/shard_map/ppermute | solution.py:478
  50.2 0.5 collective-permute-start.21
  50.7 1.6 %collective-permute-start.17 = (bf16[32,256]{1,0:T(8,128)(2,1)S(1)}, bf16[32,256]{1,0:T(8,128)(2,1)S(1)}, u32[]{:S(2)}, u32[]{:S(2)}) collective-permute-start(bf16[32,256]{1,0:T(8,128)(2,1)S(1)} %get-tuple-element.75.refs_1_.refs_0_.refs_2_), channel_id=1, source_target_pairs={{0,8},{4,12},{8,0},{12,4},{16,24},{20,28},{24,16},{28,20},{1,9},{5... | collective-permute-start | bytes 49160 | tf_op jit(solution)/shard_map/ppermute | solution.py:478
  52.3 2.2 %collective-permute-done.17.refs_1_ = bf16[32,256]{1,0:T(8,128)(2,1)S(1)} collective-permute-done((bf16[32,256]{1,0:T(8,128)(2,1)S(1)}, bf16[32,256]{1,0:T(8,128)(2,1)S(1)}, u32[]{:S(2)}, u32[]{:S(2)}) %collective-permute-start.17) | collective-permute-done | bytes 16416 | tf_op jit(solution)/shard_map/ppermute | solution.py:478
  54.4 0.6 shard_map.93
  55.0 2.6 %collective-permute-start.22 = (bf16[32,256]{1,0:T(8,128)(2,1)S(1)}, bf16[32,256]{1,0:T(8,128)(2,1)S(1)}, u32[]{:S(2)}, u32[]{:S(2)}) collective-permute-start(bf16[32,256]{1,0:T(8,128)(2,1)S(1)} %get-tuple-element.78.refs_0_), channel_id=1, source_target_pairs={{0,16},{4,20},{8,24},{12,28},{16,0},{20,4},{24,8},{28,12},{1,17},{... | collective-permute-start | bytes 49160 | tf_op jit(solution)/shard_map/ppermute | solution.py:478
  57.6 2.0 %collective-permute-done.22.refs_2_.refs_1_ = bf16[32,256]{1,0:T(8,128)(2,1)S(1)} collective-permute-done((bf16[32,256]{1,0:T(8,128)(2,1)S(1)}, bf16[32,256]{1,0:T(8,128)(2,1)S(1)}, u32[]{:S(2)}, u32[]{:S(2)}) %collective-permute-start.22) | collective-permute-done | bytes 16416 | tf_op jit(solution)/shard_map/ppermute | solution.py:478
  59.7 0.1 collective-permute-start.25
  59.8 1.8 %collective-permute-done.25.refs_16_ = bf16[128,1792]{1,0:T(8,128)(2,1)S(1)} collective-permute-done((bf16[128,1792]{1,0:T(8,128)(2,1)S(1)}, bf16[128,1792]{1,0:T(8,128)(2,1)S(1)}, u32[]{:S(2)}, u32[]{:S(2)}) %collective-permute-start.25) | collective-permute-done | bytes 458784 | tf_op jit(solution)/shard_map/ppermute | solution.py:478
  61.6 1.2 %shard_map.97 = bf16[4,32,256]{2,1,0:T(8,128)(2,1)S(1)} custom-call(bf16[32,256]{1,0:T(8,128)(2,1)S(1)} %get-tuple-element.78.refs_0_, bf16[32,256]{1,0:T(8,128)(2,1)S(1)} %collective-permute-done.22.refs_2_.refs_1_, f32[4,32,128]{2,1,0:T(8,128)S(1)} %get-tuple-element.79.refs_2_, f32[4,32,128]{2,1,0:T(8,128)S(1)} %get-tuple-element.80.refs_3_, ...), custom_call_target="tpu_custom_call" | custom-call | flops 67108 | bytes 4194 | tf_op jit(solution)/shard_map/pallas_call | solution.py:446
  62.8 5.8 %all-gather = bf16[16,32,256]{2,1,0:T(8,128)(2,1)S(1)} all-gather(bf16[4,32,256]{2,1,0:T(8,128)(2,1)S(1)} %shard_map.97), channel_id=2, replica_groups=mesh['leaf'=8,'rhs'=4] {'rhs'}, dimensions={0}, use_global_device_ids=true | all-gather | bytes 327680 | tf_op jit(solution)/shard_map/all_gather | solution.py:580
  68.6 1.0 %shard_map.98 = f32[8,64,128]{2,1,0:T(8,128)} custom-call(f32[4,64,128]{2,1,0:T(8,128)S(1)} %get-tuple-element.50.far_ref, f32[4,64,128]{2,1,0:T(8,128)S(1)} %get-tuple-element.57.own_ref, bf16[4,4,32,256]{3,2,1,0:T(8,128)(2,1)S(1)} %bitcast.5, bf16[8,128,256]{2,1,0:T(8,128)(2,1)S(1)} %copy-done.3), custom_call_target="tpu_custom_call" | custom-call | flops 33554 | bytes 524 | tf_op jit(solution)/shard_map/pallas_call | solution.py:469
  (40 shorter events, 0.3 us)
Async XLA Ops:
  0.0 11.6 %copy-start.2 = (bf16[8,128,256]{2,1,0:T(8,128)(2,1)S(1)}, bf16[8,128,256]{2,1,0:T(8,128)(2,1)}, u32[]{:S(2)}) copy-start(bf16[8,128,256]{2,1,0:T(8,128)(2,1)} %refs_3_.1) | copy-start | bytes 1572868
  0.0 6.6 %collective-permute-start = (bf16[64,1024]{1,0:T(8,128)(2,1)}, bf16[64,1024]{1,0:T(8,128)(2,1)S(1)}, u32[]{:S(2)}, u32[]{:S(2)}) collective-permute-start(bf16[64,1024]{1,0:T(8,128)(2,1)} %refs_0_.1), channel_id=1, source_target_pairs={{0,2},{1,3},{2,0},{3,1},{4,6},{5,7},{6,4},{7,5},{8,10},{9,11},{10,... | collective-permute-start | bytes 393224 | tf_op jit(solution)/shard_map/ppermute | solution.py:478
  2.9 3.7 %collective-permute-start.1 = (bf16[64,1024]{1,0:T(8,128)(2,1)}, bf16[64,1024]{1,0:T(8,128)(2,1)S(1)}, u32[]{:S(2)}, u32[]{:S(2)}) collective-permute-start(bf16[64,1024]{1,0:T(8,128)(2,1)} %refs_0_.1), channel_id=1, source_target_pairs={{0,1},{1,0},{2,3},{3,2},{4,5},{5,4},{6,7},{7,6},{8,9},{9,8},{10,11... | collective-permute-start | bytes 393224 | tf_op jit(solution)/shard_map/ppermute | solution.py:478
  2.9 8.6 %copy-start.6 = (bf16[64,1024]{1,0:T(8,128)(2,1)S(1)}, bf16[64,1024]{1,0:T(8,128)(2,1)}, u32[]{:S(2)}) copy-start(bf16[64,1024]{1,0:T(8,128)(2,1)} %refs_0_.1) | copy-start | bytes 393220
  6.6 1.3 %collective-permute-start.2 = (bf16[64,1024]{1,0:T(8,128)(2,1)S(1)}, bf16[64,1024]{1,0:T(8,128)(2,1)S(1)}, u32[]{:S(2)}, u32[]{:S(2)}) collective-permute-start(bf16[64,1024]{1,0:T(8,128)(2,1)S(1)} %collective-permute-done.refs_1_), channel_id=1, source_target_pairs={{0,1},{1,0},{2,3},{3,2},{4,5},{5,4},{6,7},{7,6},{8,9},{9,8},{10,11... | collective-permute-start | bytes 393224 | tf_op jit(solution)/shard_map/ppermute | solution.py:478
  8.0 9.7 %collective-permute-start.3 = (bf16[4,128,1024]{2,1,0:T(8,128)(2,1)}, bf16[4,128,1024]{2,1,0:T(8,128)(2,1)S(1)}, u32[]{:S(2)}, u32[]{:S(2)}) collective-permute-start(bf16[4,128,1024]{2,1,0:T(8,128)(2,1)} %get-tuple-element.53.refs_4_.own_ref.refs_17_), channel_id=1, source_target_pairs={{0,1},{1,0},{2,3},{3,2},{4,5},{5,4},{6,7},{7,6},{8,9},{9,8},{10,11... | collective-permute-start | bytes 3145736 | tf_op jit(solution)/shard_map/ppermute | solution.py:478
  8.1 18.6 %collective-permute-start.7 = (bf16[3,128,768]{2,1,0:T(8,128)(2,1)}, bf16[3,128,768]{2,1,0:T(8,128)(2,1)S(1)}, u32[]{:S(2)}, u32[]{:S(2)}) collective-permute-start(bf16[3,128,768]{2,1,0:T(8,128)(2,1)} %get-tuple-element.46), channel_id=1, source_target_pairs={{0,2},{1,3},{2,0},{3,1},{4,6},{5,7},{6,4},{7,5},{8,10},{9,11},{10,... | collective-permute-start | bytes 1769480 | tf_op jit(solution)/shard_map/ppermute | solution.py:478
  9.9 1.7 %copy-start.7 = (s32[4096]{0:T(1024)S(1)}, s32[4096]{0:T(1024)}, u32[]{:S(2)}) copy-start(s32[4096]{0:T(1024)} %param.9) | copy-start | bytes 49156
  9.9 11.7 %collective-permute-start.8 = (bf16[128,1024]{1,0:T(8,128)(2,1)}, bf16[128,1024]{1,0:T(8,128)(2,1)S(1)}, u32[]{:S(2)}, u32[]{:S(2)}) collective-permute-start(bf16[128,1024]{1,0:T(8,128)(2,1)} %get-tuple-element.64.mine_ref), channel_id=1, source_target_pairs={{0,4},{4,0},{8,12},{12,8},{16,20},{20,16},{24,28},{28,24},{1,5},{5... | collective-permute-start | bytes 786440 | tf_op jit(solution)/shard_map/ppermute | solution.py:478
  11.6 1.2 %copy-start.1 = (bf16[8,128,512]{2,1,0:T(8,128)(2,1)S(1)}, bf16[8,128,512]{2,1,0:T(8,128)(2,1)}, u32[]{:S(2)}) copy-start(bf16[8,128,512]{2,1,0:T(8,128)(2,1)} %refs_2_.1) | copy-start | bytes 3145732
  16.2 8.9 %collective-permute-start.6 = (bf16[4,32,256]{2,1,0:T(8,128)(2,1)S(1)}, bf16[4,32,256]{2,1,0:T(8,128)(2,1)S(1)}, u32[]{:S(2)}, u32[]{:S(2)}) collective-permute-start(bf16[4,32,256]{2,1,0:T(8,128)(2,1)S(1)} %get-tuple-element.61), channel_id=1, source_target_pairs={{0,3},{1,2},{2,1},{3,0},{4,7},{5,6},{6,5},{7,4},{8,11},{9,10},{10,... | collective-permute-start | bytes 196616 | tf_op jit(solution)/shard_map/ppermute | solution.py:478
  16.3 10.4 %collective-permute-start.4 = (bf16[4,32,256]{2,1,0:T(8,128)(2,1)S(1)}, bf16[4,32,256]{2,1,0:T(8,128)(2,1)S(1)}, u32[]{:S(2)}, u32[]{:S(2)}) collective-permute-start(bf16[4,32,256]{2,1,0:T(8,128)(2,1)S(1)} %get-tuple-element.54), channel_id=1, source_target_pairs={{0,2},{1,3},{2,0},{3,1},{4,6},{5,7},{6,4},{7,5},{8,10},{9,11},{10,... | collective-permute-start | bytes 196616 | tf_op jit(solution)/shard_map/ppermute | solution.py:478
  17.7 3.9 %copy-start.4 = (bf16[128,1024]{1,0:T(8,128)(2,1)S(1)}, bf16[128,1024]{1,0:T(8,128)(2,1)}, u32[]{:S(2)}) copy-start(bf16[128,1024]{1,0:T(8,128)(2,1)} %get-tuple-element.64.mine_ref) | copy-start | bytes 786436
  17.7 12.9 %copy-start = (bf16[4,128,1024]{2,1,0:T(8,128)(2,1)S(1)}, bf16[4,128,1024]{2,1,0:T(8,128)(2,1)}, u32[]{:S(2)}) copy-start(bf16[4,128,1024]{2,1,0:T(8,128)(2,1)} %get-tuple-element.53.refs_4_.own_ref.refs_17_) | copy-start | bytes 3145732
  21.1 5.7 %collective-permute-start.5 = (bf16[4,32,256]{2,1,0:T(8,128)(2,1)S(1)}, bf16[4,32,256]{2,1,0:T(8,128)(2,1)S(1)}, u32[]{:S(2)}, u32[]{:S(2)}) collective-permute-start(bf16[4,32,256]{2,1,0:T(8,128)(2,1)S(1)} %get-tuple-element.60), channel_id=1, source_target_pairs={{0,1},{1,0},{2,3},{3,2},{4,5},{5,4},{6,7},{7,6},{8,9},{9,8},{10,11... | collective-permute-start | bytes 196616 | tf_op jit(solution)/shard_map/ppermute | solution.py:478
  26.8 3.8 %collective-permute-start.9 = (bf16[3,128,768]{2,1,0:T(8,128)(2,1)S(1)}, bf16[3,128,768]{2,1,0:T(8,128)(2,1)S(1)}, u32[]{:S(2)}, u32[]{:S(2)}) collective-permute-start(bf16[3,128,768]{2,1,0:T(8,128)(2,1)S(1)} %collective-permute-done.7.refs_5_), channel_id=1, source_target_pairs={{0,1},{1,0},{2,3},{3,2},{4,5},{5,4},{6,7},{7,6},{8,9},{9,8},{10,11... | collective-permute-start | bytes 1769480 | tf_op jit(solution)/shard_map/ppermute | solution.py:478
  26.8 5.3 %collective-permute-start.10 = (bf16[128,1024]{1,0:T(8,128)(2,1)S(1)}, bf16[128,1024]{1,0:T(8,128)(2,1)S(1)}, u32[]{:S(2)}, u32[]{:S(2)}) collective-permute-start(bf16[128,1024]{1,0:T(8,128)(2,1)S(1)} %get-tuple-element.70.refs_4_.refs_6_), channel_id=1, source_target_pairs={{0,1},{1,0},{2,3},{3,2},{4,5},{5,4},{6,7},{7,6},{8,9},{9,8},{10,11... | collective-permute-start | bytes 786440 | tf_op jit(solution)/shard_map/ppermute | solution.py:478
  27.3 8.5 %collective-permute-start.12 = (bf16[128,1024]{1,0:T(8,128)(2,1)S(1)}, bf16[128,1024]{1,0:T(8,128)(2,1)S(1)}, u32[]{:S(2)}, u32[]{:S(2)}) collective-permute-start(bf16[128,1024]{1,0:T(8,128)(2,1)S(1)} %get-tuple-element.70.refs_4_.refs_6_), channel_id=1, source_target_pairs={{0,2},{1,3},{2,0},{3,1},{4,6},{5,7},{6,4},{7,5},{8,10},{9,11},{10,... | collective-permute-start | bytes 786440 | tf_op jit(solution)/shard_map/ppermute | solution.py:478
  29.0 8.0 %collective-permute-start.18 = (bf16[128,1024]{1,0:T(8,128)(2,1)S(1)}, bf16[128,1024]{1,0:T(8,128)(2,1)S(1)}, u32[]{:S(2)}, u32[]{:S(2)}) collective-permute-start(bf16[128,1024]{1,0:T(8,128)(2,1)S(1)} %get-tuple-element.66.mine_ref), channel_id=1, source_target_pairs={{0,8},{4,12},{8,0},{12,4},{16,24},{20,28},{24,16},{28,20},{1,9},{5... | collective-permute-start | bytes 786440 | tf_op jit(solution)/shard_map/ppermute | solution.py:478
  32.1 3.8 %collective-permute-start.11 = (bf16[32,256]{1,0:T(8,128)(2,1)S(1)}, bf16[32,256]{1,0:T(8,128)(2,1)S(1)}, u32[]{:S(2)}, u32[]{:S(2)}) collective-permute-start(bf16[32,256]{1,0:T(8,128)(2,1)S(1)} %get-tuple-element.71.mine_ref), channel_id=1, source_target_pairs={{0,2},{1,3},{2,0},{3,1},{4,6},{5,7},{6,4},{7,5},{8,10},{9,11},{10,... | collective-permute-start | bytes 49160 | tf_op jit(solution)/shard_map/ppermute | solution.py:478
  35.9 4.8 %collective-permute-start.13 = (bf16[128,1024]{1,0:T(8,128)(2,1)S(1)}, bf16[128,1024]{1,0:T(8,128)(2,1)S(1)}, u32[]{:S(2)}, u32[]{:S(2)}) collective-permute-start(bf16[128,1024]{1,0:T(8,128)(2,1)S(1)} %collective-permute-done.12.refs_5_.refs_7_), channel_id=1, source_target_pairs={{0,1},{1,0},{2,3},{3,2},{4,5},{5,4},{6,7},{7,6},{8,9},{9,8},{10,11... | collective-permute-start | bytes 786440 | tf_op jit(solution)/shard_map/ppermute | solution.py:478
  37.1 13.0 %collective-permute-start.19 = (bf16[128,1024]{1,0:T(8,128)(2,1)S(1)}, bf16[128,1024]{1,0:T(8,128)(2,1)S(1)}, u32[]{:S(2)}, u32[]{:S(2)}) collective-permute-start(bf16[128,1024]{1,0:T(8,128)(2,1)S(1)} %shard_map.90), channel_id=1, source_target_pairs={{0,2},{1,3},{2,0},{3,1},{4,6},{5,7},{6,4},{7,5},{8,10},{9,11},{10,... | collective-permute-start | bytes 786440 | tf_op jit(solution)/shard_map/ppermute | solution.py:478
  38.1 9.4 %collective-permute-start.23 = (bf16[128,512]{1,0:T(8,128)(2,1)S(1)}, bf16[128,512]{1,0:T(8,128)(2,1)S(1)}, u32[]{:S(2)}, u32[]{:S(2)}) collective-permute-start(bf16[128,512]{1,0:T(8,128)(2,1)S(1)} %get-tuple-element.83.mine_ref), channel_id=1, source_target_pairs={{0,16},{4,20},{8,24},{12,28},{16,0},{20,4},{24,8},{28,12},{1,17},{... | collective-permute-start | bytes 393224 | tf_op jit(solution)/shard_map/ppermute | solution.py:478
  40.7 6.1 %collective-permute-start.16 = (bf16[32,256]{1,0:T(8,128)(2,1)S(1)}, bf16[32,256]{1,0:T(8,128)(2,1)S(1)}, u32[]{:S(2)}, u32[]{:S(2)}) collective-permute-start(bf16[32,256]{1,0:T(8,128)(2,1)S(1)} %get-tuple-element.74.refs_0_.refs_1_), channel_id=1, source_target_pairs={{0,6},{1,7},{2,4},{3,5},{4,2},{5,3},{6,0},{7,1},{8,14},{9,15},{10,... | collective-permute-start | bytes 49160 | tf_op jit(solution)/shard_map/ppermute | solution.py:485
  42.7 4.1 %collective-permute-start.15 = (bf16[32,256]{1,0:T(8,128)(2,1)S(1)}, bf16[32,256]{1,0:T(8,128)(2,1)S(1)}, u32[]{:S(2)}, u32[]{:S(2)}) collective-permute-start(bf16[32,256]{1,0:T(8,128)(2,1)S(1)} %get-tuple-element.74.refs_0_.refs_1_), channel_id=1, source_target_pairs={{0,4},{4,0},{8,12},{12,8},{16,20},{20,16},{24,28},{28,24},{1,5},{5... | collective-permute-start | bytes 49160 | tf_op jit(solution)/shard_map/ppermute | solution.py:478
  43.2 3.7 %collective-permute-start.14 = (bf16[32,256]{1,0:T(8,128)(2,1)S(1)}, bf16[32,256]{1,0:T(8,128)(2,1)S(1)}, u32[]{:S(2)}, u32[]{:S(2)}) collective-permute-start(bf16[32,256]{1,0:T(8,128)(2,1)S(1)} %get-tuple-element.74.refs_0_.refs_1_), channel_id=1, source_target_pairs={{0,2},{1,3},{2,0},{3,1},{4,6},{5,7},{6,4},{7,5},{8,10},{9,11},{10,... | collective-permute-start | bytes 49160 | tf_op jit(solution)/shard_map/ppermute | solution.py:478
  47.6 1.0 %copy-start.5 = (bf16[128,768]{1,0:T(8,128)(2,1)S(1)}, bf16[128,768]{1,0:T(8,128)(2,1)}, u32[]{:S(2)}) copy-start(bf16[128,768]{1,0:T(8,128)(2,1)} %get-tuple-element.86.refs_1_) | copy-start | bytes 589828
  48.6 11.1 %collective-permute-start.24 = (bf16[128,1280]{1,0:T(8,128)(2,1)S(1)}, bf16[128,1280]{1,0:T(8,128)(2,1)S(1)}, u32[]{:S(2)}, u32[]{:S(2)}) collective-permute-start(bf16[128,1280]{1,0:T(8,128)(2,1)S(1)} %shard_map.95), channel_id=1, source_target_pairs={{0,2},{1,3},{2,0},{3,1},{4,6},{5,7},{6,4},{7,5},{8,10},{9,11},{10,... | collective-permute-start | bytes 983048 | tf_op jit(solution)/shard_map/ppermute | solution.py:478
  50.0 4.4 %collective-permute-start.20 = (bf16[128,1024]{1,0:T(8,128)(2,1)S(1)}, bf16[128,1024]{1,0:T(8,128)(2,1)S(1)}, u32[]{:S(2)}, u32[]{:S(2)}) collective-permute-start(bf16[128,1024]{1,0:T(8,128)(2,1)S(1)} %shard_map.91), channel_id=1, source_target_pairs={{0,1},{1,0},{2,3},{3,2},{4,5},{5,4},{6,7},{7,6},{8,9},{9,8},{10,11... | collective-permute-start | bytes 786440 | tf_op jit(solution)/shard_map/ppermute | solution.py:478
  50.2 4.3 %collective-permute-start.21 = (bf16[128,1024]{1,0:T(8,128)(2,1)S(1)}, bf16[128,1024]{1,0:T(8,128)(2,1)S(1)}, u32[]{:S(2)}, u32[]{:S(2)}) collective-permute-start(bf16[128,1024]{1,0:T(8,128)(2,1)S(1)} %shard_map.92), channel_id=1, source_target_pairs={{0,1},{1,0},{2,3},{3,2},{4,5},{5,4},{6,7},{7,6},{8,9},{9,8},{10,11... | collective-permute-start | bytes 786440 | tf_op jit(solution)/shard_map/ppermute | solution.py:478
  50.7 3.7 %collective-permute-start.17 = (bf16[32,256]{1,0:T(8,128)(2,1)S(1)}, bf16[32,256]{1,0:T(8,128)(2,1)S(1)}, u32[]{:S(2)}, u32[]{:S(2)}) collective-permute-start(bf16[32,256]{1,0:T(8,128)(2,1)S(1)} %get-tuple-element.75.refs_1_.refs_0_.refs_2_), channel_id=1, source_target_pairs={{0,8},{4,12},{8,0},{12,4},{16,24},{20,28},{24,16},{28,20},{1,9},{5... | collective-permute-start | bytes 49160 | tf_op jit(solution)/shard_map/ppermute | solution.py:478
  55.0 4.7 %collective-permute-start.22 = (bf16[32,256]{1,0:T(8,128)(2,1)S(1)}, bf16[32,256]{1,0:T(8,128)(2,1)S(1)}, u32[]{:S(2)}, u32[]{:S(2)}) collective-permute-start(bf16[32,256]{1,0:T(8,128)(2,1)S(1)} %get-tuple-element.78.refs_0_), channel_id=1, source_target_pairs={{0,16},{4,20},{8,24},{12,28},{16,0},{20,4},{24,8},{28,12},{1,17},{... | collective-permute-start | bytes 49160 | tf_op jit(solution)/shard_map/ppermute | solution.py:478
  59.7 1.9 %collective-permute-start.25 = (bf16[128,1792]{1,0:T(8,128)(2,1)S(1)}, bf16[128,1792]{1,0:T(8,128)(2,1)S(1)}, u32[]{:S(2)}, u32[]{:S(2)}) collective-permute-start(bf16[128,1792]{1,0:T(8,128)(2,1)S(1)} %shard_map.96), channel_id=1, source_target_pairs={{0,1},{1,0},{2,3},{3,2},{4,5},{5,4},{6,7},{7,6},{8,9},{9,8},{10,11... | collective-permute-start | bytes 1376264 | tf_op jit(solution)/shard_map/ppermute | solution.py:478
  61.6 7.0 %copy-start.3 = (bf16[8,128,256]{2,1,0:T(8,128)(2,1)S(1)}, bf16[8,128,256]{2,1,0:T(8,128)(2,1)}, u32[]{:S(2)}) copy-start(bf16[8,128,256]{2,1,0:T(8,128)(2,1)} %coupling_ref.1) | copy-start | bytes 1572868

commit v2 on v1

--- a/solution.py
+++ b/solution.py
@@ -102,51 +102,74 @@
     )(inverse, basis, coupling)
 
 
-def climb_kernel(level, mine_ref, other_ref, ancestor_ref, carrier_ref):
+def climb_kernel(level, mine_ref, other_ref, ancestor_ref, *carrier_refs):
     right = (lax.axis_index("leaf") // (1 << level)) % 2 == 1
-    keep = carrier_ref.shape[1]
 
     @pl.when(right)
     def _():
         ancestor_ref[...] = mine_ref[...]
-        carrier_ref[...] = other_ref[:, :keep]
+        for ref in carrier_refs:
+            ref[...] = other_ref[:, : ref.shape[1]]
 
     @pl.when(jnp.logical_not(right))
     def _():
         ancestor_ref[...] = other_ref[...]
-        carrier_ref[...] = mine_ref[:, :keep]
+        for ref in carrier_refs:
+            ref[...] = mine_ref[:, : ref.shape[1]]
 
 
 def climb(level, mine, other, keep):
     return pl.pallas_call(
         functools.partial(climb_kernel, level),
-        out_shape=[
-            pltpu.VMEM(mine.shape, mine.dtype),
-            pltpu.VMEM((mine.shape[0], keep), mine.dtype),
-        ],
+        out_shape=[pltpu.VMEM(mine.shape, mine.dtype)]
+        + [pltpu.VMEM((mine.shape[0], size), mine.dtype) for size in keep],
         compiler_params=params(),
         cost_estimate=cost(0, 4 * mine.size),
     )(mine, other)
 
 
-def join_kernel(*refs):
+def join_kernel(cuts, *refs):
     *blocks, _, out_ref = refs
     start = 0
-    for ref in blocks:
-        width = ref.shape[1]
-        out_ref[:, start : start + width] = ref[...]
+    for ref, (first, width) in zip(blocks, cuts):
+        out_ref[:, start : start + width] = ref[:, first : first + width]
         start += width
 
 
-def join(blocks, anchor):
+def join(blocks, anchor, cuts=None):
     rows = blocks[0].shape[0]
-    width = sum(block.shape[1] for block in blocks)
-    return pl.pallas_call(
-        join_kernel,
+    cuts = cuts or [(0, block.shape[1]) for block in blocks]
+    width = sum(size for _, size in cuts)
+    return pl.pallas_call(
+        functools.partial(join_kernel, cuts),
         out_shape=pltpu.VMEM((rows, width), blocks[0].dtype),
         compiler_params=params(),
         cost_estimate=cost(0, 4 * rows * width),
     )(*blocks, anchor)
+
+
+def hop_kernel(level, top_ref, tail_ref, _, out_ref):
+    node_size = top_ref.shape[1]
+    side = (lax.axis_index("leaf") // (1 << level)) % 2
+    here = lax.axis_index("rhs") // CORES == side
+    out_ref[:, node_size:] = tail_ref[:, node_size:]
+
+    @pl.when(here)
+    def _():
+        out_ref[:, :node_size] = top_ref[...]
+
+    @pl.when(jnp.logical_not(here))
+    def _():
+        out_ref[:, :node_size] = tail_ref[:, :node_size]
+
+
+def hop(level, top, tail, anchor):
+    return pl.pallas_call(
+        functools.partial(hop_kernel, level),
+        out_shape=pltpu.VMEM(tail.shape, tail.dtype),
+        compiler_params=params(),
+        cost_estimate=cost(0, 4 * tail.size),
+    )(top, tail, anchor)
 
 
 def leaf_kernel(count, side_ref, *refs):
@@ -373,15 +396,12 @@
     solved_cross, refs = refs[: cross_levels - 1], refs[cross_levels - 1 :]
     solved_top, solved_half, refs = refs[0], refs[1], refs[2:]
     count = 2 * CORES * (cross_levels - 1)
-    cross_packs, (own_top, tail, near_tail, keep, keep_near) = refs[:count], refs[count:]
+    cross_packs, (tail, near_tail, keep, keep_near) = refs[:count], refs[count:]
     levels, total = half_levels(per_dev)
     rank = out_ref.shape[2]
     node_size = 2 * rank
     place = lax.axis_index("rhs")
 
-    def pieces(level):
-        return zip(PIECES, cross_packs[2 * CORES * level : 2 * CORES * (level + 1)])
-
     def choose(which):
         return jnp.concatenate([value[2 * which], value[2 * which + 1]], axis=1)
 
@@ -393,20 +413,28 @@
         return pl.ds(width - rank, rank)
 
     stacked = cross_pair(cross_levels - 1, inputs)
-    tops = (
-        own_top[...],
-        tail[:, :node_size],
-        near_tail[:, :node_size],
-        near_tail[:, node_size : 2 * node_size],
-    )
-    for flip, block in zip(PIECES, tops):
-        value[place ^ flip] = dot_rows(stacked, block).astype(jnp.bfloat16)
-    incoming = choose(side(cross_levels - 1))
+    half = side(cross_levels - 1)
+    for flip, ref in ((0, tail), (1, near_tail)):
+        core = (place ^ flip) % CORES
+        value[2 * half + core] = dot_rows(stacked, ref[:, :node_size]).astype(jnp.bfloat16)
+    incoming = choose(half)
     for level in range(cross_levels - 2, -1, -1):
-        for flip, ref in pieces(level):
+        packs = cross_packs[2 * CORES * level : 2 * CORES * (level + 1)]
+        own, far, near, far_near = packs
+        if level == 0:
+            couplings = [ref[:, columns(ref)] for ref in packs]
+        else:
+            start = node_size + (total + level - 1) * rank
+            couplings = [
+                own[:, columns(own)],
+                tail[:, start : start + rank],
+                near[:, columns(near)],
+                near_tail[:, start : start + rank],
+            ]
+        for flip, coupling in zip(PIECES, couplings):
             piece = place ^ flip
             solved = solved_cross[level][piece]
-            value[piece] = (solved - dot_rows(incoming, ref[:, columns(ref)])).astype(jnp.bfloat16)
+            value[piece] = (solved - dot_rows(incoming, coupling)).astype(jnp.bfloat16)
         incoming = choose(side(level))
 
     for flip, ref in ((0, keep), (1, keep_near)):
@@ -423,7 +451,7 @@
                 keep[node, :, columns(keep)],
                 tail[:, start : start + rank],
                 keep_near[node, :, columns(keep)],
-                near_tail[:, node_size + start : node_size + start + rank],
+                near_tail[:, start : start + rank],
             )
             for flip, coupling in zip(PIECES, couplings):
                 piece = place ^ flip
@@ -502,14 +530,16 @@
     devices = lax.axis_size("leaf")
     per_dev = leaf_inverse.shape[0]
     node_size = node_inverse.shape[2]
+    rank = leaf_basis.shape[2]
     cross_levels = devices.bit_length() - 1
     place = lax.axis_index("rhs")
     high, low = place // CORES, place % CORES
 
     def rise(carrier, level, anchor):
         other = after(swap(carrier, "leaf", 1 << level), anchor)
-        width = node_size if level >= cross_levels - 2 else carrier.shape[1]
-        return climb(level, carrier, other, width)
+        width = node_size if level == cross_levels - 2 else carrier.shape[1]
+        ancestor, *carriers = climb(level, carrier, other, [width] * (level < cross_levels - 1))
+        return ancestor, carriers[0] if carriers else None
 
     send, send_coupling, keep, carrier = pack(node_inverse, node_basis, node_coupling)
     across, beside = after(
@@ -547,7 +577,8 @@
     fars[0] = after(fars[0], other)
     near_far = swap(fars[0], "rhs", 1)
     cross_packs = [[ancestors[0], fars[0], nears[0], near_far]]
-    fars.append(swap(join([ancestors[1]], current), "rhs", CORES))
+    factors = [(0, node_size + rank)]
+    fars.append(swap(join([ancestors[1]], current, factors), "rhs", CORES))
     current = after(current, near_far)
     inputs = [
         current,
@@ -571,11 +602,14 @@
                 ancestor, carrier = rise(carrier, later, current)
                 ancestors.append(ancestor)
             for later in range(2, cross_levels - 1):
-                fars.append(swap(join([ancestors[later]], current), "rhs", CORES))
-            tail = swap(join([ancestors[-1], send_coupling], current), "rhs", CORES)
-
-    near_tail = swap(join([ancestors[-1], tail], inputs[1]), "rhs", 1)
-    others = [ancestors[-1], tail, near_tail, keep, keep_near]
+                fars.append(swap(join([ancestors[later]], current, factors), "rhs", CORES))
+            blocks = [ancestors[-1], send_coupling, *ancestors[1:-1]]
+            cuts = [(0, node_size), (0, send_coupling.shape[1])]
+            cuts += [(node_size + rank, rank)] * (cross_levels - 2)
+            tail = swap(join(blocks, current, cuts), "rhs", CORES)
+
+    tail = hop(cross_levels - 1, ancestors[-1], tail, inputs[1])
+    others = [tail, swap(tail, "rhs", 1), keep, keep_near]
     shares = way_down(per_dev, inputs, solved_cross, solved_top, solved_half, cross_packs, others)
     incoming = lax.all_gather(shares, "rhs", axis=0)
     return finish(far_values, own_values, incoming, leaf_coupling)

time: 69.8 us -> 69.7 us (level)
  starting transfers between devices: 26.2 us -> 23.8 us
  waiting for transfers between devices: 20 us -> 22.4 us
  Pallas kernels: 15.8 us -> 15 us
    ppermute x25, waiting for transfers between devices: 17.3 us -> 19.8 us  [swap(): lax.ppermute(block, axis, [(i, i ^ bit) for i in range(lax.axis_size(axis...]
    ppermute x25, starting transfers between devices: 24.2 us -> 22.5 us  [swap(): lax.ppermute(block, axis, [(i, i ^ bit) for i in range(lax.axis_size(axis...]
  transfers between devices with their start and end apart: 26 -> 26, of which waited for: 12 -> 12; matrix products, arithmetic and copies ran while one was open for 0% -> 0% of each run, Pallas kernels for 20% -> 19%
where the time goes in v2:
time: 69.7 us; the launch traced here: 69.4 us
  starting transfers between devices  23.8 us (34%)
  waiting for transfers between devices  22.4 us (32%)
  Pallas kernels  15 us (22%)
  blocking collectives  5.79 us (8%)
  local copies, waits for them, and re-layouts  2.13 us (3%)
    ppermute x25, starting transfers between devices, swap(): lax.ppermute(block, axis, [(i, i ^ bit) for i in range(lax.axis_size(axis...  22.5 us
    ppermute x25, waiting for transfers between devices, swap(): lax.ppermute(block, axis, [(i, i ^ bit) for i in range(lax.axis_size(axis...  19.8 us
    pallas_call x2, Pallas kernels, leaf_up(): pl.pallas_call(functools.partial(leaf_kernel, len(points)), grid_spec=plt...  6.81 us
    all_gather x1, blocking collectives, body(): incoming = lax.all_gather(shares, 'rhs', axis=0)  5.79 us
    pallas_call x1, Pallas kernels, pack(): pl.pallas_call(functools.partial(pack_kernel, per_dev), in_specs=[pl.Bloc...  2.99 us
    ppermute x1, waiting for transfers between devices, far_swap(): lax.ppermute(block, ('leaf', 'rhs'), [(i, i ^ flip) for i in range(count)])  2.59 us
    unnamed x16, local copies, waits for them, and re-layouts  2.13 us
    pallas_call x1, Pallas kernels, group_up(): pl.pallas_call(functools.partial(group_up_kernel, per_dev), out_shape=[ja...  1.48 us
  transfers between devices with their start and end apart: 26, of which 12 were waited for; matrix products, arithmetic and copies ran while one was open for 0% of the time, Pallas kernels for 19%

profile of v2, /device:TPU:0, one launch (start us, length us, event | category | flops | bytes accessed | tf_op | source)
XLA Modules:
  0.0 69.4 jit_solution(11549571584028459314)
XLA Ops:
  0.0 2.9 %collective-permute-start = (bf16[64,1024]{1,0:T(8,128)(2,1)}, bf16[64,1024]{1,0:T(8,128)(2,1)S(1)}, u32[]{:S(2)}, u32[]{:S(2)}) collective-permute-start(bf16[64,1024]{1,0:T(8,128)(2,1)} %refs_0_.1), channel_id=1, source_target_pairs={{0,2},{1,3},{2,0},{3,1},{4,6},{5,7},{6,4},{7,5},{8,10},{9,11},{10,... | collective-permute-start | bytes 393224 | tf_op jit(solution)/shard_map/ppermute | solution.py:506
  2.9 3.0 %shard_map.82 = (bf16[3,128,768]{2,1,0:T(8,128)(2,1)}, bf16[128,768]{1,0:T(8,128)(2,1)}, bf16[4,128,1024]{2,1,0:T(8,128)(2,1)}, bf16[128,1024]{1,0:T(8,128)(2,1)}) custom-call(bf16[8,128,512]{2,1,0:T(8,128)(2,1)} %inverse.1, bf16[8,128,256]{2,1,0:T(8,128)(2,1)} %basis.1, bf16[8,128,256]{2,1,0:T(8,128)(2,1)} %coupling.1), custom_call_target="tpu_custom_call" | custom-call | bytes 4194 | tf_op jit(solution)/shard_map/pallas_call | solution.py:93
  5.9 0.7 %collective-permute-done.refs_1_ = bf16[64,1024]{1,0:T(8,128)(2,1)S(1)} collective-permute-done((bf16[64,1024]{1,0:T(8,128)(2,1)}, bf16[64,1024]{1,0:T(8,128)(2,1)S(1)}, u32[]{:S(2)}, u32[]{:S(2)}) %collective-permute-start) | collective-permute-done | bytes 131104 | tf_op jit(solution)/shard_map/ppermute | solution.py:506
  6.7 1.3 %collective-permute-done.2.refs_3_ = bf16[64,1024]{1,0:T(8,128)(2,1)S(1)} collective-permute-done((bf16[64,1024]{1,0:T(8,128)(2,1)S(1)}, bf16[64,1024]{1,0:T(8,128)(2,1)S(1)}, u32[]{:S(2)}, u32[]{:S(2)}) %collective-permute-start.2) | collective-permute-done | bytes 131104 | tf_op jit(solution)/shard_map/ppermute | solution.py:506
  8.0 0.1 collective-permute-start.3
  8.1 1.8 %collective-permute-start.7 = (bf16[3,128,768]{2,1,0:T(8,128)(2,1)}, bf16[3,128,768]{2,1,0:T(8,128)(2,1)S(1)}, u32[]{:S(2)}, u32[]{:S(2)}) collective-permute-start(bf16[3,128,768]{2,1,0:T(8,128)(2,1)} %get-tuple-element.45), channel_id=1, source_target_pairs={{0,2},{1,3},{2,0},{3,1},{4,6},{5,7},{6,4},{7,5},{8,10},{9,11},{10,... | collective-permute-start | bytes 1769480 | tf_op jit(solution)/shard_map/ppermute | solution.py:506
  9.9 1.5 %collective-permute-start.8 = (bf16[128,1024]{1,0:T(8,128)(2,1)}, bf16[128,1024]{1,0:T(8,128)(2,1)S(1)}, u32[]{:S(2)}, u32[]{:S(2)}) collective-permute-start(bf16[128,1024]{1,0:T(8,128)(2,1)} %get-tuple-element.63.mine_ref), channel_id=1, source_target_pairs={{0,4},{4,0},{8,12},{12,8},{16,20},{20,16},{24,28},{28,24},{1,5},{5... | collective-permute-start | bytes 786440 | tf_op jit(solution)/shard_map/ppermute | solution.py:506
  11.4 0.1 pad_add_fusion.side_ref
  11.5 0.1 pad_add_fusion.1.side_ref
  11.6 1.2 %copy-done.1 = bf16[8,128,512]{2,1,0:T(8,128)(2,1)S(1)} copy-done((bf16[8,128,512]{2,1,0:T(8,128)(2,1)S(1)}, bf16[8,128,512]{2,1,0:T(8,128)(2,1)}, u32[]{:S(2)}) %copy-start.1) | copy-done | bytes 1048600
  12.8 3.4 %shard_map.83 = (f32[4,64,128]{2,1,0:T(8,128)S(1)}, bf16[4,32,256]{2,1,0:T(8,128)(2,1)S(1)}, bf16[4,32,256]{2,1,0:T(8,128)(2,1)S(1)}, bf16[4,4,64,256]{3,2,1,0:T(8,128)(2,1)S(1)}) custom-call(s32[2]{0:T(128)S(1)} %pad_add_fusion.side_ref, bf16[64,1024]{1,0:T(8,128)(2,1)S(1)} %copy-done.6, bf16[64,1024]{1,0:T(8,128)(2,1)S(1)} %collective-permute-done.refs_1_, ...), custom_call_target="tpu_custom_call" | custom-call | flops 1140850 | bytes 983 | tf_op jit(solution)/shard_map/pallas_call | solution.py:241
  16.2 0.1 collective-permute-start.6
  16.3 1.4 %collective-permute-start.4 = (bf16[4,32,256]{2,1,0:T(8,128)(2,1)S(1)}, bf16[4,32,256]{2,1,0:T(8,128)(2,1)S(1)}, u32[]{:S(2)}, u32[]{:S(2)}) collective-permute-start(bf16[4,32,256]{2,1,0:T(8,128)(2,1)S(1)} %get-tuple-element.53), channel_id=1, source_target_pairs={{0,2},{1,3},{2,0},{3,1},{4,6},{5,7},{6,4},{7,5},{8,10},{9,11},{10,... | collective-permute-start | bytes 196616 | tf_op jit(solution)/shard_map/ppermute | solution.py:506
  17.7 3.4 %shard_map.84 = (f32[4,64,128]{2,1,0:T(8,128)S(1)}, bf16[4,32,256]{2,1,0:T(8,128)(2,1)S(1)}, bf16[4,32,256]{2,1,0:T(8,128)(2,1)S(1)}) custom-call(s32[2]{0:T(128)S(1)} %pad_add_fusion.1.side_ref, bf16[4,4,64,256]{3,2,1,0:T(8,128)(2,1)S(1)} %get-tuple-element.55.refs_0_, s32[1,4096]{1,0:T(1,128)S(1)} %bitcast.7, bf16[8,128,512]{2,1,0:T(8,128)(2,1)S(1)} %copy-done.1, ...), custom_call_target="tpu_custom_call" | custom-call | flops 1140850 | bytes 983 | tf_op jit(solution)/shard_map/pallas_call | solution.py:241
  21.1 0.5 collective-permute-start.5
  21.7 3.5 %collective-permute-done.6.refs_3_ = bf16[4,32,256]{2,1,0:T(8,128)(2,1)S(1)} collective-permute-done((bf16[4,32,256]{2,1,0:T(8,128)(2,1)S(1)}, bf16[4,32,256]{2,1,0:T(8,128)(2,1)S(1)}, u32[]{:S(2)}, u32[]{:S(2)}) %collective-permute-start.6) | collective-permute-done | bytes 65568 | tf_op jit(solution)/shard_map/ppermute | solution.py:506
  25.2 1.6 %collective-permute-done.4.refs_1_ = bf16[4,32,256]{2,1,0:T(8,128)(2,1)S(1)} collective-permute-done((bf16[4,32,256]{2,1,0:T(8,128)(2,1)S(1)}, bf16[4,32,256]{2,1,0:T(8,128)(2,1)S(1)}, u32[]{:S(2)}, u32[]{:S(2)}) %collective-permute-start.4) | collective-permute-done | bytes 65568 | tf_op jit(solution)/shard_map/ppermute | solution.py:506
  26.8 0.5 collective-permute-start.10
  27.3 1.7 %collective-permute-start.12 = (bf16[128,1024]{1,0:T(8,128)(2,1)S(1)}, bf16[128,1024]{1,0:T(8,128)(2,1)S(1)}, u32[]{:S(2)}, u32[]{:S(2)}) collective-permute-start(bf16[128,1024]{1,0:T(8,128)(2,1)S(1)} %get-tuple-element.69.refs_4_.refs_6_), channel_id=1, source_target_pairs={{0,2},{1,3},{2,0},{3,1},{4,6},{5,7},{6,4},{7,5},{8,10},{9,11},{10,... | collective-permute-start | bytes 786440 | tf_op jit(solution)/shard_map/ppermute | solution.py:506
  29.0 1.6 %collective-permute-start.18 = (bf16[128,1024]{1,0:T(8,128)(2,1)S(1)}, bf16[128,1024]{1,0:T(8,128)(2,1)S(1)}, u32[]{:S(2)}, u32[]{:S(2)}) collective-permute-start(bf16[128,1024]{1,0:T(8,128)(2,1)S(1)} %get-tuple-element.65.mine_ref), channel_id=1, source_target_pairs={{0,8},{4,12},{8,0},{12,4},{16,24},{20,28},{24,16},{28,20},{1,9},{5... | collective-permute-start | bytes 786440 | tf_op jit(solution)/shard_map/ppermute | solution.py:506
  30.6 1.5 %shard_map.86 = (f32[3,4,32,128]{3,2,1,0:T(8,128)S(1)}, bf16[32,256]{1,0:T(8,128)(2,1)S(1)}) custom-call(bf16[4,32,256]{2,1,0:T(8,128)(2,1)S(1)} %get-tuple-element.57.refs_0_, bf16[4,32,256]{2,1,0:T(8,128)(2,1)S(1)} %collective-permute-done.4.refs_1_, bf16[4,32,256]{2,1,0:T(8,128)(2,1)S(1)} %collective-permute-done.5.refs_2_, ...), custom_call_target="tpu_custom_call" | custom-call | flops 75497 | bytes 3145 | tf_op jit(solution)/shard_map/pallas_call | solution.py:304
  32.1 0.6 collective-permute-start.11
  32.7 3.0 %collective-permute-done.12.refs_5_.refs_7_ = bf16[128,1024]{1,0:T(8,128)(2,1)S(1)} collective-permute-done((bf16[128,1024]{1,0:T(8,128)(2,1)S(1)}, bf16[128,1024]{1,0:T(8,128)(2,1)S(1)}, u32[]{:S(2)}, u32[]{:S(2)}) %collective-permute-start.12) | collective-permute-done | bytes 262176 | tf_op jit(solution)/shard_map/ppermute | solution.py:506
  35.7 0.2 collective-permute-done.11.other_ref
  35.9 1.1 %collective-permute-done.18.other_ref = bf16[128,1024]{1,0:T(8,128)(2,1)S(1)} collective-permute-done((bf16[128,1024]{1,0:T(8,128)(2,1)S(1)}, bf16[128,1024]{1,0:T(8,128)(2,1)S(1)}, u32[]{:S(2)}, u32[]{:S(2)}) %collective-permute-start.18) | collective-permute-done | bytes 262176 | tf_op jit(solution)/shard_map/ppermute | solution.py:506
  37.1 2.7 %collective-permute-start.23 = (bf16[128,512]{1,0:T(8,128)(2,1)S(1)}, bf16[128,512]{1,0:T(8,128)(2,1)S(1)}, u32[]{:S(2)}, u32[]{:S(2)}) collective-permute-start(bf16[128,512]{1,0:T(8,128)(2,1)S(1)} %get-tuple-element.82.mine_ref), channel_id=1, source_target_pairs={{0,16},{4,20},{8,24},{12,28},{16,0},{20,4},{24,8},{28,12},{1,17},{... | collective-permute-start | bytes 393224 | tf_op jit(solution)/shard_map/ppermute | solution.py:506
  39.7 0.3 shard_map.87
  40.0 0.7 %collective-permute-start.14 = (bf16[32,256]{1,0:T(8,128)(2,1)S(1)}, bf16[32,256]{1,0:T(8,128)(2,1)S(1)}, u32[]{:S(2)}, u32[]{:S(2)}) collective-permute-start(bf16[32,256]{1,0:T(8,128)(2,1)S(1)} %get-tuple-element.73.refs_0_.refs_1_), channel_id=1, source_target_pairs={{0,2},{1,3},{2,0},{3,1},{4,6},{5,7},{6,4},{7,5},{8,10},{9,11},{10,... | collective-permute-start | bytes 49160 | tf_op jit(solution)/shard_map/ppermute | solution.py:506
  40.7 1.5 %collective-permute-start.15 = (bf16[32,256]{1,0:T(8,128)(2,1)S(1)}, bf16[32,256]{1,0:T(8,128)(2,1)S(1)}, u32[]{:S(2)}, u32[]{:S(2)}) collective-permute-start(bf16[32,256]{1,0:T(8,128)(2,1)S(1)} %get-tuple-element.73.refs_0_.refs_1_), channel_id=1, source_target_pairs={{0,4},{4,0},{8,12},{12,8},{16,20},{20,16},{24,28},{28,24},{1,5},{5... | collective-permute-start | bytes 49160 | tf_op jit(solution)/shard_map/ppermute | solution.py:506
  42.3 1.3 %collective-permute-start.16 = (bf16[32,256]{1,0:T(8,128)(2,1)S(1)}, bf16[32,256]{1,0:T(8,128)(2,1)S(1)}, u32[]{:S(2)}, u32[]{:S(2)}) collective-permute-start(bf16[32,256]{1,0:T(8,128)(2,1)S(1)} %get-tuple-element.73.refs_0_.refs_1_), channel_id=1, source_target_pairs={{0,6},{1,7},{2,4},{3,5},{4,2},{5,3},{6,0},{7,1},{8,14},{9,15},{10,... | collective-permute-start | bytes 49160 | tf_op jit(solution)/shard_map/ppermute | solution.py:513
  43.6 0.7 %collective-permute-start.19 = (bf16[128,768]{1,0:T(8,128)(2,1)S(1)}, bf16[128,768]{1,0:T(8,128)(2,1)S(1)}, u32[]{:S(2)}, u32[]{:S(2)}) collective-permute-start(bf16[128,768]{1,0:T(8,128)(2,1)S(1)} %shard_map.90), channel_id=1, source_target_pairs={{0,2},{1,3},{2,0},{3,1},{4,6},{5,7},{6,4},{7,5},{8,10},{9,11},{10,... | collective-permute-start | bytes 589832 | tf_op jit(solution)/shard_map/ppermute | solution.py:506
  44.3 0.2 collective-permute-done.15.refs_2_
  44.5 2.6 %collective-permute-done.16.refs_3_ = bf16[32,256]{1,0:T(8,128)(2,1)S(1)} collective-permute-done((bf16[32,256]{1,0:T(8,128)(2,1)S(1)}, bf16[32,256]{1,0:T(8,128)(2,1)S(1)}, u32[]{:S(2)}, u32[]{:S(2)}) %collective-permute-start.16) | collective-permute-done | bytes 16416 | tf_op jit(solution)/shard_map/ppermute | solution.py:513
  47.1 0.6 shard_map.88
  47.7 0.9 %copy-done.5 = bf16[128,768]{1,0:T(8,128)(2,1)S(1)} copy-done((bf16[128,768]{1,0:T(8,128)(2,1)S(1)}, bf16[128,768]{1,0:T(8,128)(2,1)}, u32[]{:S(2)}) %copy-start.5) | copy-done | bytes 196632
  48.6 1.4 %collective-permute-start.24 = (bf16[128,1536]{1,0:T(8,128)(2,1)S(1)}, bf16[128,1536]{1,0:T(8,128)(2,1)S(1)}, u32[]{:S(2)}, u32[]{:S(2)}) collective-permute-start(bf16[128,1536]{1,0:T(8,128)(2,1)S(1)} %shard_map.95), channel_id=1, source_target_pairs={{0,2},{1,3},{2,0},{3,1},{4,6},{5,7},{6,4},{7,5},{8,10},{9,11},{10,... | collective-permute-start | bytes 1179656 | tf_op jit(solution)/shard_map/ppermute | solution.py:506
  50.1 0.1 collective-permute-start.20
  50.2 0.5 collective-permute-start.21
  50.8 1.6 %collective-permute-start.17 = (bf16[32,256]{1,0:T(8,128)(2,1)S(1)}, bf16[32,256]{1,0:T(8,128)(2,1)S(1)}, u32[]{:S(2)}, u32[]{:S(2)}) collective-permute-start(bf16[32,256]{1,0:T(8,128)(2,1)S(1)} %get-tuple-element.74.refs_1_.refs_0_.refs_3_), channel_id=1, source_target_pairs={{0,8},{4,12},{8,0},{12,4},{16,24},{20,28},{24,16},{28,20},{1,9},{5... | collective-permute-start | bytes 49160 | tf_op jit(solution)/shard_map/ppermute | solution.py:506
  52.3 2.2 %collective-permute-done.17.refs_1_ = bf16[32,256]{1,0:T(8,128)(2,1)S(1)} collective-permute-done((bf16[32,256]{1,0:T(8,128)(2,1)S(1)}, bf16[32,256]{1,0:T(8,128)(2,1)S(1)}, u32[]{:S(2)}, u32[]{:S(2)}) %collective-permute-start.17) | collective-permute-done | bytes 16416 | tf_op jit(solution)/shard_map/ppermute | solution.py:506
  54.5 0.6 shard_map.93
  55.1 0.4 collective-permute-start.22
  55.5 4.3 %collective-permute-done.22._.refs_1_ = bf16[32,256]{1,0:T(8,128)(2,1)S(1)} collective-permute-done((bf16[32,256]{1,0:T(8,128)(2,1)S(1)}, bf16[32,256]{1,0:T(8,128)(2,1)S(1)}, u32[]{:S(2)}, u32[]{:S(2)}) %collective-permute-start.22) | collective-permute-done | bytes 16416 | tf_op jit(solution)/shard_map/ppermute | solution.py:506
  59.8 0.1 collective-permute-start.25
  59.9 1.7 %collective-permute-done.25.refs_15_ = bf16[128,1536]{1,0:T(8,128)(2,1)S(1)} collective-permute-done((bf16[128,1536]{1,0:T(8,128)(2,1)S(1)}, bf16[128,1536]{1,0:T(8,128)(2,1)S(1)}, u32[]{:S(2)}, u32[]{:S(2)}) %collective-permute-start.25) | collective-permute-done | bytes 393248 | tf_op jit(solution)/shard_map/ppermute | solution.py:506
  61.6 1.1 %shard_map.97 = bf16[4,32,256]{2,1,0:T(8,128)(2,1)S(1)} custom-call(bf16[32,256]{1,0:T(8,128)(2,1)S(1)} %get-tuple-element.77.refs_0_, bf16[32,256]{1,0:T(8,128)(2,1)S(1)} %collective-permute-done.22._.refs_1_, f32[4,32,128]{2,1,0:T(8,128)S(1)} %get-tuple-element.78.refs_2_, f32[4,32,128]{2,1,0:T(8,128)S(1)} %get-tuple-element.79.refs_3_, ...), custom_call_target="tpu_custom_call" | custom-call | flops 67108 | bytes 4194 | tf_op jit(solution)/shard_map/pallas_call | solution.py:474
  62.6 5.8 %all-gather = bf16[16,32,256]{2,1,0:T(8,128)(2,1)S(1)} all-gather(bf16[4,32,256]{2,1,0:T(8,128)(2,1)S(1)} %shard_map.97), channel_id=2, replica_groups=mesh['leaf'=8,'rhs'=4] {'rhs'}, dimensions={0}, use_global_device_ids=true | all-gather | bytes 327680 | tf_op jit(solution)/shard_map/all_gather | solution.py:614
  68.4 1.0 %shard_map.98 = f32[8,64,128]{2,1,0:T(8,128)} custom-call(f32[4,64,128]{2,1,0:T(8,128)S(1)} %get-tuple-element.49.far_ref, f32[4,64,128]{2,1,0:T(8,128)S(1)} %get-tuple-element.56.own_ref, bf16[4,4,32,256]{3,2,1,0:T(8,128)(2,1)S(1)} %bitcast.5, bf16[8,128,256]{2,1,0:T(8,128)(2,1)S(1)} %copy-done.3), custom_call_target="tpu_custom_call" | custom-call | flops 33554 | bytes 524 | tf_op jit(solution)/shard_map/pallas_call | solution.py:497
  (40 shorter events, 0.3 us)
Async XLA Ops:
  0.0 11.6 %copy-start.2 = (bf16[8,128,256]{2,1,0:T(8,128)(2,1)S(1)}, bf16[8,128,256]{2,1,0:T(8,128)(2,1)}, u32[]{:S(2)}) copy-start(bf16[8,128,256]{2,1,0:T(8,128)(2,1)} %refs_3_.1) | copy-start | bytes 1572868
  0.0 6.6 %collective-permute-start = (bf16[64,1024]{1,0:T(8,128)(2,1)}, bf16[64,1024]{1,0:T(8,128)(2,1)S(1)}, u32[]{:S(2)}, u32[]{:S(2)}) collective-permute-start(bf16[64,1024]{1,0:T(8,128)(2,1)} %refs_0_.1), channel_id=1, source_target_pairs={{0,2},{1,3},{2,0},{3,1},{4,6},{5,7},{6,4},{7,5},{8,10},{9,11},{10,... | collective-permute-start | bytes 393224 | tf_op jit(solution)/shard_map/ppermute | solution.py:506
  2.9 3.7 %collective-permute-start.1 = (bf16[64,1024]{1,0:T(8,128)(2,1)}, bf16[64,1024]{1,0:T(8,128)(2,1)S(1)}, u32[]{:S(2)}, u32[]{:S(2)}) collective-permute-start(bf16[64,1024]{1,0:T(8,128)(2,1)} %refs_0_.1), channel_id=1, source_target_pairs={{0,1},{1,0},{2,3},{3,2},{4,5},{5,4},{6,7},{7,6},{8,9},{9,8},{10,11... | collective-permute-start | bytes 393224 | tf_op jit(solution)/shard_map/ppermute | solution.py:506
  2.9 8.6 %copy-start.6 = (bf16[64,1024]{1,0:T(8,128)(2,1)S(1)}, bf16[64,1024]{1,0:T(8,128)(2,1)}, u32[]{:S(2)}) copy-start(bf16[64,1024]{1,0:T(8,128)(2,1)} %refs_0_.1) | copy-start | bytes 393220
  6.6 1.3 %collective-permute-start.2 = (bf16[64,1024]{1,0:T(8,128)(2,1)S(1)}, bf16[64,1024]{1,0:T(8,128)(2,1)S(1)}, u32[]{:S(2)}, u32[]{:S(2)}) collective-permute-start(bf16[64,1024]{1,0:T(8,128)(2,1)S(1)} %collective-permute-done.refs_1_), channel_id=1, source_target_pairs={{0,1},{1,0},{2,3},{3,2},{4,5},{5,4},{6,7},{7,6},{8,9},{9,8},{10,11... | collective-permute-start | bytes 393224 | tf_op jit(solution)/shard_map/ppermute | solution.py:506
  8.0 9.7 %collective-permute-start.3 = (bf16[4,128,1024]{2,1,0:T(8,128)(2,1)}, bf16[4,128,1024]{2,1,0:T(8,128)(2,1)S(1)}, u32[]{:S(2)}, u32[]{:S(2)}) collective-permute-start(bf16[4,128,1024]{2,1,0:T(8,128)(2,1)} %get-tuple-element.52.refs_4_.own_ref.refs_16_), channel_id=1, source_target_pairs={{0,1},{1,0},{2,3},{3,2},{4,5},{5,4},{6,7},{7,6},{8,9},{9,8},{10,11... | collective-permute-start | bytes 3145736 | tf_op jit(solution)/shard_map/ppermute | solution.py:506
  8.1 18.6 %collective-permute-start.7 = (bf16[3,128,768]{2,1,0:T(8,128)(2,1)}, bf16[3,128,768]{2,1,0:T(8,128)(2,1)S(1)}, u32[]{:S(2)}, u32[]{:S(2)}) collective-permute-start(bf16[3,128,768]{2,1,0:T(8,128)(2,1)} %get-tuple-element.45), channel_id=1, source_target_pairs={{0,2},{1,3},{2,0},{3,1},{4,6},{5,7},{6,4},{7,5},{8,10},{9,11},{10,... | collective-permute-start | bytes 1769480 | tf_op jit(solution)/shard_map/ppermute | solution.py:506
  9.9 1.7 %copy-start.7 = (s32[4096]{0:T(1024)S(1)}, s32[4096]{0:T(1024)}, u32[]{:S(2)}) copy-start(s32[4096]{0:T(1024)} %param.9) | copy-start | bytes 49156
  9.9 11.7 %collective-permute-start.8 = (bf16[128,1024]{1,0:T(8,128)(2,1)}, bf16[128,1024]{1,0:T(8,128)(2,1)S(1)}, u32[]{:S(2)}, u32[]{:S(2)}) collective-permute-start(bf16[128,1024]{1,0:T(8,128)(2,1)} %get-tuple-element.63.mine_ref), channel_id=1, source_target_pairs={{0,4},{4,0},{8,12},{12,8},{16,20},{20,16},{24,28},{28,24},{1,5},{5... | collective-permute-start | bytes 786440 | tf_op jit(solution)/shard_map/ppermute | solution.py:506
  11.6 1.2 %copy-start.1 = (bf16[8,128,512]{2,1,0:T(8,128)(2,1)S(1)}, bf16[8,128,512]{2,1,0:T(8,128)(2,1)}, u32[]{:S(2)}) copy-start(bf16[8,128,512]{2,1,0:T(8,128)(2,1)} %refs_2_.1) | copy-start | bytes 3145732
  16.2 8.9 %collective-permute-start.6 = (bf16[4,32,256]{2,1,0:T(8,128)(2,1)S(1)}, bf16[4,32,256]{2,1,0:T(8,128)(2,1)S(1)}, u32[]{:S(2)}, u32[]{:S(2)}) collective-permute-start(bf16[4,32,256]{2,1,0:T(8,128)(2,1)S(1)} %get-tuple-element.60), channel_id=1, source_target_pairs={{0,3},{1,2},{2,1},{3,0},{4,7},{5,6},{6,5},{7,4},{8,11},{9,10},{10,... | collective-permute-start | bytes 196616 | tf_op jit(solution)/shard_map/ppermute | solution.py:506
  16.3 10.4 %collective-permute-start.4 = (bf16[4,32,256]{2,1,0:T(8,128)(2,1)S(1)}, bf16[4,32,256]{2,1,0:T(8,128)(2,1)S(1)}, u32[]{:S(2)}, u32[]{:S(2)}) collective-permute-start(bf16[4,32,256]{2,1,0:T(8,128)(2,1)S(1)} %get-tuple-element.53), channel_id=1, source_target_pairs={{0,2},{1,3},{2,0},{3,1},{4,6},{5,7},{6,4},{7,5},{8,10},{9,11},{10,... | collective-permute-start | bytes 196616 | tf_op jit(solution)/shard_map/ppermute | solution.py:506
  17.7 3.9 %copy-start.4 = (bf16[128,1024]{1,0:T(8,128)(2,1)S(1)}, bf16[128,1024]{1,0:T(8,128)(2,1)}, u32[]{:S(2)}) copy-start(bf16[128,1024]{1,0:T(8,128)(2,1)} %get-tuple-element.63.mine_ref) | copy-start | bytes 786436
  17.7 12.9 %copy-start = (bf16[4,128,1024]{2,1,0:T(8,128)(2,1)S(1)}, bf16[4,128,1024]{2,1,0:T(8,128)(2,1)}, u32[]{:S(2)}) copy-start(bf16[4,128,1024]{2,1,0:T(8,128)(2,1)} %get-tuple-element.52.refs_4_.own_ref.refs_16_) | copy-start | bytes 3145732
  21.1 5.7 %collective-permute-start.5 = (bf16[4,32,256]{2,1,0:T(8,128)(2,1)S(1)}, bf16[4,32,256]{2,1,0:T(8,128)(2,1)S(1)}, u32[]{:S(2)}, u32[]{:S(2)}) collective-permute-start(bf16[4,32,256]{2,1,0:T(8,128)(2,1)S(1)} %get-tuple-element.59), channel_id=1, source_target_pairs={{0,1},{1,0},{2,3},{3,2},{4,5},{5,4},{6,7},{7,6},{8,9},{9,8},{10,11... | collective-permute-start | bytes 196616 | tf_op jit(solution)/shard_map/ppermute | solution.py:506
  26.8 3.8 %collective-permute-start.9 = (bf16[3,128,768]{2,1,0:T(8,128)(2,1)S(1)}, bf16[3,128,768]{2,1,0:T(8,128)(2,1)S(1)}, u32[]{:S(2)}, u32[]{:S(2)}) collective-permute-start(bf16[3,128,768]{2,1,0:T(8,128)(2,1)S(1)} %collective-permute-done.7.refs_5_), channel_id=1, source_target_pairs={{0,1},{1,0},{2,3},{3,2},{4,5},{5,4},{6,7},{7,6},{8,9},{9,8},{10,11... | collective-permute-start | bytes 1769480 | tf_op jit(solution)/shard_map/ppermute | solution.py:506
  26.8 5.3 %collective-permute-start.10 = (bf16[128,1024]{1,0:T(8,128)(2,1)S(1)}, bf16[128,1024]{1,0:T(8,128)(2,1)S(1)}, u32[]{:S(2)}, u32[]{:S(2)}) collective-permute-start(bf16[128,1024]{1,0:T(8,128)(2,1)S(1)} %get-tuple-element.69.refs_4_.refs_6_), channel_id=1, source_target_pairs={{0,1},{1,0},{2,3},{3,2},{4,5},{5,4},{6,7},{7,6},{8,9},{9,8},{10,11... | collective-permute-start | bytes 786440 | tf_op jit(solution)/shard_map/ppermute | solution.py:506
  27.3 8.5 %collective-permute-start.12 = (bf16[128,1024]{1,0:T(8,128)(2,1)S(1)}, bf16[128,1024]{1,0:T(8,128)(2,1)S(1)}, u32[]{:S(2)}, u32[]{:S(2)}) collective-permute-start(bf16[128,1024]{1,0:T(8,128)(2,1)S(1)} %get-tuple-element.69.refs_4_.refs_6_), channel_id=1, source_target_pairs={{0,2},{1,3},{2,0},{3,1},{4,6},{5,7},{6,4},{7,5},{8,10},{9,11},{10,... | collective-permute-start | bytes 786440 | tf_op jit(solution)/shard_map/ppermute | solution.py:506
  29.0 8.0 %collective-permute-start.18 = (bf16[128,1024]{1,0:T(8,128)(2,1)S(1)}, bf16[128,1024]{1,0:T(8,128)(2,1)S(1)}, u32[]{:S(2)}, u32[]{:S(2)}) collective-permute-start(bf16[128,1024]{1,0:T(8,128)(2,1)S(1)} %get-tuple-element.65.mine_ref), channel_id=1, source_target_pairs={{0,8},{4,12},{8,0},{12,4},{16,24},{20,28},{24,16},{28,20},{1,9},{5... | collective-permute-start | bytes 786440 | tf_op jit(solution)/shard_map/ppermute | solution.py:506
  32.1 3.8 %collective-permute-start.11 = (bf16[32,256]{1,0:T(8,128)(2,1)S(1)}, bf16[32,256]{1,0:T(8,128)(2,1)S(1)}, u32[]{:S(2)}, u32[]{:S(2)}) collective-permute-start(bf16[32,256]{1,0:T(8,128)(2,1)S(1)} %get-tuple-element.70.mine_ref), channel_id=1, source_target_pairs={{0,2},{1,3},{2,0},{3,1},{4,6},{5,7},{6,4},{7,5},{8,10},{9,11},{10,... | collective-permute-start | bytes 49160 | tf_op jit(solution)/shard_map/ppermute | solution.py:506
  35.9 4.1 %collective-permute-start.13 = (bf16[128,1024]{1,0:T(8,128)(2,1)S(1)}, bf16[128,1024]{1,0:T(8,128)(2,1)S(1)}, u32[]{:S(2)}, u32[]{:S(2)}) collective-permute-start(bf16[128,1024]{1,0:T(8,128)(2,1)S(1)} %collective-permute-done.12.refs_5_.refs_7_), channel_id=1, source_target_pairs={{0,1},{1,0},{2,3},{3,2},{4,5},{5,4},{6,7},{7,6},{8,9},{9,8},{10,11... | collective-permute-start | bytes 786440 | tf_op jit(solution)/shard_map/ppermute | solution.py:506
  37.1 10.6 %collective-permute-start.23 = (bf16[128,512]{1,0:T(8,128)(2,1)S(1)}, bf16[128,512]{1,0:T(8,128)(2,1)S(1)}, u32[]{:S(2)}, u32[]{:S(2)}) collective-permute-start(bf16[128,512]{1,0:T(8,128)(2,1)S(1)} %get-tuple-element.82.mine_ref), channel_id=1, source_target_pairs={{0,16},{4,20},{8,24},{12,28},{16,0},{20,4},{24,8},{28,12},{1,17},{... | collective-permute-start | bytes 393224 | tf_op jit(solution)/shard_map/ppermute | solution.py:506
  40.0 4.3 %collective-permute-start.14 = (bf16[32,256]{1,0:T(8,128)(2,1)S(1)}, bf16[32,256]{1,0:T(8,128)(2,1)S(1)}, u32[]{:S(2)}, u32[]{:S(2)}) collective-permute-start(bf16[32,256]{1,0:T(8,128)(2,1)S(1)} %get-tuple-element.73.refs_0_.refs_1_), channel_id=1, source_target_pairs={{0,2},{1,3},{2,0},{3,1},{4,6},{5,7},{6,4},{7,5},{8,10},{9,11},{10,... | collective-permute-start | bytes 49160 | tf_op jit(solution)/shard_map/ppermute | solution.py:506
  40.7 3.7 %collective-permute-start.15 = (bf16[32,256]{1,0:T(8,128)(2,1)S(1)}, bf16[32,256]{1,0:T(8,128)(2,1)S(1)}, u32[]{:S(2)}, u32[]{:S(2)}) collective-permute-start(bf16[32,256]{1,0:T(8,128)(2,1)S(1)} %get-tuple-element.73.refs_0_.refs_1_), channel_id=1, source_target_pairs={{0,4},{4,0},{8,12},{12,8},{16,20},{20,16},{24,28},{28,24},{1,5},{5... | collective-permute-start | bytes 49160 | tf_op jit(solution)/shard_map/ppermute | solution.py:506
  42.3 4.8 %collective-permute-start.16 = (bf16[32,256]{1,0:T(8,128)(2,1)S(1)}, bf16[32,256]{1,0:T(8,128)(2,1)S(1)}, u32[]{:S(2)}, u32[]{:S(2)}) collective-permute-start(bf16[32,256]{1,0:T(8,128)(2,1)S(1)} %get-tuple-element.73.refs_0_.refs_1_), channel_id=1, source_target_pairs={{0,6},{1,7},{2,4},{3,5},{4,2},{5,3},{6,0},{7,1},{8,14},{9,15},{10,... | collective-permute-start | bytes 49160 | tf_op jit(solution)/shard_map/ppermute | solution.py:513
  43.6 6.6 %collective-permute-start.19 = (bf16[128,768]{1,0:T(8,128)(2,1)S(1)}, bf16[128,768]{1,0:T(8,128)(2,1)S(1)}, u32[]{:S(2)}, u32[]{:S(2)}) collective-permute-start(bf16[128,768]{1,0:T(8,128)(2,1)S(1)} %shard_map.90), channel_id=1, source_target_pairs={{0,2},{1,3},{2,0},{3,1},{4,6},{5,7},{6,4},{7,5},{8,10},{9,11},{10,... | collective-permute-start | bytes 589832 | tf_op jit(solution)/shard_map/ppermute | solution.py:506
  47.7 0.9 %copy-start.5 = (bf16[128,768]{1,0:T(8,128)(2,1)S(1)}, bf16[128,768]{1,0:T(8,128)(2,1)}, u32[]{:S(2)}) copy-start(bf16[128,768]{1,0:T(8,128)(2,1)} %get-tuple-element.84.refs_1_) | copy-start | bytes 589828
  48.6 11.1 %collective-permute-start.24 = (bf16[128,1536]{1,0:T(8,128)(2,1)S(1)}, bf16[128,1536]{1,0:T(8,128)(2,1)S(1)}, u32[]{:S(2)}, u32[]{:S(2)}) collective-permute-start(bf16[128,1536]{1,0:T(8,128)(2,1)S(1)} %shard_map.95), channel_id=1, source_target_pairs={{0,2},{1,3},{2,0},{3,1},{4,6},{5,7},{6,4},{7,5},{8,10},{9,11},{10,... | collective-permute-start | bytes 1179656 | tf_op jit(solution)/shard_map/ppermute | solution.py:506
  50.1 4.4 %collective-permute-start.20 = (bf16[128,1024]{1,0:T(8,128)(2,1)S(1)}, bf16[128,1024]{1,0:T(8,128)(2,1)S(1)}, u32[]{:S(2)}, u32[]{:S(2)}) collective-permute-start(bf16[128,1024]{1,0:T(8,128)(2,1)S(1)} %shard_map.91), channel_id=1, source_target_pairs={{0,1},{1,0},{2,3},{3,2},{4,5},{5,4},{6,7},{7,6},{8,9},{9,8},{10,11... | collective-permute-start | bytes 786440 | tf_op jit(solution)/shard_map/ppermute | solution.py:506
  50.2 4.3 %collective-permute-start.21 = (bf16[128,768]{1,0:T(8,128)(2,1)S(1)}, bf16[128,768]{1,0:T(8,128)(2,1)S(1)}, u32[]{:S(2)}, u32[]{:S(2)}) collective-permute-start(bf16[128,768]{1,0:T(8,128)(2,1)S(1)} %shard_map.92), channel_id=1, source_target_pairs={{0,1},{1,0},{2,3},{3,2},{4,5},{5,4},{6,7},{7,6},{8,9},{9,8},{10,11... | collective-permute-start | bytes 589832 | tf_op jit(solution)/shard_map/ppermute | solution.py:506
  50.8 3.7 %collective-permute-start.17 = (bf16[32,256]{1,0:T(8,128)(2,1)S(1)}, bf16[32,256]{1,0:T(8,128)(2,1)S(1)}, u32[]{:S(2)}, u32[]{:S(2)}) collective-permute-start(bf16[32,256]{1,0:T(8,128)(2,1)S(1)} %get-tuple-element.74.refs_1_.refs_0_.refs_3_), channel_id=1, source_target_pairs={{0,8},{4,12},{8,0},{12,4},{16,24},{20,28},{24,16},{28,20},{1,9},{5... | collective-permute-start | bytes 49160 | tf_op jit(solution)/shard_map/ppermute | solution.py:506
  55.1 4.7 %collective-permute-start.22 = (bf16[32,256]{1,0:T(8,128)(2,1)S(1)}, bf16[32,256]{1,0:T(8,128)(2,1)S(1)}, u32[]{:S(2)}, u32[]{:S(2)}) collective-permute-start(bf16[32,256]{1,0:T(8,128)(2,1)S(1)} %get-tuple-element.77.refs_0_), channel_id=1, source_target_pairs={{0,16},{4,20},{8,24},{12,28},{16,0},{20,4},{24,8},{28,12},{1,17},{... | collective-permute-start | bytes 49160 | tf_op jit(solution)/shard_map/ppermute | solution.py:506
  59.8 1.8 %collective-permute-start.25 = (bf16[128,1536]{1,0:T(8,128)(2,1)S(1)}, bf16[128,1536]{1,0:T(8,128)(2,1)S(1)}, u32[]{:S(2)}, u32[]{:S(2)}) collective-permute-start(bf16[128,1536]{1,0:T(8,128)(2,1)S(1)} %shard_map.96.refs_14_), channel_id=1, source_target_pairs={{0,1},{1,0},{2,3},{3,2},{4,5},{5,4},{6,7},{7,6},{8,9},{9,8},{10,11... | collective-permute-start | bytes 1179656 | tf_op jit(solution)/shard_map/ppermute | solution.py:506
  61.6 6.9 %copy-start.3 = (bf16[8,128,256]{2,1,0:T(8,128)(2,1)S(1)}, bf16[8,128,256]{2,1,0:T(8,128)(2,1)}, u32[]{:S(2)}) copy-start(bf16[8,128,256]{2,1,0:T(8,128)(2,1)} %coupling_ref.1) | copy-start | bytes 1572868

commit v3 on v2

--- a/solution.py
+++ b/solution.py
@@ -396,7 +396,8 @@
     solved_cross, refs = refs[: cross_levels - 1], refs[cross_levels - 1 :]
     solved_top, solved_half, refs = refs[0], refs[1], refs[2:]
     count = 2 * CORES * (cross_levels - 1)
-    cross_packs, (tail, near_tail, keep, keep_near) = refs[:count], refs[count:]
+    cross_packs, others = refs[:count], refs[count:]
+    tail, near_tail, half_tail, near_half_tail, keep, keep_near = others
     levels, total = half_levels(per_dev)
     rank = out_ref.shape[2]
     node_size = 2 * rank
@@ -420,17 +421,14 @@
     incoming = choose(half)
     for level in range(cross_levels - 2, -1, -1):
         packs = cross_packs[2 * CORES * level : 2 * CORES * (level + 1)]
-        own, far, near, far_near = packs
-        if level == 0:
-            couplings = [ref[:, columns(ref)] for ref in packs]
-        else:
-            start = node_size + (total + level - 1) * rank
-            couplings = [
-                own[:, columns(own)],
-                tail[:, start : start + rank],
-                near[:, columns(near)],
-                near_tail[:, start : start + rank],
-            ]
+        own, _, near, _ = packs
+        start = node_size + level * rank
+        couplings = [
+            own[:, columns(own)],
+            tail[:, start : start + rank],
+            near[:, columns(near)],
+            near_tail[:, start : start + rank],
+        ]
         for flip, coupling in zip(PIECES, couplings):
             piece = place ^ flip
             solved = solved_cross[level][piece]
@@ -446,12 +444,12 @@
         following = []
         for n in range(count):
             node = base + n
-            start = node_size + node * rank
+            start = node * rank
             couplings = (
                 keep[node, :, columns(keep)],
-                tail[:, start : start + rank],
+                half_tail[:, start : start + rank],
                 keep_near[node, :, columns(keep)],
-                near_tail[:, start : start + rank],
+                near_half_tail[:, start : start + rank],
             )
             for flip, coupling in zip(PIECES, couplings):
                 piece = place ^ flip
@@ -566,18 +564,19 @@
     parts = [own_same, far_same, swap(own_cross, "rhs", 1), far_cross]
     half_far = after(half_far, (parts, carrier))
     half_near = swap(half_far, "rhs", 1)
-    fars = [swap(after(ancestors[0], half_far), "rhs", CORES)]
-    nears = [swap(after(ancestors[0], half_far), "rhs", 1)]
+    factors = [(0, node_size + rank)]
+    fars = [swap(join([ancestors[0]], half_far, factors), "rhs", CORES)]
 
     solved_half, current = group_up(per_dev, parts, [keep, half_far, keep_near, half_near])
-    other = swap(after(current, nears[0]), "rhs", CORES)
+    own_near = swap(join([ancestors[0]], current), "rhs", 1)
+    other = swap(current, "rhs", CORES)
+    half_tail = swap(join([send_coupling], other), "rhs", CORES)
     ancestor, carrier = rise(carrier, 1, other)
     ancestors.append(ancestor)
-    solved_top, current = half_up(current, other, keep, keep_near)
+    solved_top, current = half_up(current, after(other, own_near), keep, keep_near)
     fars[0] = after(fars[0], other)
     near_far = swap(fars[0], "rhs", 1)
-    cross_packs = [[ancestors[0], fars[0], nears[0], near_far]]
-    factors = [(0, node_size + rank)]
+    cross_packs = [[ancestors[0], fars[0], own_near, near_far]]
     fars.append(swap(join([ancestors[1]], current, factors), "rhs", CORES))
     current = after(current, near_far)
     inputs = [
@@ -586,6 +585,7 @@
         swap(current, "leaf", 1),
         far_swap(current, 1, CORES),
     ]
+    inputs = after(inputs, half_tail)
 
     solved_cross = []
     for level in range(cross_levels - 1):
@@ -603,13 +603,12 @@
                 ancestors.append(ancestor)
             for later in range(2, cross_levels - 1):
                 fars.append(swap(join([ancestors[later]], current, factors), "rhs", CORES))
-            blocks = [ancestors[-1], send_coupling, *ancestors[1:-1]]
-            cuts = [(0, node_size), (0, send_coupling.shape[1])]
-            cuts += [(node_size + rank, rank)] * (cross_levels - 2)
-            tail = swap(join(blocks, current, cuts), "rhs", CORES)
+            near_half_tail = swap(join([half_tail], current), "rhs", 1)
+            cuts = [(0, node_size)] + [(node_size + rank, rank)] * (cross_levels - 1)
+            tail = swap(join([ancestors[-1], *ancestors[:-1]], current, cuts), "rhs", CORES)
 
     tail = hop(cross_levels - 1, ancestors[-1], tail, inputs[1])
-    others = [tail, swap(tail, "rhs", 1), keep, keep_near]
+    others = [tail, swap(tail, "rhs", 1), half_tail, near_half_tail, keep, keep_near]
     shares = way_down(per_dev, inputs, solved_cross, solved_top, solved_half, cross_packs, others)
     incoming = lax.all_gather(shares, "rhs", axis=0)
     return finish(far_values, own_values, incoming, leaf_coupling)

time: 69.7 us -> 69.6 us (level)
  starting transfers between devices: 23.8 us -> 26.6 us
  waiting for transfers between devices: 22.4 us -> 20.3 us
  local copies, waits for them, and re-layouts: 2.13 us -> 1.25 us
    ppermute x25 -> x27, starting transfers between devices: 22.5 us -> 25.2 us  [swap(): lax.ppermute(block, axis, [(i, i ^ bit) for i in range(lax.axis_size(axis...]
    ppermute x1, waiting for transfers between devices: 2.59 us -> 1.13 us  [far_swap(): lax.ppermute(block, ('leaf', 'rhs'), [(i, i ^ flip) for i in range(count)])]
    unnamed x16, local copies, waits for them, and re-layouts: 2.13 us -> 1.25 us
    ppermute x25 -> x27, waiting for transfers between devices: 19.8 us -> 19.2 us  [swap(): lax.ppermute(block, axis, [(i, i ^ bit) for i in range(lax.axis_size(axis...]
  transfers between devices with their start and end apart: 26 -> 28, of which waited for: 12 -> 13; matrix products, arithmetic and copies ran while one was open for 0% -> 0% of each run, Pallas kernels for 19% -> 19%
where the time goes in v3:
time: 69.6 us; the launch traced here: 69.4 us
  starting transfers between devices  26.6 us (38%)
  waiting for transfers between devices  20.3 us (29%)
  Pallas kernels  15.1 us (22%)
  blocking collectives  5.79 us (8%)
  local copies, waits for them, and re-layouts  1.25 us (2%)
    ppermute x27, starting transfers between devices, swap(): lax.ppermute(block, axis, [(i, i ^ bit) for i in range(lax.axis_size(axis...  25.2 us
    ppermute x27, waiting for transfers between devices, swap(): lax.ppermute(block, axis, [(i, i ^ bit) for i in range(lax.axis_size(axis...  19.2 us
    pallas_call x2, Pallas kernels, leaf_up(): pl.pallas_call(functools.partial(leaf_kernel, len(points)), grid_spec=plt...  6.81 us
    all_gather x1, blocking collectives, body(): incoming = lax.all_gather(shares, 'rhs', axis=0)  5.79 us
    pallas_call x1, Pallas kernels, pack(): pl.pallas_call(functools.partial(pack_kernel, per_dev), in_specs=[pl.Bloc...  2.99 us
    pallas_call x1, Pallas kernels, group_up(): pl.pallas_call(functools.partial(group_up_kernel, per_dev), out_shape=[ja...  1.48 us
  transfers between devices with their start and end apart: 28, of which 13 were waited for; matrix products, arithmetic and copies ran while one was open for 0% of the time, Pallas kernels for 19%

profile of v3, /device:TPU:0, one launch (start us, length us, event | category | flops | bytes accessed | tf_op | source)
XLA Modules:
  0.0 69.4 jit_solution(10084565127445726379)
XLA Ops:
  0.0 2.9 %collective-permute-start = (bf16[64,1024]{1,0:T(8,128)(2,1)}, bf16[64,1024]{1,0:T(8,128)(2,1)S(1)}, u32[]{:S(2)}, u32[]{:S(2)}) collective-permute-start(bf16[64,1024]{1,0:T(8,128)(2,1)} %refs_0_.1), channel_id=1, source_target_pairs={{0,2},{1,3},{2,0},{3,1},{4,6},{5,7},{6,4},{7,5},{8,10},{9,11},{10,... | collective-permute-start | bytes 393224 | tf_op jit(solution)/shard_map/ppermute | solution.py:504
  2.9 3.0 %shard_map.82 = (bf16[3,128,768]{2,1,0:T(8,128)(2,1)}, bf16[128,768]{1,0:T(8,128)(2,1)}, bf16[4,128,1024]{2,1,0:T(8,128)(2,1)}, bf16[128,1024]{1,0:T(8,128)(2,1)}) custom-call(bf16[8,128,512]{2,1,0:T(8,128)(2,1)} %inverse.1, bf16[8,128,256]{2,1,0:T(8,128)(2,1)} %basis.1, bf16[8,128,256]{2,1,0:T(8,128)(2,1)} %coupling.1), custom_call_target="tpu_custom_call" | custom-call | bytes 4194 | tf_op jit(solution)/shard_map/pallas_call | solution.py:93
  5.9 0.7 %collective-permute-done.refs_1_ = bf16[64,1024]{1,0:T(8,128)(2,1)S(1)} collective-permute-done((bf16[64,1024]{1,0:T(8,128)(2,1)}, bf16[64,1024]{1,0:T(8,128)(2,1)S(1)}, u32[]{:S(2)}, u32[]{:S(2)}) %collective-permute-start) | collective-permute-done | bytes 131104 | tf_op jit(solution)/shard_map/ppermute | solution.py:504
  6.7 1.3 %collective-permute-done.2.refs_3_ = bf16[64,1024]{1,0:T(8,128)(2,1)S(1)} collective-permute-done((bf16[64,1024]{1,0:T(8,128)(2,1)S(1)}, bf16[64,1024]{1,0:T(8,128)(2,1)S(1)}, u32[]{:S(2)}, u32[]{:S(2)}) %collective-permute-start.2) | collective-permute-done | bytes 131104 | tf_op jit(solution)/shard_map/ppermute | solution.py:504
  8.0 0.1 collective-permute-start.3
  8.1 1.8 %collective-permute-start.7 = (bf16[3,128,768]{2,1,0:T(8,128)(2,1)}, bf16[3,128,768]{2,1,0:T(8,128)(2,1)S(1)}, u32[]{:S(2)}, u32[]{:S(2)}) collective-permute-start(bf16[3,128,768]{2,1,0:T(8,128)(2,1)} %get-tuple-element.48), channel_id=1, source_target_pairs={{0,2},{1,3},{2,0},{3,1},{4,6},{5,7},{6,4},{7,5},{8,10},{9,11},{10,... | collective-permute-start | bytes 1769480 | tf_op jit(solution)/shard_map/ppermute | solution.py:504
  9.9 1.5 %collective-permute-start.8 = (bf16[128,1024]{1,0:T(8,128)(2,1)}, bf16[128,1024]{1,0:T(8,128)(2,1)S(1)}, u32[]{:S(2)}, u32[]{:S(2)}) collective-permute-start(bf16[128,1024]{1,0:T(8,128)(2,1)} %get-tuple-element.66.mine_ref), channel_id=1, source_target_pairs={{0,4},{4,0},{8,12},{12,8},{16,20},{20,16},{24,28},{28,24},{1,5},{5... | collective-permute-start | bytes 786440 | tf_op jit(solution)/shard_map/ppermute | solution.py:504
  11.4 0.1 pad_add_fusion.side_ref
  11.5 0.1 pad_add_fusion.1.side_ref
  11.6 1.2 %copy-done.1 = bf16[8,128,512]{2,1,0:T(8,128)(2,1)S(1)} copy-done((bf16[8,128,512]{2,1,0:T(8,128)(2,1)S(1)}, bf16[8,128,512]{2,1,0:T(8,128)(2,1)}, u32[]{:S(2)}) %copy-start.1) | copy-done | bytes 1048600
  12.8 3.4 %shard_map.83 = (f32[4,64,128]{2,1,0:T(8,128)S(1)}, bf16[4,32,256]{2,1,0:T(8,128)(2,1)S(1)}, bf16[4,32,256]{2,1,0:T(8,128)(2,1)S(1)}, bf16[4,4,64,256]{3,2,1,0:T(8,128)(2,1)S(1)}) custom-call(s32[2]{0:T(128)S(1)} %pad_add_fusion.side_ref, bf16[64,1024]{1,0:T(8,128)(2,1)S(1)} %copy-done.6, bf16[64,1024]{1,0:T(8,128)(2,1)S(1)} %collective-permute-done.refs_1_, ...), custom_call_target="tpu_custom_call" | custom-call | flops 1140850 | bytes 983 | tf_op jit(solution)/shard_map/pallas_call | solution.py:241
  16.2 0.1 collective-permute-start.6
  16.3 1.4 %collective-permute-start.4 = (bf16[4,32,256]{2,1,0:T(8,128)(2,1)S(1)}, bf16[4,32,256]{2,1,0:T(8,128)(2,1)S(1)}, u32[]{:S(2)}, u32[]{:S(2)}) collective-permute-start(bf16[4,32,256]{2,1,0:T(8,128)(2,1)S(1)} %get-tuple-element.56), channel_id=1, source_target_pairs={{0,2},{1,3},{2,0},{3,1},{4,6},{5,7},{6,4},{7,5},{8,10},{9,11},{10,... | collective-permute-start | bytes 196616 | tf_op jit(solution)/shard_map/ppermute | solution.py:504
  17.7 3.4 %shard_map.84 = (f32[4,64,128]{2,1,0:T(8,128)S(1)}, bf16[4,32,256]{2,1,0:T(8,128)(2,1)S(1)}, bf16[4,32,256]{2,1,0:T(8,128)(2,1)S(1)}) custom-call(s32[2]{0:T(128)S(1)} %pad_add_fusion.1.side_ref, bf16[4,4,64,256]{3,2,1,0:T(8,128)(2,1)S(1)} %get-tuple-element.58.refs_0_, s32[1,4096]{1,0:T(1,128)S(1)} %bitcast.7, bf16[8,128,512]{2,1,0:T(8,128)(2,1)S(1)} %copy-done.1, ...), custom_call_target="tpu_custom_call" | custom-call | flops 1140850 | bytes 983 | tf_op jit(solution)/shard_map/pallas_call | solution.py:241
  21.1 0.5 collective-permute-start.5
  21.7 3.5 %collective-permute-done.6.refs_3_ = bf16[4,32,256]{2,1,0:T(8,128)(2,1)S(1)} collective-permute-done((bf16[4,32,256]{2,1,0:T(8,128)(2,1)S(1)}, bf16[4,32,256]{2,1,0:T(8,128)(2,1)S(1)}, u32[]{:S(2)}, u32[]{:S(2)}) %collective-permute-start.6) | collective-permute-done | bytes 65568 | tf_op jit(solution)/shard_map/ppermute | solution.py:504
  25.2 1.6 %collective-permute-done.4.refs_1_ = bf16[4,32,256]{2,1,0:T(8,128)(2,1)S(1)} collective-permute-done((bf16[4,32,256]{2,1,0:T(8,128)(2,1)S(1)}, bf16[4,32,256]{2,1,0:T(8,128)(2,1)S(1)}, u32[]{:S(2)}, u32[]{:S(2)}) %collective-permute-start.4) | collective-permute-done | bytes 65568 | tf_op jit(solution)/shard_map/ppermute | solution.py:504
  26.8 1.8 %collective-permute-start.12 = (bf16[128,768]{1,0:T(8,128)(2,1)S(1)}, bf16[128,768]{1,0:T(8,128)(2,1)S(1)}, u32[]{:S(2)}, u32[]{:S(2)}) collective-permute-start(bf16[128,768]{1,0:T(8,128)(2,1)S(1)} %shard_map.89), channel_id=1, source_target_pairs={{0,2},{1,3},{2,0},{3,1},{4,6},{5,7},{6,4},{7,5},{8,10},{9,11},{10,... | collective-permute-start | bytes 589832 | tf_op jit(solution)/shard_map/ppermute | solution.py:504
  28.6 1.6 %collective-permute-start.19 = (bf16[128,1024]{1,0:T(8,128)(2,1)S(1)}, bf16[128,1024]{1,0:T(8,128)(2,1)S(1)}, u32[]{:S(2)}, u32[]{:S(2)}) collective-permute-start(bf16[128,1024]{1,0:T(8,128)(2,1)S(1)} %get-tuple-element.68.mine_ref), channel_id=1, source_target_pairs={{0,8},{4,12},{8,0},{12,4},{16,24},{20,28},{24,16},{28,20},{1,9},{5... | collective-permute-start | bytes 786440 | tf_op jit(solution)/shard_map/ppermute | solution.py:504
  30.2 1.5 %shard_map.86 = (f32[3,4,32,128]{3,2,1,0:T(8,128)S(1)}, bf16[32,256]{1,0:T(8,128)(2,1)S(1)}) custom-call(bf16[4,32,256]{2,1,0:T(8,128)(2,1)S(1)} %get-tuple-element.60.refs_0_, bf16[4,32,256]{2,1,0:T(8,128)(2,1)S(1)} %collective-permute-done.4.refs_1_, bf16[4,32,256]{2,1,0:T(8,128)(2,1)S(1)} %collective-permute-done.5.refs_2_, ...), custom_call_target="tpu_custom_call" | custom-call | flops 75497 | bytes 3145 | tf_op jit(solution)/shard_map/pallas_call | solution.py:304
  31.7 0.1 collective-permute-start.11
  31.8 0.6 collective-permute-start.10
  32.4 1.8 %collective-permute-done.12.refs_5_.refs_7_ = bf16[128,768]{1,0:T(8,128)(2,1)S(1)} collective-permute-done((bf16[128,768]{1,0:T(8,128)(2,1)S(1)}, bf16[128,768]{1,0:T(8,128)(2,1)S(1)}, u32[]{:S(2)}, u32[]{:S(2)}) %collective-permute-start.12) | collective-permute-done | bytes 196640 | tf_op jit(solution)/shard_map/ppermute | solution.py:504
  34.2 1.4 %collective-permute-done.10.other_ref.refs_1_ = bf16[32,256]{1,0:T(8,128)(2,1)S(1)} collective-permute-done((bf16[32,256]{1,0:T(8,128)(2,1)S(1)}, bf16[32,256]{1,0:T(8,128)(2,1)S(1)}, u32[]{:S(2)}, u32[]{:S(2)}) %collective-permute-start.10) | collective-permute-done | bytes 16416 | tf_op jit(solution)/shard_map/ppermute | solution.py:504
  35.6 0.7 %collective-permute-start.17 = (bf16[128,768]{1,0:T(8,128)(2,1)S(1)}, bf16[128,768]{1,0:T(8,128)(2,1)S(1)}, u32[]{:S(2)}, u32[]{:S(2)}) collective-permute-start(bf16[128,768]{1,0:T(8,128)(2,1)S(1)} %shard_map.90), channel_id=1, source_target_pairs={{0,2},{1,3},{2,0},{3,1},{4,6},{5,7},{6,4},{7,5},{8,10},{9,11},{10,... | collective-permute-start | bytes 589832 | tf_op jit(solution)/shard_map/ppermute | solution.py:504
  36.4 0.7 collective-permute-done.19.other_ref
  37.1 0.3 shard_map.88
  37.4 0.7 %collective-permute-start.20 = (bf16[128,768]{1,0:T(8,128)(2,1)S(1)}, bf16[128,768]{1,0:T(8,128)(2,1)S(1)}, u32[]{:S(2)}, u32[]{:S(2)}) collective-permute-start(bf16[128,768]{1,0:T(8,128)(2,1)S(1)} %shard_map.93), channel_id=1, source_target_pairs={{0,2},{1,3},{2,0},{3,1},{4,6},{5,7},{6,4},{7,5},{8,10},{9,11},{10,... | collective-permute-start | bytes 589832 | tf_op jit(solution)/shard_map/ppermute | solution.py:504
  38.2 2.6 %collective-permute-start.24 = (bf16[128,512]{1,0:T(8,128)(2,1)S(1)}, bf16[128,512]{1,0:T(8,128)(2,1)S(1)}, u32[]{:S(2)}, u32[]{:S(2)}) collective-permute-start(bf16[128,512]{1,0:T(8,128)(2,1)S(1)} %get-tuple-element.89.mine_ref), channel_id=1, source_target_pairs={{0,16},{4,20},{8,24},{12,28},{16,0},{20,4},{24,8},{28,12},{1,17},{... | collective-permute-start | bytes 393224 | tf_op jit(solution)/shard_map/ppermute | solution.py:504
  40.8 1.4 %collective-permute-start.14 = (bf16[32,256]{1,0:T(8,128)(2,1)S(1)}, bf16[32,256]{1,0:T(8,128)(2,1)S(1)}, u32[]{:S(2)}, u32[]{:S(2)}) collective-permute-start(bf16[32,256]{1,0:T(8,128)(2,1)S(1)} %get-tuple-element.77.refs_0_.refs_1_), channel_id=1, source_target_pairs={{0,2},{1,3},{2,0},{3,1},{4,6},{5,7},{6,4},{7,5},{8,10},{9,11},{10,... | collective-permute-start | bytes 49160 | tf_op jit(solution)/shard_map/ppermute | solution.py:504
  42.1 1.5 %collective-permute-start.15 = (bf16[32,256]{1,0:T(8,128)(2,1)S(1)}, bf16[32,256]{1,0:T(8,128)(2,1)S(1)}, u32[]{:S(2)}, u32[]{:S(2)}) collective-permute-start(bf16[32,256]{1,0:T(8,128)(2,1)S(1)} %get-tuple-element.77.refs_0_.refs_1_), channel_id=1, source_target_pairs={{0,4},{4,0},{8,12},{12,8},{16,20},{20,16},{24,28},{28,24},{1,5},{5... | collective-permute-start | bytes 49160 | tf_op jit(solution)/shard_map/ppermute | solution.py:504
  43.6 1.4 %collective-permute-start.16 = (bf16[32,256]{1,0:T(8,128)(2,1)S(1)}, bf16[32,256]{1,0:T(8,128)(2,1)S(1)}, u32[]{:S(2)}, u32[]{:S(2)}) collective-permute-start(bf16[32,256]{1,0:T(8,128)(2,1)S(1)} %get-tuple-element.77.refs_0_.refs_1_), channel_id=1, source_target_pairs={{0,6},{1,7},{2,4},{3,5},{4,2},{5,3},{6,0},{7,1},{8,14},{9,15},{10,... | collective-permute-start | bytes 49160 | tf_op jit(solution)/shard_map/ppermute | solution.py:511
  45.0 2.7 %collective-permute-done.14.refs_1_ = bf16[32,256]{1,0:T(8,128)(2,1)S(1)} collective-permute-done((bf16[32,256]{1,0:T(8,128)(2,1)S(1)}, bf16[32,256]{1,0:T(8,128)(2,1)S(1)}, u32[]{:S(2)}, u32[]{:S(2)}) %collective-permute-start.14) | collective-permute-done | bytes 16416 | tf_op jit(solution)/shard_map/ppermute | solution.py:504
  47.7 1.1 %collective-permute-done.16.refs_3_ = bf16[32,256]{1,0:T(8,128)(2,1)S(1)} collective-permute-done((bf16[32,256]{1,0:T(8,128)(2,1)S(1)}, bf16[32,256]{1,0:T(8,128)(2,1)S(1)}, u32[]{:S(2)}, u32[]{:S(2)}) %collective-permute-start.16) | collective-permute-done | bytes 16416 | tf_op jit(solution)/shard_map/ppermute | solution.py:511
  48.9 0.6 shard_map.91
  49.7 0.7 %collective-permute-start.25 = (bf16[128,1024]{1,0:T(8,128)(2,1)S(1)}, bf16[128,1024]{1,0:T(8,128)(2,1)S(1)}, u32[]{:S(2)}, u32[]{:S(2)}) collective-permute-start(bf16[128,1024]{1,0:T(8,128)(2,1)S(1)} %shard_map.98), channel_id=1, source_target_pairs={{0,2},{1,3},{2,0},{3,1},{4,6},{5,7},{6,4},{7,5},{8,10},{9,11},{10,... | collective-permute-start | bytes 786440 | tf_op jit(solution)/shard_map/ppermute | solution.py:504
  50.4 0.2 collective-permute-start.22
  50.7 1.6 %collective-permute-start.18 = (bf16[32,256]{1,0:T(8,128)(2,1)S(1)}, bf16[32,256]{1,0:T(8,128)(2,1)S(1)}, u32[]{:S(2)}, u32[]{:S(2)}) collective-permute-start(bf16[32,256]{1,0:T(8,128)(2,1)S(1)} %get-tuple-element.81.refs_1_.refs_0_.refs_3_), channel_id=1, source_target_pairs={{0,8},{4,12},{8,0},{12,4},{16,24},{20,28},{24,16},{28,20},{1,9},{5... | collective-permute-start | bytes 49160 | tf_op jit(solution)/shard_map/ppermute | solution.py:504
  52.2 2.2 %collective-permute-done.18.refs_1_ = bf16[32,256]{1,0:T(8,128)(2,1)S(1)} collective-permute-done((bf16[32,256]{1,0:T(8,128)(2,1)S(1)}, bf16[32,256]{1,0:T(8,128)(2,1)S(1)}, u32[]{:S(2)}, u32[]{:S(2)}) %collective-permute-start.18) | collective-permute-done | bytes 16416 | tf_op jit(solution)/shard_map/ppermute | solution.py:504
  54.4 0.6 shard_map.96
  55.0 2.6 %collective-permute-start.23 = (bf16[32,256]{1,0:T(8,128)(2,1)S(1)}, bf16[32,256]{1,0:T(8,128)(2,1)S(1)}, u32[]{:S(2)}, u32[]{:S(2)}) collective-permute-start(bf16[32,256]{1,0:T(8,128)(2,1)S(1)} %get-tuple-element.84.refs_0_), channel_id=1, source_target_pairs={{0,16},{4,20},{8,24},{12,28},{16,0},{20,4},{24,8},{28,12},{1,17},{... | collective-permute-start | bytes 49160 | tf_op jit(solution)/shard_map/ppermute | solution.py:504
  57.6 0.8 %collective-permute-done.25.tail_ref = bf16[128,1024]{1,0:T(8,128)(2,1)S(1)} collective-permute-done((bf16[128,1024]{1,0:T(8,128)(2,1)S(1)}, bf16[128,1024]{1,0:T(8,128)(2,1)S(1)}, u32[]{:S(2)}, u32[]{:S(2)}) %collective-permute-start.25) | collective-permute-done | bytes 262176 | tf_op jit(solution)/shard_map/ppermute | solution.py:504
  58.4 1.3 %collective-permute-done.23._.refs_1_ = bf16[32,256]{1,0:T(8,128)(2,1)S(1)} collective-permute-done((bf16[32,256]{1,0:T(8,128)(2,1)S(1)}, bf16[32,256]{1,0:T(8,128)(2,1)S(1)}, u32[]{:S(2)}, u32[]{:S(2)}) %collective-permute-start.23) | collective-permute-done | bytes 16416 | tf_op jit(solution)/shard_map/ppermute | solution.py:504
  59.8 0.6 collective-permute-start.27
  60.3 1.2 %collective-permute-done.27.refs_17_ = bf16[128,768]{1,0:T(8,128)(2,1)S(1)} collective-permute-done((bf16[128,768]{1,0:T(8,128)(2,1)S(1)}, bf16[128,768]{1,0:T(8,128)(2,1)S(1)}, u32[]{:S(2)}, u32[]{:S(2)}) %collective-permute-start.27) | collective-permute-done | bytes 196640 | tf_op jit(solution)/shard_map/ppermute | solution.py:504
  61.6 1.1 %shard_map.101 = bf16[4,32,256]{2,1,0:T(8,128)(2,1)S(1)} custom-call(bf16[32,256]{1,0:T(8,128)(2,1)S(1)} %get-tuple-element.84.refs_0_, bf16[32,256]{1,0:T(8,128)(2,1)S(1)} %collective-permute-done.23._.refs_1_, f32[4,32,128]{2,1,0:T(8,128)S(1)} %get-tuple-element.85.refs_2_, f32[4,32,128]{2,1,0:T(8,128)S(1)} %get-tuple-element.86.refs_3_, ...), custom_call_target="tpu_custom_call" | custom-call | flops 67108 | bytes 4194 | tf_op jit(solution)/shard_map/pallas_call | solution.py:472
  62.7 5.8 %all-gather = bf16[16,32,256]{2,1,0:T(8,128)(2,1)S(1)} all-gather(bf16[4,32,256]{2,1,0:T(8,128)(2,1)S(1)} %shard_map.101), channel_id=2, replica_groups=mesh['leaf'=8,'rhs'=4] {'rhs'}, dimensions={0}, use_global_device_ids=true | all-gather | bytes 327680 | tf_op jit(solution)/shard_map/all_gather | solution.py:613
  68.4 1.0 %shard_map.102 = f32[8,64,128]{2,1,0:T(8,128)} custom-call(f32[4,64,128]{2,1,0:T(8,128)S(1)} %get-tuple-element.52.far_ref, f32[4,64,128]{2,1,0:T(8,128)S(1)} %get-tuple-element.59.own_ref, bf16[4,4,32,256]{3,2,1,0:T(8,128)(2,1)S(1)} %bitcast.5, bf16[8,128,256]{2,1,0:T(8,128)(2,1)S(1)} %copy-done.3), custom_call_target="tpu_custom_call" | custom-call | flops 33554 | bytes 524 | tf_op jit(solution)/shard_map/pallas_call | solution.py:495
  (48 shorter events, 0.5 us)
Async XLA Ops:
  0.0 11.6 %copy-start.2 = (bf16[8,128,256]{2,1,0:T(8,128)(2,1)S(1)}, bf16[8,128,256]{2,1,0:T(8,128)(2,1)}, u32[]{:S(2)}) copy-start(bf16[8,128,256]{2,1,0:T(8,128)(2,1)} %refs_3_.1) | copy-start | bytes 1572868
  0.0 6.6 %collective-permute-start = (bf16[64,1024]{1,0:T(8,128)(2,1)}, bf16[64,1024]{1,0:T(8,128)(2,1)S(1)}, u32[]{:S(2)}, u32[]{:S(2)}) collective-permute-start(bf16[64,1024]{1,0:T(8,128)(2,1)} %refs_0_.1), channel_id=1, source_target_pairs={{0,2},{1,3},{2,0},{3,1},{4,6},{5,7},{6,4},{7,5},{8,10},{9,11},{10,... | collective-permute-start | bytes 393224 | tf_op jit(solution)/shard_map/ppermute | solution.py:504
  2.9 3.7 %collective-permute-start.1 = (bf16[64,1024]{1,0:T(8,128)(2,1)}, bf16[64,1024]{1,0:T(8,128)(2,1)S(1)}, u32[]{:S(2)}, u32[]{:S(2)}) collective-permute-start(bf16[64,1024]{1,0:T(8,128)(2,1)} %refs_0_.1), channel_id=1, source_target_pairs={{0,1},{1,0},{2,3},{3,2},{4,5},{5,4},{6,7},{7,6},{8,9},{9,8},{10,11... | collective-permute-start | bytes 393224 | tf_op jit(solution)/shard_map/ppermute | solution.py:504
  2.9 8.6 %copy-start.6 = (bf16[64,1024]{1,0:T(8,128)(2,1)S(1)}, bf16[64,1024]{1,0:T(8,128)(2,1)}, u32[]{:S(2)}) copy-start(bf16[64,1024]{1,0:T(8,128)(2,1)} %refs_0_.1) | copy-start | bytes 393220
  6.6 1.3 %collective-permute-start.2 = (bf16[64,1024]{1,0:T(8,128)(2,1)S(1)}, bf16[64,1024]{1,0:T(8,128)(2,1)S(1)}, u32[]{:S(2)}, u32[]{:S(2)}) collective-permute-start(bf16[64,1024]{1,0:T(8,128)(2,1)S(1)} %collective-permute-done.refs_1_), channel_id=1, source_target_pairs={{0,1},{1,0},{2,3},{3,2},{4,5},{5,4},{6,7},{7,6},{8,9},{9,8},{10,11... | collective-permute-start | bytes 393224 | tf_op jit(solution)/shard_map/ppermute | solution.py:504
  8.0 9.7 %collective-permute-start.3 = (bf16[4,128,1024]{2,1,0:T(8,128)(2,1)}, bf16[4,128,1024]{2,1,0:T(8,128)(2,1)S(1)}, u32[]{:S(2)}, u32[]{:S(2)}) collective-permute-start(bf16[4,128,1024]{2,1,0:T(8,128)(2,1)} %get-tuple-element.55.refs_4_.own_ref.refs_18_), channel_id=1, source_target_pairs={{0,1},{1,0},{2,3},{3,2},{4,5},{5,4},{6,7},{7,6},{8,9},{9,8},{10,11... | collective-permute-start | bytes 3145736 | tf_op jit(solution)/shard_map/ppermute | solution.py:504
  8.1 18.6 %collective-permute-start.7 = (bf16[3,128,768]{2,1,0:T(8,128)(2,1)}, bf16[3,128,768]{2,1,0:T(8,128)(2,1)S(1)}, u32[]{:S(2)}, u32[]{:S(2)}) collective-permute-start(bf16[3,128,768]{2,1,0:T(8,128)(2,1)} %get-tuple-element.48), channel_id=1, source_target_pairs={{0,2},{1,3},{2,0},{3,1},{4,6},{5,7},{6,4},{7,5},{8,10},{9,11},{10,... | collective-permute-start | bytes 1769480 | tf_op jit(solution)/shard_map/ppermute | solution.py:504
  9.9 1.7 %copy-start.7 = (s32[4096]{0:T(1024)S(1)}, s32[4096]{0:T(1024)}, u32[]{:S(2)}) copy-start(s32[4096]{0:T(1024)} %param.9) | copy-start | bytes 49156
  9.9 11.7 %collective-permute-start.8 = (bf16[128,1024]{1,0:T(8,128)(2,1)}, bf16[128,1024]{1,0:T(8,128)(2,1)S(1)}, u32[]{:S(2)}, u32[]{:S(2)}) collective-permute-start(bf16[128,1024]{1,0:T(8,128)(2,1)} %get-tuple-element.66.mine_ref), channel_id=1, source_target_pairs={{0,4},{4,0},{8,12},{12,8},{16,20},{20,16},{24,28},{28,24},{1,5},{5... | collective-permute-start | bytes 786440 | tf_op jit(solution)/shard_map/ppermute | solution.py:504
  11.6 1.2 %copy-start.1 = (bf16[8,128,512]{2,1,0:T(8,128)(2,1)S(1)}, bf16[8,128,512]{2,1,0:T(8,128)(2,1)}, u32[]{:S(2)}) copy-start(bf16[8,128,512]{2,1,0:T(8,128)(2,1)} %refs_2_.1) | copy-start | bytes 3145732
  16.2 8.9 %collective-permute-start.6 = (bf16[4,32,256]{2,1,0:T(8,128)(2,1)S(1)}, bf16[4,32,256]{2,1,0:T(8,128)(2,1)S(1)}, u32[]{:S(2)}, u32[]{:S(2)}) collective-permute-start(bf16[4,32,256]{2,1,0:T(8,128)(2,1)S(1)} %get-tuple-element.63), channel_id=1, source_target_pairs={{0,3},{1,2},{2,1},{3,0},{4,7},{5,6},{6,5},{7,4},{8,11},{9,10},{10,... | collective-permute-start | bytes 196616 | tf_op jit(solution)/shard_map/ppermute | solution.py:504
  16.3 10.4 %collective-permute-start.4 = (bf16[4,32,256]{2,1,0:T(8,128)(2,1)S(1)}, bf16[4,32,256]{2,1,0:T(8,128)(2,1)S(1)}, u32[]{:S(2)}, u32[]{:S(2)}) collective-permute-start(bf16[4,32,256]{2,1,0:T(8,128)(2,1)S(1)} %get-tuple-element.56), channel_id=1, source_target_pairs={{0,2},{1,3},{2,0},{3,1},{4,6},{5,7},{6,4},{7,5},{8,10},{9,11},{10,... | collective-permute-start | bytes 196616 | tf_op jit(solution)/shard_map/ppermute | solution.py:504
  17.7 3.9 %copy-start.4 = (bf16[128,1024]{1,0:T(8,128)(2,1)S(1)}, bf16[128,1024]{1,0:T(8,128)(2,1)}, u32[]{:S(2)}) copy-start(bf16[128,1024]{1,0:T(8,128)(2,1)} %get-tuple-element.66.mine_ref) | copy-start | bytes 786436
  21.1 9.1 %copy-start = (bf16[4,128,1024]{2,1,0:T(8,128)(2,1)S(1)}, bf16[4,128,1024]{2,1,0:T(8,128)(2,1)}, u32[]{:S(2)}) copy-start(bf16[4,128,1024]{2,1,0:T(8,128)(2,1)} %get-tuple-element.55.refs_4_.own_ref.refs_18_) | copy-start | bytes 3145732
  21.1 5.6 %collective-permute-start.5 = (bf16[4,32,256]{2,1,0:T(8,128)(2,1)S(1)}, bf16[4,32,256]{2,1,0:T(8,128)(2,1)S(1)}, u32[]{:S(2)}, u32[]{:S(2)}) collective-permute-start(bf16[4,32,256]{2,1,0:T(8,128)(2,1)S(1)} %get-tuple-element.62), channel_id=1, source_target_pairs={{0,1},{1,0},{2,3},{3,2},{4,5},{5,4},{6,7},{7,6},{8,9},{9,8},{10,11... | collective-permute-start | bytes 196616 | tf_op jit(solution)/shard_map/ppermute | solution.py:504
  26.8 3.4 %collective-permute-start.9 = (bf16[3,128,768]{2,1,0:T(8,128)(2,1)S(1)}, bf16[3,128,768]{2,1,0:T(8,128)(2,1)S(1)}, u32[]{:S(2)}, u32[]{:S(2)}) collective-permute-start(bf16[3,128,768]{2,1,0:T(8,128)(2,1)S(1)} %collective-permute-done.7.refs_5_.refs_1_), channel_id=1, source_target_pairs={{0,1},{1,0},{2,3},{3,2},{4,5},{5,4},{6,7},{7,6},{8,9},{9,8},{10,11... | collective-permute-start | bytes 1769480 | tf_op jit(solution)/shard_map/ppermute | solution.py:504
  26.8 7.4 %collective-permute-start.12 = (bf16[128,768]{1,0:T(8,128)(2,1)S(1)}, bf16[128,768]{1,0:T(8,128)(2,1)S(1)}, u32[]{:S(2)}, u32[]{:S(2)}) collective-permute-start(bf16[128,768]{1,0:T(8,128)(2,1)S(1)} %shard_map.89), channel_id=1, source_target_pairs={{0,2},{1,3},{2,0},{3,1},{4,6},{5,7},{6,4},{7,5},{8,10},{9,11},{10,... | collective-permute-start | bytes 589832 | tf_op jit(solution)/shard_map/ppermute | solution.py:504
  28.6 8.4 %collective-permute-start.19 = (bf16[128,1024]{1,0:T(8,128)(2,1)S(1)}, bf16[128,1024]{1,0:T(8,128)(2,1)S(1)}, u32[]{:S(2)}, u32[]{:S(2)}) collective-permute-start(bf16[128,1024]{1,0:T(8,128)(2,1)S(1)} %get-tuple-element.68.mine_ref), channel_id=1, source_target_pairs={{0,8},{4,12},{8,0},{12,4},{16,24},{20,28},{24,16},{28,20},{1,9},{5... | collective-permute-start | bytes 786440 | tf_op jit(solution)/shard_map/ppermute | solution.py:504
  31.7 3.9 %copy-start.5 = (bf16[128,768]{1,0:T(8,128)(2,1)S(1)}, bf16[128,768]{1,0:T(8,128)(2,1)}, u32[]{:S(2)}) copy-start(bf16[128,768]{1,0:T(8,128)(2,1)} %get-tuple-element.76.refs_0_) | copy-start | bytes 589828
  31.7 5.4 %collective-permute-start.11 = (bf16[128,1024]{1,0:T(8,128)(2,1)S(1)}, bf16[128,1024]{1,0:T(8,128)(2,1)S(1)}, u32[]{:S(2)}, u32[]{:S(2)}) collective-permute-start(bf16[128,1024]{1,0:T(8,128)(2,1)S(1)} %shard_map.87), channel_id=1, source_target_pairs={{0,1},{1,0},{2,3},{3,2},{4,5},{5,4},{6,7},{7,6},{8,9},{9,8},{10,11... | collective-permute-start | bytes 786440 | tf_op jit(solution)/shard_map/ppermute | solution.py:504
  31.8 3.8 %collective-permute-start.10 = (bf16[32,256]{1,0:T(8,128)(2,1)S(1)}, bf16[32,256]{1,0:T(8,128)(2,1)S(1)}, u32[]{:S(2)}, u32[]{:S(2)}) collective-permute-start(bf16[32,256]{1,0:T(8,128)(2,1)S(1)} %get-tuple-element.70.refs_1_.mine_ref), channel_id=1, source_target_pairs={{0,2},{1,3},{2,0},{3,1},{4,6},{5,7},{6,4},{7,5},{8,10},{9,11},{10,... | collective-permute-start | bytes 49160 | tf_op jit(solution)/shard_map/ppermute | solution.py:504
  35.6 5.2 %collective-permute-start.13 = (bf16[128,768]{1,0:T(8,128)(2,1)S(1)}, bf16[128,768]{1,0:T(8,128)(2,1)S(1)}, u32[]{:S(2)}, u32[]{:S(2)}) collective-permute-start(bf16[128,768]{1,0:T(8,128)(2,1)S(1)} %collective-permute-done.12.refs_5_.refs_7_), channel_id=1, source_target_pairs={{0,1},{1,0},{2,3},{3,2},{4,5},{5,4},{6,7},{7,6},{8,9},{9,8},{10,11... | collective-permute-start | bytes 589832 | tf_op jit(solution)/shard_map/ppermute | solution.py:504
  35.6 8.0 %collective-permute-start.17 = (bf16[128,768]{1,0:T(8,128)(2,1)S(1)}, bf16[128,768]{1,0:T(8,128)(2,1)S(1)}, u32[]{:S(2)}, u32[]{:S(2)}) collective-permute-start(bf16[128,768]{1,0:T(8,128)(2,1)S(1)} %shard_map.90), channel_id=1, source_target_pairs={{0,2},{1,3},{2,0},{3,1},{4,6},{5,7},{6,4},{7,5},{8,10},{9,11},{10,... | collective-permute-start | bytes 589832 | tf_op jit(solution)/shard_map/ppermute | solution.py:504
  37.4 13.0 %collective-permute-start.20 = (bf16[128,768]{1,0:T(8,128)(2,1)S(1)}, bf16[128,768]{1,0:T(8,128)(2,1)S(1)}, u32[]{:S(2)}, u32[]{:S(2)}) collective-permute-start(bf16[128,768]{1,0:T(8,128)(2,1)S(1)} %shard_map.93), channel_id=1, source_target_pairs={{0,2},{1,3},{2,0},{3,1},{4,6},{5,7},{6,4},{7,5},{8,10},{9,11},{10,... | collective-permute-start | bytes 589832 | tf_op jit(solution)/shard_map/ppermute | solution.py:504
  38.2 11.4 %collective-permute-start.24 = (bf16[128,512]{1,0:T(8,128)(2,1)S(1)}, bf16[128,512]{1,0:T(8,128)(2,1)S(1)}, u32[]{:S(2)}, u32[]{:S(2)}) collective-permute-start(bf16[128,512]{1,0:T(8,128)(2,1)S(1)} %get-tuple-element.89.mine_ref), channel_id=1, source_target_pairs={{0,16},{4,20},{8,24},{12,28},{16,0},{20,4},{24,8},{28,12},{1,17},{... | collective-permute-start | bytes 393224 | tf_op jit(solution)/shard_map/ppermute | solution.py:504
  40.8 7.0 %collective-permute-start.14 = (bf16[32,256]{1,0:T(8,128)(2,1)S(1)}, bf16[32,256]{1,0:T(8,128)(2,1)S(1)}, u32[]{:S(2)}, u32[]{:S(2)}) collective-permute-start(bf16[32,256]{1,0:T(8,128)(2,1)S(1)} %get-tuple-element.77.refs_0_.refs_1_), channel_id=1, source_target_pairs={{0,2},{1,3},{2,0},{3,1},{4,6},{5,7},{6,4},{7,5},{8,10},{9,11},{10,... | collective-permute-start | bytes 49160 | tf_op jit(solution)/shard_map/ppermute | solution.py:504
  42.1 5.6 %collective-permute-start.15 = (bf16[32,256]{1,0:T(8,128)(2,1)S(1)}, bf16[32,256]{1,0:T(8,128)(2,1)S(1)}, u32[]{:S(2)}, u32[]{:S(2)}) collective-permute-start(bf16[32,256]{1,0:T(8,128)(2,1)S(1)} %get-tuple-element.77.refs_0_.refs_1_), channel_id=1, source_target_pairs={{0,4},{4,0},{8,12},{12,8},{16,20},{20,16},{24,28},{28,24},{1,5},{5... | collective-permute-start | bytes 49160 | tf_op jit(solution)/shard_map/ppermute | solution.py:504
  43.6 5.2 %collective-permute-start.16 = (bf16[32,256]{1,0:T(8,128)(2,1)S(1)}, bf16[32,256]{1,0:T(8,128)(2,1)S(1)}, u32[]{:S(2)}, u32[]{:S(2)}) collective-permute-start(bf16[32,256]{1,0:T(8,128)(2,1)S(1)} %get-tuple-element.77.refs_0_.refs_1_), channel_id=1, source_target_pairs={{0,6},{1,7},{2,4},{3,5},{4,2},{5,3},{6,0},{7,1},{8,14},{9,15},{10,... | collective-permute-start | bytes 49160 | tf_op jit(solution)/shard_map/ppermute | solution.py:511
  49.5 4.9 %collective-permute-start.21 = (bf16[128,1024]{1,0:T(8,128)(2,1)S(1)}, bf16[128,1024]{1,0:T(8,128)(2,1)S(1)}, u32[]{:S(2)}, u32[]{:S(2)}) collective-permute-start(bf16[128,1024]{1,0:T(8,128)(2,1)S(1)} %shard_map.94), channel_id=1, source_target_pairs={{0,1},{1,0},{2,3},{3,2},{4,5},{5,4},{6,7},{7,6},{8,9},{9,8},{10,11... | collective-permute-start | bytes 786440 | tf_op jit(solution)/shard_map/ppermute | solution.py:504
  49.7 8.7 %collective-permute-start.25 = (bf16[128,1024]{1,0:T(8,128)(2,1)S(1)}, bf16[128,1024]{1,0:T(8,128)(2,1)S(1)}, u32[]{:S(2)}, u32[]{:S(2)}) collective-permute-start(bf16[128,1024]{1,0:T(8,128)(2,1)S(1)} %shard_map.98), channel_id=1, source_target_pairs={{0,2},{1,3},{2,0},{3,1},{4,6},{5,7},{6,4},{7,5},{8,10},{9,11},{10,... | collective-permute-start | bytes 786440 | tf_op jit(solution)/shard_map/ppermute | solution.py:504
  50.4 4.0 %collective-permute-start.22 = (bf16[128,768]{1,0:T(8,128)(2,1)S(1)}, bf16[128,768]{1,0:T(8,128)(2,1)S(1)}, u32[]{:S(2)}, u32[]{:S(2)}) collective-permute-start(bf16[128,768]{1,0:T(8,128)(2,1)S(1)} %shard_map.95), channel_id=1, source_target_pairs={{0,1},{1,0},{2,3},{3,2},{4,5},{5,4},{6,7},{7,6},{8,9},{9,8},{10,11... | collective-permute-start | bytes 589832 | tf_op jit(solution)/shard_map/ppermute | solution.py:504
  50.7 3.7 %collective-permute-start.18 = (bf16[32,256]{1,0:T(8,128)(2,1)S(1)}, bf16[32,256]{1,0:T(8,128)(2,1)S(1)}, u32[]{:S(2)}, u32[]{:S(2)}) collective-permute-start(bf16[32,256]{1,0:T(8,128)(2,1)S(1)} %get-tuple-element.81.refs_1_.refs_0_.refs_3_), channel_id=1, source_target_pairs={{0,8},{4,12},{8,0},{12,4},{16,24},{20,28},{24,16},{28,20},{1,9},{5... | collective-permute-start | bytes 49160 | tf_op jit(solution)/shard_map/ppermute | solution.py:504
  55.0 4.7 %collective-permute-start.23 = (bf16[32,256]{1,0:T(8,128)(2,1)S(1)}, bf16[32,256]{1,0:T(8,128)(2,1)S(1)}, u32[]{:S(2)}, u32[]{:S(2)}) collective-permute-start(bf16[32,256]{1,0:T(8,128)(2,1)S(1)} %get-tuple-element.84.refs_0_), channel_id=1, source_target_pairs={{0,16},{4,20},{8,24},{12,28},{16,0},{20,4},{24,8},{28,12},{1,17},{... | collective-permute-start | bytes 49160 | tf_op jit(solution)/shard_map/ppermute | solution.py:504
  59.7 1.9 %collective-permute-start.26 = (bf16[128,1024]{1,0:T(8,128)(2,1)S(1)}, bf16[128,1024]{1,0:T(8,128)(2,1)S(1)}, u32[]{:S(2)}, u32[]{:S(2)}) collective-permute-start(bf16[128,1024]{1,0:T(8,128)(2,1)S(1)} %shard_map.99.refs_14_), channel_id=1, source_target_pairs={{0,1},{1,0},{2,3},{3,2},{4,5},{5,4},{6,7},{7,6},{8,9},{9,8},{10,11... | collective-permute-start | bytes 786440 | tf_op jit(solution)/shard_map/ppermute | solution.py:504
  59.8 1.8 %collective-permute-start.27 = (bf16[128,768]{1,0:T(8,128)(2,1)S(1)}, bf16[128,768]{1,0:T(8,128)(2,1)S(1)}, u32[]{:S(2)}, u32[]{:S(2)}) collective-permute-start(bf16[128,768]{1,0:T(8,128)(2,1)S(1)} %shard_map.100), channel_id=1, source_target_pairs={{0,1},{1,0},{2,3},{3,2},{4,5},{5,4},{6,7},{7,6},{8,9},{9,8},{10,11... | collective-permute-start | bytes 589832 | tf_op jit(solution)/shard_map/ppermute | solution.py:504
  61.6 6.9 %copy-start.3 = (bf16[8,128,256]{2,1,0:T(8,128)(2,1)S(1)}, bf16[8,128,256]{2,1,0:T(8,128)(2,1)}, u32[]{:S(2)}) copy-start(bf16[8,128,256]{2,1,0:T(8,128)(2,1)} %coupling_ref.1) | copy-start | bytes 1572868

commit v4 on v2

--- a/solution.py
+++ b/solution.py
@@ -102,7 +102,11 @@
     )(inverse, basis, coupling)
 
 
-def climb_kernel(level, mine_ref, other_ref, ancestor_ref, *carrier_refs):
+def climb_kernel(level, count, mine_ref, other_ref, *refs):
+    extras, (ancestor_ref, *outs) = refs[:count], refs[count:]
+    carrier_refs, passed = outs[: len(outs) - count], outs[len(outs) - count :]
+    for ref, extra in zip(passed, extras):
+        ref[...] = extra[...]
     right = (lax.axis_index("leaf") // (1 << level)) % 2 == 1
 
     @pl.when(right)
@@ -118,14 +122,15 @@
             ref[...] = mine_ref[:, : ref.shape[1]]
 
 
-def climb(level, mine, other, keep):
-    return pl.pallas_call(
-        functools.partial(climb_kernel, level),
+def climb(level, mine, other, keep, extras=()):
+    return pl.pallas_call(
+        functools.partial(climb_kernel, level, len(extras)),
         out_shape=[pltpu.VMEM(mine.shape, mine.dtype)]
-        + [pltpu.VMEM((mine.shape[0], size), mine.dtype) for size in keep],
+        + [pltpu.VMEM((mine.shape[0], size), mine.dtype) for size in keep]
+        + [pltpu.VMEM(extra.shape, extra.dtype) for extra in extras],
         compiler_params=params(),
         cost_estimate=cost(0, 4 * mine.size),
-    )(mine, other)
+    )(mine, other, *extras)
 
 
 def join_kernel(cuts, *refs):
@@ -535,11 +540,12 @@
     place = lax.axis_index("rhs")
     high, low = place // CORES, place % CORES
 
-    def rise(carrier, level, anchor):
+    def rise(carrier, level, anchor, extras=()):
         other = after(swap(carrier, "leaf", 1 << level), anchor)
         width = node_size if level == cross_levels - 2 else carrier.shape[1]
-        ancestor, *carriers = climb(level, carrier, other, [width] * (level < cross_levels - 1))
-        return ancestor, carriers[0] if carriers else None
+        keep = [width] * (level < cross_levels - 1)
+        ancestor, *carriers = climb(level, carrier, other, keep, extras)
+        return (ancestor, *(carriers or [None]))
 
     send, send_coupling, keep, carrier = pack(node_inverse, node_basis, node_coupling)
     across, beside = after(
@@ -559,7 +565,7 @@
     own_values, own_same, own_cross = leaf_up(
         jnp.stack([high, low]), [after(joined, keep_near)], *leaves
     )
-    ancestor, carrier = rise(carrier, 0, own_same)
+    ancestor, carrier, send_coupling = rise(carrier, 0, own_same, [send_coupling])
     ancestors = [ancestor]
     far_same = after(swap(far_same, "rhs", CORES), own_same)
     far_cross = after(swap(far_cross, "rhs", CORES + 1), own_same)
@@ -567,16 +573,16 @@
     half_far = after(half_far, (parts, carrier))
     half_near = swap(half_far, "rhs", 1)
     fars = [swap(after(ancestors[0], half_far), "rhs", CORES)]
-    nears = [swap(after(ancestors[0], half_far), "rhs", 1)]
 
     solved_half, current = group_up(per_dev, parts, [keep, half_far, keep_near, half_near])
-    other = swap(after(current, nears[0]), "rhs", CORES)
+    own_near = swap(join([ancestors[0]], current), "rhs", 1)
+    other = swap(current, "rhs", CORES)
     ancestor, carrier = rise(carrier, 1, other)
     ancestors.append(ancestor)
-    solved_top, current = half_up(current, other, keep, keep_near)
+    solved_top, current = half_up(current, after(other, own_near), keep, keep_near)
     fars[0] = after(fars[0], other)
     near_far = swap(fars[0], "rhs", 1)
-    cross_packs = [[ancestors[0], fars[0], nears[0], near_far]]
+    cross_packs = [[ancestors[0], fars[0], own_near, near_far]]
     factors = [(0, node_size + rank)]
     fars.append(swap(join([ancestors[1]], current, factors), "rhs", CORES))
     current = after(current, near_far)

time: 69.7 us -> 69.2 us (level)
  local copies, waits for them, and re-layouts: 2.13 us -> 1.25 us
    unnamed x16, local copies, waits for them, and re-layouts: 2.13 us -> 1.25 us
  transfers between devices with their start and end apart: 26 -> 26, of which waited for: 12 -> 13; matrix products, arithmetic and copies ran while one was open for 0% -> 0% of each run, Pallas kernels for 19% -> 19%
where the time goes in v4:
time: 69.2 us; the launch traced here: 69 us
  starting transfers between devices  23.8 us (34%)
  waiting for transfers between devices  22.4 us (32%)
  Pallas kernels  15.1 us (22%)
  blocking collectives  6.14 us (9%)
  local copies, waits for them, and re-layouts  1.25 us (2%)
    ppermute x25, starting transfers between devices, swap(): lax.ppermute(block, axis, [(i, i ^ bit) for i in range(lax.axis_size(axis...  22.4 us
    ppermute x25, waiting for transfers between devices, swap(): lax.ppermute(block, axis, [(i, i ^ bit) for i in range(lax.axis_size(axis...  19.9 us
    pallas_call x2, Pallas kernels, leaf_up(): pl.pallas_call(functools.partial(leaf_kernel, len(points)), grid_spec=plt...  6.81 us
    all_gather x1, blocking collectives, body(): incoming = lax.all_gather(shares, 'rhs', axis=0)  6.14 us
    pallas_call x1, Pallas kernels, pack(): pl.pallas_call(functools.partial(pack_kernel, per_dev), in_specs=[pl.Bloc...  2.99 us
    ppermute x1, waiting for transfers between devices, far_swap(): lax.ppermute(block, ('leaf', 'rhs'), [(i, i ^ flip) for i in range(count)])  2.59 us
    pallas_call x1, Pallas kernels, group_up(): pl.pallas_call(functools.partial(group_up_kernel, per_dev), out_shape=[ja...  1.48 us
  transfers between devices with their start and end apart: 26, of which 13 were waited for; matrix products, arithmetic and copies ran while one was open for 0% of the time, Pallas kernels for 19%

profile of v4, /device:TPU:0, one launch (start us, length us, event | category | flops | bytes accessed | tf_op | source)
XLA Modules:
  0.0 69.0 jit_solution(13347225255723020775)
XLA Ops:
  0.0 2.9 %collective-permute-start = (bf16[64,1024]{1,0:T(8,128)(2,1)}, bf16[64,1024]{1,0:T(8,128)(2,1)S(1)}, u32[]{:S(2)}, u32[]{:S(2)}) collective-permute-start(bf16[64,1024]{1,0:T(8,128)(2,1)} %refs_0_.1), channel_id=1, source_target_pairs={{0,2},{1,3},{2,0},{3,1},{4,6},{5,7},{6,4},{7,5},{8,10},{9,11},{10,... | collective-permute-start | bytes 393224 | tf_op jit(solution)/shard_map/ppermute | solution.py:511
  2.9 3.0 %shard_map.82 = (bf16[3,128,768]{2,1,0:T(8,128)(2,1)}, bf16[128,768]{1,0:T(8,128)(2,1)}, bf16[4,128,1024]{2,1,0:T(8,128)(2,1)}, bf16[128,1024]{1,0:T(8,128)(2,1)}) custom-call(bf16[8,128,512]{2,1,0:T(8,128)(2,1)} %inverse.1, bf16[8,128,256]{2,1,0:T(8,128)(2,1)} %basis.1, bf16[8,128,256]{2,1,0:T(8,128)(2,1)} %coupling.1), custom_call_target="tpu_custom_call" | custom-call | bytes 4194 | tf_op jit(solution)/shard_map/pallas_call | solution.py:93
  5.9 0.7 %collective-permute-done.refs_1_ = bf16[64,1024]{1,0:T(8,128)(2,1)S(1)} collective-permute-done((bf16[64,1024]{1,0:T(8,128)(2,1)}, bf16[64,1024]{1,0:T(8,128)(2,1)S(1)}, u32[]{:S(2)}, u32[]{:S(2)}) %collective-permute-start) | collective-permute-done | bytes 131104 | tf_op jit(solution)/shard_map/ppermute | solution.py:511
  6.7 1.3 %collective-permute-done.2.refs_3_ = bf16[64,1024]{1,0:T(8,128)(2,1)S(1)} collective-permute-done((bf16[64,1024]{1,0:T(8,128)(2,1)S(1)}, bf16[64,1024]{1,0:T(8,128)(2,1)S(1)}, u32[]{:S(2)}, u32[]{:S(2)}) %collective-permute-start.2) | collective-permute-done | bytes 131104 | tf_op jit(solution)/shard_map/ppermute | solution.py:511
  8.0 0.1 collective-permute-start.3
  8.1 1.8 %collective-permute-start.7 = (bf16[3,128,768]{2,1,0:T(8,128)(2,1)}, bf16[3,128,768]{2,1,0:T(8,128)(2,1)S(1)}, u32[]{:S(2)}, u32[]{:S(2)}) collective-permute-start(bf16[3,128,768]{2,1,0:T(8,128)(2,1)} %get-tuple-element.46), channel_id=1, source_target_pairs={{0,2},{1,3},{2,0},{3,1},{4,6},{5,7},{6,4},{7,5},{8,10},{9,11},{10,... | collective-permute-start | bytes 1769480 | tf_op jit(solution)/shard_map/ppermute | solution.py:511
  9.9 1.5 %collective-permute-start.8 = (bf16[128,1024]{1,0:T(8,128)(2,1)}, bf16[128,1024]{1,0:T(8,128)(2,1)S(1)}, u32[]{:S(2)}, u32[]{:S(2)}) collective-permute-start(bf16[128,1024]{1,0:T(8,128)(2,1)} %get-tuple-element.64.mine_ref), channel_id=1, source_target_pairs={{0,4},{4,0},{8,12},{12,8},{16,20},{20,16},{24,28},{28,24},{1,5},{5... | collective-permute-start | bytes 786440 | tf_op jit(solution)/shard_map/ppermute | solution.py:511
  11.4 0.1 pad_add_fusion.side_ref
  11.5 0.1 pad_add_fusion.1.side_ref
  11.6 1.2 %copy-done.1 = bf16[8,128,512]{2,1,0:T(8,128)(2,1)S(1)} copy-done((bf16[8,128,512]{2,1,0:T(8,128)(2,1)S(1)}, bf16[8,128,512]{2,1,0:T(8,128)(2,1)}, u32[]{:S(2)}) %copy-start.1) | copy-done | bytes 1048600
  12.8 3.4 %shard_map.83 = (f32[4,64,128]{2,1,0:T(8,128)S(1)}, bf16[4,32,256]{2,1,0:T(8,128)(2,1)S(1)}, bf16[4,32,256]{2,1,0:T(8,128)(2,1)S(1)}, bf16[4,4,64,256]{3,2,1,0:T(8,128)(2,1)S(1)}) custom-call(s32[2]{0:T(128)S(1)} %pad_add_fusion.side_ref, bf16[64,1024]{1,0:T(8,128)(2,1)S(1)} %copy-done.6, bf16[64,1024]{1,0:T(8,128)(2,1)S(1)} %collective-permute-done.refs_1_, ...), custom_call_target="tpu_custom_call" | custom-call | flops 1140850 | bytes 983 | tf_op jit(solution)/shard_map/pallas_call | solution.py:246
  16.2 0.1 collective-permute-start.6
  16.3 1.4 %collective-permute-start.4 = (bf16[4,32,256]{2,1,0:T(8,128)(2,1)S(1)}, bf16[4,32,256]{2,1,0:T(8,128)(2,1)S(1)}, u32[]{:S(2)}, u32[]{:S(2)}) collective-permute-start(bf16[4,32,256]{2,1,0:T(8,128)(2,1)S(1)} %get-tuple-element.54), channel_id=1, source_target_pairs={{0,2},{1,3},{2,0},{3,1},{4,6},{5,7},{6,4},{7,5},{8,10},{9,11},{10,... | collective-permute-start | bytes 196616 | tf_op jit(solution)/shard_map/ppermute | solution.py:511
  17.7 3.4 %shard_map.84 = (f32[4,64,128]{2,1,0:T(8,128)S(1)}, bf16[4,32,256]{2,1,0:T(8,128)(2,1)S(1)}, bf16[4,32,256]{2,1,0:T(8,128)(2,1)S(1)}) custom-call(s32[2]{0:T(128)S(1)} %pad_add_fusion.1.side_ref, bf16[4,4,64,256]{3,2,1,0:T(8,128)(2,1)S(1)} %get-tuple-element.56.refs_0_, s32[1,4096]{1,0:T(1,128)S(1)} %bitcast.7, bf16[8,128,512]{2,1,0:T(8,128)(2,1)S(1)} %copy-done.1, ...), custom_call_target="tpu_custom_call" | custom-call | flops 1140850 | bytes 983 | tf_op jit(solution)/shard_map/pallas_call | solution.py:246
  21.1 0.5 collective-permute-start.5
  21.6 3.5 %collective-permute-done.6.refs_3_ = bf16[4,32,256]{2,1,0:T(8,128)(2,1)S(1)} collective-permute-done((bf16[4,32,256]{2,1,0:T(8,128)(2,1)S(1)}, bf16[4,32,256]{2,1,0:T(8,128)(2,1)S(1)}, u32[]{:S(2)}, u32[]{:S(2)}) %collective-permute-start.6) | collective-permute-done | bytes 65568 | tf_op jit(solution)/shard_map/ppermute | solution.py:511
  25.2 1.6 %collective-permute-done.4.refs_1_ = bf16[4,32,256]{2,1,0:T(8,128)(2,1)S(1)} collective-permute-done((bf16[4,32,256]{2,1,0:T(8,128)(2,1)S(1)}, bf16[4,32,256]{2,1,0:T(8,128)(2,1)S(1)}, u32[]{:S(2)}, u32[]{:S(2)}) %collective-permute-start.4) | collective-permute-done | bytes 65568 | tf_op jit(solution)/shard_map/ppermute | solution.py:511
  26.8 0.1 collective-permute-start.9
  26.9 1.8 %collective-permute-start.12 = (bf16[128,1024]{1,0:T(8,128)(2,1)S(1)}, bf16[128,1024]{1,0:T(8,128)(2,1)S(1)}, u32[]{:S(2)}, u32[]{:S(2)}) collective-permute-start(bf16[128,1024]{1,0:T(8,128)(2,1)S(1)} %get-tuple-element.73.refs_0_.refs_4_.refs_6_), channel_id=1, source_target_pairs={{0,2},{1,3},{2,0},{3,1},{4,6},{5,7},{6,4},{7,5},{8,10},{9,11},{10,... | collective-permute-start | bytes 786440 | tf_op jit(solution)/shard_map/ppermute | solution.py:511
  28.7 1.6 %collective-permute-start.18 = (bf16[128,1024]{1,0:T(8,128)(2,1)S(1)}, bf16[128,1024]{1,0:T(8,128)(2,1)S(1)}, u32[]{:S(2)}, u32[]{:S(2)}) collective-permute-start(bf16[128,1024]{1,0:T(8,128)(2,1)S(1)} %get-tuple-element.67.mine_ref), channel_id=1, source_target_pairs={{0,8},{4,12},{8,0},{12,4},{16,24},{20,28},{24,16},{28,20},{1,9},{5... | collective-permute-start | bytes 786440 | tf_op jit(solution)/shard_map/ppermute | solution.py:511
  30.3 1.5 %shard_map.86 = (f32[3,4,32,128]{3,2,1,0:T(8,128)S(1)}, bf16[32,256]{1,0:T(8,128)(2,1)S(1)}) custom-call(bf16[4,32,256]{2,1,0:T(8,128)(2,1)S(1)} %get-tuple-element.58.refs_0_, bf16[4,32,256]{2,1,0:T(8,128)(2,1)S(1)} %collective-permute-done.4.refs_1_, bf16[4,32,256]{2,1,0:T(8,128)(2,1)S(1)} %collective-permute-done.5.refs_2_, ...), custom_call_target="tpu_custom_call" | custom-call | flops 75497 | bytes 3145 | tf_op jit(solution)/shard_map/pallas_call | solution.py:309
  31.8 0.5 collective-permute-start.10
  32.4 0.1 collective-permute-start.11
  32.4 3.4 %collective-permute-done.12.refs_5_.refs_7_ = bf16[128,1024]{1,0:T(8,128)(2,1)S(1)} collective-permute-done((bf16[128,1024]{1,0:T(8,128)(2,1)S(1)}, bf16[128,1024]{1,0:T(8,128)(2,1)S(1)}, u32[]{:S(2)}, u32[]{:S(2)}) %collective-permute-start.12) | collective-permute-done | bytes 262176 | tf_op jit(solution)/shard_map/ppermute | solution.py:511
  35.8 0.2 collective-permute-done.10.other_ref
  36.0 1.1 %collective-permute-done.18.other_ref = bf16[128,1024]{1,0:T(8,128)(2,1)S(1)} collective-permute-done((bf16[128,1024]{1,0:T(8,128)(2,1)S(1)}, bf16[128,1024]{1,0:T(8,128)(2,1)S(1)}, u32[]{:S(2)}, u32[]{:S(2)}) %collective-permute-start.18) | collective-permute-done | bytes 262176 | tf_op jit(solution)/shard_map/ppermute | solution.py:511
  37.1 2.7 %collective-permute-start.23 = (bf16[128,512]{1,0:T(8,128)(2,1)S(1)}, bf16[128,512]{1,0:T(8,128)(2,1)S(1)}, u32[]{:S(2)}, u32[]{:S(2)}) collective-permute-start(bf16[128,512]{1,0:T(8,128)(2,1)S(1)} %get-tuple-element.84.mine_ref), channel_id=1, source_target_pairs={{0,16},{4,20},{8,24},{12,28},{16,0},{20,4},{24,8},{28,12},{1,17},{... | collective-permute-start | bytes 393224 | tf_op jit(solution)/shard_map/ppermute | solution.py:511
  39.8 0.3 shard_map.88
  40.1 0.7 %collective-permute-start.14 = (bf16[32,256]{1,0:T(8,128)(2,1)S(1)}, bf16[32,256]{1,0:T(8,128)(2,1)S(1)}, u32[]{:S(2)}, u32[]{:S(2)}) collective-permute-start(bf16[32,256]{1,0:T(8,128)(2,1)S(1)} %get-tuple-element.75.refs_0_.refs_1_), channel_id=1, source_target_pairs={{0,2},{1,3},{2,0},{3,1},{4,6},{5,7},{6,4},{7,5},{8,10},{9,11},{10,... | collective-permute-start | bytes 49160 | tf_op jit(solution)/shard_map/ppermute | solution.py:511
  40.8 1.5 %collective-permute-start.15 = (bf16[32,256]{1,0:T(8,128)(2,1)S(1)}, bf16[32,256]{1,0:T(8,128)(2,1)S(1)}, u32[]{:S(2)}, u32[]{:S(2)}) collective-permute-start(bf16[32,256]{1,0:T(8,128)(2,1)S(1)} %get-tuple-element.75.refs_0_.refs_1_), channel_id=1, source_target_pairs={{0,4},{4,0},{8,12},{12,8},{16,20},{20,16},{24,28},{28,24},{1,5},{5... | collective-permute-start | bytes 49160 | tf_op jit(solution)/shard_map/ppermute | solution.py:511
  42.4 1.3 %collective-permute-start.16 = (bf16[32,256]{1,0:T(8,128)(2,1)S(1)}, bf16[32,256]{1,0:T(8,128)(2,1)S(1)}, u32[]{:S(2)}, u32[]{:S(2)}) collective-permute-start(bf16[32,256]{1,0:T(8,128)(2,1)S(1)} %get-tuple-element.75.refs_0_.refs_1_), channel_id=1, source_target_pairs={{0,6},{1,7},{2,4},{3,5},{4,2},{5,3},{6,0},{7,1},{8,14},{9,15},{10,... | collective-permute-start | bytes 49160 | tf_op jit(solution)/shard_map/ppermute | solution.py:518
  43.7 0.7 %collective-permute-start.19 = (bf16[128,768]{1,0:T(8,128)(2,1)S(1)}, bf16[128,768]{1,0:T(8,128)(2,1)S(1)}, u32[]{:S(2)}, u32[]{:S(2)}) collective-permute-start(bf16[128,768]{1,0:T(8,128)(2,1)S(1)} %shard_map.91), channel_id=1, source_target_pairs={{0,2},{1,3},{2,0},{3,1},{4,6},{5,7},{6,4},{7,5},{8,10},{9,11},{10,... | collective-permute-start | bytes 589832 | tf_op jit(solution)/shard_map/ppermute | solution.py:511
  44.4 0.2 collective-permute-done.15.refs_2_
  44.6 2.6 %collective-permute-done.16.refs_3_ = bf16[32,256]{1,0:T(8,128)(2,1)S(1)} collective-permute-done((bf16[32,256]{1,0:T(8,128)(2,1)S(1)}, bf16[32,256]{1,0:T(8,128)(2,1)S(1)}, u32[]{:S(2)}, u32[]{:S(2)}) %collective-permute-start.16) | collective-permute-done | bytes 16416 | tf_op jit(solution)/shard_map/ppermute | solution.py:518
  47.2 0.6 shard_map.89
  47.8 1.4 %collective-permute-start.24 = (bf16[128,1536]{1,0:T(8,128)(2,1)S(1)}, bf16[128,1536]{1,0:T(8,128)(2,1)S(1)}, u32[]{:S(2)}, u32[]{:S(2)}) collective-permute-start(bf16[128,1536]{1,0:T(8,128)(2,1)S(1)} %shard_map.96), channel_id=1, source_target_pairs={{0,2},{1,3},{2,0},{3,1},{4,6},{5,7},{6,4},{7,5},{8,10},{9,11},{10,... | collective-permute-start | bytes 1179656 | tf_op jit(solution)/shard_map/ppermute | solution.py:511
  49.4 0.3 collective-permute-done.19.refs_0_.refs_3_.refs_11_
  49.7 0.3 collective-permute-start.21
  50.0 1.7 %collective-permute-start.17 = (bf16[32,256]{1,0:T(8,128)(2,1)S(1)}, bf16[32,256]{1,0:T(8,128)(2,1)S(1)}, u32[]{:S(2)}, u32[]{:S(2)}) collective-permute-start(bf16[32,256]{1,0:T(8,128)(2,1)S(1)} %get-tuple-element.76.refs_1_.refs_0_.refs_3_), channel_id=1, source_target_pairs={{0,8},{4,12},{8,0},{12,4},{16,24},{20,28},{24,16},{28,20},{1,9},{5... | collective-permute-start | bytes 49160 | tf_op jit(solution)/shard_map/ppermute | solution.py:511
  51.7 2.0 %collective-permute-done.17.refs_1_ = bf16[32,256]{1,0:T(8,128)(2,1)S(1)} collective-permute-done((bf16[32,256]{1,0:T(8,128)(2,1)S(1)}, bf16[32,256]{1,0:T(8,128)(2,1)S(1)}, u32[]{:S(2)}, u32[]{:S(2)}) %collective-permute-start.17) | collective-permute-done | bytes 16416 | tf_op jit(solution)/shard_map/ppermute | solution.py:511
  53.7 0.6 shard_map.94
  54.3 0.8 %collective-permute-start.22 = (bf16[32,256]{1,0:T(8,128)(2,1)S(1)}, bf16[32,256]{1,0:T(8,128)(2,1)S(1)}, u32[]{:S(2)}, u32[]{:S(2)}) collective-permute-start(bf16[32,256]{1,0:T(8,128)(2,1)S(1)} %get-tuple-element.79.refs_0_), channel_id=1, source_target_pairs={{0,16},{4,20},{8,24},{12,28},{16,0},{20,4},{24,8},{28,12},{1,17},{... | collective-permute-start | bytes 49160 | tf_op jit(solution)/shard_map/ppermute | solution.py:511
  55.1 3.8 %collective-permute-done.22._.refs_1_ = bf16[32,256]{1,0:T(8,128)(2,1)S(1)} collective-permute-done((bf16[32,256]{1,0:T(8,128)(2,1)S(1)}, bf16[32,256]{1,0:T(8,128)(2,1)S(1)}, u32[]{:S(2)}, u32[]{:S(2)}) %collective-permute-start.22) | collective-permute-done | bytes 16416 | tf_op jit(solution)/shard_map/ppermute | solution.py:511
  59.0 0.1 collective-permute-start.25
  59.1 1.7 %collective-permute-done.25.refs_15_ = bf16[128,1536]{1,0:T(8,128)(2,1)S(1)} collective-permute-done((bf16[128,1536]{1,0:T(8,128)(2,1)S(1)}, bf16[128,1536]{1,0:T(8,128)(2,1)S(1)}, u32[]{:S(2)}, u32[]{:S(2)}) %collective-permute-start.25) | collective-permute-done | bytes 393248 | tf_op jit(solution)/shard_map/ppermute | solution.py:511
  60.8 1.1 %shard_map.98 = bf16[4,32,256]{2,1,0:T(8,128)(2,1)S(1)} custom-call(bf16[32,256]{1,0:T(8,128)(2,1)S(1)} %get-tuple-element.79.refs_0_, bf16[32,256]{1,0:T(8,128)(2,1)S(1)} %collective-permute-done.22._.refs_1_, f32[4,32,128]{2,1,0:T(8,128)S(1)} %get-tuple-element.80.refs_2_, f32[4,32,128]{2,1,0:T(8,128)S(1)} %get-tuple-element.81.refs_3_, ...), custom_call_target="tpu_custom_call" | custom-call | flops 67108 | bytes 4194 | tf_op jit(solution)/shard_map/pallas_call | solution.py:479
  61.9 6.1 %all-gather = bf16[16,32,256]{2,1,0:T(8,128)(2,1)S(1)} all-gather(bf16[4,32,256]{2,1,0:T(8,128)(2,1)S(1)} %shard_map.98), channel_id=2, replica_groups=mesh['leaf'=8,'rhs'=4] {'rhs'}, dimensions={0}, use_global_device_ids=true | all-gather | bytes 327680 | tf_op jit(solution)/shard_map/all_gather | solution.py:620
  68.0 1.0 %shard_map.99 = f32[8,64,128]{2,1,0:T(8,128)} custom-call(f32[4,64,128]{2,1,0:T(8,128)S(1)} %get-tuple-element.50.far_ref, f32[4,64,128]{2,1,0:T(8,128)S(1)} %get-tuple-element.57.own_ref, bf16[4,4,32,256]{3,2,1,0:T(8,128)(2,1)S(1)} %bitcast.5, bf16[8,128,256]{2,1,0:T(8,128)(2,1)S(1)} %copy-done.3), custom_call_target="tpu_custom_call" | custom-call | flops 33554 | bytes 524 | tf_op jit(solution)/shard_map/pallas_call | solution.py:502
  (41 shorter events, 0.4 us)
Async XLA Ops:
  0.0 11.6 %copy-start.2 = (bf16[8,128,256]{2,1,0:T(8,128)(2,1)S(1)}, bf16[8,128,256]{2,1,0:T(8,128)(2,1)}, u32[]{:S(2)}) copy-start(bf16[8,128,256]{2,1,0:T(8,128)(2,1)} %refs_3_.1) | copy-start | bytes 1572868
  0.0 6.6 %collective-permute-start = (bf16[64,1024]{1,0:T(8,128)(2,1)}, bf16[64,1024]{1,0:T(8,128)(2,1)S(1)}, u32[]{:S(2)}, u32[]{:S(2)}) collective-permute-start(bf16[64,1024]{1,0:T(8,128)(2,1)} %refs_0_.1), channel_id=1, source_target_pairs={{0,2},{1,3},{2,0},{3,1},{4,6},{5,7},{6,4},{7,5},{8,10},{9,11},{10,... | collective-permute-start | bytes 393224 | tf_op jit(solution)/shard_map/ppermute | solution.py:511
  2.9 3.7 %collective-permute-start.1 = (bf16[64,1024]{1,0:T(8,128)(2,1)}, bf16[64,1024]{1,0:T(8,128)(2,1)S(1)}, u32[]{:S(2)}, u32[]{:S(2)}) collective-permute-start(bf16[64,1024]{1,0:T(8,128)(2,1)} %refs_0_.1), channel_id=1, source_target_pairs={{0,1},{1,0},{2,3},{3,2},{4,5},{5,4},{6,7},{7,6},{8,9},{9,8},{10,11... | collective-permute-start | bytes 393224 | tf_op jit(solution)/shard_map/ppermute | solution.py:511
  2.9 8.6 %copy-start.6 = (bf16[64,1024]{1,0:T(8,128)(2,1)S(1)}, bf16[64,1024]{1,0:T(8,128)(2,1)}, u32[]{:S(2)}) copy-start(bf16[64,1024]{1,0:T(8,128)(2,1)} %refs_0_.1) | copy-start | bytes 393220
  6.6 1.3 %collective-permute-start.2 = (bf16[64,1024]{1,0:T(8,128)(2,1)S(1)}, bf16[64,1024]{1,0:T(8,128)(2,1)S(1)}, u32[]{:S(2)}, u32[]{:S(2)}) collective-permute-start(bf16[64,1024]{1,0:T(8,128)(2,1)S(1)} %collective-permute-done.refs_1_), channel_id=1, source_target_pairs={{0,1},{1,0},{2,3},{3,2},{4,5},{5,4},{6,7},{7,6},{8,9},{9,8},{10,11... | collective-permute-start | bytes 393224 | tf_op jit(solution)/shard_map/ppermute | solution.py:511
  8.0 9.7 %collective-permute-start.3 = (bf16[4,128,1024]{2,1,0:T(8,128)(2,1)}, bf16[4,128,1024]{2,1,0:T(8,128)(2,1)S(1)}, u32[]{:S(2)}, u32[]{:S(2)}) collective-permute-start(bf16[4,128,1024]{2,1,0:T(8,128)(2,1)} %get-tuple-element.53.refs_4_.own_ref.refs_16_), channel_id=1, source_target_pairs={{0,1},{1,0},{2,3},{3,2},{4,5},{5,4},{6,7},{7,6},{8,9},{9,8},{10,11... | collective-permute-start | bytes 3145736 | tf_op jit(solution)/shard_map/ppermute | solution.py:511
  8.1 18.7 %collective-permute-start.7 = (bf16[3,128,768]{2,1,0:T(8,128)(2,1)}, bf16[3,128,768]{2,1,0:T(8,128)(2,1)S(1)}, u32[]{:S(2)}, u32[]{:S(2)}) collective-permute-start(bf16[3,128,768]{2,1,0:T(8,128)(2,1)} %get-tuple-element.46), channel_id=1, source_target_pairs={{0,2},{1,3},{2,0},{3,1},{4,6},{5,7},{6,4},{7,5},{8,10},{9,11},{10,... | collective-permute-start | bytes 1769480 | tf_op jit(solution)/shard_map/ppermute | solution.py:511
  9.9 1.7 %copy-start.7 = (s32[4096]{0:T(1024)S(1)}, s32[4096]{0:T(1024)}, u32[]{:S(2)}) copy-start(s32[4096]{0:T(1024)} %param.9) | copy-start | bytes 49156
  9.9 11.7 %collective-permute-start.8 = (bf16[128,1024]{1,0:T(8,128)(2,1)}, bf16[128,1024]{1,0:T(8,128)(2,1)S(1)}, u32[]{:S(2)}, u32[]{:S(2)}) collective-permute-start(bf16[128,1024]{1,0:T(8,128)(2,1)} %get-tuple-element.64.mine_ref), channel_id=1, source_target_pairs={{0,4},{4,0},{8,12},{12,8},{16,20},{20,16},{24,28},{28,24},{1,5},{5... | collective-permute-start | bytes 786440 | tf_op jit(solution)/shard_map/ppermute | solution.py:511
  11.6 1.2 %copy-start.1 = (bf16[8,128,512]{2,1,0:T(8,128)(2,1)S(1)}, bf16[8,128,512]{2,1,0:T(8,128)(2,1)}, u32[]{:S(2)}) copy-start(bf16[8,128,512]{2,1,0:T(8,128)(2,1)} %refs_2_.1) | copy-start | bytes 3145732
  16.2 8.9 %collective-permute-start.6 = (bf16[4,32,256]{2,1,0:T(8,128)(2,1)S(1)}, bf16[4,32,256]{2,1,0:T(8,128)(2,1)S(1)}, u32[]{:S(2)}, u32[]{:S(2)}) collective-permute-start(bf16[4,32,256]{2,1,0:T(8,128)(2,1)S(1)} %get-tuple-element.61), channel_id=1, source_target_pairs={{0,3},{1,2},{2,1},{3,0},{4,7},{5,6},{6,5},{7,4},{8,11},{9,10},{10,... | collective-permute-start | bytes 196616 | tf_op jit(solution)/shard_map/ppermute | solution.py:511
  16.3 10.4 %collective-permute-start.4 = (bf16[4,32,256]{2,1,0:T(8,128)(2,1)S(1)}, bf16[4,32,256]{2,1,0:T(8,128)(2,1)S(1)}, u32[]{:S(2)}, u32[]{:S(2)}) collective-permute-start(bf16[4,32,256]{2,1,0:T(8,128)(2,1)S(1)} %get-tuple-element.54), channel_id=1, source_target_pairs={{0,2},{1,3},{2,0},{3,1},{4,6},{5,7},{6,4},{7,5},{8,10},{9,11},{10,... | collective-permute-start | bytes 196616 | tf_op jit(solution)/shard_map/ppermute | solution.py:511
  17.7 9.1 %copy-start.4 = (bf16[128,1024]{1,0:T(8,128)(2,1)S(1)}, bf16[128,1024]{1,0:T(8,128)(2,1)}, u32[]{:S(2)}) copy-start(bf16[128,1024]{1,0:T(8,128)(2,1)} %get-tuple-element.64.mine_ref) | copy-start | bytes 786436
  17.7 9.1 %copy-start.5 = (bf16[128,768]{1,0:T(8,128)(2,1)S(1)}, bf16[128,768]{1,0:T(8,128)(2,1)}, u32[]{:S(2)}) copy-start(bf16[128,768]{1,0:T(8,128)(2,1)} %get-tuple-element.66.refs_0_) | copy-start | bytes 589828
  17.7 12.6 %copy-start = (bf16[4,128,1024]{2,1,0:T(8,128)(2,1)S(1)}, bf16[4,128,1024]{2,1,0:T(8,128)(2,1)}, u32[]{:S(2)}) copy-start(bf16[4,128,1024]{2,1,0:T(8,128)(2,1)} %get-tuple-element.53.refs_4_.own_ref.refs_16_) | copy-start | bytes 3145732
  21.1 5.7 %collective-permute-start.5 = (bf16[4,32,256]{2,1,0:T(8,128)(2,1)S(1)}, bf16[4,32,256]{2,1,0:T(8,128)(2,1)S(1)}, u32[]{:S(2)}, u32[]{:S(2)}) collective-permute-start(bf16[4,32,256]{2,1,0:T(8,128)(2,1)S(1)} %get-tuple-element.60), channel_id=1, source_target_pairs={{0,1},{1,0},{2,3},{3,2},{4,5},{5,4},{6,7},{7,6},{8,9},{9,8},{10,11... | collective-permute-start | bytes 196616 | tf_op jit(solution)/shard_map/ppermute | solution.py:511
  26.8 3.5 %collective-permute-start.9 = (bf16[3,128,768]{2,1,0:T(8,128)(2,1)S(1)}, bf16[3,128,768]{2,1,0:T(8,128)(2,1)S(1)}, u32[]{:S(2)}, u32[]{:S(2)}) collective-permute-start(bf16[3,128,768]{2,1,0:T(8,128)(2,1)S(1)} %collective-permute-done.7.refs_5_), channel_id=1, source_target_pairs={{0,1},{1,0},{2,3},{3,2},{4,5},{5,4},{6,7},{7,6},{8,9},{9,8},{10,11... | collective-permute-start | bytes 1769480 | tf_op jit(solution)/shard_map/ppermute | solution.py:511
  26.9 8.9 %collective-permute-start.12 = (bf16[128,1024]{1,0:T(8,128)(2,1)S(1)}, bf16[128,1024]{1,0:T(8,128)(2,1)S(1)}, u32[]{:S(2)}, u32[]{:S(2)}) collective-permute-start(bf16[128,1024]{1,0:T(8,128)(2,1)S(1)} %get-tuple-element.73.refs_0_.refs_4_.refs_6_), channel_id=1, source_target_pairs={{0,2},{1,3},{2,0},{3,1},{4,6},{5,7},{6,4},{7,5},{8,10},{9,11},{10,... | collective-permute-start | bytes 786440 | tf_op jit(solution)/shard_map/ppermute | solution.py:511
  28.7 8.4 %collective-permute-start.18 = (bf16[128,1024]{1,0:T(8,128)(2,1)S(1)}, bf16[128,1024]{1,0:T(8,128)(2,1)S(1)}, u32[]{:S(2)}, u32[]{:S(2)}) collective-permute-start(bf16[128,1024]{1,0:T(8,128)(2,1)S(1)} %get-tuple-element.67.mine_ref), channel_id=1, source_target_pairs={{0,8},{4,12},{8,0},{12,4},{16,24},{20,28},{24,16},{28,20},{1,9},{5... | collective-permute-start | bytes 786440 | tf_op jit(solution)/shard_map/ppermute | solution.py:511
  31.8 4.2 %collective-permute-start.10 = (bf16[32,256]{1,0:T(8,128)(2,1)S(1)}, bf16[32,256]{1,0:T(8,128)(2,1)S(1)}, u32[]{:S(2)}, u32[]{:S(2)}) collective-permute-start(bf16[32,256]{1,0:T(8,128)(2,1)S(1)} %get-tuple-element.69.refs_1_.mine_ref), channel_id=1, source_target_pairs={{0,2},{1,3},{2,0},{3,1},{4,6},{5,7},{6,4},{7,5},{8,10},{9,11},{10,... | collective-permute-start | bytes 49160 | tf_op jit(solution)/shard_map/ppermute | solution.py:511
  32.4 7.4 %collective-permute-start.11 = (bf16[128,1024]{1,0:T(8,128)(2,1)S(1)}, bf16[128,1024]{1,0:T(8,128)(2,1)S(1)}, u32[]{:S(2)}, u32[]{:S(2)}) collective-permute-start(bf16[128,1024]{1,0:T(8,128)(2,1)S(1)} %shard_map.87), channel_id=1, source_target_pairs={{0,1},{1,0},{2,3},{3,2},{4,5},{5,4},{6,7},{7,6},{8,9},{9,8},{10,11... | collective-permute-start | bytes 786440 | tf_op jit(solution)/shard_map/ppermute | solution.py:511
  36.0 4.1 %collective-permute-start.13 = (bf16[128,1024]{1,0:T(8,128)(2,1)S(1)}, bf16[128,1024]{1,0:T(8,128)(2,1)S(1)}, u32[]{:S(2)}, u32[]{:S(2)}) collective-permute-start(bf16[128,1024]{1,0:T(8,128)(2,1)S(1)} %collective-permute-done.12.refs_5_.refs_7_), channel_id=1, source_target_pairs={{0,1},{1,0},{2,3},{3,2},{4,5},{5,4},{6,7},{7,6},{8,9},{9,8},{10,11... | collective-permute-start | bytes 786440 | tf_op jit(solution)/shard_map/ppermute | solution.py:511
  37.1 10.6 %collective-permute-start.23 = (bf16[128,512]{1,0:T(8,128)(2,1)S(1)}, bf16[128,512]{1,0:T(8,128)(2,1)S(1)}, u32[]{:S(2)}, u32[]{:S(2)}) collective-permute-start(bf16[128,512]{1,0:T(8,128)(2,1)S(1)} %get-tuple-element.84.mine_ref), channel_id=1, source_target_pairs={{0,16},{4,20},{8,24},{12,28},{16,0},{20,4},{24,8},{28,12},{1,17},{... | collective-permute-start | bytes 393224 | tf_op jit(solution)/shard_map/ppermute | solution.py:511
  40.1 4.3 %collective-permute-start.14 = (bf16[32,256]{1,0:T(8,128)(2,1)S(1)}, bf16[32,256]{1,0:T(8,128)(2,1)S(1)}, u32[]{:S(2)}, u32[]{:S(2)}) collective-permute-start(bf16[32,256]{1,0:T(8,128)(2,1)S(1)} %get-tuple-element.75.refs_0_.refs_1_), channel_id=1, source_target_pairs={{0,2},{1,3},{2,0},{3,1},{4,6},{5,7},{6,4},{7,5},{8,10},{9,11},{10,... | collective-permute-start | bytes 49160 | tf_op jit(solution)/shard_map/ppermute | solution.py:511
  40.8 3.7 %collective-permute-start.15 = (bf16[32,256]{1,0:T(8,128)(2,1)S(1)}, bf16[32,256]{1,0:T(8,128)(2,1)S(1)}, u32[]{:S(2)}, u32[]{:S(2)}) collective-permute-start(bf16[32,256]{1,0:T(8,128)(2,1)S(1)} %get-tuple-element.75.refs_0_.refs_1_), channel_id=1, source_target_pairs={{0,4},{4,0},{8,12},{12,8},{16,20},{20,16},{24,28},{28,24},{1,5},{5... | collective-permute-start | bytes 49160 | tf_op jit(solution)/shard_map/ppermute | solution.py:511
  42.4 4.8 %collective-permute-start.16 = (bf16[32,256]{1,0:T(8,128)(2,1)S(1)}, bf16[32,256]{1,0:T(8,128)(2,1)S(1)}, u32[]{:S(2)}, u32[]{:S(2)}) collective-permute-start(bf16[32,256]{1,0:T(8,128)(2,1)S(1)} %get-tuple-element.75.refs_0_.refs_1_), channel_id=1, source_target_pairs={{0,6},{1,7},{2,4},{3,5},{4,2},{5,3},{6,0},{7,1},{8,14},{9,15},{10,... | collective-permute-start | bytes 49160 | tf_op jit(solution)/shard_map/ppermute | solution.py:518
  43.7 6.0 %collective-permute-start.19 = (bf16[128,768]{1,0:T(8,128)(2,1)S(1)}, bf16[128,768]{1,0:T(8,128)(2,1)S(1)}, u32[]{:S(2)}, u32[]{:S(2)}) collective-permute-start(bf16[128,768]{1,0:T(8,128)(2,1)S(1)} %shard_map.91), channel_id=1, source_target_pairs={{0,2},{1,3},{2,0},{3,1},{4,6},{5,7},{6,4},{7,5},{8,10},{9,11},{10,... | collective-permute-start | bytes 589832 | tf_op jit(solution)/shard_map/ppermute | solution.py:511
  47.8 11.1 %collective-permute-start.24 = (bf16[128,1536]{1,0:T(8,128)(2,1)S(1)}, bf16[128,1536]{1,0:T(8,128)(2,1)S(1)}, u32[]{:S(2)}, u32[]{:S(2)}) collective-permute-start(bf16[128,1536]{1,0:T(8,128)(2,1)S(1)} %shard_map.96), channel_id=1, source_target_pairs={{0,2},{1,3},{2,0},{3,1},{4,6},{5,7},{6,4},{7,5},{8,10},{9,11},{10,... | collective-permute-start | bytes 1179656 | tf_op jit(solution)/shard_map/ppermute | solution.py:511
  49.3 4.4 %collective-permute-start.20 = (bf16[128,1024]{1,0:T(8,128)(2,1)S(1)}, bf16[128,1024]{1,0:T(8,128)(2,1)S(1)}, u32[]{:S(2)}, u32[]{:S(2)}) collective-permute-start(bf16[128,1024]{1,0:T(8,128)(2,1)S(1)} %shard_map.92), channel_id=1, source_target_pairs={{0,1},{1,0},{2,3},{3,2},{4,5},{5,4},{6,7},{7,6},{8,9},{9,8},{10,11... | collective-permute-start | bytes 786440 | tf_op jit(solution)/shard_map/ppermute | solution.py:511
  49.7 4.0 %collective-permute-start.21 = (bf16[128,768]{1,0:T(8,128)(2,1)S(1)}, bf16[128,768]{1,0:T(8,128)(2,1)S(1)}, u32[]{:S(2)}, u32[]{:S(2)}) collective-permute-start(bf16[128,768]{1,0:T(8,128)(2,1)S(1)} %shard_map.93), channel_id=1, source_target_pairs={{0,1},{1,0},{2,3},{3,2},{4,5},{5,4},{6,7},{7,6},{8,9},{9,8},{10,11... | collective-permute-start | bytes 589832 | tf_op jit(solution)/shard_map/ppermute | solution.py:511
  50.0 3.7 %collective-permute-start.17 = (bf16[32,256]{1,0:T(8,128)(2,1)S(1)}, bf16[32,256]{1,0:T(8,128)(2,1)S(1)}, u32[]{:S(2)}, u32[]{:S(2)}) collective-permute-start(bf16[32,256]{1,0:T(8,128)(2,1)S(1)} %get-tuple-element.76.refs_1_.refs_0_.refs_3_), channel_id=1, source_target_pairs={{0,8},{4,12},{8,0},{12,4},{16,24},{20,28},{24,16},{28,20},{1,9},{5... | collective-permute-start | bytes 49160 | tf_op jit(solution)/shard_map/ppermute | solution.py:511
  54.3 4.7 %collective-permute-start.22 = (bf16[32,256]{1,0:T(8,128)(2,1)S(1)}, bf16[32,256]{1,0:T(8,128)(2,1)S(1)}, u32[]{:S(2)}, u32[]{:S(2)}) collective-permute-start(bf16[32,256]{1,0:T(8,128)(2,1)S(1)} %get-tuple-element.79.refs_0_), channel_id=1, source_target_pairs={{0,16},{4,20},{8,24},{12,28},{16,0},{20,4},{24,8},{28,12},{1,17},{... | collective-permute-start | bytes 49160 | tf_op jit(solution)/shard_map/ppermute | solution.py:511
  59.0 1.8 %collective-permute-start.25 = (bf16[128,1536]{1,0:T(8,128)(2,1)S(1)}, bf16[128,1536]{1,0:T(8,128)(2,1)S(1)}, u32[]{:S(2)}, u32[]{:S(2)}) collective-permute-start(bf16[128,1536]{1,0:T(8,128)(2,1)S(1)} %shard_map.97.refs_14_), channel_id=1, source_target_pairs={{0,1},{1,0},{2,3},{3,2},{4,5},{5,4},{6,7},{7,6},{8,9},{9,8},{10,11... | collective-permute-start | bytes 1179656 | tf_op jit(solution)/shard_map/ppermute | solution.py:511
  60.8 7.2 %copy-start.3 = (bf16[8,128,256]{2,1,0:T(8,128)(2,1)S(1)}, bf16[8,128,256]{2,1,0:T(8,128)(2,1)}, u32[]{:S(2)}) copy-start(bf16[8,128,256]{2,1,0:T(8,128)(2,1)} %coupling_ref.1) | copy-start | bytes 1572868

commit v5 on v4

--- a/solution.py
+++ b/solution.py
@@ -154,18 +154,16 @@
 
 
 def hop_kernel(level, top_ref, tail_ref, _, out_ref):
-    node_size = top_ref.shape[1]
     side = (lax.axis_index("leaf") // (1 << level)) % 2
     here = lax.axis_index("rhs") // CORES == side
-    out_ref[:, node_size:] = tail_ref[:, node_size:]
 
     @pl.when(here)
     def _():
-        out_ref[:, :node_size] = top_ref[...]
+        out_ref[...] = top_ref[...]
 
     @pl.when(jnp.logical_not(here))
     def _():
-        out_ref[:, :node_size] = tail_ref[:, :node_size]
+        out_ref[...] = tail_ref[...]
 
 
 def hop(level, top, tail, anchor):
@@ -278,12 +276,18 @@
 
 def group_up_kernel(per_dev, *refs):
     *refs, solved_ref, out_ref = refs
-    parts, packs = refs[: 2 * CORES], refs[2 * CORES :]
+    parts, (own, far, near, *far_near) = refs[: 2 * CORES], refs[2 * CORES :]
     levels, _ = half_levels(per_dev)
     rank = parts[0].shape[2]
 
     def pieces(node, start, width):
-        return [ref[node, :, pl.ds(start, width)] for ref in packs]
+        columns = pl.ds(start, width)
+        return [
+            own[node, :, columns],
+            far[node, :, columns],
+            near[node, :, columns],
+            far_near[node][:, columns],
+        ]
 
     sums = sum(ref[...].astype(jnp.float32) for ref in parts).astype(jnp.bfloat16)
     current = [sums[i] for i in range(sums.shape[0])]
@@ -401,7 +405,8 @@
     solved_cross, refs = refs[: cross_levels - 1], refs[cross_levels - 1 :]
     solved_top, solved_half, refs = refs[0], refs[1], refs[2:]
     count = 2 * CORES * (cross_levels - 1)
-    cross_packs, (tail, near_tail, keep, keep_near) = refs[:count], refs[count:]
+    cross_packs, others = refs[:count], refs[count:]
+    tail, near_tail, half_tail, near_half_tail, keep, keep_near = others
     levels, total = half_levels(per_dev)
     rank = out_ref.shape[2]
     node_size = 2 * rank
@@ -425,17 +430,7 @@
     incoming = choose(half)
     for level in range(cross_levels - 2, -1, -1):
         packs = cross_packs[2 * CORES * level : 2 * CORES * (level + 1)]
-        own, far, near, far_near = packs
-        if level == 0:
-            couplings = [ref[:, columns(ref)] for ref in packs]
-        else:
-            start = node_size + (total + level - 1) * rank
-            couplings = [
-                own[:, columns(own)],
-                tail[:, start : start + rank],
-                near[:, columns(near)],
-                near_tail[:, start : start + rank],
-            ]
+        couplings = [ref[:, columns(ref)] for ref in packs]
         for flip, coupling in zip(PIECES, couplings):
             piece = place ^ flip
             solved = solved_cross[level][piece]
@@ -451,12 +446,12 @@
         following = []
         for n in range(count):
             node = base + n
-            start = node_size + node * rank
+            start = node * rank
             couplings = (
                 keep[node, :, columns(keep)],
-                tail[:, start : start + rank],
+                half_tail[:, start : start + rank],
                 keep_near[node, :, columns(keep)],
-                near_tail[:, start : start + rank],
+                near_half_tail[:, start : start + rank],
             )
             for flip, coupling in zip(PIECES, couplings):
                 piece = place ^ flip
@@ -571,20 +566,22 @@
     far_cross = after(swap(far_cross, "rhs", CORES + 1), own_same)
     parts = [own_same, far_same, swap(own_cross, "rhs", 1), far_cross]
     half_far = after(half_far, (parts, carrier))
-    half_near = swap(half_far, "rhs", 1)
+    half_near = [swap(half_far[n], "rhs", 1) for n in range(half_far.shape[0])]
+    ancestor, carrier = rise(carrier, 1, parts)
+    ancestors.append(ancestor)
+    parts = after(parts, ancestor)
     fars = [swap(after(ancestors[0], half_far), "rhs", CORES)]
 
-    solved_half, current = group_up(per_dev, parts, [keep, half_far, keep_near, half_near])
-    own_near = swap(join([ancestors[0]], current), "rhs", 1)
-    other = swap(current, "rhs", CORES)
-    ancestor, carrier = rise(carrier, 1, other)
-    ancestors.append(ancestor)
+    solved_half, current = group_up(per_dev, parts, [keep, half_far, keep_near, *half_near])
+    own_near = swap(after(ancestors[0], half_far), "rhs", 1)
+    other = swap(after(current, own_near), "rhs", CORES)
     solved_top, current = half_up(current, after(other, own_near), keep, keep_near)
     fars[0] = after(fars[0], other)
     near_far = swap(fars[0], "rhs", 1)
     cross_packs = [[ancestors[0], fars[0], own_near, near_far]]
-    factors = [(0, node_size + rank)]
-    fars.append(swap(join([ancestors[1]], current, factors), "rhs", CORES))
+    anchor = other
+    fars.append(swap(join([ancestors[1]], anchor), "rhs", CORES))
+    half_tail = swap(join([send_coupling], current), "rhs", CORES)
     current = after(current, near_far)
     inputs = [
         current,
@@ -593,6 +590,10 @@
         far_swap(current, 1, CORES),
     ]
 
+    for level in range(2, cross_levels):
+        ancestor, carrier = rise(carrier, level, other)
+        ancestors.append(ancestor)
+    inputs = after(inputs, ancestors[-1])
     solved_cross = []
     for level in range(cross_levels - 1):
         if level > 0:
@@ -604,18 +605,13 @@
         solved_cross.append(solved)
         inputs = [current, swap(current, "leaf", 2 << level)]
         if level == 0:
-            for later in range(2, cross_levels):
-                ancestor, carrier = rise(carrier, later, current)
-                ancestors.append(ancestor)
             for later in range(2, cross_levels - 1):
-                fars.append(swap(join([ancestors[later]], current, factors), "rhs", CORES))
-            blocks = [ancestors[-1], send_coupling, *ancestors[1:-1]]
-            cuts = [(0, node_size), (0, send_coupling.shape[1])]
-            cuts += [(node_size + rank, rank)] * (cross_levels - 2)
-            tail = swap(join(blocks, current, cuts), "rhs", CORES)
-
+                fars.append(swap(join([ancestors[later]], current), "rhs", CORES))
+            tail = swap(join([ancestors[-1]], current), "rhs", CORES)
+
+    near_half_tail = swap(join([half_tail], current), "rhs", 1)
     tail = hop(cross_levels - 1, ancestors[-1], tail, inputs[1])
-    others = [tail, swap(tail, "rhs", 1), keep, keep_near]
+    others = [tail, swap(tail, "rhs", 1), half_tail, near_half_tail, keep, keep_near]
     shares = way_down(per_dev, inputs, solved_cross, solved_top, solved_half, cross_packs, others)
     incoming = lax.all_gather(shares, "rhs", axis=0)
     return finish(far_values, own_values, incoming, leaf_coupling)

time: 69.2 us -> 70.7 us (1.022)
  starting transfers between devices: 23.8 us -> 26.5 us
  waiting for transfers between devices: 22.4 us -> 21.6 us
    ppermute x25 -> x29, starting transfers between devices: 22.4 us -> 25 us  [swap(): lax.ppermute(block, axis, [(i, i ^ bit) for i in range(lax.axis_size(axis...]
    ppermute x1, waiting for transfers between devices: 2.59 us -> 0.31 us  [far_swap(): lax.ppermute(block, ('leaf', 'rhs'), [(i, i ^ flip) for i in range(count)])]
    ppermute x25 -> x29, waiting for transfers between devices: 19.9 us -> 21.3 us  [swap(): lax.ppermute(block, axis, [(i, i ^ bit) for i in range(lax.axis_size(axis...]
  transfers between devices with their start and end apart: 26 -> 30, of which waited for: 13 -> 16; matrix products, arithmetic and copies ran while one was open for 0% -> 0% of each run, Pallas kernels for 19% -> 18%
where the time goes in v5:
time: 70.7 us; the launch traced here: 70.5 us
  starting transfers between devices  26.5 us (37%)
  waiting for transfers between devices  21.6 us (31%)
  Pallas kernels  15 us (21%)
  blocking collectives  5.79 us (8%)
  local copies, waits for them, and re-layouts  1.29 us (2%)
    ppermute x29, starting transfers between devices, swap(): lax.ppermute(block, axis, [(i, i ^ bit) for i in range(lax.axis_size(axis...  25 us
    ppermute x29, waiting for transfers between devices, swap(): lax.ppermute(block, axis, [(i, i ^ bit) for i in range(lax.axis_size(axis...  21.3 us
    pallas_call x2, Pallas kernels, leaf_up(): pl.pallas_call(functools.partial(leaf_kernel, len(points)), grid_spec=plt...  6.81 us
    all_gather x1, blocking collectives, body(): incoming = lax.all_gather(shares, 'rhs', axis=0)  5.79 us
    pallas_call x1, Pallas kernels, pack(): pl.pallas_call(functools.partial(pack_kernel, per_dev), in_specs=[pl.Bloc...  2.99 us
    pallas_call x1, Pallas kernels, group_up(): pl.pallas_call(functools.partial(group_up_kernel, per_dev), out_shape=[ja...  1.48 us
    ppermute x1, starting transfers between devices, far_swap(): lax.ppermute(block, ('leaf', 'rhs'), [(i, i ^ flip) for i in range(count)])  1.42 us
  transfers between devices with their start and end apart: 30, of which 16 were waited for; matrix products, arithmetic and copies ran while one was open for 0% of the time, Pallas kernels for 18%

profile of v5, /device:TPU:0, one launch (start us, length us, event | category | flops | bytes accessed | tf_op | source)
XLA Modules:
  0.0 70.5 jit_solution(13648362733994561872)
XLA Ops:
  0.0 2.9 %collective-permute-start = (bf16[64,1024]{1,0:T(8,128)(2,1)}, bf16[64,1024]{1,0:T(8,128)(2,1)S(1)}, u32[]{:S(2)}, u32[]{:S(2)}) collective-permute-start(bf16[64,1024]{1,0:T(8,128)(2,1)} %refs_0_.1), channel_id=1, source_target_pairs={{0,2},{1,3},{2,0},{3,1},{4,6},{5,7},{6,4},{7,5},{8,10},{9,11},{10,... | collective-permute-start | bytes 393224 | tf_op jit(solution)/shard_map/ppermute | solution.py:506
  2.9 3.0 %shard_map.82 = (bf16[3,128,768]{2,1,0:T(8,128)(2,1)}, bf16[128,768]{1,0:T(8,128)(2,1)}, bf16[4,128,1024]{2,1,0:T(8,128)(2,1)}, bf16[128,1024]{1,0:T(8,128)(2,1)}) custom-call(bf16[8,128,512]{2,1,0:T(8,128)(2,1)} %inverse.1, bf16[8,128,256]{2,1,0:T(8,128)(2,1)} %basis.1, bf16[8,128,256]{2,1,0:T(8,128)(2,1)} %coupling.1), custom_call_target="tpu_custom_call" | custom-call | bytes 4194 | tf_op jit(solution)/shard_map/pallas_call | solution.py:93
  5.9 0.7 collective-permute-done.refs_1_
  6.7 1.3 %collective-permute-done.2.refs_3_ = bf16[64,1024]{1,0:T(8,128)(2,1)S(1)} collective-permute-done((bf16[64,1024]{1,0:T(8,128)(2,1)S(1)}, bf16[64,1024]{1,0:T(8,128)(2,1)S(1)}, u32[]{:S(2)}, u32[]{:S(2)}) %collective-permute-start.2) | collective-permute-done | bytes 131104 | tf_op jit(solution)/shard_map/ppermute | solution.py:506
  8.0 0.1 collective-permute-start.3
  8.1 1.8 %collective-permute-start.9 = (bf16[3,128,768]{2,1,0:T(8,128)(2,1)}, bf16[3,128,768]{2,1,0:T(8,128)(2,1)S(1)}, u32[]{:S(2)}, u32[]{:S(2)}) collective-permute-start(bf16[3,128,768]{2,1,0:T(8,128)(2,1)} %get-tuple-element.55), channel_id=1, source_target_pairs={{0,2},{1,3},{2,0},{3,1},{4,6},{5,7},{6,4},{7,5},{8,10},{9,11},{10,... | collective-permute-start | bytes 1769480 | tf_op jit(solution)/shard_map/ppermute | solution.py:506
  9.9 1.5 %collective-permute-start.7 = (bf16[128,1024]{1,0:T(8,128)(2,1)}, bf16[128,1024]{1,0:T(8,128)(2,1)S(1)}, u32[]{:S(2)}, u32[]{:S(2)}) collective-permute-start(bf16[128,1024]{1,0:T(8,128)(2,1)} %get-tuple-element.73.mine_ref), channel_id=1, source_target_pairs={{0,4},{4,0},{8,12},{12,8},{16,20},{20,16},{24,28},{28,24},{1,5},{5... | collective-permute-start | bytes 786440 | tf_op jit(solution)/shard_map/ppermute | solution.py:506
  11.4 0.1 pad_add_fusion.side_ref
  11.6 1.2 %copy-done.1 = bf16[8,128,512]{2,1,0:T(8,128)(2,1)S(1)} copy-done((bf16[8,128,512]{2,1,0:T(8,128)(2,1)S(1)}, bf16[8,128,512]{2,1,0:T(8,128)(2,1)}, u32[]{:S(2)}) %copy-start.1) | copy-done | bytes 1048600
  12.8 3.4 %shard_map.83 = (f32[4,64,128]{2,1,0:T(8,128)S(1)}, bf16[4,32,256]{2,1,0:T(8,128)(2,1)S(1)}, bf16[4,32,256]{2,1,0:T(8,128)(2,1)S(1)}, bf16[4,4,64,256]{3,2,1,0:T(8,128)(2,1)S(1)}) custom-call(s32[2]{0:T(128)S(1)} %pad_add_fusion.side_ref, bf16[64,1024]{1,0:T(8,128)(2,1)S(1)} %copy-done.6, bf16[64,1024]{1,0:T(8,128)(2,1)S(1)} %collective-permute-done.refs_1_, ...), custom_call_target="tpu_custom_call" | custom-call | flops 1140850 | bytes 983 | tf_op jit(solution)/shard_map/pallas_call | solution.py:244
  16.3 1.4 %collective-permute-start.4 = (bf16[4,32,256]{2,1,0:T(8,128)(2,1)S(1)}, bf16[4,32,256]{2,1,0:T(8,128)(2,1)S(1)}, u32[]{:S(2)}, u32[]{:S(2)}) collective-permute-start(bf16[4,32,256]{2,1,0:T(8,128)(2,1)S(1)} %get-tuple-element.63), channel_id=1, source_target_pairs={{0,2},{1,3},{2,0},{3,1},{4,6},{5,7},{6,4},{7,5},{8,10},{9,11},{10,... | collective-permute-start | bytes 196616 | tf_op jit(solution)/shard_map/ppermute | solution.py:506
  17.7 3.4 %shard_map.84 = (f32[4,64,128]{2,1,0:T(8,128)S(1)}, bf16[4,32,256]{2,1,0:T(8,128)(2,1)S(1)}, bf16[4,32,256]{2,1,0:T(8,128)(2,1)S(1)}) custom-call(s32[2]{0:T(128)S(1)} %pad_add_fusion.1.side_ref, bf16[4,4,64,256]{3,2,1,0:T(8,128)(2,1)S(1)} %get-tuple-element.65.refs_0_, s32[1,4096]{1,0:T(1,128)S(1)} %bitcast.13, bf16[8,128,512]{2,1,0:T(8,128)(2,1)S(1)} %copy-done.1, ...), custom_call_target="tpu_custom_call" | custom-call | flops 1140850 | bytes 983 | tf_op jit(solution)/shard_map/pallas_call | solution.py:244
  21.1 0.5 collective-permute-start.5
  21.7 1.6 %collective-permute-start.8 = (bf16[128,1024]{1,0:T(8,128)(2,1)S(1)}, bf16[128,1024]{1,0:T(8,128)(2,1)S(1)}, u32[]{:S(2)}, u32[]{:S(2)}) collective-permute-start(bf16[128,1024]{1,0:T(8,128)(2,1)S(1)} %get-tuple-element.76.mine_ref), channel_id=1, source_target_pairs={{0,8},{4,12},{8,0},{12,4},{16,24},{20,28},{24,16},{28,20},{1,9},{5... | collective-permute-start | bytes 786440 | tf_op jit(solution)/shard_map/ppermute | solution.py:506
  23.4 1.8 %collective-permute-done.6.refs_3_ = bf16[4,32,256]{2,1,0:T(8,128)(2,1)S(1)} collective-permute-done((bf16[4,32,256]{2,1,0:T(8,128)(2,1)S(1)}, bf16[4,32,256]{2,1,0:T(8,128)(2,1)S(1)}, u32[]{:S(2)}, u32[]{:S(2)}) %collective-permute-start.6) | collective-permute-done | bytes 65568 | tf_op jit(solution)/shard_map/ppermute | solution.py:506
  25.2 1.6 %collective-permute-done.4.refs_1_ = bf16[4,32,256]{2,1,0:T(8,128)(2,1)S(1)} collective-permute-done((bf16[4,32,256]{2,1,0:T(8,128)(2,1)S(1)}, bf16[4,32,256]{2,1,0:T(8,128)(2,1)S(1)}, u32[]{:S(2)}, u32[]{:S(2)}) %collective-permute-start.4) | collective-permute-done | bytes 65568 | tf_op jit(solution)/shard_map/ppermute | solution.py:506
  26.8 1.8 %collective-permute-start.15 = (bf16[128,1024]{1,0:T(8,128)(2,1)S(1)}, bf16[128,1024]{1,0:T(8,128)(2,1)S(1)}, u32[]{:S(2)}, u32[]{:S(2)}) collective-permute-start(bf16[128,1024]{1,0:T(8,128)(2,1)S(1)} %get-tuple-element.86.refs_4_.refs_6_), channel_id=1, source_target_pairs={{0,2},{1,3},{2,0},{3,1},{4,6},{5,7},{6,4},{7,5},{8,10},{9,11},{10,... | collective-permute-start | bytes 786440 | tf_op jit(solution)/shard_map/ppermute | solution.py:506
  28.6 0.2 collective-permute-start.10
  28.9 0.4 collective-permute-start.11
  29.2 0.8 %collective-permute-done.8.other_ref = bf16[128,1024]{1,0:T(8,128)(2,1)S(1)} collective-permute-done((bf16[128,1024]{1,0:T(8,128)(2,1)S(1)}, bf16[128,1024]{1,0:T(8,128)(2,1)S(1)}, u32[]{:S(2)}, u32[]{:S(2)}) %collective-permute-start.8) | collective-permute-done | bytes 262176 | tf_op jit(solution)/shard_map/ppermute | solution.py:506
  30.1 0.3 collective-permute-done.11.refs_8_
  30.4 1.1 %collective-permute-done.12.refs_9_ = bf16[128,768]{1,0:T(8,128)(2,1)S(1)} collective-permute-done((bf16[128,768]{1,0:T(8,128)(2,1)S(1)}, bf16[128,768]{1,0:T(8,128)(2,1)S(1)}, u32[]{:S(2)}, u32[]{:S(2)}) %collective-permute-start.12) | collective-permute-done | bytes 196640 | tf_op jit(solution)/shard_map/ppermute | solution.py:506
  31.5 1.5 %shard_map.87 = (f32[3,4,32,128]{3,2,1,0:T(8,128)S(1)}, bf16[32,256]{1,0:T(8,128)(2,1)S(1)}) custom-call(bf16[4,32,256]{2,1,0:T(8,128)(2,1)S(1)} %get-tuple-element.79.refs_0_, bf16[4,32,256]{2,1,0:T(8,128)(2,1)S(1)} %collective-permute-done.4.refs_1_, bf16[4,32,256]{2,1,0:T(8,128)(2,1)S(1)} %collective-permute-done.5.refs_2_, ...), custom_call_target="tpu_custom_call" | custom-call | flops 75497 | bytes 3145 | tf_op jit(solution)/shard_map/pallas_call | solution.py:313
  33.0 0.8 %collective-permute-start.14 = (bf16[32,256]{1,0:T(8,128)(2,1)S(1)}, bf16[32,256]{1,0:T(8,128)(2,1)S(1)}, u32[]{:S(2)}, u32[]{:S(2)}) collective-permute-start(bf16[32,256]{1,0:T(8,128)(2,1)S(1)} %get-tuple-element.87.mine_ref), channel_id=1, source_target_pairs={{0,2},{1,3},{2,0},{3,1},{4,6},{5,7},{6,4},{7,5},{8,10},{9,11},{10,... | collective-permute-start | bytes 49160 | tf_op jit(solution)/shard_map/ppermute | solution.py:506
  33.8 1.7 %collective-permute-done.15.refs_5_.refs_7_ = bf16[128,1024]{1,0:T(8,128)(2,1)S(1)} collective-permute-done((bf16[128,1024]{1,0:T(8,128)(2,1)S(1)}, bf16[128,1024]{1,0:T(8,128)(2,1)S(1)}, u32[]{:S(2)}, u32[]{:S(2)}) %collective-permute-start.15) | collective-permute-done | bytes 262176 | tf_op jit(solution)/shard_map/ppermute | solution.py:506
  35.5 1.3 %collective-permute-done.14.other_ref.refs_1_ = bf16[32,256]{1,0:T(8,128)(2,1)S(1)} collective-permute-done((bf16[32,256]{1,0:T(8,128)(2,1)S(1)}, bf16[32,256]{1,0:T(8,128)(2,1)S(1)}, u32[]{:S(2)}, u32[]{:S(2)}) %collective-permute-start.14) | collective-permute-done | bytes 16416 | tf_op jit(solution)/shard_map/ppermute | solution.py:506
  36.8 0.9 %collective-permute-start.22 = (bf16[128,1024]{1,0:T(8,128)(2,1)S(1)}, bf16[128,1024]{1,0:T(8,128)(2,1)S(1)}, u32[]{:S(2)}, u32[]{:S(2)}) collective-permute-start(bf16[128,1024]{1,0:T(8,128)(2,1)S(1)} %shard_map.91), channel_id=1, source_target_pairs={{0,2},{1,3},{2,0},{3,1},{4,6},{5,7},{6,4},{7,5},{8,10},{9,11},{10,... | collective-permute-start | bytes 786440 | tf_op jit(solution)/shard_map/ppermute | solution.py:506
  37.7 2.6 %collective-permute-start.20 = (bf16[128,512]{1,0:T(8,128)(2,1)S(1)}, bf16[128,512]{1,0:T(8,128)(2,1)S(1)}, u32[]{:S(2)}, u32[]{:S(2)}) collective-permute-start(bf16[128,512]{1,0:T(8,128)(2,1)S(1)} %get-tuple-element.92.mine_ref), channel_id=1, source_target_pairs={{0,16},{4,20},{8,24},{12,28},{16,0},{20,4},{24,8},{28,12},{1,17},{... | collective-permute-start | bytes 393224 | tf_op jit(solution)/shard_map/ppermute | solution.py:506
  40.3 0.3 shard_map.88
  40.6 1.3 %collective-permute-start.17 = (bf16[32,256]{1,0:T(8,128)(2,1)S(1)}, bf16[32,256]{1,0:T(8,128)(2,1)S(1)}, u32[]{:S(2)}, u32[]{:S(2)}) collective-permute-start(bf16[32,256]{1,0:T(8,128)(2,1)S(1)} %get-tuple-element.94.refs_0_.refs_1_), channel_id=1, source_target_pairs={{0,2},{1,3},{2,0},{3,1},{4,6},{5,7},{6,4},{7,5},{8,10},{9,11},{10,... | collective-permute-start | bytes 49160 | tf_op jit(solution)/shard_map/ppermute | solution.py:506
  41.9 0.8 %collective-permute-start.18 = (bf16[32,256]{1,0:T(8,128)(2,1)S(1)}, bf16[32,256]{1,0:T(8,128)(2,1)S(1)}, u32[]{:S(2)}, u32[]{:S(2)}) collective-permute-start(bf16[32,256]{1,0:T(8,128)(2,1)S(1)} %get-tuple-element.94.refs_0_.refs_1_), channel_id=1, source_target_pairs={{0,4},{4,0},{8,12},{12,8},{16,20},{20,16},{24,28},{28,24},{1,5},{5... | collective-permute-start | bytes 49160 | tf_op jit(solution)/shard_map/ppermute | solution.py:506
  42.7 1.4 %collective-permute-start.19 = (bf16[32,256]{1,0:T(8,128)(2,1)S(1)}, bf16[32,256]{1,0:T(8,128)(2,1)S(1)}, u32[]{:S(2)}, u32[]{:S(2)}) collective-permute-start(bf16[32,256]{1,0:T(8,128)(2,1)S(1)} %get-tuple-element.94.refs_0_.refs_1_), channel_id=1, source_target_pairs={{0,6},{1,7},{2,4},{3,5},{4,2},{5,3},{6,0},{7,1},{8,14},{9,15},{10,... | collective-permute-start | bytes 49160 | tf_op jit(solution)/shard_map/ppermute | solution.py:513
  44.1 2.9 %collective-permute-done.20.other_ref = bf16[128,512]{1,0:T(8,128)(2,1)S(1)} collective-permute-done((bf16[128,512]{1,0:T(8,128)(2,1)S(1)}, bf16[128,512]{1,0:T(8,128)(2,1)S(1)}, u32[]{:S(2)}, u32[]{:S(2)}) %collective-permute-start.20) | collective-permute-done | bytes 131104 | tf_op jit(solution)/shard_map/ppermute | solution.py:506
  47.0 0.3 collective-permute-done.19.refs_3_
  47.4 0.6 shard_map.90
  48.1 0.5 collective-permute-start.23
  48.6 1.5 %collective-permute-start.28 = (bf16[128,768]{1,0:T(8,128)(2,1)S(1)}, bf16[128,768]{1,0:T(8,128)(2,1)S(1)}, u32[]{:S(2)}, u32[]{:S(2)}) collective-permute-start(bf16[128,768]{1,0:T(8,128)(2,1)S(1)} %shard_map.97), channel_id=1, source_target_pairs={{0,2},{1,3},{2,0},{3,1},{4,6},{5,7},{6,4},{7,5},{8,10},{9,11},{10,... | collective-permute-start | bytes 589832 | tf_op jit(solution)/shard_map/ppermute | solution.py:506
  50.2 0.6 collective-permute-start.26
  50.8 1.6 %collective-permute-start.21 = (bf16[32,256]{1,0:T(8,128)(2,1)S(1)}, bf16[32,256]{1,0:T(8,128)(2,1)S(1)}, u32[]{:S(2)}, u32[]{:S(2)}) collective-permute-start(bf16[32,256]{1,0:T(8,128)(2,1)S(1)} %get-tuple-element.98.refs_1_.refs_0_), channel_id=1, source_target_pairs={{0,8},{4,12},{8,0},{12,4},{16,24},{20,28},{24,16},{28,20},{1,9},{5... | collective-permute-start | bytes 49160 | tf_op jit(solution)/shard_map/ppermute | solution.py:506
  52.4 2.2 %collective-permute-done.21.refs_1_ = bf16[32,256]{1,0:T(8,128)(2,1)S(1)} collective-permute-done((bf16[32,256]{1,0:T(8,128)(2,1)S(1)}, bf16[32,256]{1,0:T(8,128)(2,1)S(1)}, u32[]{:S(2)}, u32[]{:S(2)}) %collective-permute-start.21) | collective-permute-done | bytes 16416 | tf_op jit(solution)/shard_map/ppermute | solution.py:506
  54.5 0.6 shard_map.94
  55.1 1.3 %collective-permute-done.28.refs_0_.refs_16_ = bf16[128,768]{1,0:T(8,128)(2,1)S(1)} collective-permute-done((bf16[128,768]{1,0:T(8,128)(2,1)S(1)}, bf16[128,768]{1,0:T(8,128)(2,1)S(1)}, u32[]{:S(2)}, u32[]{:S(2)}) %collective-permute-start.28) | collective-permute-done | bytes 196640 | tf_op jit(solution)/shard_map/ppermute | solution.py:506
  56.5 1.9 %collective-permute-start.25 = (bf16[32,256]{1,0:T(8,128)(2,1)S(1)}, bf16[32,256]{1,0:T(8,128)(2,1)S(1)}, u32[]{:S(2)}, u32[]{:S(2)}) collective-permute-start(bf16[32,256]{1,0:T(8,128)(2,1)S(1)} %get-tuple-element.99.refs_1_.refs_0_), channel_id=1, source_target_pairs={{0,16},{4,20},{8,24},{12,28},{16,0},{20,4},{24,8},{28,12},{1,17},{... | collective-permute-start | bytes 49160 | tf_op jit(solution)/shard_map/ppermute | solution.py:506
  58.4 2.8 %collective-permute-done.25._.refs_1_ = bf16[32,256]{1,0:T(8,128)(2,1)S(1)} collective-permute-done((bf16[32,256]{1,0:T(8,128)(2,1)S(1)}, bf16[32,256]{1,0:T(8,128)(2,1)S(1)}, u32[]{:S(2)}, u32[]{:S(2)}) %collective-permute-start.25) | collective-permute-done | bytes 16416 | tf_op jit(solution)/shard_map/ppermute | solution.py:506
  61.3 1.3 %collective-permute-done.27.refs_15_ = bf16[128,512]{1,0:T(8,128)(2,1)S(1)} collective-permute-done((bf16[128,512]{1,0:T(8,128)(2,1)S(1)}, bf16[128,512]{1,0:T(8,128)(2,1)S(1)}, u32[]{:S(2)}, u32[]{:S(2)}) %collective-permute-start.27) | collective-permute-done | bytes 131104 | tf_op jit(solution)/shard_map/ppermute | solution.py:506
  62.7 1.1 %shard_map.99 = bf16[4,32,256]{2,1,0:T(8,128)(2,1)S(1)} custom-call(bf16[32,256]{1,0:T(8,128)(2,1)S(1)} %get-tuple-element.99.refs_1_.refs_0_, bf16[32,256]{1,0:T(8,128)(2,1)S(1)} %collective-permute-done.25._.refs_1_, f32[4,32,128]{2,1,0:T(8,128)S(1)} %get-tuple-element.100.refs_2_, f32[4,32,128]{2,1,0:T(8,128)S(1)} %get-tuple-element.101.refs_3_, ...), custom_call_target="tpu_custom_call" | custom-call | flops 67108 | bytes 4194 | tf_op jit(solution)/shard_map/pallas_call | solution.py:474
  63.7 5.8 %all-gather = bf16[16,32,256]{2,1,0:T(8,128)(2,1)S(1)} all-gather(bf16[4,32,256]{2,1,0:T(8,128)(2,1)S(1)} %shard_map.99), channel_id=2, replica_groups=mesh['leaf'=8,'rhs'=4] {'rhs'}, dimensions={0}, use_global_device_ids=true | all-gather | bytes 327680 | tf_op jit(solution)/shard_map/all_gather | solution.py:616
  69.5 1.0 %shard_map.100 = f32[8,64,128]{2,1,0:T(8,128)} custom-call(f32[4,64,128]{2,1,0:T(8,128)S(1)} %get-tuple-element.59.far_ref, f32[4,64,128]{2,1,0:T(8,128)S(1)} %get-tuple-element.66.own_ref, bf16[4,4,32,256]{3,2,1,0:T(8,128)(2,1)S(1)} %bitcast.11, bf16[8,128,256]{2,1,0:T(8,128)(2,1)S(1)} %copy-done.3), custom_call_target="tpu_custom_call" | custom-call | flops 33554 | bytes 524 | tf_op jit(solution)/shard_map/pallas_call | solution.py:497
  (51 shorter events, 0.7 us)
Async XLA Ops:
  0.0 11.6 %copy-start.2 = (bf16[8,128,256]{2,1,0:T(8,128)(2,1)S(1)}, bf16[8,128,256]{2,1,0:T(8,128)(2,1)}, u32[]{:S(2)}) copy-start(bf16[8,128,256]{2,1,0:T(8,128)(2,1)} %refs_3_.1) | copy-start | bytes 1572868
  0.0 6.6 %collective-permute-start = (bf16[64,1024]{1,0:T(8,128)(2,1)}, bf16[64,1024]{1,0:T(8,128)(2,1)S(1)}, u32[]{:S(2)}, u32[]{:S(2)}) collective-permute-start(bf16[64,1024]{1,0:T(8,128)(2,1)} %refs_0_.1), channel_id=1, source_target_pairs={{0,2},{1,3},{2,0},{3,1},{4,6},{5,7},{6,4},{7,5},{8,10},{9,11},{10,... | collective-permute-start | bytes 393224 | tf_op jit(solution)/shard_map/ppermute | solution.py:506
  2.9 3.7 %collective-permute-start.1 = (bf16[64,1024]{1,0:T(8,128)(2,1)}, bf16[64,1024]{1,0:T(8,128)(2,1)S(1)}, u32[]{:S(2)}, u32[]{:S(2)}) collective-permute-start(bf16[64,1024]{1,0:T(8,128)(2,1)} %refs_0_.1), channel_id=1, source_target_pairs={{0,1},{1,0},{2,3},{3,2},{4,5},{5,4},{6,7},{7,6},{8,9},{9,8},{10,11... | collective-permute-start | bytes 393224 | tf_op jit(solution)/shard_map/ppermute | solution.py:506
  2.9 8.6 %copy-start.6 = (bf16[64,1024]{1,0:T(8,128)(2,1)S(1)}, bf16[64,1024]{1,0:T(8,128)(2,1)}, u32[]{:S(2)}) copy-start(bf16[64,1024]{1,0:T(8,128)(2,1)} %refs_0_.1) | copy-start | bytes 393220
  6.6 1.3 %collective-permute-start.2 = (bf16[64,1024]{1,0:T(8,128)(2,1)S(1)}, bf16[64,1024]{1,0:T(8,128)(2,1)S(1)}, u32[]{:S(2)}, u32[]{:S(2)}) collective-permute-start(bf16[64,1024]{1,0:T(8,128)(2,1)S(1)} %collective-permute-done.refs_1_), channel_id=1, source_target_pairs={{0,1},{1,0},{2,3},{3,2},{4,5},{5,4},{6,7},{7,6},{8,9},{9,8},{10,11... | collective-permute-start | bytes 393224 | tf_op jit(solution)/shard_map/ppermute | solution.py:506
  8.0 9.7 %collective-permute-start.3 = (bf16[4,128,1024]{2,1,0:T(8,128)(2,1)}, bf16[4,128,1024]{2,1,0:T(8,128)(2,1)S(1)}, u32[]{:S(2)}, u32[]{:S(2)}) collective-permute-start(bf16[4,128,1024]{2,1,0:T(8,128)(2,1)} %get-tuple-element.62.refs_4_.own_ref.refs_18_), channel_id=1, source_target_pairs={{0,1},{1,0},{2,3},{3,2},{4,5},{5,4},{6,7},{7,6},{8,9},{9,8},{10,11... | collective-permute-start | bytes 3145736 | tf_op jit(solution)/shard_map/ppermute | solution.py:506
  8.1 18.6 %collective-permute-start.9 = (bf16[3,128,768]{2,1,0:T(8,128)(2,1)}, bf16[3,128,768]{2,1,0:T(8,128)(2,1)S(1)}, u32[]{:S(2)}, u32[]{:S(2)}) collective-permute-start(bf16[3,128,768]{2,1,0:T(8,128)(2,1)} %get-tuple-element.55), channel_id=1, source_target_pairs={{0,2},{1,3},{2,0},{3,1},{4,6},{5,7},{6,4},{7,5},{8,10},{9,11},{10,... | collective-permute-start | bytes 1769480 | tf_op jit(solution)/shard_map/ppermute | solution.py:506
  9.9 1.7 %copy-start.7 = (s32[4096]{0:T(1024)S(1)}, s32[4096]{0:T(1024)}, u32[]{:S(2)}) copy-start(s32[4096]{0:T(1024)} %param.9) | copy-start | bytes 49156
  9.9 11.7 %collective-permute-start.7 = (bf16[128,1024]{1,0:T(8,128)(2,1)}, bf16[128,1024]{1,0:T(8,128)(2,1)S(1)}, u32[]{:S(2)}, u32[]{:S(2)}) collective-permute-start(bf16[128,1024]{1,0:T(8,128)(2,1)} %get-tuple-element.73.mine_ref), channel_id=1, source_target_pairs={{0,4},{4,0},{8,12},{12,8},{16,20},{20,16},{24,28},{28,24},{1,5},{5... | collective-permute-start | bytes 786440 | tf_op jit(solution)/shard_map/ppermute | solution.py:506
  11.6 1.2 %copy-start.1 = (bf16[8,128,512]{2,1,0:T(8,128)(2,1)S(1)}, bf16[8,128,512]{2,1,0:T(8,128)(2,1)}, u32[]{:S(2)}) copy-start(bf16[8,128,512]{2,1,0:T(8,128)(2,1)} %refs_2_.1) | copy-start | bytes 3145732
  16.2 8.9 %collective-permute-start.6 = (bf16[4,32,256]{2,1,0:T(8,128)(2,1)S(1)}, bf16[4,32,256]{2,1,0:T(8,128)(2,1)S(1)}, u32[]{:S(2)}, u32[]{:S(2)}) collective-permute-start(bf16[4,32,256]{2,1,0:T(8,128)(2,1)S(1)} %get-tuple-element.70), channel_id=1, source_target_pairs={{0,3},{1,2},{2,1},{3,0},{4,7},{5,6},{6,5},{7,4},{8,11},{9,10},{10,... | collective-permute-start | bytes 196616 | tf_op jit(solution)/shard_map/ppermute | solution.py:506
  16.3 10.4 %collective-permute-start.4 = (bf16[4,32,256]{2,1,0:T(8,128)(2,1)S(1)}, bf16[4,32,256]{2,1,0:T(8,128)(2,1)S(1)}, u32[]{:S(2)}, u32[]{:S(2)}) collective-permute-start(bf16[4,32,256]{2,1,0:T(8,128)(2,1)S(1)} %get-tuple-element.63), channel_id=1, source_target_pairs={{0,2},{1,3},{2,0},{3,1},{4,6},{5,7},{6,4},{7,5},{8,10},{9,11},{10,... | collective-permute-start | bytes 196616 | tf_op jit(solution)/shard_map/ppermute | solution.py:506
  17.7 3.9 %copy-start.4 = (bf16[128,1024]{1,0:T(8,128)(2,1)S(1)}, bf16[128,1024]{1,0:T(8,128)(2,1)}, u32[]{:S(2)}) copy-start(bf16[128,1024]{1,0:T(8,128)(2,1)} %get-tuple-element.73.mine_ref) | copy-start | bytes 786436
  17.7 3.9 %copy-start.5 = (bf16[128,768]{1,0:T(8,128)(2,1)S(1)}, bf16[128,768]{1,0:T(8,128)(2,1)}, u32[]{:S(2)}) copy-start(bf16[128,768]{1,0:T(8,128)(2,1)} %get-tuple-element.75.refs_0_) | copy-start | bytes 589828
  21.1 5.7 %collective-permute-start.5 = (bf16[4,32,256]{2,1,0:T(8,128)(2,1)S(1)}, bf16[4,32,256]{2,1,0:T(8,128)(2,1)S(1)}, u32[]{:S(2)}, u32[]{:S(2)}) collective-permute-start(bf16[4,32,256]{2,1,0:T(8,128)(2,1)S(1)} %get-tuple-element.69), channel_id=1, source_target_pairs={{0,1},{1,0},{2,3},{3,2},{4,5},{5,4},{6,7},{7,6},{8,9},{9,8},{10,11... | collective-permute-start | bytes 196616 | tf_op jit(solution)/shard_map/ppermute | solution.py:506
  21.6 9.8 %copy-start = (bf16[4,128,1024]{2,1,0:T(8,128)(2,1)S(1)}, bf16[4,128,1024]{2,1,0:T(8,128)(2,1)}, u32[]{:S(2)}) copy-start(bf16[4,128,1024]{2,1,0:T(8,128)(2,1)} %get-tuple-element.62.refs_4_.own_ref.refs_18_) | copy-start | bytes 3145732
  21.7 8.3 %collective-permute-start.8 = (bf16[128,1024]{1,0:T(8,128)(2,1)S(1)}, bf16[128,1024]{1,0:T(8,128)(2,1)S(1)}, u32[]{:S(2)}, u32[]{:S(2)}) collective-permute-start(bf16[128,1024]{1,0:T(8,128)(2,1)S(1)} %get-tuple-element.76.mine_ref), channel_id=1, source_target_pairs={{0,8},{4,12},{8,0},{12,4},{16,24},{20,28},{24,16},{28,20},{1,9},{5... | collective-permute-start | bytes 786440 | tf_op jit(solution)/shard_map/ppermute | solution.py:506
  26.8 6.2 %collective-permute-start.13 = (bf16[128,1024]{1,0:T(8,128)(2,1)S(1)}, bf16[128,1024]{1,0:T(8,128)(2,1)S(1)}, u32[]{:S(2)}, u32[]{:S(2)}) collective-permute-start(bf16[128,1024]{1,0:T(8,128)(2,1)S(1)} %get-tuple-element.86.refs_4_.refs_6_), channel_id=1, source_target_pairs={{0,1},{1,0},{2,3},{3,2},{4,5},{5,4},{6,7},{7,6},{8,9},{9,8},{10,11... | collective-permute-start | bytes 786440 | tf_op jit(solution)/shard_map/ppermute | solution.py:506
  26.8 8.7 %collective-permute-start.15 = (bf16[128,1024]{1,0:T(8,128)(2,1)S(1)}, bf16[128,1024]{1,0:T(8,128)(2,1)S(1)}, u32[]{:S(2)}, u32[]{:S(2)}) collective-permute-start(bf16[128,1024]{1,0:T(8,128)(2,1)S(1)} %get-tuple-element.86.refs_4_.refs_6_), channel_id=1, source_target_pairs={{0,2},{1,3},{2,0},{3,1},{4,6},{5,7},{6,4},{7,5},{8,10},{9,11},{10,... | collective-permute-start | bytes 786440 | tf_op jit(solution)/shard_map/ppermute | solution.py:506
  28.6 1.5 %collective-permute-start.10 = (bf16[128,768]{1,0:T(8,128)(2,1)S(1)}, bf16[128,768]{1,0:T(8,128)(2,1)S(1)}, u32[]{:S(2)}, u32[]{:S(2)}) collective-permute-start(bf16[128,768]{1,0:T(8,128)(2,1)S(1)} %get-tuple-element.107), channel_id=1, source_target_pairs={{0,1},{1,0},{2,3},{3,2},{4,5},{5,4},{6,7},{7,6},{8,9},{9,8},{10,11... | collective-permute-start | bytes 589832 | tf_op jit(solution)/shard_map/ppermute | solution.py:506
  28.9 1.6 %collective-permute-start.11 = (bf16[128,768]{1,0:T(8,128)(2,1)S(1)}, bf16[128,768]{1,0:T(8,128)(2,1)S(1)}, u32[]{:S(2)}, u32[]{:S(2)}) collective-permute-start(bf16[128,768]{1,0:T(8,128)(2,1)S(1)} %get-tuple-element.106), channel_id=1, source_target_pairs={{0,1},{1,0},{2,3},{3,2},{4,5},{5,4},{6,7},{7,6},{8,9},{9,8},{10,11... | collective-permute-start | bytes 589832 | tf_op jit(solution)/shard_map/ppermute | solution.py:506
  30.1 1.4 %collective-permute-start.12 = (bf16[128,768]{1,0:T(8,128)(2,1)S(1)}, bf16[128,768]{1,0:T(8,128)(2,1)S(1)}, u32[]{:S(2)}, u32[]{:S(2)}) collective-permute-start(bf16[128,768]{1,0:T(8,128)(2,1)S(1)} %get-tuple-element.105), channel_id=1, source_target_pairs={{0,1},{1,0},{2,3},{3,2},{4,5},{5,4},{6,7},{7,6},{8,9},{9,8},{10,11... | collective-permute-start | bytes 589832 | tf_op jit(solution)/shard_map/ppermute | solution.py:506
  33.0 3.8 %collective-permute-start.14 = (bf16[32,256]{1,0:T(8,128)(2,1)S(1)}, bf16[32,256]{1,0:T(8,128)(2,1)S(1)}, u32[]{:S(2)}, u32[]{:S(2)}) collective-permute-start(bf16[32,256]{1,0:T(8,128)(2,1)S(1)} %get-tuple-element.87.mine_ref), channel_id=1, source_target_pairs={{0,2},{1,3},{2,0},{3,1},{4,6},{5,7},{6,4},{7,5},{8,10},{9,11},{10,... | collective-permute-start | bytes 49160 | tf_op jit(solution)/shard_map/ppermute | solution.py:506
  36.8 3.8 %collective-permute-start.16 = (bf16[128,1024]{1,0:T(8,128)(2,1)S(1)}, bf16[128,1024]{1,0:T(8,128)(2,1)S(1)}, u32[]{:S(2)}, u32[]{:S(2)}) collective-permute-start(bf16[128,1024]{1,0:T(8,128)(2,1)S(1)} %collective-permute-done.15.refs_5_.refs_7_), channel_id=1, source_target_pairs={{0,1},{1,0},{2,3},{3,2},{4,5},{5,4},{6,7},{7,6},{8,9},{9,8},{10,11... | collective-permute-start | bytes 786440 | tf_op jit(solution)/shard_map/ppermute | solution.py:506
  36.8 11.2 %collective-permute-start.22 = (bf16[128,1024]{1,0:T(8,128)(2,1)S(1)}, bf16[128,1024]{1,0:T(8,128)(2,1)S(1)}, u32[]{:S(2)}, u32[]{:S(2)}) collective-permute-start(bf16[128,1024]{1,0:T(8,128)(2,1)S(1)} %shard_map.91), channel_id=1, source_target_pairs={{0,2},{1,3},{2,0},{3,1},{4,6},{5,7},{6,4},{7,5},{8,10},{9,11},{10,... | collective-permute-start | bytes 786440 | tf_op jit(solution)/shard_map/ppermute | solution.py:506
  37.7 9.3 %collective-permute-start.20 = (bf16[128,512]{1,0:T(8,128)(2,1)S(1)}, bf16[128,512]{1,0:T(8,128)(2,1)S(1)}, u32[]{:S(2)}, u32[]{:S(2)}) collective-permute-start(bf16[128,512]{1,0:T(8,128)(2,1)S(1)} %get-tuple-element.92.mine_ref), channel_id=1, source_target_pairs={{0,16},{4,20},{8,24},{12,28},{16,0},{20,4},{24,8},{28,12},{1,17},{... | collective-permute-start | bytes 393224 | tf_op jit(solution)/shard_map/ppermute | solution.py:506
  40.6 6.4 %collective-permute-start.17 = (bf16[32,256]{1,0:T(8,128)(2,1)S(1)}, bf16[32,256]{1,0:T(8,128)(2,1)S(1)}, u32[]{:S(2)}, u32[]{:S(2)}) collective-permute-start(bf16[32,256]{1,0:T(8,128)(2,1)S(1)} %get-tuple-element.94.refs_0_.refs_1_), channel_id=1, source_target_pairs={{0,2},{1,3},{2,0},{3,1},{4,6},{5,7},{6,4},{7,5},{8,10},{9,11},{10,... | collective-permute-start | bytes 49160 | tf_op jit(solution)/shard_map/ppermute | solution.py:506
  41.9 5.2 %collective-permute-start.18 = (bf16[32,256]{1,0:T(8,128)(2,1)S(1)}, bf16[32,256]{1,0:T(8,128)(2,1)S(1)}, u32[]{:S(2)}, u32[]{:S(2)}) collective-permute-start(bf16[32,256]{1,0:T(8,128)(2,1)S(1)} %get-tuple-element.94.refs_0_.refs_1_), channel_id=1, source_target_pairs={{0,4},{4,0},{8,12},{12,8},{16,20},{20,16},{24,28},{28,24},{1,5},{5... | collective-permute-start | bytes 49160 | tf_op jit(solution)/shard_map/ppermute | solution.py:506
  42.7 4.6 %collective-permute-start.19 = (bf16[32,256]{1,0:T(8,128)(2,1)S(1)}, bf16[32,256]{1,0:T(8,128)(2,1)S(1)}, u32[]{:S(2)}, u32[]{:S(2)}) collective-permute-start(bf16[32,256]{1,0:T(8,128)(2,1)S(1)} %get-tuple-element.94.refs_0_.refs_1_), channel_id=1, source_target_pairs={{0,6},{1,7},{2,4},{3,5},{4,2},{5,3},{6,0},{7,1},{8,14},{9,15},{10,... | collective-permute-start | bytes 49160 | tf_op jit(solution)/shard_map/ppermute | solution.py:513
  48.0 6.5 %collective-permute-start.24 = (bf16[128,1024]{1,0:T(8,128)(2,1)S(1)}, bf16[128,1024]{1,0:T(8,128)(2,1)S(1)}, u32[]{:S(2)}, u32[]{:S(2)}) collective-permute-start(bf16[128,1024]{1,0:T(8,128)(2,1)S(1)} %shard_map.93), channel_id=1, source_target_pairs={{0,1},{1,0},{2,3},{3,2},{4,5},{5,4},{6,7},{7,6},{8,9},{9,8},{10,11... | collective-permute-start | bytes 786440 | tf_op jit(solution)/shard_map/ppermute | solution.py:506
  48.1 6.4 %collective-permute-start.23 = (bf16[128,1024]{1,0:T(8,128)(2,1)S(1)}, bf16[128,1024]{1,0:T(8,128)(2,1)S(1)}, u32[]{:S(2)}, u32[]{:S(2)}) collective-permute-start(bf16[128,1024]{1,0:T(8,128)(2,1)S(1)} %shard_map.92), channel_id=1, source_target_pairs={{0,1},{1,0},{2,3},{3,2},{4,5},{5,4},{6,7},{7,6},{8,9},{9,8},{10,11... | collective-permute-start | bytes 786440 | tf_op jit(solution)/shard_map/ppermute | solution.py:506
  48.6 7.8 %collective-permute-start.28 = (bf16[128,768]{1,0:T(8,128)(2,1)S(1)}, bf16[128,768]{1,0:T(8,128)(2,1)S(1)}, u32[]{:S(2)}, u32[]{:S(2)}) collective-permute-start(bf16[128,768]{1,0:T(8,128)(2,1)S(1)} %shard_map.97), channel_id=1, source_target_pairs={{0,2},{1,3},{2,0},{3,1},{4,6},{5,7},{6,4},{7,5},{8,10},{9,11},{10,... | collective-permute-start | bytes 589832 | tf_op jit(solution)/shard_map/ppermute | solution.py:506
  50.2 8.2 %collective-permute-start.26 = (bf16[128,512]{1,0:T(8,128)(2,1)S(1)}, bf16[128,512]{1,0:T(8,128)(2,1)S(1)}, u32[]{:S(2)}, u32[]{:S(2)}) collective-permute-start(bf16[128,512]{1,0:T(8,128)(2,1)S(1)} %shard_map.95), channel_id=1, source_target_pairs={{0,2},{1,3},{2,0},{3,1},{4,6},{5,7},{6,4},{7,5},{8,10},{9,11},{10,... | collective-permute-start | bytes 393224 | tf_op jit(solution)/shard_map/ppermute | solution.py:506
  50.8 3.7 %collective-permute-start.21 = (bf16[32,256]{1,0:T(8,128)(2,1)S(1)}, bf16[32,256]{1,0:T(8,128)(2,1)S(1)}, u32[]{:S(2)}, u32[]{:S(2)}) collective-permute-start(bf16[32,256]{1,0:T(8,128)(2,1)S(1)} %get-tuple-element.98.refs_1_.refs_0_), channel_id=1, source_target_pairs={{0,8},{4,12},{8,0},{12,4},{16,24},{20,28},{24,16},{28,20},{1,9},{5... | collective-permute-start | bytes 49160 | tf_op jit(solution)/shard_map/ppermute | solution.py:506
  56.5 6.2 %collective-permute-start.29 = (bf16[128,768]{1,0:T(8,128)(2,1)S(1)}, bf16[128,768]{1,0:T(8,128)(2,1)S(1)}, u32[]{:S(2)}, u32[]{:S(2)}) collective-permute-start(bf16[128,768]{1,0:T(8,128)(2,1)S(1)} %shard_map.98), channel_id=1, source_target_pairs={{0,1},{1,0},{2,3},{3,2},{4,5},{5,4},{6,7},{7,6},{8,9},{9,8},{10,11... | collective-permute-start | bytes 589832 | tf_op jit(solution)/shard_map/ppermute | solution.py:506
  56.5 4.7 %collective-permute-start.25 = (bf16[32,256]{1,0:T(8,128)(2,1)S(1)}, bf16[32,256]{1,0:T(8,128)(2,1)S(1)}, u32[]{:S(2)}, u32[]{:S(2)}) collective-permute-start(bf16[32,256]{1,0:T(8,128)(2,1)S(1)} %get-tuple-element.99.refs_1_.refs_0_), channel_id=1, source_target_pairs={{0,16},{4,20},{8,24},{12,28},{16,0},{20,4},{24,8},{28,12},{1,17},{... | collective-permute-start | bytes 49160 | tf_op jit(solution)/shard_map/ppermute | solution.py:506
  61.3 1.4 %collective-permute-start.27 = (bf16[128,512]{1,0:T(8,128)(2,1)S(1)}, bf16[128,512]{1,0:T(8,128)(2,1)S(1)}, u32[]{:S(2)}, u32[]{:S(2)}) collective-permute-start(bf16[128,512]{1,0:T(8,128)(2,1)S(1)} %shard_map.96.refs_14_), channel_id=1, source_target_pairs={{0,1},{1,0},{2,3},{3,2},{4,5},{5,4},{6,7},{7,6},{8,9},{9,8},{10,11... | collective-permute-start | bytes 393224 | tf_op jit(solution)/shard_map/ppermute | solution.py:506
  62.7 6.9 %copy-start.3 = (bf16[8,128,256]{2,1,0:T(8,128)(2,1)S(1)}, bf16[8,128,256]{2,1,0:T(8,128)(2,1)}, u32[]{:S(2)}) copy-start(bf16[8,128,256]{2,1,0:T(8,128)(2,1)} %coupling_ref.1) | copy-start | bytes 1572868

commit v6 on v4

--- a/solution.py
+++ b/solution.py
@@ -364,6 +364,7 @@
 
 def cross_pair(level, refs):
     half = len(refs) // 2
+    refs = refs[::-1] if half > 1 else refs
     is_right = (lax.axis_index("leaf") // (1 << level)) % 2 == 1
     return order_pair(is_right, total_of(refs[:half]), total_of(refs[half:]))
 
@@ -425,17 +426,7 @@
     incoming = choose(half)
     for level in range(cross_levels - 2, -1, -1):
         packs = cross_packs[2 * CORES * level : 2 * CORES * (level + 1)]
-        own, far, near, far_near = packs
-        if level == 0:
-            couplings = [ref[:, columns(ref)] for ref in packs]
-        else:
-            start = node_size + (total + level - 1) * rank
-            couplings = [
-                own[:, columns(own)],
-                tail[:, start : start + rank],
-                near[:, columns(near)],
-                near_tail[:, start : start + rank],
-            ]
+        couplings = [ref[:, columns(ref)] for ref in packs]
         for flip, coupling in zip(PIECES, couplings):
             piece = place ^ flip
             solved = solved_cross[level][piece]
@@ -583,15 +574,12 @@
     fars[0] = after(fars[0], other)
     near_far = swap(fars[0], "rhs", 1)
     cross_packs = [[ancestors[0], fars[0], own_near, near_far]]
-    factors = [(0, node_size + rank)]
-    fars.append(swap(join([ancestors[1]], current, factors), "rhs", CORES))
+    fars.append(swap(join([ancestors[1]], current), "rhs", CORES))
     current = after(current, near_far)
-    inputs = [
-        current,
-        swap(current, "rhs", CORES),
-        swap(current, "leaf", 1),
-        far_swap(current, 1, CORES),
-    ]
+    diagonal = far_swap(current, 1, CORES)
+    beside = swap(current, "leaf", 1)
+    across = swap(current, "rhs", CORES)
+    inputs = [diagonal, beside, across, current]
 
     solved_cross = []
     for level in range(cross_levels - 1):
@@ -608,11 +596,8 @@
                 ancestor, carrier = rise(carrier, later, current)
                 ancestors.append(ancestor)
             for later in range(2, cross_levels - 1):
-                fars.append(swap(join([ancestors[later]], current, factors), "rhs", CORES))
-            blocks = [ancestors[-1], send_coupling, *ancestors[1:-1]]
-            cuts = [(0, node_size), (0, send_coupling.shape[1])]
-            cuts += [(node_size + rank, rank)] * (cross_levels - 2)
-            tail = swap(join(blocks, current, cuts), "rhs", CORES)
+                fars.append(swap(join([ancestors[later]], current), "rhs", CORES))
+            tail = swap(join([ancestors[-1], send_coupling], current), "rhs", CORES)
 
     tail = hop(cross_levels - 1, ancestors[-1], tail, inputs[1])
     others = [tail, swap(tail, "rhs", 1), keep, keep_near]

time: 69.2 us -> 68.6 us (level)
  waiting for transfers between devices: 22.4 us -> 20.7 us
  starting transfers between devices: 23.8 us -> 25.2 us
    ppermute x25, waiting for transfers between devices: 19.9 us -> 18 us  [swap(): lax.ppermute(block, axis, [(i, i ^ bit) for i in range(lax.axis_size(axis...]
    ppermute x1, starting transfers between devices: 1.33 us -> 2.34 us  [far_swap(): lax.ppermute(block, ('leaf', 'rhs'), [(i, i ^ flip) for i in range(count)])]
  transfers between devices with their start and end apart: 26 -> 26, of which waited for: 13 -> 12; matrix products, arithmetic and copies ran while one was open for 0% -> 0% of each run, Pallas kernels for 19% -> 19%
where the time goes in v6:
time: 68.6 us; the launch traced here: 68.4 us
  starting transfers between devices  25.2 us (37%)
  waiting for transfers between devices  20.7 us (30%)
  Pallas kernels  15.1 us (22%)
  blocking collectives  5.79 us (8%)
  local copies, waits for them, and re-layouts  1.25 us (2%)
    ppermute x25, starting transfers between devices, swap(): lax.ppermute(block, axis, [(i, i ^ bit) for i in range(lax.axis_size(axis...  22.9 us
    ppermute x25, waiting for transfers between devices, swap(): lax.ppermute(block, axis, [(i, i ^ bit) for i in range(lax.axis_size(axis...  18 us
    pallas_call x2, Pallas kernels, leaf_up(): pl.pallas_call(functools.partial(leaf_kernel, len(points)), grid_spec=plt...  6.81 us
    all_gather x1, blocking collectives, body(): incoming = lax.all_gather(shares, 'rhs', axis=0)  5.79 us
    pallas_call x1, Pallas kernels, pack(): pl.pallas_call(functools.partial(pack_kernel, per_dev), in_specs=[pl.Bloc...  2.99 us
    ppermute x1, waiting for transfers between devices, far_swap(): lax.ppermute(block, ('leaf', 'rhs'), [(i, i ^ flip) for i in range(count)])  2.74 us
    ppermute x1, starting transfers between devices, far_swap(): lax.ppermute(block, ('leaf', 'rhs'), [(i, i ^ flip) for i in range(count)])  2.34 us
    pallas_call x1, Pallas kernels, group_up(): pl.pallas_call(functools.partial(group_up_kernel, per_dev), out_shape=[ja...  1.48 us
  transfers between devices with their start and end apart: 26, of which 12 were waited for; matrix products, arithmetic and copies ran while one was open for 0% of the time, Pallas kernels for 19%

profile of v6, /device:TPU:0, one launch (start us, length us, event | category | flops | bytes accessed | tf_op | source)
XLA Modules:
  0.0 68.4 jit_solution(728350095837677323)
XLA Ops:
  0.0 2.9 %collective-permute-start = (bf16[64,1024]{1,0:T(8,128)(2,1)}, bf16[64,1024]{1,0:T(8,128)(2,1)S(1)}, u32[]{:S(2)}, u32[]{:S(2)}) collective-permute-start(bf16[64,1024]{1,0:T(8,128)(2,1)} %refs_0_.1), channel_id=1, source_target_pairs={{0,2},{1,3},{2,0},{3,1},{4,6},{5,7},{6,4},{7,5},{8,10},{9,11},{10,... | collective-permute-start | bytes 393224 | tf_op jit(solution)/shard_map/ppermute | solution.py:502
  2.9 3.0 %shard_map.82 = (bf16[3,128,768]{2,1,0:T(8,128)(2,1)}, bf16[128,768]{1,0:T(8,128)(2,1)}, bf16[4,128,1024]{2,1,0:T(8,128)(2,1)}, bf16[128,1024]{1,0:T(8,128)(2,1)}) custom-call(bf16[8,128,512]{2,1,0:T(8,128)(2,1)} %inverse.1, bf16[8,128,256]{2,1,0:T(8,128)(2,1)} %basis.1, bf16[8,128,256]{2,1,0:T(8,128)(2,1)} %coupling.1), custom_call_target="tpu_custom_call" | custom-call | bytes 4194 | tf_op jit(solution)/shard_map/pallas_call | solution.py:93
  5.9 0.7 %collective-permute-done.refs_1_ = bf16[64,1024]{1,0:T(8,128)(2,1)S(1)} collective-permute-done((bf16[64,1024]{1,0:T(8,128)(2,1)}, bf16[64,1024]{1,0:T(8,128)(2,1)S(1)}, u32[]{:S(2)}, u32[]{:S(2)}) %collective-permute-start) | collective-permute-done | bytes 131104 | tf_op jit(solution)/shard_map/ppermute | solution.py:502
  6.7 1.3 %collective-permute-done.2.refs_3_ = bf16[64,1024]{1,0:T(8,128)(2,1)S(1)} collective-permute-done((bf16[64,1024]{1,0:T(8,128)(2,1)S(1)}, bf16[64,1024]{1,0:T(8,128)(2,1)S(1)}, u32[]{:S(2)}, u32[]{:S(2)}) %collective-permute-start.2) | collective-permute-done | bytes 131104 | tf_op jit(solution)/shard_map/ppermute | solution.py:502
  8.0 0.1 collective-permute-start.3
  8.1 1.8 %collective-permute-start.7 = (bf16[3,128,768]{2,1,0:T(8,128)(2,1)}, bf16[3,128,768]{2,1,0:T(8,128)(2,1)S(1)}, u32[]{:S(2)}, u32[]{:S(2)}) collective-permute-start(bf16[3,128,768]{2,1,0:T(8,128)(2,1)} %get-tuple-element.46), channel_id=1, source_target_pairs={{0,2},{1,3},{2,0},{3,1},{4,6},{5,7},{6,4},{7,5},{8,10},{9,11},{10,... | collective-permute-start | bytes 1769480 | tf_op jit(solution)/shard_map/ppermute | solution.py:502
  9.9 1.5 %collective-permute-start.8 = (bf16[128,1024]{1,0:T(8,128)(2,1)}, bf16[128,1024]{1,0:T(8,128)(2,1)S(1)}, u32[]{:S(2)}, u32[]{:S(2)}) collective-permute-start(bf16[128,1024]{1,0:T(8,128)(2,1)} %get-tuple-element.64.mine_ref), channel_id=1, source_target_pairs={{0,4},{4,0},{8,12},{12,8},{16,20},{20,16},{24,28},{28,24},{1,5},{5... | collective-permute-start | bytes 786440 | tf_op jit(solution)/shard_map/ppermute | solution.py:502
  11.4 0.1 pad_add_fusion.side_ref
  11.5 0.1 pad_add_fusion.1.side_ref
  11.6 1.2 %copy-done.1 = bf16[8,128,512]{2,1,0:T(8,128)(2,1)S(1)} copy-done((bf16[8,128,512]{2,1,0:T(8,128)(2,1)S(1)}, bf16[8,128,512]{2,1,0:T(8,128)(2,1)}, u32[]{:S(2)}) %copy-start.1) | copy-done | bytes 1048600
  12.8 3.4 %shard_map.83 = (f32[4,64,128]{2,1,0:T(8,128)S(1)}, bf16[4,32,256]{2,1,0:T(8,128)(2,1)S(1)}, bf16[4,32,256]{2,1,0:T(8,128)(2,1)S(1)}, bf16[4,4,64,256]{3,2,1,0:T(8,128)(2,1)S(1)}) custom-call(s32[2]{0:T(128)S(1)} %pad_add_fusion.side_ref, bf16[64,1024]{1,0:T(8,128)(2,1)S(1)} %copy-done.6, bf16[64,1024]{1,0:T(8,128)(2,1)S(1)} %collective-permute-done.refs_1_, ...), custom_call_target="tpu_custom_call" | custom-call | flops 1140850 | bytes 983 | tf_op jit(solution)/shard_map/pallas_call | solution.py:246
  16.2 0.1 collective-permute-start.6
  16.3 1.4 %collective-permute-start.4 = (bf16[4,32,256]{2,1,0:T(8,128)(2,1)S(1)}, bf16[4,32,256]{2,1,0:T(8,128)(2,1)S(1)}, u32[]{:S(2)}, u32[]{:S(2)}) collective-permute-start(bf16[4,32,256]{2,1,0:T(8,128)(2,1)S(1)} %get-tuple-element.54), channel_id=1, source_target_pairs={{0,2},{1,3},{2,0},{3,1},{4,6},{5,7},{6,4},{7,5},{8,10},{9,11},{10,... | collective-permute-start | bytes 196616 | tf_op jit(solution)/shard_map/ppermute | solution.py:502
  17.7 3.4 %shard_map.84 = (f32[4,64,128]{2,1,0:T(8,128)S(1)}, bf16[4,32,256]{2,1,0:T(8,128)(2,1)S(1)}, bf16[4,32,256]{2,1,0:T(8,128)(2,1)S(1)}) custom-call(s32[2]{0:T(128)S(1)} %pad_add_fusion.1.side_ref, bf16[4,4,64,256]{3,2,1,0:T(8,128)(2,1)S(1)} %get-tuple-element.56.refs_0_, s32[1,4096]{1,0:T(1,128)S(1)} %bitcast.7, bf16[8,128,512]{2,1,0:T(8,128)(2,1)S(1)} %copy-done.1, ...), custom_call_target="tpu_custom_call" | custom-call | flops 1140850 | bytes 983 | tf_op jit(solution)/shard_map/pallas_call | solution.py:246
  21.1 0.5 collective-permute-start.5
  21.6 3.5 %collective-permute-done.6.refs_3_ = bf16[4,32,256]{2,1,0:T(8,128)(2,1)S(1)} collective-permute-done((bf16[4,32,256]{2,1,0:T(8,128)(2,1)S(1)}, bf16[4,32,256]{2,1,0:T(8,128)(2,1)S(1)}, u32[]{:S(2)}, u32[]{:S(2)}) %collective-permute-start.6) | collective-permute-done | bytes 65568 | tf_op jit(solution)/shard_map/ppermute | solution.py:502
  25.2 1.6 %collective-permute-done.4.refs_1_ = bf16[4,32,256]{2,1,0:T(8,128)(2,1)S(1)} collective-permute-done((bf16[4,32,256]{2,1,0:T(8,128)(2,1)S(1)}, bf16[4,32,256]{2,1,0:T(8,128)(2,1)S(1)}, u32[]{:S(2)}, u32[]{:S(2)}) %collective-permute-start.4) | collective-permute-done | bytes 65568 | tf_op jit(solution)/shard_map/ppermute | solution.py:502
  26.8 0.1 collective-permute-start.9
  26.9 1.8 %collective-permute-start.12 = (bf16[128,1024]{1,0:T(8,128)(2,1)S(1)}, bf16[128,1024]{1,0:T(8,128)(2,1)S(1)}, u32[]{:S(2)}, u32[]{:S(2)}) collective-permute-start(bf16[128,1024]{1,0:T(8,128)(2,1)S(1)} %get-tuple-element.73.refs_0_.refs_4_.refs_6_), channel_id=1, source_target_pairs={{0,2},{1,3},{2,0},{3,1},{4,6},{5,7},{6,4},{7,5},{8,10},{9,11},{10,... | collective-permute-start | bytes 786440 | tf_op jit(solution)/shard_map/ppermute | solution.py:502
  28.7 1.6 %collective-permute-start.18 = (bf16[128,1024]{1,0:T(8,128)(2,1)S(1)}, bf16[128,1024]{1,0:T(8,128)(2,1)S(1)}, u32[]{:S(2)}, u32[]{:S(2)}) collective-permute-start(bf16[128,1024]{1,0:T(8,128)(2,1)S(1)} %get-tuple-element.67.mine_ref), channel_id=1, source_target_pairs={{0,8},{4,12},{8,0},{12,4},{16,24},{20,28},{24,16},{28,20},{1,9},{5... | collective-permute-start | bytes 786440 | tf_op jit(solution)/shard_map/ppermute | solution.py:502
  30.3 1.5 %shard_map.86 = (f32[3,4,32,128]{3,2,1,0:T(8,128)S(1)}, bf16[32,256]{1,0:T(8,128)(2,1)S(1)}) custom-call(bf16[4,32,256]{2,1,0:T(8,128)(2,1)S(1)} %get-tuple-element.58.refs_0_, bf16[4,32,256]{2,1,0:T(8,128)(2,1)S(1)} %collective-permute-done.4.refs_1_, bf16[4,32,256]{2,1,0:T(8,128)(2,1)S(1)} %collective-permute-done.5.refs_2_, ...), custom_call_target="tpu_custom_call" | custom-call | flops 75497 | bytes 3145 | tf_op jit(solution)/shard_map/pallas_call | solution.py:309
  31.8 0.1 collective-permute-start.11
  31.9 0.6 collective-permute-start.10
  32.5 3.3 %collective-permute-done.12.refs_5_.refs_7_ = bf16[128,1024]{1,0:T(8,128)(2,1)S(1)} collective-permute-done((bf16[128,1024]{1,0:T(8,128)(2,1)S(1)}, bf16[128,1024]{1,0:T(8,128)(2,1)S(1)}, u32[]{:S(2)}, u32[]{:S(2)}) %collective-permute-start.12) | collective-permute-done | bytes 262176 | tf_op jit(solution)/shard_map/ppermute | solution.py:502
  35.8 0.2 collective-permute-done.10.other_ref
  36.0 1.1 %collective-permute-done.18.other_ref = bf16[128,1024]{1,0:T(8,128)(2,1)S(1)} collective-permute-done((bf16[128,1024]{1,0:T(8,128)(2,1)S(1)}, bf16[128,1024]{1,0:T(8,128)(2,1)S(1)}, u32[]{:S(2)}, u32[]{:S(2)}) %collective-permute-start.18) | collective-permute-done | bytes 262176 | tf_op jit(solution)/shard_map/ppermute | solution.py:502
  37.2 0.3 shard_map.88
  37.5 0.7 %collective-permute-start.19 = (bf16[128,1024]{1,0:T(8,128)(2,1)S(1)}, bf16[128,1024]{1,0:T(8,128)(2,1)S(1)}, u32[]{:S(2)}, u32[]{:S(2)}) collective-permute-start(bf16[128,1024]{1,0:T(8,128)(2,1)S(1)} %shard_map.91), channel_id=1, source_target_pairs={{0,2},{1,3},{2,0},{3,1},{4,6},{5,7},{6,4},{7,5},{8,10},{9,11},{10,... | collective-permute-start | bytes 786440 | tf_op jit(solution)/shard_map/ppermute | solution.py:502
  38.2 2.6 %collective-permute-start.23 = (bf16[128,512]{1,0:T(8,128)(2,1)S(1)}, bf16[128,512]{1,0:T(8,128)(2,1)S(1)}, u32[]{:S(2)}, u32[]{:S(2)}) collective-permute-start(bf16[128,512]{1,0:T(8,128)(2,1)S(1)} %get-tuple-element.84.mine_ref), channel_id=1, source_target_pairs={{0,16},{4,20},{8,24},{12,28},{16,0},{20,4},{24,8},{28,12},{1,17},{... | collective-permute-start | bytes 393224 | tf_op jit(solution)/shard_map/ppermute | solution.py:502
  40.8 2.3 %collective-permute-start.14 = (bf16[32,256]{1,0:T(8,128)(2,1)S(1)}, bf16[32,256]{1,0:T(8,128)(2,1)S(1)}, u32[]{:S(2)}, u32[]{:S(2)}) collective-permute-start(bf16[32,256]{1,0:T(8,128)(2,1)S(1)} %get-tuple-element.75.refs_3_.refs_1_), channel_id=1, source_target_pairs={{0,6},{1,7},{2,4},{3,5},{4,2},{5,3},{6,0},{7,1},{8,14},{9,15},{10,... | collective-permute-start | bytes 49160 | tf_op jit(solution)/shard_map/ppermute | solution.py:509
  43.1 0.5 collective-permute-start.15
  43.6 0.6 collective-permute-start.16
  44.3 2.7 %collective-permute-done.14.refs_0_ = bf16[32,256]{1,0:T(8,128)(2,1)S(1)} collective-permute-done((bf16[32,256]{1,0:T(8,128)(2,1)S(1)}, bf16[32,256]{1,0:T(8,128)(2,1)S(1)}, u32[]{:S(2)}, u32[]{:S(2)}) %collective-permute-start.14) | collective-permute-done | bytes 16416 | tf_op jit(solution)/shard_map/ppermute | solution.py:509
  47.1 0.3 collective-permute-done.16.refs_2_
  47.4 0.6 shard_map.89
  48.1 1.1 %collective-permute-start.24 = (bf16[128,1280]{1,0:T(8,128)(2,1)S(1)}, bf16[128,1280]{1,0:T(8,128)(2,1)S(1)}, u32[]{:S(2)}, u32[]{:S(2)}) collective-permute-start(bf16[128,1280]{1,0:T(8,128)(2,1)S(1)} %shard_map.96), channel_id=1, source_target_pairs={{0,2},{1,3},{2,0},{3,1},{4,6},{5,7},{6,4},{7,5},{8,10},{9,11},{10,... | collective-permute-start | bytes 983048 | tf_op jit(solution)/shard_map/ppermute | solution.py:502
  49.2 0.1 collective-permute-start.20
  49.3 0.5 collective-permute-start.21
  49.8 1.6 %collective-permute-start.17 = (bf16[32,256]{1,0:T(8,128)(2,1)S(1)}, bf16[32,256]{1,0:T(8,128)(2,1)S(1)}, u32[]{:S(2)}, u32[]{:S(2)}) collective-permute-start(bf16[32,256]{1,0:T(8,128)(2,1)S(1)} %get-tuple-element.76.refs_1_.refs_0_.refs_2_), channel_id=1, source_target_pairs={{0,8},{4,12},{8,0},{12,4},{16,24},{20,28},{24,16},{28,20},{1,9},{5... | collective-permute-start | bytes 49160 | tf_op jit(solution)/shard_map/ppermute | solution.py:502
  51.4 2.2 %collective-permute-done.17.refs_1_ = bf16[32,256]{1,0:T(8,128)(2,1)S(1)} collective-permute-done((bf16[32,256]{1,0:T(8,128)(2,1)S(1)}, bf16[32,256]{1,0:T(8,128)(2,1)S(1)}, u32[]{:S(2)}, u32[]{:S(2)}) %collective-permute-start.17) | collective-permute-done | bytes 16416 | tf_op jit(solution)/shard_map/ppermute | solution.py:502
  53.6 0.6 shard_map.94
  54.2 2.6 %collective-permute-start.22 = (bf16[32,256]{1,0:T(8,128)(2,1)S(1)}, bf16[32,256]{1,0:T(8,128)(2,1)S(1)}, u32[]{:S(2)}, u32[]{:S(2)}) collective-permute-start(bf16[32,256]{1,0:T(8,128)(2,1)S(1)} %get-tuple-element.79.refs_0_), channel_id=1, source_target_pairs={{0,16},{4,20},{8,24},{12,28},{16,0},{20,4},{24,8},{28,12},{1,17},{... | collective-permute-start | bytes 49160 | tf_op jit(solution)/shard_map/ppermute | solution.py:502
  56.8 2.0 %collective-permute-done.22._.refs_1_ = bf16[32,256]{1,0:T(8,128)(2,1)S(1)} collective-permute-done((bf16[32,256]{1,0:T(8,128)(2,1)S(1)}, bf16[32,256]{1,0:T(8,128)(2,1)S(1)}, u32[]{:S(2)}, u32[]{:S(2)}) %collective-permute-start.22) | collective-permute-done | bytes 16416 | tf_op jit(solution)/shard_map/ppermute | solution.py:502
  58.9 0.1 collective-permute-start.25
  58.9 1.6 %collective-permute-done.25.refs_15_ = bf16[128,1280]{1,0:T(8,128)(2,1)S(1)} collective-permute-done((bf16[128,1280]{1,0:T(8,128)(2,1)S(1)}, bf16[128,1280]{1,0:T(8,128)(2,1)S(1)}, u32[]{:S(2)}, u32[]{:S(2)}) %collective-permute-start.25) | collective-permute-done | bytes 327712 | tf_op jit(solution)/shard_map/ppermute | solution.py:502
  60.6 1.1 %shard_map.98 = bf16[4,32,256]{2,1,0:T(8,128)(2,1)S(1)} custom-call(bf16[32,256]{1,0:T(8,128)(2,1)S(1)} %get-tuple-element.79.refs_0_, bf16[32,256]{1,0:T(8,128)(2,1)S(1)} %collective-permute-done.22._.refs_1_, f32[4,32,128]{2,1,0:T(8,128)S(1)} %get-tuple-element.80.refs_2_, f32[4,32,128]{2,1,0:T(8,128)S(1)} %get-tuple-element.81.refs_3_, ...), custom_call_target="tpu_custom_call" | custom-call | flops 67108 | bytes 4194 | tf_op jit(solution)/shard_map/pallas_call | solution.py:470
  61.6 5.8 %all-gather = bf16[16,32,256]{2,1,0:T(8,128)(2,1)S(1)} all-gather(bf16[4,32,256]{2,1,0:T(8,128)(2,1)S(1)} %shard_map.98), channel_id=2, replica_groups=mesh['leaf'=8,'rhs'=4] {'rhs'}, dimensions={0}, use_global_device_ids=true | all-gather | bytes 327680 | tf_op jit(solution)/shard_map/all_gather | solution.py:605
  67.4 1.0 %shard_map.99 = f32[8,64,128]{2,1,0:T(8,128)} custom-call(f32[4,64,128]{2,1,0:T(8,128)S(1)} %get-tuple-element.50.far_ref, f32[4,64,128]{2,1,0:T(8,128)S(1)} %get-tuple-element.57.own_ref, bf16[4,4,32,256]{3,2,1,0:T(8,128)(2,1)S(1)} %bitcast.5, bf16[8,128,256]{2,1,0:T(8,128)(2,1)S(1)} %copy-done.3), custom_call_target="tpu_custom_call" | custom-call | flops 33554 | bytes 524 | tf_op jit(solution)/shard_map/pallas_call | solution.py:493
  (41 shorter events, 0.4 us)
Async XLA Ops:
  0.0 11.6 %copy-start.2 = (bf16[8,128,256]{2,1,0:T(8,128)(2,1)S(1)}, bf16[8,128,256]{2,1,0:T(8,128)(2,1)}, u32[]{:S(2)}) copy-start(bf16[8,128,256]{2,1,0:T(8,128)(2,1)} %refs_3_.1) | copy-start | bytes 1572868
  0.0 6.6 %collective-permute-start = (bf16[64,1024]{1,0:T(8,128)(2,1)}, bf16[64,1024]{1,0:T(8,128)(2,1)S(1)}, u32[]{:S(2)}, u32[]{:S(2)}) collective-permute-start(bf16[64,1024]{1,0:T(8,128)(2,1)} %refs_0_.1), channel_id=1, source_target_pairs={{0,2},{1,3},{2,0},{3,1},{4,6},{5,7},{6,4},{7,5},{8,10},{9,11},{10,... | collective-permute-start | bytes 393224 | tf_op jit(solution)/shard_map/ppermute | solution.py:502
  2.9 3.7 %collective-permute-start.1 = (bf16[64,1024]{1,0:T(8,128)(2,1)}, bf16[64,1024]{1,0:T(8,128)(2,1)S(1)}, u32[]{:S(2)}, u32[]{:S(2)}) collective-permute-start(bf16[64,1024]{1,0:T(8,128)(2,1)} %refs_0_.1), channel_id=1, source_target_pairs={{0,1},{1,0},{2,3},{3,2},{4,5},{5,4},{6,7},{7,6},{8,9},{9,8},{10,11... | collective-permute-start | bytes 393224 | tf_op jit(solution)/shard_map/ppermute | solution.py:502
  2.9 8.6 %copy-start.6 = (bf16[64,1024]{1,0:T(8,128)(2,1)S(1)}, bf16[64,1024]{1,0:T(8,128)(2,1)}, u32[]{:S(2)}) copy-start(bf16[64,1024]{1,0:T(8,128)(2,1)} %refs_0_.1) | copy-start | bytes 393220
  6.6 1.3 %collective-permute-start.2 = (bf16[64,1024]{1,0:T(8,128)(2,1)S(1)}, bf16[64,1024]{1,0:T(8,128)(2,1)S(1)}, u32[]{:S(2)}, u32[]{:S(2)}) collective-permute-start(bf16[64,1024]{1,0:T(8,128)(2,1)S(1)} %collective-permute-done.refs_1_), channel_id=1, source_target_pairs={{0,1},{1,0},{2,3},{3,2},{4,5},{5,4},{6,7},{7,6},{8,9},{9,8},{10,11... | collective-permute-start | bytes 393224 | tf_op jit(solution)/shard_map/ppermute | solution.py:502
  8.0 9.7 %collective-permute-start.3 = (bf16[4,128,1024]{2,1,0:T(8,128)(2,1)}, bf16[4,128,1024]{2,1,0:T(8,128)(2,1)S(1)}, u32[]{:S(2)}, u32[]{:S(2)}) collective-permute-start(bf16[4,128,1024]{2,1,0:T(8,128)(2,1)} %get-tuple-element.53.refs_4_.own_ref.refs_16_), channel_id=1, source_target_pairs={{0,1},{1,0},{2,3},{3,2},{4,5},{5,4},{6,7},{7,6},{8,9},{9,8},{10,11... | collective-permute-start | bytes 3145736 | tf_op jit(solution)/shard_map/ppermute | solution.py:502
  8.1 18.7 %collective-permute-start.7 = (bf16[3,128,768]{2,1,0:T(8,128)(2,1)}, bf16[3,128,768]{2,1,0:T(8,128)(2,1)S(1)}, u32[]{:S(2)}, u32[]{:S(2)}) collective-permute-start(bf16[3,128,768]{2,1,0:T(8,128)(2,1)} %get-tuple-element.46), channel_id=1, source_target_pairs={{0,2},{1,3},{2,0},{3,1},{4,6},{5,7},{6,4},{7,5},{8,10},{9,11},{10,... | collective-permute-start | bytes 1769480 | tf_op jit(solution)/shard_map/ppermute | solution.py:502
  9.9 1.7 %copy-start.7 = (s32[4096]{0:T(1024)S(1)}, s32[4096]{0:T(1024)}, u32[]{:S(2)}) copy-start(s32[4096]{0:T(1024)} %param.9) | copy-start | bytes 49156
  9.9 11.7 %collective-permute-start.8 = (bf16[128,1024]{1,0:T(8,128)(2,1)}, bf16[128,1024]{1,0:T(8,128)(2,1)S(1)}, u32[]{:S(2)}, u32[]{:S(2)}) collective-permute-start(bf16[128,1024]{1,0:T(8,128)(2,1)} %get-tuple-element.64.mine_ref), channel_id=1, source_target_pairs={{0,4},{4,0},{8,12},{12,8},{16,20},{20,16},{24,28},{28,24},{1,5},{5... | collective-permute-start | bytes 786440 | tf_op jit(solution)/shard_map/ppermute | solution.py:502
  11.6 1.2 %copy-start.1 = (bf16[8,128,512]{2,1,0:T(8,128)(2,1)S(1)}, bf16[8,128,512]{2,1,0:T(8,128)(2,1)}, u32[]{:S(2)}) copy-start(bf16[8,128,512]{2,1,0:T(8,128)(2,1)} %refs_2_.1) | copy-start | bytes 3145732
  16.2 8.9 %collective-permute-start.6 = (bf16[4,32,256]{2,1,0:T(8,128)(2,1)S(1)}, bf16[4,32,256]{2,1,0:T(8,128)(2,1)S(1)}, u32[]{:S(2)}, u32[]{:S(2)}) collective-permute-start(bf16[4,32,256]{2,1,0:T(8,128)(2,1)S(1)} %get-tuple-element.61), channel_id=1, source_target_pairs={{0,3},{1,2},{2,1},{3,0},{4,7},{5,6},{6,5},{7,4},{8,11},{9,10},{10,... | collective-permute-start | bytes 196616 | tf_op jit(solution)/shard_map/ppermute | solution.py:502
  16.3 10.4 %collective-permute-start.4 = (bf16[4,32,256]{2,1,0:T(8,128)(2,1)S(1)}, bf16[4,32,256]{2,1,0:T(8,128)(2,1)S(1)}, u32[]{:S(2)}, u32[]{:S(2)}) collective-permute-start(bf16[4,32,256]{2,1,0:T(8,128)(2,1)S(1)} %get-tuple-element.54), channel_id=1, source_target_pairs={{0,2},{1,3},{2,0},{3,1},{4,6},{5,7},{6,4},{7,5},{8,10},{9,11},{10,... | collective-permute-start | bytes 196616 | tf_op jit(solution)/shard_map/ppermute | solution.py:502
  17.7 9.1 %copy-start.4 = (bf16[128,1024]{1,0:T(8,128)(2,1)S(1)}, bf16[128,1024]{1,0:T(8,128)(2,1)}, u32[]{:S(2)}) copy-start(bf16[128,1024]{1,0:T(8,128)(2,1)} %get-tuple-element.64.mine_ref) | copy-start | bytes 786436
  17.7 9.1 %copy-start.5 = (bf16[128,768]{1,0:T(8,128)(2,1)S(1)}, bf16[128,768]{1,0:T(8,128)(2,1)}, u32[]{:S(2)}) copy-start(bf16[128,768]{1,0:T(8,128)(2,1)} %get-tuple-element.66.refs_0_) | copy-start | bytes 589828
  17.7 12.6 %copy-start = (bf16[4,128,1024]{2,1,0:T(8,128)(2,1)S(1)}, bf16[4,128,1024]{2,1,0:T(8,128)(2,1)}, u32[]{:S(2)}) copy-start(bf16[4,128,1024]{2,1,0:T(8,128)(2,1)} %get-tuple-element.53.refs_4_.own_ref.refs_16_) | copy-start | bytes 3145732
  21.1 5.7 %collective-permute-start.5 = (bf16[4,32,256]{2,1,0:T(8,128)(2,1)S(1)}, bf16[4,32,256]{2,1,0:T(8,128)(2,1)S(1)}, u32[]{:S(2)}, u32[]{:S(2)}) collective-permute-start(bf16[4,32,256]{2,1,0:T(8,128)(2,1)S(1)} %get-tuple-element.60), channel_id=1, source_target_pairs={{0,1},{1,0},{2,3},{3,2},{4,5},{5,4},{6,7},{7,6},{8,9},{9,8},{10,11... | collective-permute-start | bytes 196616 | tf_op jit(solution)/shard_map/ppermute | solution.py:502
  26.8 3.5 %collective-permute-start.9 = (bf16[3,128,768]{2,1,0:T(8,128)(2,1)S(1)}, bf16[3,128,768]{2,1,0:T(8,128)(2,1)S(1)}, u32[]{:S(2)}, u32[]{:S(2)}) collective-permute-start(bf16[3,128,768]{2,1,0:T(8,128)(2,1)S(1)} %collective-permute-done.7.refs_5_), channel_id=1, source_target_pairs={{0,1},{1,0},{2,3},{3,2},{4,5},{5,4},{6,7},{7,6},{8,9},{9,8},{10,11... | collective-permute-start | bytes 1769480 | tf_op jit(solution)/shard_map/ppermute | solution.py:502
  26.9 8.9 %collective-permute-start.12 = (bf16[128,1024]{1,0:T(8,128)(2,1)S(1)}, bf16[128,1024]{1,0:T(8,128)(2,1)S(1)}, u32[]{:S(2)}, u32[]{:S(2)}) collective-permute-start(bf16[128,1024]{1,0:T(8,128)(2,1)S(1)} %get-tuple-element.73.refs_0_.refs_4_.refs_6_), channel_id=1, source_target_pairs={{0,2},{1,3},{2,0},{3,1},{4,6},{5,7},{6,4},{7,5},{8,10},{9,11},{10,... | collective-permute-start | bytes 786440 | tf_op jit(solution)/shard_map/ppermute | solution.py:502
  28.7 8.4 %collective-permute-start.18 = (bf16[128,1024]{1,0:T(8,128)(2,1)S(1)}, bf16[128,1024]{1,0:T(8,128)(2,1)S(1)}, u32[]{:S(2)}, u32[]{:S(2)}) collective-permute-start(bf16[128,1024]{1,0:T(8,128)(2,1)S(1)} %get-tuple-element.67.mine_ref), channel_id=1, source_target_pairs={{0,8},{4,12},{8,0},{12,4},{16,24},{20,28},{24,16},{28,20},{1,9},{5... | collective-permute-start | bytes 786440 | tf_op jit(solution)/shard_map/ppermute | solution.py:502
  31.8 5.3 %collective-permute-start.11 = (bf16[128,1024]{1,0:T(8,128)(2,1)S(1)}, bf16[128,1024]{1,0:T(8,128)(2,1)S(1)}, u32[]{:S(2)}, u32[]{:S(2)}) collective-permute-start(bf16[128,1024]{1,0:T(8,128)(2,1)S(1)} %shard_map.87), channel_id=1, source_target_pairs={{0,1},{1,0},{2,3},{3,2},{4,5},{5,4},{6,7},{7,6},{8,9},{9,8},{10,11... | collective-permute-start | bytes 786440 | tf_op jit(solution)/shard_map/ppermute | solution.py:502
  31.9 4.1 %collective-permute-start.10 = (bf16[32,256]{1,0:T(8,128)(2,1)S(1)}, bf16[32,256]{1,0:T(8,128)(2,1)S(1)}, u32[]{:S(2)}, u32[]{:S(2)}) collective-permute-start(bf16[32,256]{1,0:T(8,128)(2,1)S(1)} %get-tuple-element.69.refs_1_.mine_ref), channel_id=1, source_target_pairs={{0,2},{1,3},{2,0},{3,1},{4,6},{5,7},{6,4},{7,5},{8,10},{9,11},{10,... | collective-permute-start | bytes 49160 | tf_op jit(solution)/shard_map/ppermute | solution.py:502
  36.0 4.8 %collective-permute-start.13 = (bf16[128,1024]{1,0:T(8,128)(2,1)S(1)}, bf16[128,1024]{1,0:T(8,128)(2,1)S(1)}, u32[]{:S(2)}, u32[]{:S(2)}) collective-permute-start(bf16[128,1024]{1,0:T(8,128)(2,1)S(1)} %collective-permute-done.12.refs_5_.refs_7_), channel_id=1, source_target_pairs={{0,1},{1,0},{2,3},{3,2},{4,5},{5,4},{6,7},{7,6},{8,9},{9,8},{10,11... | collective-permute-start | bytes 786440 | tf_op jit(solution)/shard_map/ppermute | solution.py:502
  37.5 11.8 %collective-permute-start.19 = (bf16[128,1024]{1,0:T(8,128)(2,1)S(1)}, bf16[128,1024]{1,0:T(8,128)(2,1)S(1)}, u32[]{:S(2)}, u32[]{:S(2)}) collective-permute-start(bf16[128,1024]{1,0:T(8,128)(2,1)S(1)} %shard_map.91), channel_id=1, source_target_pairs={{0,2},{1,3},{2,0},{3,1},{4,6},{5,7},{6,4},{7,5},{8,10},{9,11},{10,... | collective-permute-start | bytes 786440 | tf_op jit(solution)/shard_map/ppermute | solution.py:502
  38.2 9.8 %collective-permute-start.23 = (bf16[128,512]{1,0:T(8,128)(2,1)S(1)}, bf16[128,512]{1,0:T(8,128)(2,1)S(1)}, u32[]{:S(2)}, u32[]{:S(2)}) collective-permute-start(bf16[128,512]{1,0:T(8,128)(2,1)S(1)} %get-tuple-element.84.mine_ref), channel_id=1, source_target_pairs={{0,16},{4,20},{8,24},{12,28},{16,0},{20,4},{24,8},{28,12},{1,17},{... | collective-permute-start | bytes 393224 | tf_op jit(solution)/shard_map/ppermute | solution.py:502
  40.8 6.2 %collective-permute-start.14 = (bf16[32,256]{1,0:T(8,128)(2,1)S(1)}, bf16[32,256]{1,0:T(8,128)(2,1)S(1)}, u32[]{:S(2)}, u32[]{:S(2)}) collective-permute-start(bf16[32,256]{1,0:T(8,128)(2,1)S(1)} %get-tuple-element.75.refs_3_.refs_1_), channel_id=1, source_target_pairs={{0,6},{1,7},{2,4},{3,5},{4,2},{5,3},{6,0},{7,1},{8,14},{9,15},{10,... | collective-permute-start | bytes 49160 | tf_op jit(solution)/shard_map/ppermute | solution.py:509
  43.1 3.9 %collective-permute-start.15 = (bf16[32,256]{1,0:T(8,128)(2,1)S(1)}, bf16[32,256]{1,0:T(8,128)(2,1)S(1)}, u32[]{:S(2)}, u32[]{:S(2)}) collective-permute-start(bf16[32,256]{1,0:T(8,128)(2,1)S(1)} %get-tuple-element.75.refs_3_.refs_1_), channel_id=1, source_target_pairs={{0,4},{4,0},{8,12},{12,8},{16,20},{20,16},{24,28},{28,24},{1,5},{5... | collective-permute-start | bytes 49160 | tf_op jit(solution)/shard_map/ppermute | solution.py:502
  43.6 3.7 %collective-permute-start.16 = (bf16[32,256]{1,0:T(8,128)(2,1)S(1)}, bf16[32,256]{1,0:T(8,128)(2,1)S(1)}, u32[]{:S(2)}, u32[]{:S(2)}) collective-permute-start(bf16[32,256]{1,0:T(8,128)(2,1)S(1)} %get-tuple-element.75.refs_3_.refs_1_), channel_id=1, source_target_pairs={{0,2},{1,3},{2,0},{3,1},{4,6},{5,7},{6,4},{7,5},{8,10},{9,11},{10,... | collective-permute-start | bytes 49160 | tf_op jit(solution)/shard_map/ppermute | solution.py:502
  48.1 8.7 %collective-permute-start.24 = (bf16[128,1280]{1,0:T(8,128)(2,1)S(1)}, bf16[128,1280]{1,0:T(8,128)(2,1)S(1)}, u32[]{:S(2)}, u32[]{:S(2)}) collective-permute-start(bf16[128,1280]{1,0:T(8,128)(2,1)S(1)} %shard_map.96), channel_id=1, source_target_pairs={{0,2},{1,3},{2,0},{3,1},{4,6},{5,7},{6,4},{7,5},{8,10},{9,11},{10,... | collective-permute-start | bytes 983048 | tf_op jit(solution)/shard_map/ppermute | solution.py:502
  49.2 4.4 %collective-permute-start.20 = (bf16[128,1024]{1,0:T(8,128)(2,1)S(1)}, bf16[128,1024]{1,0:T(8,128)(2,1)S(1)}, u32[]{:S(2)}, u32[]{:S(2)}) collective-permute-start(bf16[128,1024]{1,0:T(8,128)(2,1)S(1)} %shard_map.92), channel_id=1, source_target_pairs={{0,1},{1,0},{2,3},{3,2},{4,5},{5,4},{6,7},{7,6},{8,9},{9,8},{10,11... | collective-permute-start | bytes 786440 | tf_op jit(solution)/shard_map/ppermute | solution.py:502
  49.3 4.3 %collective-permute-start.21 = (bf16[128,1024]{1,0:T(8,128)(2,1)S(1)}, bf16[128,1024]{1,0:T(8,128)(2,1)S(1)}, u32[]{:S(2)}, u32[]{:S(2)}) collective-permute-start(bf16[128,1024]{1,0:T(8,128)(2,1)S(1)} %shard_map.93), channel_id=1, source_target_pairs={{0,1},{1,0},{2,3},{3,2},{4,5},{5,4},{6,7},{7,6},{8,9},{9,8},{10,11... | collective-permute-start | bytes 786440 | tf_op jit(solution)/shard_map/ppermute | solution.py:502
  49.8 3.7 %collective-permute-start.17 = (bf16[32,256]{1,0:T(8,128)(2,1)S(1)}, bf16[32,256]{1,0:T(8,128)(2,1)S(1)}, u32[]{:S(2)}, u32[]{:S(2)}) collective-permute-start(bf16[32,256]{1,0:T(8,128)(2,1)S(1)} %get-tuple-element.76.refs_1_.refs_0_.refs_2_), channel_id=1, source_target_pairs={{0,8},{4,12},{8,0},{12,4},{16,24},{20,28},{24,16},{28,20},{1,9},{5... | collective-permute-start | bytes 49160 | tf_op jit(solution)/shard_map/ppermute | solution.py:502
  54.2 4.7 %collective-permute-start.22 = (bf16[32,256]{1,0:T(8,128)(2,1)S(1)}, bf16[32,256]{1,0:T(8,128)(2,1)S(1)}, u32[]{:S(2)}, u32[]{:S(2)}) collective-permute-start(bf16[32,256]{1,0:T(8,128)(2,1)S(1)} %get-tuple-element.79.refs_0_), channel_id=1, source_target_pairs={{0,16},{4,20},{8,24},{12,28},{16,0},{20,4},{24,8},{28,12},{1,17},{... | collective-permute-start | bytes 49160 | tf_op jit(solution)/shard_map/ppermute | solution.py:502
  58.9 1.7 %collective-permute-start.25 = (bf16[128,1280]{1,0:T(8,128)(2,1)S(1)}, bf16[128,1280]{1,0:T(8,128)(2,1)S(1)}, u32[]{:S(2)}, u32[]{:S(2)}) collective-permute-start(bf16[128,1280]{1,0:T(8,128)(2,1)S(1)} %shard_map.97.refs_14_), channel_id=1, source_target_pairs={{0,1},{1,0},{2,3},{3,2},{4,5},{5,4},{6,7},{7,6},{8,9},{9,8},{10,11... | collective-permute-start | bytes 983048 | tf_op jit(solution)/shard_map/ppermute | solution.py:502
  60.6 6.9 %copy-start.3 = (bf16[8,128,256]{2,1,0:T(8,128)(2,1)S(1)}, bf16[8,128,256]{2,1,0:T(8,128)(2,1)}, u32[]{:S(2)}) copy-start(bf16[8,128,256]{2,1,0:T(8,128)(2,1)} %coupling_ref.1) | copy-start | bytes 1572868

commit v7 on v6

--- a/solution.py
+++ b/solution.py
@@ -402,11 +402,12 @@
     solved_cross, refs = refs[: cross_levels - 1], refs[cross_levels - 1 :]
     solved_top, solved_half, refs = refs[0], refs[1], refs[2:]
     count = 2 * CORES * (cross_levels - 1)
-    cross_packs, (tail, near_tail, keep, keep_near) = refs[:count], refs[count:]
+    cross_packs, (both, keep, keep_near) = refs[:count], refs[count:]
     levels, total = half_levels(per_dev)
     rank = out_ref.shape[2]
     node_size = 2 * rank
     place = lax.axis_index("rhs")
+    tail, near_tail = both.at[place % CORES], both.at[(place + 1) % CORES]
 
     def choose(which):
         return jnp.concatenate([value[2 * which], value[2 * which + 1]], axis=1)
@@ -599,8 +600,11 @@
                 fars.append(swap(join([ancestors[later]], current), "rhs", CORES))
             tail = swap(join([ancestors[-1], send_coupling], current), "rhs", CORES)
 
-    tail = hop(cross_levels - 1, ancestors[-1], tail, inputs[1])
-    others = [tail, swap(tail, "rhs", 1), keep, keep_near]
+    tail = hop(cross_levels - 1, ancestors[-1], tail, current)
+    shares = lax.axis_size("rhs")
+    cores = [[i + core for core in range(CORES)] for i in range(0, shares, CORES)]
+    both = lax.all_gather(tail, "rhs", axis_index_groups=cores)
+    others = [both, keep, keep_near]
     shares = way_down(per_dev, inputs, solved_cross, solved_top, solved_half, cross_packs, others)
     incoming = lax.all_gather(shares, "rhs", axis=0)
     return finish(far_values, own_values, incoming, leaf_coupling)

time: 68.6 us -> 67.2 us (0.980)
  waiting for transfers between devices: 20.7 us -> 17 us
  blocking collectives: 5.79 us -> 8.07 us
    ppermute x25 -> x24, waiting for transfers between devices: 18 us -> 14.3 us  [swap(): lax.ppermute(block, axis, [(i, i ^ bit) for i in range(lax.axis_size(axis...]
    all_gather x0 -> x1, blocking collectives: none -> 2.28 us  [body(): both = lax.all_gather(tail, 'rhs', axis_index_groups=cores)]
    ppermute x25 -> x24, starting transfers between devices: 22.9 us -> 22.8 us  [swap(): lax.ppermute(block, axis, [(i, i ^ bit) for i in range(lax.axis_size(axis...]
  transfers between devices with their start and end apart: 26 -> 25, of which waited for: 12 -> 10; matrix products, arithmetic and copies ran while one was open for 0% -> 0% of each run, Pallas kernels for 19% -> 19%
where the time goes in v7:
time: 67.2 us; the launch traced here: 67 us
  starting transfers between devices  25.2 us (38%)
  waiting for transfers between devices  17 us (25%)
  Pallas kernels  15.1 us (22%)
  blocking collectives  8.07 us (12%)
  local copies, waits for them, and re-layouts  1.25 us (2%)
    ppermute x24, starting transfers between devices, swap(): lax.ppermute(block, axis, [(i, i ^ bit) for i in range(lax.axis_size(axis...  22.8 us
    ppermute x24, waiting for transfers between devices, swap(): lax.ppermute(block, axis, [(i, i ^ bit) for i in range(lax.axis_size(axis...  14.3 us
    pallas_call x2, Pallas kernels, leaf_up(): pl.pallas_call(functools.partial(leaf_kernel, len(points)), grid_spec=plt...  6.81 us
    all_gather x1, blocking collectives, body(): incoming = lax.all_gather(shares, 'rhs', axis=0)  5.8 us
    pallas_call x1, Pallas kernels, pack(): pl.pallas_call(functools.partial(pack_kernel, per_dev), in_specs=[pl.Bloc...  2.99 us
    ppermute x1, waiting for transfers between devices, far_swap(): lax.ppermute(block, ('leaf', 'rhs'), [(i, i ^ flip) for i in range(count)])  2.74 us
    ppermute x1, starting transfers between devices, far_swap(): lax.ppermute(block, ('leaf', 'rhs'), [(i, i ^ flip) for i in range(count)])  2.34 us
    all_gather x1, blocking collectives, body(): both = lax.all_gather(tail, 'rhs', axis_index_groups=cores)  2.28 us
  transfers between devices with their start and end apart: 25, of which 10 were waited for; matrix products, arithmetic and copies ran while one was open for 0% of the time, Pallas kernels for 19%

profile of v7, /device:TPU:0, one launch (start us, length us, event | category | flops | bytes accessed | tf_op | source)
XLA Modules:
  0.0 67.0 jit_solution(4705726293782788539)
XLA Ops:
  0.0 2.9 %collective-permute-start = (bf16[64,1024]{1,0:T(8,128)(2,1)}, bf16[64,1024]{1,0:T(8,128)(2,1)S(1)}, u32[]{:S(2)}, u32[]{:S(2)}) collective-permute-start(bf16[64,1024]{1,0:T(8,128)(2,1)} %refs_0_.1), channel_id=1, source_target_pairs={{0,2},{1,3},{2,0},{3,1},{4,6},{5,7},{6,4},{7,5},{8,10},{9,11},{10,... | collective-permute-start | bytes 393224 | tf_op jit(solution)/shard_map/ppermute | solution.py:503
  2.9 3.0 %shard_map.82 = (bf16[3,128,768]{2,1,0:T(8,128)(2,1)}, bf16[128,768]{1,0:T(8,128)(2,1)}, bf16[4,128,1024]{2,1,0:T(8,128)(2,1)}, bf16[128,1024]{1,0:T(8,128)(2,1)}) custom-call(bf16[8,128,512]{2,1,0:T(8,128)(2,1)} %inverse.1, bf16[8,128,256]{2,1,0:T(8,128)(2,1)} %basis.1, bf16[8,128,256]{2,1,0:T(8,128)(2,1)} %coupling.1), custom_call_target="tpu_custom_call" | custom-call | bytes 4194 | tf_op jit(solution)/shard_map/pallas_call | solution.py:93
  5.9 0.7 %collective-permute-done.refs_1_ = bf16[64,1024]{1,0:T(8,128)(2,1)S(1)} collective-permute-done((bf16[64,1024]{1,0:T(8,128)(2,1)}, bf16[64,1024]{1,0:T(8,128)(2,1)S(1)}, u32[]{:S(2)}, u32[]{:S(2)}) %collective-permute-start) | collective-permute-done | bytes 131104 | tf_op jit(solution)/shard_map/ppermute | solution.py:503
  6.7 1.3 %collective-permute-done.2.refs_3_ = bf16[64,1024]{1,0:T(8,128)(2,1)S(1)} collective-permute-done((bf16[64,1024]{1,0:T(8,128)(2,1)S(1)}, bf16[64,1024]{1,0:T(8,128)(2,1)S(1)}, u32[]{:S(2)}, u32[]{:S(2)}) %collective-permute-start.2) | collective-permute-done | bytes 131104 | tf_op jit(solution)/shard_map/ppermute | solution.py:503
  8.0 0.1 collective-permute-start.3
  8.1 1.8 %collective-permute-start.7 = (bf16[3,128,768]{2,1,0:T(8,128)(2,1)}, bf16[3,128,768]{2,1,0:T(8,128)(2,1)S(1)}, u32[]{:S(2)}, u32[]{:S(2)}) collective-permute-start(bf16[3,128,768]{2,1,0:T(8,128)(2,1)} %get-tuple-element.46), channel_id=1, source_target_pairs={{0,2},{1,3},{2,0},{3,1},{4,6},{5,7},{6,4},{7,5},{8,10},{9,11},{10,... | collective-permute-start | bytes 1769480 | tf_op jit(solution)/shard_map/ppermute | solution.py:503
  9.9 1.5 %collective-permute-start.8 = (bf16[128,1024]{1,0:T(8,128)(2,1)}, bf16[128,1024]{1,0:T(8,128)(2,1)S(1)}, u32[]{:S(2)}, u32[]{:S(2)}) collective-permute-start(bf16[128,1024]{1,0:T(8,128)(2,1)} %get-tuple-element.64.mine_ref), channel_id=1, source_target_pairs={{0,4},{4,0},{8,12},{12,8},{16,20},{20,16},{24,28},{28,24},{1,5},{5... | collective-permute-start | bytes 786440 | tf_op jit(solution)/shard_map/ppermute | solution.py:503
  11.4 0.1 pad_add_fusion.side_ref
  11.5 0.1 pad_add_fusion.1.side_ref
  11.6 1.2 %copy-done.1 = bf16[8,128,512]{2,1,0:T(8,128)(2,1)S(1)} copy-done((bf16[8,128,512]{2,1,0:T(8,128)(2,1)S(1)}, bf16[8,128,512]{2,1,0:T(8,128)(2,1)}, u32[]{:S(2)}) %copy-start.1) | copy-done | bytes 1048600
  12.8 3.4 %shard_map.83 = (f32[4,64,128]{2,1,0:T(8,128)S(1)}, bf16[4,32,256]{2,1,0:T(8,128)(2,1)S(1)}, bf16[4,32,256]{2,1,0:T(8,128)(2,1)S(1)}, bf16[4,4,64,256]{3,2,1,0:T(8,128)(2,1)S(1)}) custom-call(s32[2]{0:T(128)S(1)} %pad_add_fusion.side_ref, bf16[64,1024]{1,0:T(8,128)(2,1)S(1)} %copy-done.6, bf16[64,1024]{1,0:T(8,128)(2,1)S(1)} %collective-permute-done.refs_1_, ...), custom_call_target="tpu_custom_call" | custom-call | flops 1140850 | bytes 983 | tf_op jit(solution)/shard_map/pallas_call | solution.py:246
  16.2 0.1 collective-permute-start.6
  16.3 1.4 %collective-permute-start.4 = (bf16[4,32,256]{2,1,0:T(8,128)(2,1)S(1)}, bf16[4,32,256]{2,1,0:T(8,128)(2,1)S(1)}, u32[]{:S(2)}, u32[]{:S(2)}) collective-permute-start(bf16[4,32,256]{2,1,0:T(8,128)(2,1)S(1)} %get-tuple-element.54), channel_id=1, source_target_pairs={{0,2},{1,3},{2,0},{3,1},{4,6},{5,7},{6,4},{7,5},{8,10},{9,11},{10,... | collective-permute-start | bytes 196616 | tf_op jit(solution)/shard_map/ppermute | solution.py:503
  17.7 3.4 %shard_map.84 = (f32[4,64,128]{2,1,0:T(8,128)S(1)}, bf16[4,32,256]{2,1,0:T(8,128)(2,1)S(1)}, bf16[4,32,256]{2,1,0:T(8,128)(2,1)S(1)}) custom-call(s32[2]{0:T(128)S(1)} %pad_add_fusion.1.side_ref, bf16[4,4,64,256]{3,2,1,0:T(8,128)(2,1)S(1)} %get-tuple-element.56.refs_0_, s32[1,4096]{1,0:T(1,128)S(1)} %bitcast.9, bf16[8,128,512]{2,1,0:T(8,128)(2,1)S(1)} %copy-done.1, ...), custom_call_target="tpu_custom_call" | custom-call | flops 1140850 | bytes 983 | tf_op jit(solution)/shard_map/pallas_call | solution.py:246
  21.1 0.5 collective-permute-start.5
  21.6 3.5 %collective-permute-done.6.refs_3_ = bf16[4,32,256]{2,1,0:T(8,128)(2,1)S(1)} collective-permute-done((bf16[4,32,256]{2,1,0:T(8,128)(2,1)S(1)}, bf16[4,32,256]{2,1,0:T(8,128)(2,1)S(1)}, u32[]{:S(2)}, u32[]{:S(2)}) %collective-permute-start.6) | collective-permute-done | bytes 65568 | tf_op jit(solution)/shard_map/ppermute | solution.py:503
  25.2 1.6 %collective-permute-done.4.refs_1_ = bf16[4,32,256]{2,1,0:T(8,128)(2,1)S(1)} collective-permute-done((bf16[4,32,256]{2,1,0:T(8,128)(2,1)S(1)}, bf16[4,32,256]{2,1,0:T(8,128)(2,1)S(1)}, u32[]{:S(2)}, u32[]{:S(2)}) %collective-permute-start.4) | collective-permute-done | bytes 65568 | tf_op jit(solution)/shard_map/ppermute | solution.py:503
  26.8 0.1 shard_map.85
  26.8 0.1 collective-permute-start.9
  26.9 1.8 %collective-permute-start.12 = (bf16[128,1024]{1,0:T(8,128)(2,1)S(1)}, bf16[128,1024]{1,0:T(8,128)(2,1)S(1)}, u32[]{:S(2)}, u32[]{:S(2)}) collective-permute-start(bf16[128,1024]{1,0:T(8,128)(2,1)S(1)} %get-tuple-element.73.refs_0_.refs_4_.refs_6_), channel_id=1, source_target_pairs={{0,2},{1,3},{2,0},{3,1},{4,6},{5,7},{6,4},{7,5},{8,10},{9,11},{10,... | collective-permute-start | bytes 786440 | tf_op jit(solution)/shard_map/ppermute | solution.py:503
  28.7 1.6 %collective-permute-start.18 = (bf16[128,1024]{1,0:T(8,128)(2,1)S(1)}, bf16[128,1024]{1,0:T(8,128)(2,1)S(1)}, u32[]{:S(2)}, u32[]{:S(2)}) collective-permute-start(bf16[128,1024]{1,0:T(8,128)(2,1)S(1)} %get-tuple-element.67.mine_ref), channel_id=1, source_target_pairs={{0,8},{4,12},{8,0},{12,4},{16,24},{20,28},{24,16},{28,20},{1,9},{5... | collective-permute-start | bytes 786440 | tf_op jit(solution)/shard_map/ppermute | solution.py:503
  30.3 1.5 %shard_map.86 = (f32[3,4,32,128]{3,2,1,0:T(8,128)S(1)}, bf16[32,256]{1,0:T(8,128)(2,1)S(1)}) custom-call(bf16[4,32,256]{2,1,0:T(8,128)(2,1)S(1)} %get-tuple-element.58.refs_0_, bf16[4,32,256]{2,1,0:T(8,128)(2,1)S(1)} %collective-permute-done.4.refs_1_, bf16[4,32,256]{2,1,0:T(8,128)(2,1)S(1)} %collective-permute-done.5.refs_2_, ...), custom_call_target="tpu_custom_call" | custom-call | flops 75497 | bytes 3145 | tf_op jit(solution)/shard_map/pallas_call | solution.py:309
  31.8 0.1 collective-permute-start.11
  31.9 0.6 collective-permute-start.10
  32.5 3.3 %collective-permute-done.12.refs_5_.refs_7_ = bf16[128,1024]{1,0:T(8,128)(2,1)S(1)} collective-permute-done((bf16[128,1024]{1,0:T(8,128)(2,1)S(1)}, bf16[128,1024]{1,0:T(8,128)(2,1)S(1)}, u32[]{:S(2)}, u32[]{:S(2)}) %collective-permute-start.12) | collective-permute-done | bytes 262176 | tf_op jit(solution)/shard_map/ppermute | solution.py:503
  35.8 0.2 collective-permute-done.10.other_ref
  36.0 1.1 %collective-permute-done.18.other_ref = bf16[128,1024]{1,0:T(8,128)(2,1)S(1)} collective-permute-done((bf16[128,1024]{1,0:T(8,128)(2,1)S(1)}, bf16[128,1024]{1,0:T(8,128)(2,1)S(1)}, u32[]{:S(2)}, u32[]{:S(2)}) %collective-permute-start.18) | collective-permute-done | bytes 262176 | tf_op jit(solution)/shard_map/ppermute | solution.py:503
  37.2 0.3 shard_map.88
  37.5 0.7 %collective-permute-start.19 = (bf16[128,1024]{1,0:T(8,128)(2,1)S(1)}, bf16[128,1024]{1,0:T(8,128)(2,1)S(1)}, u32[]{:S(2)}, u32[]{:S(2)}) collective-permute-start(bf16[128,1024]{1,0:T(8,128)(2,1)S(1)} %shard_map.91), channel_id=1, source_target_pairs={{0,2},{1,3},{2,0},{3,1},{4,6},{5,7},{6,4},{7,5},{8,10},{9,11},{10,... | collective-permute-start | bytes 786440 | tf_op jit(solution)/shard_map/ppermute | solution.py:503
  38.2 2.6 %collective-permute-start.23 = (bf16[128,512]{1,0:T(8,128)(2,1)S(1)}, bf16[128,512]{1,0:T(8,128)(2,1)S(1)}, u32[]{:S(2)}, u32[]{:S(2)}) collective-permute-start(bf16[128,512]{1,0:T(8,128)(2,1)S(1)} %get-tuple-element.84.mine_ref), channel_id=1, source_target_pairs={{0,16},{4,20},{8,24},{12,28},{16,0},{20,4},{24,8},{28,12},{1,17},{... | collective-permute-start | bytes 393224 | tf_op jit(solution)/shard_map/ppermute | solution.py:503
  40.8 2.3 %collective-permute-start.14 = (bf16[32,256]{1,0:T(8,128)(2,1)S(1)}, bf16[32,256]{1,0:T(8,128)(2,1)S(1)}, u32[]{:S(2)}, u32[]{:S(2)}) collective-permute-start(bf16[32,256]{1,0:T(8,128)(2,1)S(1)} %get-tuple-element.75.refs_3_.refs_1_), channel_id=1, source_target_pairs={{0,6},{1,7},{2,4},{3,5},{4,2},{5,3},{6,0},{7,1},{8,14},{9,15},{10,... | collective-permute-start | bytes 49160 | tf_op jit(solution)/shard_map/ppermute | solution.py:510
  43.1 0.5 collective-permute-start.15
  43.6 0.6 collective-permute-start.16
  44.3 2.7 %collective-permute-done.14.refs_0_ = bf16[32,256]{1,0:T(8,128)(2,1)S(1)} collective-permute-done((bf16[32,256]{1,0:T(8,128)(2,1)S(1)}, bf16[32,256]{1,0:T(8,128)(2,1)S(1)}, u32[]{:S(2)}, u32[]{:S(2)}) %collective-permute-start.14) | collective-permute-done | bytes 16416 | tf_op jit(solution)/shard_map/ppermute | solution.py:510
  47.0 0.0 collective-permute-done.15.refs_1_
  47.1 0.3 collective-permute-done.16.refs_2_
  47.4 0.6 shard_map.89
  48.1 1.1 %collective-permute-start.24 = (bf16[128,1280]{1,0:T(8,128)(2,1)S(1)}, bf16[128,1280]{1,0:T(8,128)(2,1)S(1)}, u32[]{:S(2)}, u32[]{:S(2)}) collective-permute-start(bf16[128,1280]{1,0:T(8,128)(2,1)S(1)} %shard_map.96), channel_id=1, source_target_pairs={{0,2},{1,3},{2,0},{3,1},{4,6},{5,7},{6,4},{7,5},{8,10},{9,11},{10,... | collective-permute-start | bytes 983048 | tf_op jit(solution)/shard_map/ppermute | solution.py:503
  49.2 0.1 collective-permute-start.20
  49.3 0.5 collective-permute-start.21
  49.8 1.6 %collective-permute-start.17 = (bf16[32,256]{1,0:T(8,128)(2,1)S(1)}, bf16[32,256]{1,0:T(8,128)(2,1)S(1)}, u32[]{:S(2)}, u32[]{:S(2)}) collective-permute-start(bf16[32,256]{1,0:T(8,128)(2,1)S(1)} %get-tuple-element.76.refs_1_.refs_0_.refs_2_), channel_id=1, source_target_pairs={{0,8},{4,12},{8,0},{12,4},{16,24},{20,28},{24,16},{28,20},{1,9},{5... | collective-permute-start | bytes 49160 | tf_op jit(solution)/shard_map/ppermute | solution.py:503
  51.4 2.2 %collective-permute-done.17.refs_1_ = bf16[32,256]{1,0:T(8,128)(2,1)S(1)} collective-permute-done((bf16[32,256]{1,0:T(8,128)(2,1)S(1)}, bf16[32,256]{1,0:T(8,128)(2,1)S(1)}, u32[]{:S(2)}, u32[]{:S(2)}) %collective-permute-start.17) | collective-permute-done | bytes 16416 | tf_op jit(solution)/shard_map/ppermute | solution.py:503
  53.6 0.6 shard_map.94
  54.2 2.6 %collective-permute-start.22 = (bf16[32,256]{1,0:T(8,128)(2,1)S(1)}, bf16[32,256]{1,0:T(8,128)(2,1)S(1)}, u32[]{:S(2)}, u32[]{:S(2)}) collective-permute-start(bf16[32,256]{1,0:T(8,128)(2,1)S(1)} %get-tuple-element.79._.refs_0_), channel_id=1, source_target_pairs={{0,16},{4,20},{8,24},{12,28},{16,0},{20,4},{24,8},{28,12},{1,17},{... | collective-permute-start | bytes 49160 | tf_op jit(solution)/shard_map/ppermute | solution.py:503
  56.8 2.3 %all-gather = bf16[256,1280]{1,0:T(8,128)(2,1)S(1)} all-gather(bf16[128,1280]{1,0:T(8,128)(2,1)S(1)} %shard_map.97), channel_id=2, replica_groups={{0,1},{2,3},{4,5},{6,7},{8,9},{10,11},{12,13},{14,15},{16,17},{18,19},{..., dimensions={0}, use_global_device_ids=true | all-gather | bytes 983040 | tf_op jit(solution)/shard_map/all_gather | solution.py:606
  59.1 1.1 %shard_map.98 = bf16[4,32,256]{2,1,0:T(8,128)(2,1)S(1)} custom-call(bf16[32,256]{1,0:T(8,128)(2,1)S(1)} %get-tuple-element.79._.refs_0_, bf16[32,256]{1,0:T(8,128)(2,1)S(1)} %collective-permute-done.22.refs_1_, f32[4,32,128]{2,1,0:T(8,128)S(1)} %get-tuple-element.80.refs_2_, f32[4,32,128]{2,1,0:T(8,128)S(1)} %get-tuple-element.81.refs_3_, ...), custom_call_target="tpu_custom_call" | custom-call | flops 67108 | bytes 4194 | tf_op jit(solution)/shard_map/pallas_call | solution.py:471
  60.2 5.8 %all-gather.1 = bf16[16,32,256]{2,1,0:T(8,128)(2,1)S(1)} all-gather(bf16[4,32,256]{2,1,0:T(8,128)(2,1)S(1)} %shard_map.98), channel_id=3, replica_groups=mesh['leaf'=8,'rhs'=4] {'rhs'}, dimensions={0}, use_global_device_ids=true | all-gather | bytes 327680 | tf_op jit(solution)/shard_map/all_gather | solution.py:609
  66.0 1.0 %shard_map.99 = f32[8,64,128]{2,1,0:T(8,128)} custom-call(f32[4,64,128]{2,1,0:T(8,128)S(1)} %get-tuple-element.50.far_ref, f32[4,64,128]{2,1,0:T(8,128)S(1)} %get-tuple-element.57.own_ref, bf16[4,4,32,256]{3,2,1,0:T(8,128)(2,1)S(1)} %bitcast.7, bf16[8,128,256]{2,1,0:T(8,128)(2,1)S(1)} %copy-done.3), custom_call_target="tpu_custom_call" | custom-call | flops 33554 | bytes 524 | tf_op jit(solution)/shard_map/pallas_call | solution.py:494
  (40 shorter events, 0.3 us)
Async XLA Ops:
  0.0 11.6 %copy-start.2 = (bf16[8,128,256]{2,1,0:T(8,128)(2,1)S(1)}, bf16[8,128,256]{2,1,0:T(8,128)(2,1)}, u32[]{:S(2)}) copy-start(bf16[8,128,256]{2,1,0:T(8,128)(2,1)} %refs_3_.1) | copy-start | bytes 1572868
  0.0 6.6 %collective-permute-start = (bf16[64,1024]{1,0:T(8,128)(2,1)}, bf16[64,1024]{1,0:T(8,128)(2,1)S(1)}, u32[]{:S(2)}, u32[]{:S(2)}) collective-permute-start(bf16[64,1024]{1,0:T(8,128)(2,1)} %refs_0_.1), channel_id=1, source_target_pairs={{0,2},{1,3},{2,0},{3,1},{4,6},{5,7},{6,4},{7,5},{8,10},{9,11},{10,... | collective-permute-start | bytes 393224 | tf_op jit(solution)/shard_map/ppermute | solution.py:503
  2.9 3.7 %collective-permute-start.1 = (bf16[64,1024]{1,0:T(8,128)(2,1)}, bf16[64,1024]{1,0:T(8,128)(2,1)S(1)}, u32[]{:S(2)}, u32[]{:S(2)}) collective-permute-start(bf16[64,1024]{1,0:T(8,128)(2,1)} %refs_0_.1), channel_id=1, source_target_pairs={{0,1},{1,0},{2,3},{3,2},{4,5},{5,4},{6,7},{7,6},{8,9},{9,8},{10,11... | collective-permute-start | bytes 393224 | tf_op jit(solution)/shard_map/ppermute | solution.py:503
  2.9 8.6 %copy-start.6 = (bf16[64,1024]{1,0:T(8,128)(2,1)S(1)}, bf16[64,1024]{1,0:T(8,128)(2,1)}, u32[]{:S(2)}) copy-start(bf16[64,1024]{1,0:T(8,128)(2,1)} %refs_0_.1) | copy-start | bytes 393220
  6.6 1.3 %collective-permute-start.2 = (bf16[64,1024]{1,0:T(8,128)(2,1)S(1)}, bf16[64,1024]{1,0:T(8,128)(2,1)S(1)}, u32[]{:S(2)}, u32[]{:S(2)}) collective-permute-start(bf16[64,1024]{1,0:T(8,128)(2,1)S(1)} %collective-permute-done.refs_1_), channel_id=1, source_target_pairs={{0,1},{1,0},{2,3},{3,2},{4,5},{5,4},{6,7},{7,6},{8,9},{9,8},{10,11... | collective-permute-start | bytes 393224 | tf_op jit(solution)/shard_map/ppermute | solution.py:503
  8.0 9.7 %collective-permute-start.3 = (bf16[4,128,1024]{2,1,0:T(8,128)(2,1)}, bf16[4,128,1024]{2,1,0:T(8,128)(2,1)S(1)}, u32[]{:S(2)}, u32[]{:S(2)}) collective-permute-start(bf16[4,128,1024]{2,1,0:T(8,128)(2,1)} %get-tuple-element.53.refs_4_.own_ref.refs_15_), channel_id=1, source_target_pairs={{0,1},{1,0},{2,3},{3,2},{4,5},{5,4},{6,7},{7,6},{8,9},{9,8},{10,11... | collective-permute-start | bytes 3145736 | tf_op jit(solution)/shard_map/ppermute | solution.py:503
  8.1 18.7 %collective-permute-start.7 = (bf16[3,128,768]{2,1,0:T(8,128)(2,1)}, bf16[3,128,768]{2,1,0:T(8,128)(2,1)S(1)}, u32[]{:S(2)}, u32[]{:S(2)}) collective-permute-start(bf16[3,128,768]{2,1,0:T(8,128)(2,1)} %get-tuple-element.46), channel_id=1, source_target_pairs={{0,2},{1,3},{2,0},{3,1},{4,6},{5,7},{6,4},{7,5},{8,10},{9,11},{10,... | collective-permute-start | bytes 1769480 | tf_op jit(solution)/shard_map/ppermute | solution.py:503
  9.9 1.7 %copy-start.7 = (s32[4096]{0:T(1024)S(1)}, s32[4096]{0:T(1024)}, u32[]{:S(2)}) copy-start(s32[4096]{0:T(1024)} %param.9) | copy-start | bytes 49156
  9.9 11.7 %collective-permute-start.8 = (bf16[128,1024]{1,0:T(8,128)(2,1)}, bf16[128,1024]{1,0:T(8,128)(2,1)S(1)}, u32[]{:S(2)}, u32[]{:S(2)}) collective-permute-start(bf16[128,1024]{1,0:T(8,128)(2,1)} %get-tuple-element.64.mine_ref), channel_id=1, source_target_pairs={{0,4},{4,0},{8,12},{12,8},{16,20},{20,16},{24,28},{28,24},{1,5},{5... | collective-permute-start | bytes 786440 | tf_op jit(solution)/shard_map/ppermute | solution.py:503
  11.6 1.2 %copy-start.1 = (bf16[8,128,512]{2,1,0:T(8,128)(2,1)S(1)}, bf16[8,128,512]{2,1,0:T(8,128)(2,1)}, u32[]{:S(2)}) copy-start(bf16[8,128,512]{2,1,0:T(8,128)(2,1)} %refs_2_.1) | copy-start | bytes 3145732
  16.2 8.9 %collective-permute-start.6 = (bf16[4,32,256]{2,1,0:T(8,128)(2,1)S(1)}, bf16[4,32,256]{2,1,0:T(8,128)(2,1)S(1)}, u32[]{:S(2)}, u32[]{:S(2)}) collective-permute-start(bf16[4,32,256]{2,1,0:T(8,128)(2,1)S(1)} %get-tuple-element.61), channel_id=1, source_target_pairs={{0,3},{1,2},{2,1},{3,0},{4,7},{5,6},{6,5},{7,4},{8,11},{9,10},{10,... | collective-permute-start | bytes 196616 | tf_op jit(solution)/shard_map/ppermute | solution.py:503
  16.3 10.4 %collective-permute-start.4 = (bf16[4,32,256]{2,1,0:T(8,128)(2,1)S(1)}, bf16[4,32,256]{2,1,0:T(8,128)(2,1)S(1)}, u32[]{:S(2)}, u32[]{:S(2)}) collective-permute-start(bf16[4,32,256]{2,1,0:T(8,128)(2,1)S(1)} %get-tuple-element.54), channel_id=1, source_target_pairs={{0,2},{1,3},{2,0},{3,1},{4,6},{5,7},{6,4},{7,5},{8,10},{9,11},{10,... | collective-permute-start | bytes 196616 | tf_op jit(solution)/shard_map/ppermute | solution.py:503
  17.7 9.1 %copy-start.4 = (bf16[128,1024]{1,0:T(8,128)(2,1)S(1)}, bf16[128,1024]{1,0:T(8,128)(2,1)}, u32[]{:S(2)}) copy-start(bf16[128,1024]{1,0:T(8,128)(2,1)} %get-tuple-element.64.mine_ref) | copy-start | bytes 786436
  17.7 9.1 %copy-start.5 = (bf16[128,768]{1,0:T(8,128)(2,1)S(1)}, bf16[128,768]{1,0:T(8,128)(2,1)}, u32[]{:S(2)}) copy-start(bf16[128,768]{1,0:T(8,128)(2,1)} %get-tuple-element.66.refs_0_) | copy-start | bytes 589828
  17.7 12.6 %copy-start = (bf16[4,128,1024]{2,1,0:T(8,128)(2,1)S(1)}, bf16[4,128,1024]{2,1,0:T(8,128)(2,1)}, u32[]{:S(2)}) copy-start(bf16[4,128,1024]{2,1,0:T(8,128)(2,1)} %get-tuple-element.53.refs_4_.own_ref.refs_15_) | copy-start | bytes 3145732
  21.1 5.7 %collective-permute-start.5 = (bf16[4,32,256]{2,1,0:T(8,128)(2,1)S(1)}, bf16[4,32,256]{2,1,0:T(8,128)(2,1)S(1)}, u32[]{:S(2)}, u32[]{:S(2)}) collective-permute-start(bf16[4,32,256]{2,1,0:T(8,128)(2,1)S(1)} %get-tuple-element.60), channel_id=1, source_target_pairs={{0,1},{1,0},{2,3},{3,2},{4,5},{5,4},{6,7},{7,6},{8,9},{9,8},{10,11... | collective-permute-start | bytes 196616 | tf_op jit(solution)/shard_map/ppermute | solution.py:503
  26.8 3.5 %collective-permute-start.9 = (bf16[3,128,768]{2,1,0:T(8,128)(2,1)S(1)}, bf16[3,128,768]{2,1,0:T(8,128)(2,1)S(1)}, u32[]{:S(2)}, u32[]{:S(2)}) collective-permute-start(bf16[3,128,768]{2,1,0:T(8,128)(2,1)S(1)} %collective-permute-done.7.refs_5_), channel_id=1, source_target_pairs={{0,1},{1,0},{2,3},{3,2},{4,5},{5,4},{6,7},{7,6},{8,9},{9,8},{10,11... | collective-permute-start | bytes 1769480 | tf_op jit(solution)/shard_map/ppermute | solution.py:503
  26.9 8.9 %collective-permute-start.12 = (bf16[128,1024]{1,0:T(8,128)(2,1)S(1)}, bf16[128,1024]{1,0:T(8,128)(2,1)S(1)}, u32[]{:S(2)}, u32[]{:S(2)}) collective-permute-start(bf16[128,1024]{1,0:T(8,128)(2,1)S(1)} %get-tuple-element.73.refs_0_.refs_4_.refs_6_), channel_id=1, source_target_pairs={{0,2},{1,3},{2,0},{3,1},{4,6},{5,7},{6,4},{7,5},{8,10},{9,11},{10,... | collective-permute-start | bytes 786440 | tf_op jit(solution)/shard_map/ppermute | solution.py:503
  28.7 8.4 %collective-permute-start.18 = (bf16[128,1024]{1,0:T(8,128)(2,1)S(1)}, bf16[128,1024]{1,0:T(8,128)(2,1)S(1)}, u32[]{:S(2)}, u32[]{:S(2)}) collective-permute-start(bf16[128,1024]{1,0:T(8,128)(2,1)S(1)} %get-tuple-element.67.mine_ref), channel_id=1, source_target_pairs={{0,8},{4,12},{8,0},{12,4},{16,24},{20,28},{24,16},{28,20},{1,9},{5... | collective-permute-start | bytes 786440 | tf_op jit(solution)/shard_map/ppermute | solution.py:503
  31.8 5.3 %collective-permute-start.11 = (bf16[128,1024]{1,0:T(8,128)(2,1)S(1)}, bf16[128,1024]{1,0:T(8,128)(2,1)S(1)}, u32[]{:S(2)}, u32[]{:S(2)}) collective-permute-start(bf16[128,1024]{1,0:T(8,128)(2,1)S(1)} %shard_map.87), channel_id=1, source_target_pairs={{0,1},{1,0},{2,3},{3,2},{4,5},{5,4},{6,7},{7,6},{8,9},{9,8},{10,11... | collective-permute-start | bytes 786440 | tf_op jit(solution)/shard_map/ppermute | solution.py:503
  31.9 4.1 %collective-permute-start.10 = (bf16[32,256]{1,0:T(8,128)(2,1)S(1)}, bf16[32,256]{1,0:T(8,128)(2,1)S(1)}, u32[]{:S(2)}, u32[]{:S(2)}) collective-permute-start(bf16[32,256]{1,0:T(8,128)(2,1)S(1)} %get-tuple-element.69.refs_1_.mine_ref), channel_id=1, source_target_pairs={{0,2},{1,3},{2,0},{3,1},{4,6},{5,7},{6,4},{7,5},{8,10},{9,11},{10,... | collective-permute-start | bytes 49160 | tf_op jit(solution)/shard_map/ppermute | solution.py:503
  36.0 4.8 %collective-permute-start.13 = (bf16[128,1024]{1,0:T(8,128)(2,1)S(1)}, bf16[128,1024]{1,0:T(8,128)(2,1)S(1)}, u32[]{:S(2)}, u32[]{:S(2)}) collective-permute-start(bf16[128,1024]{1,0:T(8,128)(2,1)S(1)} %collective-permute-done.12.refs_5_.refs_7_), channel_id=1, source_target_pairs={{0,1},{1,0},{2,3},{3,2},{4,5},{5,4},{6,7},{7,6},{8,9},{9,8},{10,11... | collective-permute-start | bytes 786440 | tf_op jit(solution)/shard_map/ppermute | solution.py:503
  37.5 11.8 %collective-permute-start.19 = (bf16[128,1024]{1,0:T(8,128)(2,1)S(1)}, bf16[128,1024]{1,0:T(8,128)(2,1)S(1)}, u32[]{:S(2)}, u32[]{:S(2)}) collective-permute-start(bf16[128,1024]{1,0:T(8,128)(2,1)S(1)} %shard_map.91), channel_id=1, source_target_pairs={{0,2},{1,3},{2,0},{3,1},{4,6},{5,7},{6,4},{7,5},{8,10},{9,11},{10,... | collective-permute-start | bytes 786440 | tf_op jit(solution)/shard_map/ppermute | solution.py:503
  38.2 9.8 %collective-permute-start.23 = (bf16[128,512]{1,0:T(8,128)(2,1)S(1)}, bf16[128,512]{1,0:T(8,128)(2,1)S(1)}, u32[]{:S(2)}, u32[]{:S(2)}) collective-permute-start(bf16[128,512]{1,0:T(8,128)(2,1)S(1)} %get-tuple-element.84.mine_ref), channel_id=1, source_target_pairs={{0,16},{4,20},{8,24},{12,28},{16,0},{20,4},{24,8},{28,12},{1,17},{... | collective-permute-start | bytes 393224 | tf_op jit(solution)/shard_map/ppermute | solution.py:503
  40.8 6.2 %collective-permute-start.14 = (bf16[32,256]{1,0:T(8,128)(2,1)S(1)}, bf16[32,256]{1,0:T(8,128)(2,1)S(1)}, u32[]{:S(2)}, u32[]{:S(2)}) collective-permute-start(bf16[32,256]{1,0:T(8,128)(2,1)S(1)} %get-tuple-element.75.refs_3_.refs_1_), channel_id=1, source_target_pairs={{0,6},{1,7},{2,4},{3,5},{4,2},{5,3},{6,0},{7,1},{8,14},{9,15},{10,... | collective-permute-start | bytes 49160 | tf_op jit(solution)/shard_map/ppermute | solution.py:510
  43.1 3.9 %collective-permute-start.15 = (bf16[32,256]{1,0:T(8,128)(2,1)S(1)}, bf16[32,256]{1,0:T(8,128)(2,1)S(1)}, u32[]{:S(2)}, u32[]{:S(2)}) collective-permute-start(bf16[32,256]{1,0:T(8,128)(2,1)S(1)} %get-tuple-element.75.refs_3_.refs_1_), channel_id=1, source_target_pairs={{0,4},{4,0},{8,12},{12,8},{16,20},{20,16},{24,28},{28,24},{1,5},{5... | collective-permute-start | bytes 49160 | tf_op jit(solution)/shard_map/ppermute | solution.py:503
  43.6 3.7 %collective-permute-start.16 = (bf16[32,256]{1,0:T(8,128)(2,1)S(1)}, bf16[32,256]{1,0:T(8,128)(2,1)S(1)}, u32[]{:S(2)}, u32[]{:S(2)}) collective-permute-start(bf16[32,256]{1,0:T(8,128)(2,1)S(1)} %get-tuple-element.75.refs_3_.refs_1_), channel_id=1, source_target_pairs={{0,2},{1,3},{2,0},{3,1},{4,6},{5,7},{6,4},{7,5},{8,10},{9,11},{10,... | collective-permute-start | bytes 49160 | tf_op jit(solution)/shard_map/ppermute | solution.py:503
  48.1 8.7 %collective-permute-start.24 = (bf16[128,1280]{1,0:T(8,128)(2,1)S(1)}, bf16[128,1280]{1,0:T(8,128)(2,1)S(1)}, u32[]{:S(2)}, u32[]{:S(2)}) collective-permute-start(bf16[128,1280]{1,0:T(8,128)(2,1)S(1)} %shard_map.96), channel_id=1, source_target_pairs={{0,2},{1,3},{2,0},{3,1},{4,6},{5,7},{6,4},{7,5},{8,10},{9,11},{10,... | collective-permute-start | bytes 983048 | tf_op jit(solution)/shard_map/ppermute | solution.py:503
  49.2 4.4 %collective-permute-start.20 = (bf16[128,1024]{1,0:T(8,128)(2,1)S(1)}, bf16[128,1024]{1,0:T(8,128)(2,1)S(1)}, u32[]{:S(2)}, u32[]{:S(2)}) collective-permute-start(bf16[128,1024]{1,0:T(8,128)(2,1)S(1)} %shard_map.92), channel_id=1, source_target_pairs={{0,1},{1,0},{2,3},{3,2},{4,5},{5,4},{6,7},{7,6},{8,9},{9,8},{10,11... | collective-permute-start | bytes 786440 | tf_op jit(solution)/shard_map/ppermute | solution.py:503
  49.3 4.3 %collective-permute-start.21 = (bf16[128,1024]{1,0:T(8,128)(2,1)S(1)}, bf16[128,1024]{1,0:T(8,128)(2,1)S(1)}, u32[]{:S(2)}, u32[]{:S(2)}) collective-permute-start(bf16[128,1024]{1,0:T(8,128)(2,1)S(1)} %shard_map.93), channel_id=1, source_target_pairs={{0,1},{1,0},{2,3},{3,2},{4,5},{5,4},{6,7},{7,6},{8,9},{9,8},{10,11... | collective-permute-start | bytes 786440 | tf_op jit(solution)/shard_map/ppermute | solution.py:503
  49.8 3.7 %collective-permute-start.17 = (bf16[32,256]{1,0:T(8,128)(2,1)S(1)}, bf16[32,256]{1,0:T(8,128)(2,1)S(1)}, u32[]{:S(2)}, u32[]{:S(2)}) collective-permute-start(bf16[32,256]{1,0:T(8,128)(2,1)S(1)} %get-tuple-element.76.refs_1_.refs_0_.refs_2_), channel_id=1, source_target_pairs={{0,8},{4,12},{8,0},{12,4},{16,24},{20,28},{24,16},{28,20},{1,9},{5... | collective-permute-start | bytes 49160 | tf_op jit(solution)/shard_map/ppermute | solution.py:503
  54.2 4.9 %collective-permute-start.22 = (bf16[32,256]{1,0:T(8,128)(2,1)S(1)}, bf16[32,256]{1,0:T(8,128)(2,1)S(1)}, u32[]{:S(2)}, u32[]{:S(2)}) collective-permute-start(bf16[32,256]{1,0:T(8,128)(2,1)S(1)} %get-tuple-element.79._.refs_0_), channel_id=1, source_target_pairs={{0,16},{4,20},{8,24},{12,28},{16,0},{20,4},{24,8},{28,12},{1,17},{... | collective-permute-start | bytes 49160 | tf_op jit(solution)/shard_map/ppermute | solution.py:503
  59.1 6.9 %copy-start.3 = (bf16[8,128,256]{2,1,0:T(8,128)(2,1)S(1)}, bf16[8,128,256]{2,1,0:T(8,128)(2,1)}, u32[]{:S(2)}) copy-start(bf16[8,128,256]{2,1,0:T(8,128)(2,1)} %coupling_ref.1) | copy-start | bytes 1572868

commit v8 on v7

--- a/solution.py
+++ b/solution.py
@@ -477,23 +477,35 @@
     )(*operands)
 
 
-def finish_kernel(far_ref, own_ref, incoming_ref, coupling_ref, out_ref):
+def finish_kernel(far_ref, own_ref, incoming_ref, coupling_ref, out_ref, results, sems):
     half = own_ref.shape[0]
     high = lax.axis_index("rhs") // CORES
-    for values_ref, side in ((far_ref, 1 - high), (own_ref, high)):
+    started = []
+    for part, (values_ref, side) in enumerate(((own_ref, high), (far_ref, 1 - high))):
         for i in range(half):
             leaf = side * half + i
+            slot = part * half + i
             incoming = jnp.concatenate(
                 [incoming_ref[side * CORES + core, i] for core in range(CORES)], axis=0
             )
-            out_ref[leaf] = values_ref[i] - dot_rows(incoming, coupling_ref[leaf])
+            results[slot] = values_ref[i] - dot_rows(incoming, coupling_ref[leaf])
+            copy = pltpu.make_async_copy(results.at[slot], out_ref.at[leaf], sems.at[slot])
+            copy.start()
+            started.append(copy)
+    for copy in started:
+        copy.wait()
 
 
 def finish(far, own, incoming, coupling):
     half, targets, rows = own.shape
+    shape = (2 * half, targets, rows)
+    vmem = pl.BlockSpec(memory_space=pltpu.VMEM)
     return pl.pallas_call(
         finish_kernel,
-        out_shape=jax.ShapeDtypeStruct((2 * half, targets, rows), jnp.float32),
+        in_specs=[vmem] * 4,
+        out_specs=pl.BlockSpec(memory_space=pl.ANY),
+        out_shape=jax.ShapeDtypeStruct(shape, jnp.float32),
+        scratch_shapes=[pltpu.VMEM(shape, jnp.float32), pltpu.SemaphoreType.DMA((2 * half,))],
         compiler_params=params(),
         cost_estimate=cost(4 * half * targets * rows * coupling.shape[2], 16 * own.size),
     )(far, own, incoming, coupling)

time: 67.2 us -> 67.2 us (level)
  no operation moved by 1% of the time
where the time goes in v8:
time: 67.2 us; the launch traced here: 67 us
  starting transfers between devices  25.2 us (38%)
  waiting for transfers between devices  17.1 us (25%)
  Pallas kernels  15.1 us (22%)
  blocking collectives  8.07 us (12%)
  local copies, waits for them, and re-layouts  1.25 us (2%)
    ppermute x24, starting transfers between devices, swap(): lax.ppermute(block, axis, [(i, i ^ bit) for i in range(lax.axis_size(axis...  22.8 us
    ppermute x24, waiting for transfers between devices, swap(): lax.ppermute(block, axis, [(i, i ^ bit) for i in range(lax.axis_size(axis...  14.3 us
    pallas_call x2, Pallas kernels, leaf_up(): pl.pallas_call(functools.partial(leaf_kernel, len(points)), grid_spec=plt...  6.81 us
    all_gather x1, blocking collectives, body(): incoming = lax.all_gather(shares, 'rhs', axis=0)  5.8 us
    pallas_call x1, Pallas kernels, pack(): pl.pallas_call(functools.partial(pack_kernel, per_dev), in_specs=[pl.Bloc...  2.99 us
    ppermute x1, waiting for transfers between devices, far_swap(): lax.ppermute(block, ('leaf', 'rhs'), [(i, i ^ flip) for i in range(count)])  2.74 us
    ppermute x1, starting transfers between devices, far_swap(): lax.ppermute(block, ('leaf', 'rhs'), [(i, i ^ flip) for i in range(count)])  2.34 us
    all_gather x1, blocking collectives, body(): both = lax.all_gather(tail, 'rhs', axis_index_groups=cores)  2.28 us
  transfers between devices with their start and end apart: 25, of which 10 were waited for; matrix products, arithmetic and copies ran while one was open for 0% of the time, Pallas kernels for 19%

profile of v8, /device:TPU:0, one launch (start us, length us, event | category | flops | bytes accessed | tf_op | source)
XLA Modules:
  0.0 67.0 jit_solution(13420581199914730385)
XLA Ops:
  0.0 2.9 %collective-permute-start = (bf16[64,1024]{1,0:T(8,128)(2,1)}, bf16[64,1024]{1,0:T(8,128)(2,1)S(1)}, u32[]{:S(2)}, u32[]{:S(2)}) collective-permute-start(bf16[64,1024]{1,0:T(8,128)(2,1)} %refs_0_.1), channel_id=1, source_target_pairs={{0,2},{1,3},{2,0},{3,1},{4,6},{5,7},{6,4},{7,5},{8,10},{9,11},{10,... | collective-permute-start | bytes 393224 | tf_op jit(solution)/shard_map/ppermute | solution.py:515
  2.9 3.0 %shard_map.82 = (bf16[3,128,768]{2,1,0:T(8,128)(2,1)}, bf16[128,768]{1,0:T(8,128)(2,1)}, bf16[4,128,1024]{2,1,0:T(8,128)(2,1)}, bf16[128,1024]{1,0:T(8,128)(2,1)}) custom-call(bf16[8,128,512]{2,1,0:T(8,128)(2,1)} %inverse.1, bf16[8,128,256]{2,1,0:T(8,128)(2,1)} %basis.1, bf16[8,128,256]{2,1,0:T(8,128)(2,1)} %coupling.1), custom_call_target="tpu_custom_call" | custom-call | bytes 4194 | tf_op jit(solution)/shard_map/pallas_call | solution.py:93
  5.9 0.7 %collective-permute-done.refs_1_ = bf16[64,1024]{1,0:T(8,128)(2,1)S(1)} collective-permute-done((bf16[64,1024]{1,0:T(8,128)(2,1)}, bf16[64,1024]{1,0:T(8,128)(2,1)S(1)}, u32[]{:S(2)}, u32[]{:S(2)}) %collective-permute-start) | collective-permute-done | bytes 131104 | tf_op jit(solution)/shard_map/ppermute | solution.py:515
  6.7 1.3 %collective-permute-done.2.refs_3_ = bf16[64,1024]{1,0:T(8,128)(2,1)S(1)} collective-permute-done((bf16[64,1024]{1,0:T(8,128)(2,1)S(1)}, bf16[64,1024]{1,0:T(8,128)(2,1)S(1)}, u32[]{:S(2)}, u32[]{:S(2)}) %collective-permute-start.2) | collective-permute-done | bytes 131104 | tf_op jit(solution)/shard_map/ppermute | solution.py:515
  8.0 0.1 collective-permute-start.3
  8.1 1.8 %collective-permute-start.7 = (bf16[3,128,768]{2,1,0:T(8,128)(2,1)}, bf16[3,128,768]{2,1,0:T(8,128)(2,1)S(1)}, u32[]{:S(2)}, u32[]{:S(2)}) collective-permute-start(bf16[3,128,768]{2,1,0:T(8,128)(2,1)} %get-tuple-element.46), channel_id=1, source_target_pairs={{0,2},{1,3},{2,0},{3,1},{4,6},{5,7},{6,4},{7,5},{8,10},{9,11},{10,... | collective-permute-start | bytes 1769480 | tf_op jit(solution)/shard_map/ppermute | solution.py:515
  9.9 1.5 %collective-permute-start.8 = (bf16[128,1024]{1,0:T(8,128)(2,1)}, bf16[128,1024]{1,0:T(8,128)(2,1)S(1)}, u32[]{:S(2)}, u32[]{:S(2)}) collective-permute-start(bf16[128,1024]{1,0:T(8,128)(2,1)} %get-tuple-element.64.mine_ref), channel_id=1, source_target_pairs={{0,4},{4,0},{8,12},{12,8},{16,20},{20,16},{24,28},{28,24},{1,5},{5... | collective-permute-start | bytes 786440 | tf_op jit(solution)/shard_map/ppermute | solution.py:515
  11.4 0.1 pad_add_fusion.side_ref
  11.5 0.1 pad_add_fusion.1.side_ref
  11.6 1.2 %copy-done.1 = bf16[8,128,512]{2,1,0:T(8,128)(2,1)S(1)} copy-done((bf16[8,128,512]{2,1,0:T(8,128)(2,1)S(1)}, bf16[8,128,512]{2,1,0:T(8,128)(2,1)}, u32[]{:S(2)}) %copy-start.1) | copy-done | bytes 1048600
  12.8 3.4 %shard_map.83 = (f32[4,64,128]{2,1,0:T(8,128)S(1)}, bf16[4,32,256]{2,1,0:T(8,128)(2,1)S(1)}, bf16[4,32,256]{2,1,0:T(8,128)(2,1)S(1)}, bf16[4,4,64,256]{3,2,1,0:T(8,128)(2,1)S(1)}) custom-call(s32[2]{0:T(128)S(1)} %pad_add_fusion.side_ref, bf16[64,1024]{1,0:T(8,128)(2,1)S(1)} %copy-done.6, bf16[64,1024]{1,0:T(8,128)(2,1)S(1)} %collective-permute-done.refs_1_, ...), custom_call_target="tpu_custom_call" | custom-call | flops 1140850 | bytes 983 | tf_op jit(solution)/shard_map/pallas_call | solution.py:246
  16.2 0.1 collective-permute-start.6
  16.3 1.4 %collective-permute-start.4 = (bf16[4,32,256]{2,1,0:T(8,128)(2,1)S(1)}, bf16[4,32,256]{2,1,0:T(8,128)(2,1)S(1)}, u32[]{:S(2)}, u32[]{:S(2)}) collective-permute-start(bf16[4,32,256]{2,1,0:T(8,128)(2,1)S(1)} %get-tuple-element.54), channel_id=1, source_target_pairs={{0,2},{1,3},{2,0},{3,1},{4,6},{5,7},{6,4},{7,5},{8,10},{9,11},{10,... | collective-permute-start | bytes 196616 | tf_op jit(solution)/shard_map/ppermute | solution.py:515
  17.7 3.4 %shard_map.84 = (f32[4,64,128]{2,1,0:T(8,128)S(1)}, bf16[4,32,256]{2,1,0:T(8,128)(2,1)S(1)}, bf16[4,32,256]{2,1,0:T(8,128)(2,1)S(1)}) custom-call(s32[2]{0:T(128)S(1)} %pad_add_fusion.1.side_ref, bf16[4,4,64,256]{3,2,1,0:T(8,128)(2,1)S(1)} %get-tuple-element.56.refs_0_, s32[1,4096]{1,0:T(1,128)S(1)} %bitcast.9, bf16[8,128,512]{2,1,0:T(8,128)(2,1)S(1)} %copy-done.1, ...), custom_call_target="tpu_custom_call" | custom-call | flops 1140850 | bytes 983 | tf_op jit(solution)/shard_map/pallas_call | solution.py:246
  21.1 0.5 collective-permute-start.5
  21.6 3.5 %collective-permute-done.6.refs_3_ = bf16[4,32,256]{2,1,0:T(8,128)(2,1)S(1)} collective-permute-done((bf16[4,32,256]{2,1,0:T(8,128)(2,1)S(1)}, bf16[4,32,256]{2,1,0:T(8,128)(2,1)S(1)}, u32[]{:S(2)}, u32[]{:S(2)}) %collective-permute-start.6) | collective-permute-done | bytes 65568 | tf_op jit(solution)/shard_map/ppermute | solution.py:515
  25.2 1.6 %collective-permute-done.4.refs_1_ = bf16[4,32,256]{2,1,0:T(8,128)(2,1)S(1)} collective-permute-done((bf16[4,32,256]{2,1,0:T(8,128)(2,1)S(1)}, bf16[4,32,256]{2,1,0:T(8,128)(2,1)S(1)}, u32[]{:S(2)}, u32[]{:S(2)}) %collective-permute-start.4) | collective-permute-done | bytes 65568 | tf_op jit(solution)/shard_map/ppermute | solution.py:515
  26.8 0.1 shard_map.85
  26.8 0.1 collective-permute-start.9
  26.9 1.8 %collective-permute-start.12 = (bf16[128,1024]{1,0:T(8,128)(2,1)S(1)}, bf16[128,1024]{1,0:T(8,128)(2,1)S(1)}, u32[]{:S(2)}, u32[]{:S(2)}) collective-permute-start(bf16[128,1024]{1,0:T(8,128)(2,1)S(1)} %get-tuple-element.73.refs_0_.refs_4_.refs_6_), channel_id=1, source_target_pairs={{0,2},{1,3},{2,0},{3,1},{4,6},{5,7},{6,4},{7,5},{8,10},{9,11},{10,... | collective-permute-start | bytes 786440 | tf_op jit(solution)/shard_map/ppermute | solution.py:515
  28.7 1.6 %collective-permute-start.18 = (bf16[128,1024]{1,0:T(8,128)(2,1)S(1)}, bf16[128,1024]{1,0:T(8,128)(2,1)S(1)}, u32[]{:S(2)}, u32[]{:S(2)}) collective-permute-start(bf16[128,1024]{1,0:T(8,128)(2,1)S(1)} %get-tuple-element.67.mine_ref), channel_id=1, source_target_pairs={{0,8},{4,12},{8,0},{12,4},{16,24},{20,28},{24,16},{28,20},{1,9},{5... | collective-permute-start | bytes 786440 | tf_op jit(solution)/shard_map/ppermute | solution.py:515
  30.3 1.5 %shard_map.86 = (f32[3,4,32,128]{3,2,1,0:T(8,128)S(1)}, bf16[32,256]{1,0:T(8,128)(2,1)S(1)}) custom-call(bf16[4,32,256]{2,1,0:T(8,128)(2,1)S(1)} %get-tuple-element.58.refs_0_, bf16[4,32,256]{2,1,0:T(8,128)(2,1)S(1)} %collective-permute-done.4.refs_1_, bf16[4,32,256]{2,1,0:T(8,128)(2,1)S(1)} %collective-permute-done.5.refs_2_, ...), custom_call_target="tpu_custom_call" | custom-call | flops 75497 | bytes 3145 | tf_op jit(solution)/shard_map/pallas_call | solution.py:309
  31.8 0.1 collective-permute-start.11
  31.9 0.6 collective-permute-start.10
  32.5 3.3 %collective-permute-done.12.refs_5_.refs_7_ = bf16[128,1024]{1,0:T(8,128)(2,1)S(1)} collective-permute-done((bf16[128,1024]{1,0:T(8,128)(2,1)S(1)}, bf16[128,1024]{1,0:T(8,128)(2,1)S(1)}, u32[]{:S(2)}, u32[]{:S(2)}) %collective-permute-start.12) | collective-permute-done | bytes 262176 | tf_op jit(solution)/shard_map/ppermute | solution.py:515
  35.8 0.2 collective-permute-done.10.other_ref
  36.0 1.1 %collective-permute-done.18.other_ref = bf16[128,1024]{1,0:T(8,128)(2,1)S(1)} collective-permute-done((bf16[128,1024]{1,0:T(8,128)(2,1)S(1)}, bf16[128,1024]{1,0:T(8,128)(2,1)S(1)}, u32[]{:S(2)}, u32[]{:S(2)}) %collective-permute-start.18) | collective-permute-done | bytes 262176 | tf_op jit(solution)/shard_map/ppermute | solution.py:515
  37.2 0.3 shard_map.88
  37.5 0.7 %collective-permute-start.19 = (bf16[128,1024]{1,0:T(8,128)(2,1)S(1)}, bf16[128,1024]{1,0:T(8,128)(2,1)S(1)}, u32[]{:S(2)}, u32[]{:S(2)}) collective-permute-start(bf16[128,1024]{1,0:T(8,128)(2,1)S(1)} %shard_map.91), channel_id=1, source_target_pairs={{0,2},{1,3},{2,0},{3,1},{4,6},{5,7},{6,4},{7,5},{8,10},{9,11},{10,... | collective-permute-start | bytes 786440 | tf_op jit(solution)/shard_map/ppermute | solution.py:515
  38.2 2.6 %collective-permute-start.23 = (bf16[128,512]{1,0:T(8,128)(2,1)S(1)}, bf16[128,512]{1,0:T(8,128)(2,1)S(1)}, u32[]{:S(2)}, u32[]{:S(2)}) collective-permute-start(bf16[128,512]{1,0:T(8,128)(2,1)S(1)} %get-tuple-element.84.mine_ref), channel_id=1, source_target_pairs={{0,16},{4,20},{8,24},{12,28},{16,0},{20,4},{24,8},{28,12},{1,17},{... | collective-permute-start | bytes 393224 | tf_op jit(solution)/shard_map/ppermute | solution.py:515
  40.8 2.3 %collective-permute-start.14 = (bf16[32,256]{1,0:T(8,128)(2,1)S(1)}, bf16[32,256]{1,0:T(8,128)(2,1)S(1)}, u32[]{:S(2)}, u32[]{:S(2)}) collective-permute-start(bf16[32,256]{1,0:T(8,128)(2,1)S(1)} %get-tuple-element.75.refs_3_.refs_1_), channel_id=1, source_target_pairs={{0,6},{1,7},{2,4},{3,5},{4,2},{5,3},{6,0},{7,1},{8,14},{9,15},{10,... | collective-permute-start | bytes 49160 | tf_op jit(solution)/shard_map/ppermute | solution.py:522
  43.1 0.5 collective-permute-start.15
  43.6 0.6 collective-permute-start.16
  44.3 2.7 %collective-permute-done.14.refs_0_ = bf16[32,256]{1,0:T(8,128)(2,1)S(1)} collective-permute-done((bf16[32,256]{1,0:T(8,128)(2,1)S(1)}, bf16[32,256]{1,0:T(8,128)(2,1)S(1)}, u32[]{:S(2)}, u32[]{:S(2)}) %collective-permute-start.14) | collective-permute-done | bytes 16416 | tf_op jit(solution)/shard_map/ppermute | solution.py:522
  47.0 0.0 collective-permute-done.15.refs_1_
  47.1 0.3 collective-permute-done.16.refs_2_
  47.4 0.6 shard_map.89
  48.1 1.1 %collective-permute-start.24 = (bf16[128,1280]{1,0:T(8,128)(2,1)S(1)}, bf16[128,1280]{1,0:T(8,128)(2,1)S(1)}, u32[]{:S(2)}, u32[]{:S(2)}) collective-permute-start(bf16[128,1280]{1,0:T(8,128)(2,1)S(1)} %shard_map.96), channel_id=1, source_target_pairs={{0,2},{1,3},{2,0},{3,1},{4,6},{5,7},{6,4},{7,5},{8,10},{9,11},{10,... | collective-permute-start | bytes 983048 | tf_op jit(solution)/shard_map/ppermute | solution.py:515
  49.2 0.1 collective-permute-start.20
  49.3 0.5 collective-permute-start.21
  49.8 1.6 %collective-permute-start.17 = (bf16[32,256]{1,0:T(8,128)(2,1)S(1)}, bf16[32,256]{1,0:T(8,128)(2,1)S(1)}, u32[]{:S(2)}, u32[]{:S(2)}) collective-permute-start(bf16[32,256]{1,0:T(8,128)(2,1)S(1)} %get-tuple-element.76.refs_1_.refs_0_.refs_2_), channel_id=1, source_target_pairs={{0,8},{4,12},{8,0},{12,4},{16,24},{20,28},{24,16},{28,20},{1,9},{5... | collective-permute-start | bytes 49160 | tf_op jit(solution)/shard_map/ppermute | solution.py:515
  51.4 2.2 %collective-permute-done.17.refs_1_ = bf16[32,256]{1,0:T(8,128)(2,1)S(1)} collective-permute-done((bf16[32,256]{1,0:T(8,128)(2,1)S(1)}, bf16[32,256]{1,0:T(8,128)(2,1)S(1)}, u32[]{:S(2)}, u32[]{:S(2)}) %collective-permute-start.17) | collective-permute-done | bytes 16416 | tf_op jit(solution)/shard_map/ppermute | solution.py:515
  53.6 0.6 shard_map.94
  54.2 2.6 %collective-permute-start.22 = (bf16[32,256]{1,0:T(8,128)(2,1)S(1)}, bf16[32,256]{1,0:T(8,128)(2,1)S(1)}, u32[]{:S(2)}, u32[]{:S(2)}) collective-permute-start(bf16[32,256]{1,0:T(8,128)(2,1)S(1)} %get-tuple-element.79._.refs_0_), channel_id=1, source_target_pairs={{0,16},{4,20},{8,24},{12,28},{16,0},{20,4},{24,8},{28,12},{1,17},{... | collective-permute-start | bytes 49160 | tf_op jit(solution)/shard_map/ppermute | solution.py:515
  56.8 2.3 %all-gather = bf16[256,1280]{1,0:T(8,128)(2,1)S(1)} all-gather(bf16[128,1280]{1,0:T(8,128)(2,1)S(1)} %shard_map.97), channel_id=2, replica_groups={{0,1},{2,3},{4,5},{6,7},{8,9},{10,11},{12,13},{14,15},{16,17},{18,19},{..., dimensions={0}, use_global_device_ids=true | all-gather | bytes 983040 | tf_op jit(solution)/shard_map/all_gather | solution.py:618
  59.1 1.1 %shard_map.98 = bf16[4,32,256]{2,1,0:T(8,128)(2,1)S(1)} custom-call(bf16[32,256]{1,0:T(8,128)(2,1)S(1)} %get-tuple-element.79._.refs_0_, bf16[32,256]{1,0:T(8,128)(2,1)S(1)} %collective-permute-done.22.refs_1_, f32[4,32,128]{2,1,0:T(8,128)S(1)} %get-tuple-element.80.refs_2_, f32[4,32,128]{2,1,0:T(8,128)S(1)} %get-tuple-element.81.refs_3_, ...), custom_call_target="tpu_custom_call" | custom-call | flops 67108 | bytes 4194 | tf_op jit(solution)/shard_map/pallas_call | solution.py:471
  60.2 5.8 %all-gather.1 = bf16[16,32,256]{2,1,0:T(8,128)(2,1)S(1)} all-gather(bf16[4,32,256]{2,1,0:T(8,128)(2,1)S(1)} %shard_map.98), channel_id=3, replica_groups=mesh['leaf'=8,'rhs'=4] {'rhs'}, dimensions={0}, use_global_device_ids=true | all-gather | bytes 327680 | tf_op jit(solution)/shard_map/all_gather | solution.py:621
  66.0 1.0 %shard_map.99 = f32[8,64,128]{2,1,0:T(8,128)} custom-call(f32[4,64,128]{2,1,0:T(8,128)S(1)} %get-tuple-element.50.far_ref, f32[4,64,128]{2,1,0:T(8,128)S(1)} %get-tuple-element.57.own_ref, bf16[4,4,32,256]{3,2,1,0:T(8,128)(2,1)S(1)} %bitcast.7, bf16[8,128,256]{2,1,0:T(8,128)(2,1)S(1)} %copy-done.3), custom_call_target="tpu_custom_call" | custom-call | flops 33554 | bytes 524 | tf_op jit(solution)/shard_map/pallas_call | solution.py:503
  (40 shorter events, 0.3 us)
Async XLA Ops:
  0.0 11.6 %copy-start.2 = (bf16[8,128,256]{2,1,0:T(8,128)(2,1)S(1)}, bf16[8,128,256]{2,1,0:T(8,128)(2,1)}, u32[]{:S(2)}) copy-start(bf16[8,128,256]{2,1,0:T(8,128)(2,1)} %refs_3_.1) | copy-start | bytes 1572868
  0.0 6.6 %collective-permute-start = (bf16[64,1024]{1,0:T(8,128)(2,1)}, bf16[64,1024]{1,0:T(8,128)(2,1)S(1)}, u32[]{:S(2)}, u32[]{:S(2)}) collective-permute-start(bf16[64,1024]{1,0:T(8,128)(2,1)} %refs_0_.1), channel_id=1, source_target_pairs={{0,2},{1,3},{2,0},{3,1},{4,6},{5,7},{6,4},{7,5},{8,10},{9,11},{10,... | collective-permute-start | bytes 393224 | tf_op jit(solution)/shard_map/ppermute | solution.py:515
  2.9 3.7 %collective-permute-start.1 = (bf16[64,1024]{1,0:T(8,128)(2,1)}, bf16[64,1024]{1,0:T(8,128)(2,1)S(1)}, u32[]{:S(2)}, u32[]{:S(2)}) collective-permute-start(bf16[64,1024]{1,0:T(8,128)(2,1)} %refs_0_.1), channel_id=1, source_target_pairs={{0,1},{1,0},{2,3},{3,2},{4,5},{5,4},{6,7},{7,6},{8,9},{9,8},{10,11... | collective-permute-start | bytes 393224 | tf_op jit(solution)/shard_map/ppermute | solution.py:515
  2.9 8.6 %copy-start.6 = (bf16[64,1024]{1,0:T(8,128)(2,1)S(1)}, bf16[64,1024]{1,0:T(8,128)(2,1)}, u32[]{:S(2)}) copy-start(bf16[64,1024]{1,0:T(8,128)(2,1)} %refs_0_.1) | copy-start | bytes 393220
  6.6 1.3 %collective-permute-start.2 = (bf16[64,1024]{1,0:T(8,128)(2,1)S(1)}, bf16[64,1024]{1,0:T(8,128)(2,1)S(1)}, u32[]{:S(2)}, u32[]{:S(2)}) collective-permute-start(bf16[64,1024]{1,0:T(8,128)(2,1)S(1)} %collective-permute-done.refs_1_), channel_id=1, source_target_pairs={{0,1},{1,0},{2,3},{3,2},{4,5},{5,4},{6,7},{7,6},{8,9},{9,8},{10,11... | collective-permute-start | bytes 393224 | tf_op jit(solution)/shard_map/ppermute | solution.py:515
  8.0 9.7 %collective-permute-start.3 = (bf16[4,128,1024]{2,1,0:T(8,128)(2,1)}, bf16[4,128,1024]{2,1,0:T(8,128)(2,1)S(1)}, u32[]{:S(2)}, u32[]{:S(2)}) collective-permute-start(bf16[4,128,1024]{2,1,0:T(8,128)(2,1)} %get-tuple-element.53.refs_4_.own_ref.refs_15_), channel_id=1, source_target_pairs={{0,1},{1,0},{2,3},{3,2},{4,5},{5,4},{6,7},{7,6},{8,9},{9,8},{10,11... | collective-permute-start | bytes 3145736 | tf_op jit(solution)/shard_map/ppermute | solution.py:515
  8.1 18.7 %collective-permute-start.7 = (bf16[3,128,768]{2,1,0:T(8,128)(2,1)}, bf16[3,128,768]{2,1,0:T(8,128)(2,1)S(1)}, u32[]{:S(2)}, u32[]{:S(2)}) collective-permute-start(bf16[3,128,768]{2,1,0:T(8,128)(2,1)} %get-tuple-element.46), channel_id=1, source_target_pairs={{0,2},{1,3},{2,0},{3,1},{4,6},{5,7},{6,4},{7,5},{8,10},{9,11},{10,... | collective-permute-start | bytes 1769480 | tf_op jit(solution)/shard_map/ppermute | solution.py:515
  9.9 1.7 %copy-start.7 = (s32[4096]{0:T(1024)S(1)}, s32[4096]{0:T(1024)}, u32[]{:S(2)}) copy-start(s32[4096]{0:T(1024)} %param.9) | copy-start | bytes 49156
  9.9 11.7 %collective-permute-start.8 = (bf16[128,1024]{1,0:T(8,128)(2,1)}, bf16[128,1024]{1,0:T(8,128)(2,1)S(1)}, u32[]{:S(2)}, u32[]{:S(2)}) collective-permute-start(bf16[128,1024]{1,0:T(8,128)(2,1)} %get-tuple-element.64.mine_ref), channel_id=1, source_target_pairs={{0,4},{4,0},{8,12},{12,8},{16,20},{20,16},{24,28},{28,24},{1,5},{5... | collective-permute-start | bytes 786440 | tf_op jit(solution)/shard_map/ppermute | solution.py:515
  11.6 1.2 %copy-start.1 = (bf16[8,128,512]{2,1,0:T(8,128)(2,1)S(1)}, bf16[8,128,512]{2,1,0:T(8,128)(2,1)}, u32[]{:S(2)}) copy-start(bf16[8,128,512]{2,1,0:T(8,128)(2,1)} %refs_2_.1) | copy-start | bytes 3145732
  16.2 8.9 %collective-permute-start.6 = (bf16[4,32,256]{2,1,0:T(8,128)(2,1)S(1)}, bf16[4,32,256]{2,1,0:T(8,128)(2,1)S(1)}, u32[]{:S(2)}, u32[]{:S(2)}) collective-permute-start(bf16[4,32,256]{2,1,0:T(8,128)(2,1)S(1)} %get-tuple-element.61), channel_id=1, source_target_pairs={{0,3},{1,2},{2,1},{3,0},{4,7},{5,6},{6,5},{7,4},{8,11},{9,10},{10,... | collective-permute-start | bytes 196616 | tf_op jit(solution)/shard_map/ppermute | solution.py:515
  16.3 10.4 %collective-permute-start.4 = (bf16[4,32,256]{2,1,0:T(8,128)(2,1)S(1)}, bf16[4,32,256]{2,1,0:T(8,128)(2,1)S(1)}, u32[]{:S(2)}, u32[]{:S(2)}) collective-permute-start(bf16[4,32,256]{2,1,0:T(8,128)(2,1)S(1)} %get-tuple-element.54), channel_id=1, source_target_pairs={{0,2},{1,3},{2,0},{3,1},{4,6},{5,7},{6,4},{7,5},{8,10},{9,11},{10,... | collective-permute-start | bytes 196616 | tf_op jit(solution)/shard_map/ppermute | solution.py:515
  17.7 9.1 %copy-start.4 = (bf16[128,1024]{1,0:T(8,128)(2,1)S(1)}, bf16[128,1024]{1,0:T(8,128)(2,1)}, u32[]{:S(2)}) copy-start(bf16[128,1024]{1,0:T(8,128)(2,1)} %get-tuple-element.64.mine_ref) | copy-start | bytes 786436
  17.7 9.1 %copy-start.5 = (bf16[128,768]{1,0:T(8,128)(2,1)S(1)}, bf16[128,768]{1,0:T(8,128)(2,1)}, u32[]{:S(2)}) copy-start(bf16[128,768]{1,0:T(8,128)(2,1)} %get-tuple-element.66.refs_0_) | copy-start | bytes 589828
  17.7 12.6 %copy-start = (bf16[4,128,1024]{2,1,0:T(8,128)(2,1)S(1)}, bf16[4,128,1024]{2,1,0:T(8,128)(2,1)}, u32[]{:S(2)}) copy-start(bf16[4,128,1024]{2,1,0:T(8,128)(2,1)} %get-tuple-element.53.refs_4_.own_ref.refs_15_) | copy-start | bytes 3145732
  21.1 5.7 %collective-permute-start.5 = (bf16[4,32,256]{2,1,0:T(8,128)(2,1)S(1)}, bf16[4,32,256]{2,1,0:T(8,128)(2,1)S(1)}, u32[]{:S(2)}, u32[]{:S(2)}) collective-permute-start(bf16[4,32,256]{2,1,0:T(8,128)(2,1)S(1)} %get-tuple-element.60), channel_id=1, source_target_pairs={{0,1},{1,0},{2,3},{3,2},{4,5},{5,4},{6,7},{7,6},{8,9},{9,8},{10,11... | collective-permute-start | bytes 196616 | tf_op jit(solution)/shard_map/ppermute | solution.py:515
  26.8 3.5 %collective-permute-start.9 = (bf16[3,128,768]{2,1,0:T(8,128)(2,1)S(1)}, bf16[3,128,768]{2,1,0:T(8,128)(2,1)S(1)}, u32[]{:S(2)}, u32[]{:S(2)}) collective-permute-start(bf16[3,128,768]{2,1,0:T(8,128)(2,1)S(1)} %collective-permute-done.7.refs_5_), channel_id=1, source_target_pairs={{0,1},{1,0},{2,3},{3,2},{4,5},{5,4},{6,7},{7,6},{8,9},{9,8},{10,11... | collective-permute-start | bytes 1769480 | tf_op jit(solution)/shard_map/ppermute | solution.py:515
  26.9 8.9 %collective-permute-start.12 = (bf16[128,1024]{1,0:T(8,128)(2,1)S(1)}, bf16[128,1024]{1,0:T(8,128)(2,1)S(1)}, u32[]{:S(2)}, u32[]{:S(2)}) collective-permute-start(bf16[128,1024]{1,0:T(8,128)(2,1)S(1)} %get-tuple-element.73.refs_0_.refs_4_.refs_6_), channel_id=1, source_target_pairs={{0,2},{1,3},{2,0},{3,1},{4,6},{5,7},{6,4},{7,5},{8,10},{9,11},{10,... | collective-permute-start | bytes 786440 | tf_op jit(solution)/shard_map/ppermute | solution.py:515
  28.7 8.4 %collective-permute-start.18 = (bf16[128,1024]{1,0:T(8,128)(2,1)S(1)}, bf16[128,1024]{1,0:T(8,128)(2,1)S(1)}, u32[]{:S(2)}, u32[]{:S(2)}) collective-permute-start(bf16[128,1024]{1,0:T(8,128)(2,1)S(1)} %get-tuple-element.67.mine_ref), channel_id=1, source_target_pairs={{0,8},{4,12},{8,0},{12,4},{16,24},{20,28},{24,16},{28,20},{1,9},{5... | collective-permute-start | bytes 786440 | tf_op jit(solution)/shard_map/ppermute | solution.py:515
  31.8 5.3 %collective-permute-start.11 = (bf16[128,1024]{1,0:T(8,128)(2,1)S(1)}, bf16[128,1024]{1,0:T(8,128)(2,1)S(1)}, u32[]{:S(2)}, u32[]{:S(2)}) collective-permute-start(bf16[128,1024]{1,0:T(8,128)(2,1)S(1)} %shard_map.87), channel_id=1, source_target_pairs={{0,1},{1,0},{2,3},{3,2},{4,5},{5,4},{6,7},{7,6},{8,9},{9,8},{10,11... | collective-permute-start | bytes 786440 | tf_op jit(solution)/shard_map/ppermute | solution.py:515
  31.9 4.1 %collective-permute-start.10 = (bf16[32,256]{1,0:T(8,128)(2,1)S(1)}, bf16[32,256]{1,0:T(8,128)(2,1)S(1)}, u32[]{:S(2)}, u32[]{:S(2)}) collective-permute-start(bf16[32,256]{1,0:T(8,128)(2,1)S(1)} %get-tuple-element.69.refs_1_.mine_ref), channel_id=1, source_target_pairs={{0,2},{1,3},{2,0},{3,1},{4,6},{5,7},{6,4},{7,5},{8,10},{9,11},{10,... | collective-permute-start | bytes 49160 | tf_op jit(solution)/shard_map/ppermute | solution.py:515
  36.0 4.8 %collective-permute-start.13 = (bf16[128,1024]{1,0:T(8,128)(2,1)S(1)}, bf16[128,1024]{1,0:T(8,128)(2,1)S(1)}, u32[]{:S(2)}, u32[]{:S(2)}) collective-permute-start(bf16[128,1024]{1,0:T(8,128)(2,1)S(1)} %collective-permute-done.12.refs_5_.refs_7_), channel_id=1, source_target_pairs={{0,1},{1,0},{2,3},{3,2},{4,5},{5,4},{6,7},{7,6},{8,9},{9,8},{10,11... | collective-permute-start | bytes 786440 | tf_op jit(solution)/shard_map/ppermute | solution.py:515
  37.5 11.8 %collective-permute-start.19 = (bf16[128,1024]{1,0:T(8,128)(2,1)S(1)}, bf16[128,1024]{1,0:T(8,128)(2,1)S(1)}, u32[]{:S(2)}, u32[]{:S(2)}) collective-permute-start(bf16[128,1024]{1,0:T(8,128)(2,1)S(1)} %shard_map.91), channel_id=1, source_target_pairs={{0,2},{1,3},{2,0},{3,1},{4,6},{5,7},{6,4},{7,5},{8,10},{9,11},{10,... | collective-permute-start | bytes 786440 | tf_op jit(solution)/shard_map/ppermute | solution.py:515
  38.2 9.8 %collective-permute-start.23 = (bf16[128,512]{1,0:T(8,128)(2,1)S(1)}, bf16[128,512]{1,0:T(8,128)(2,1)S(1)}, u32[]{:S(2)}, u32[]{:S(2)}) collective-permute-start(bf16[128,512]{1,0:T(8,128)(2,1)S(1)} %get-tuple-element.84.mine_ref), channel_id=1, source_target_pairs={{0,16},{4,20},{8,24},{12,28},{16,0},{20,4},{24,8},{28,12},{1,17},{... | collective-permute-start | bytes 393224 | tf_op jit(solution)/shard_map/ppermute | solution.py:515
  40.8 6.2 %collective-permute-start.14 = (bf16[32,256]{1,0:T(8,128)(2,1)S(1)}, bf16[32,256]{1,0:T(8,128)(2,1)S(1)}, u32[]{:S(2)}, u32[]{:S(2)}) collective-permute-start(bf16[32,256]{1,0:T(8,128)(2,1)S(1)} %get-tuple-element.75.refs_3_.refs_1_), channel_id=1, source_target_pairs={{0,6},{1,7},{2,4},{3,5},{4,2},{5,3},{6,0},{7,1},{8,14},{9,15},{10,... | collective-permute-start | bytes 49160 | tf_op jit(solution)/shard_map/ppermute | solution.py:522
  43.1 3.9 %collective-permute-start.15 = (bf16[32,256]{1,0:T(8,128)(2,1)S(1)}, bf16[32,256]{1,0:T(8,128)(2,1)S(1)}, u32[]{:S(2)}, u32[]{:S(2)}) collective-permute-start(bf16[32,256]{1,0:T(8,128)(2,1)S(1)} %get-tuple-element.75.refs_3_.refs_1_), channel_id=1, source_target_pairs={{0,4},{4,0},{8,12},{12,8},{16,20},{20,16},{24,28},{28,24},{1,5},{5... | collective-permute-start | bytes 49160 | tf_op jit(solution)/shard_map/ppermute | solution.py:515
  43.6 3.7 %collective-permute-start.16 = (bf16[32,256]{1,0:T(8,128)(2,1)S(1)}, bf16[32,256]{1,0:T(8,128)(2,1)S(1)}, u32[]{:S(2)}, u32[]{:S(2)}) collective-permute-start(bf16[32,256]{1,0:T(8,128)(2,1)S(1)} %get-tuple-element.75.refs_3_.refs_1_), channel_id=1, source_target_pairs={{0,2},{1,3},{2,0},{3,1},{4,6},{5,7},{6,4},{7,5},{8,10},{9,11},{10,... | collective-permute-start | bytes 49160 | tf_op jit(solution)/shard_map/ppermute | solution.py:515
  48.1 8.7 %collective-permute-start.24 = (bf16[128,1280]{1,0:T(8,128)(2,1)S(1)}, bf16[128,1280]{1,0:T(8,128)(2,1)S(1)}, u32[]{:S(2)}, u32[]{:S(2)}) collective-permute-start(bf16[128,1280]{1,0:T(8,128)(2,1)S(1)} %shard_map.96), channel_id=1, source_target_pairs={{0,2},{1,3},{2,0},{3,1},{4,6},{5,7},{6,4},{7,5},{8,10},{9,11},{10,... | collective-permute-start | bytes 983048 | tf_op jit(solution)/shard_map/ppermute | solution.py:515
  49.2 4.4 %collective-permute-start.20 = (bf16[128,1024]{1,0:T(8,128)(2,1)S(1)}, bf16[128,1024]{1,0:T(8,128)(2,1)S(1)}, u32[]{:S(2)}, u32[]{:S(2)}) collective-permute-start(bf16[128,1024]{1,0:T(8,128)(2,1)S(1)} %shard_map.92), channel_id=1, source_target_pairs={{0,1},{1,0},{2,3},{3,2},{4,5},{5,4},{6,7},{7,6},{8,9},{9,8},{10,11... | collective-permute-start | bytes 786440 | tf_op jit(solution)/shard_map/ppermute | solution.py:515
  49.3 4.3 %collective-permute-start.21 = (bf16[128,1024]{1,0:T(8,128)(2,1)S(1)}, bf16[128,1024]{1,0:T(8,128)(2,1)S(1)}, u32[]{:S(2)}, u32[]{:S(2)}) collective-permute-start(bf16[128,1024]{1,0:T(8,128)(2,1)S(1)} %shard_map.93), channel_id=1, source_target_pairs={{0,1},{1,0},{2,3},{3,2},{4,5},{5,4},{6,7},{7,6},{8,9},{9,8},{10,11... | collective-permute-start | bytes 786440 | tf_op jit(solution)/shard_map/ppermute | solution.py:515
  49.8 3.7 %collective-permute-start.17 = (bf16[32,256]{1,0:T(8,128)(2,1)S(1)}, bf16[32,256]{1,0:T(8,128)(2,1)S(1)}, u32[]{:S(2)}, u32[]{:S(2)}) collective-permute-start(bf16[32,256]{1,0:T(8,128)(2,1)S(1)} %get-tuple-element.76.refs_1_.refs_0_.refs_2_), channel_id=1, source_target_pairs={{0,8},{4,12},{8,0},{12,4},{16,24},{20,28},{24,16},{28,20},{1,9},{5... | collective-permute-start | bytes 49160 | tf_op jit(solution)/shard_map/ppermute | solution.py:515
  54.2 4.9 %collective-permute-start.22 = (bf16[32,256]{1,0:T(8,128)(2,1)S(1)}, bf16[32,256]{1,0:T(8,128)(2,1)S(1)}, u32[]{:S(2)}, u32[]{:S(2)}) collective-permute-start(bf16[32,256]{1,0:T(8,128)(2,1)S(1)} %get-tuple-element.79._.refs_0_), channel_id=1, source_target_pairs={{0,16},{4,20},{8,24},{12,28},{16,0},{20,4},{24,8},{28,12},{1,17},{... | collective-permute-start | bytes 49160 | tf_op jit(solution)/shard_map/ppermute | solution.py:515
  59.1 6.9 %copy-start.3 = (bf16[8,128,256]{2,1,0:T(8,128)(2,1)S(1)}, bf16[8,128,256]{2,1,0:T(8,128)(2,1)}, u32[]{:S(2)}) copy-start(bf16[8,128,256]{2,1,0:T(8,128)(2,1)} %coupling_ref.1) | copy-start | bytes 1572868

commit v9 on v7

--- a/solution.py
+++ b/solution.py
@@ -369,9 +369,15 @@
     return order_pair(is_right, total_of(refs[:half]), total_of(refs[half:]))
 
 
+def from_cores(packs):
+    if len(packs[-1].shape) == 2:
+        return packs
+    return [*packs[:-1], packs[-1].at[(lax.axis_index("rhs") + 1) % CORES]]
+
+
 def cross_up_kernel(level, *refs):
     *refs, solved_ref, out_ref = refs
-    inputs, packs = refs[: -2 * CORES], refs[-2 * CORES :]
+    inputs, packs = refs[: -2 * CORES], from_cores(refs[-2 * CORES :])
     rank = out_ref.shape[1]
     compressed = solve_node(
         cross_pair(level, inputs),
@@ -426,7 +432,7 @@
         value[2 * half + core] = dot_rows(stacked, ref[:, :node_size]).astype(jnp.bfloat16)
     incoming = choose(half)
     for level in range(cross_levels - 2, -1, -1):
-        packs = cross_packs[2 * CORES * level : 2 * CORES * (level + 1)]
+        packs = from_cores(cross_packs[2 * CORES * level : 2 * CORES * (level + 1)])
         couplings = [ref[:, columns(ref)] for ref in packs]
         for flip, coupling in zip(PIECES, couplings):
             piece = place ^ flip
@@ -503,6 +509,12 @@
     return lax.ppermute(block, axis, [(i, i ^ bit) for i in range(lax.axis_size(axis))])
 
 
+def gather_cores(block):
+    shares = lax.axis_size("rhs")
+    cores = [[i + core for core in range(CORES)] for i in range(0, shares, CORES)]
+    return lax.all_gather(block, "rhs", axis_index_groups=cores)
+
+
 def far_swap(block, leaf_bit, rhs_bit):
     shares = lax.axis_size("rhs")
     flip = leaf_bit * shares + rhs_bit
@@ -580,14 +592,14 @@
     diagonal = far_swap(current, 1, CORES)
     beside = swap(current, "leaf", 1)
     across = swap(current, "rhs", CORES)
-    inputs = [diagonal, beside, across, current]
+    inputs = after([diagonal, beside, across, current], fars[1])
 
     solved_cross = []
     for level in range(cross_levels - 1):
         if level > 0:
             own, far = ancestors[level], fars[level]
             own_near = swap(join([own], current), "rhs", 1)
-            far_near = swap(join([far], current), "rhs", 1)
+            far_near = gather_cores(join([far], current))
             cross_packs.append([own, far, own_near, far_near])
         solved, current = cross_up(level, inputs, cross_packs[level])
         solved_cross.append(solved)
@@ -601,10 +613,7 @@
             tail = swap(join([ancestors[-1], send_coupling], current), "rhs", CORES)
 
     tail = hop(cross_levels - 1, ancestors[-1], tail, current)
-    shares = lax.axis_size("rhs")
-    cores = [[i + core for core in range(CORES)] for i in range(0, shares, CORES)]
-    both = lax.all_gather(tail, "rhs", axis_index_groups=cores)
-    others = [both, keep, keep_near]
+    others = [gather_cores(tail), keep, keep_near]
     shares = way_down(per_dev, inputs, solved_cross, solved_top, solved_half, cross_packs, others)
     incoming = lax.all_gather(shares, "rhs", axis=0)
     return finish(far_values, own_values, incoming, leaf_coupling)

time: 67.2 us -> 67.2 us (level)
  blocking collectives: 8.07 us -> 10.4 us
  waiting for transfers between devices: 17 us -> 15.3 us
    all_gather x1 -> x2, blocking collectives: 2.28 us -> 4.46 us  [gather_cores(): return lax.all_gather(block, 'rhs', axis_index_groups=cores)]
    ppermute x24 -> x23, waiting for transfers between devices: 14.3 us -> 12.5 us  [swap(): lax.ppermute(block, axis, [(i, i ^ bit) for i in range(lax.axis_size(axis...]
    ppermute x24 -> x23, starting transfers between devices: 22.8 us -> 22.3 us  [swap(): lax.ppermute(block, axis, [(i, i ^ bit) for i in range(lax.axis_size(axis...]
  transfers between devices with their start and end apart: 25 -> 24, of which waited for: 10 -> 10; matrix products, arithmetic and copies ran while one was open for 0% -> 0% of each run, Pallas kernels for 19% -> 19%
where the time goes in v9:
time: 67.2 us; the launch traced here: 67 us
  starting transfers between devices  24.7 us (37%)
  waiting for transfers between devices  15.3 us (23%)
  Pallas kernels  15.1 us (22%)
  blocking collectives  10.4 us (15%)
  local copies, waits for them, and re-layouts  1.25 us (2%)
    ppermute x23, starting transfers between devices, swap(): lax.ppermute(block, axis, [(i, i ^ bit) for i in range(lax.axis_size(axis...  22.3 us
    ppermute x23, waiting for transfers between devices, swap(): lax.ppermute(block, axis, [(i, i ^ bit) for i in range(lax.axis_size(axis...  12.5 us
    pallas_call x2, Pallas kernels, leaf_up(): pl.pallas_call(functools.partial(leaf_kernel, len(points)), grid_spec=plt...  6.81 us
    all_gather x1, blocking collectives, body(): incoming = lax.all_gather(shares, 'rhs', axis=0)  5.9 us
    all_gather x2, blocking collectives, gather_cores(): return lax.all_gather(block, 'rhs', axis_index_groups=cores)  4.46 us
    pallas_call x1, Pallas kernels, pack(): pl.pallas_call(functools.partial(pack_kernel, per_dev), in_specs=[pl.Bloc...  2.99 us
    ppermute x1, waiting for transfers between devices, far_swap(): lax.ppermute(block, ('leaf', 'rhs'), [(i, i ^ flip) for i in range(count)])  2.74 us
    ppermute x1, starting transfers between devices, far_swap(): lax.ppermute(block, ('leaf', 'rhs'), [(i, i ^ flip) for i in range(count)])  2.34 us
  transfers between devices with their start and end apart: 24, of which 10 were waited for; matrix products, arithmetic and copies ran while one was open for 0% of the time, Pallas kernels for 19%

profile of v9, /device:TPU:0, one launch (start us, length us, event | category | flops | bytes accessed | tf_op | source)
XLA Modules:
  0.0 67.0 jit_solution(7294002900191125279)
XLA Ops:
  0.0 2.9 %collective-permute-start = (bf16[64,1024]{1,0:T(8,128)(2,1)}, bf16[64,1024]{1,0:T(8,128)(2,1)S(1)}, u32[]{:S(2)}, u32[]{:S(2)}) collective-permute-start(bf16[64,1024]{1,0:T(8,128)(2,1)} %refs_0_.1), channel_id=1, source_target_pairs={{0,2},{1,3},{2,0},{3,1},{4,6},{5,7},{6,4},{7,5},{8,10},{9,11},{10,... | collective-permute-start | bytes 393224 | tf_op jit(solution)/shard_map/ppermute | solution.py:509
  2.9 3.0 %shard_map.82 = (bf16[3,128,768]{2,1,0:T(8,128)(2,1)}, bf16[128,768]{1,0:T(8,128)(2,1)}, bf16[4,128,1024]{2,1,0:T(8,128)(2,1)}, bf16[128,1024]{1,0:T(8,128)(2,1)}) custom-call(bf16[8,128,512]{2,1,0:T(8,128)(2,1)} %inverse.1, bf16[8,128,256]{2,1,0:T(8,128)(2,1)} %basis.1, bf16[8,128,256]{2,1,0:T(8,128)(2,1)} %coupling.1), custom_call_target="tpu_custom_call" | custom-call | bytes 4194 | tf_op jit(solution)/shard_map/pallas_call | solution.py:93
  5.9 0.7 %collective-permute-done.refs_1_ = bf16[64,1024]{1,0:T(8,128)(2,1)S(1)} collective-permute-done((bf16[64,1024]{1,0:T(8,128)(2,1)}, bf16[64,1024]{1,0:T(8,128)(2,1)S(1)}, u32[]{:S(2)}, u32[]{:S(2)}) %collective-permute-start) | collective-permute-done | bytes 131104 | tf_op jit(solution)/shard_map/ppermute | solution.py:509
  6.7 1.3 %collective-permute-done.2.refs_3_ = bf16[64,1024]{1,0:T(8,128)(2,1)S(1)} collective-permute-done((bf16[64,1024]{1,0:T(8,128)(2,1)S(1)}, bf16[64,1024]{1,0:T(8,128)(2,1)S(1)}, u32[]{:S(2)}, u32[]{:S(2)}) %collective-permute-start.2) | collective-permute-done | bytes 131104 | tf_op jit(solution)/shard_map/ppermute | solution.py:509
  8.0 0.1 collective-permute-start.3
  8.1 1.8 %collective-permute-start.7 = (bf16[3,128,768]{2,1,0:T(8,128)(2,1)}, bf16[3,128,768]{2,1,0:T(8,128)(2,1)S(1)}, u32[]{:S(2)}, u32[]{:S(2)}) collective-permute-start(bf16[3,128,768]{2,1,0:T(8,128)(2,1)} %get-tuple-element.50), channel_id=1, source_target_pairs={{0,2},{1,3},{2,0},{3,1},{4,6},{5,7},{6,4},{7,5},{8,10},{9,11},{10,... | collective-permute-start | bytes 1769480 | tf_op jit(solution)/shard_map/ppermute | solution.py:509
  9.9 1.5 %collective-permute-start.8 = (bf16[128,1024]{1,0:T(8,128)(2,1)}, bf16[128,1024]{1,0:T(8,128)(2,1)S(1)}, u32[]{:S(2)}, u32[]{:S(2)}) collective-permute-start(bf16[128,1024]{1,0:T(8,128)(2,1)} %get-tuple-element.68.mine_ref), channel_id=1, source_target_pairs={{0,4},{4,0},{8,12},{12,8},{16,20},{20,16},{24,28},{28,24},{1,5},{5... | collective-permute-start | bytes 786440 | tf_op jit(solution)/shard_map/ppermute | solution.py:509
  11.4 0.1 pad_add_fusion.side_ref
  11.5 0.1 pad_add_fusion.1.side_ref
  11.6 1.2 %copy-done.1 = bf16[8,128,512]{2,1,0:T(8,128)(2,1)S(1)} copy-done((bf16[8,128,512]{2,1,0:T(8,128)(2,1)S(1)}, bf16[8,128,512]{2,1,0:T(8,128)(2,1)}, u32[]{:S(2)}) %copy-start.1) | copy-done | bytes 1048600
  12.8 3.4 %shard_map.83 = (f32[4,64,128]{2,1,0:T(8,128)S(1)}, bf16[4,32,256]{2,1,0:T(8,128)(2,1)S(1)}, bf16[4,32,256]{2,1,0:T(8,128)(2,1)S(1)}, bf16[4,4,64,256]{3,2,1,0:T(8,128)(2,1)S(1)}) custom-call(s32[2]{0:T(128)S(1)} %pad_add_fusion.side_ref, bf16[64,1024]{1,0:T(8,128)(2,1)S(1)} %copy-done.6, bf16[64,1024]{1,0:T(8,128)(2,1)S(1)} %collective-permute-done.refs_1_, ...), custom_call_target="tpu_custom_call" | custom-call | flops 1140850 | bytes 983 | tf_op jit(solution)/shard_map/pallas_call | solution.py:246
  16.2 0.1 collective-permute-start.6
  16.3 1.4 %collective-permute-start.4 = (bf16[4,32,256]{2,1,0:T(8,128)(2,1)S(1)}, bf16[4,32,256]{2,1,0:T(8,128)(2,1)S(1)}, u32[]{:S(2)}, u32[]{:S(2)}) collective-permute-start(bf16[4,32,256]{2,1,0:T(8,128)(2,1)S(1)} %get-tuple-element.58), channel_id=1, source_target_pairs={{0,2},{1,3},{2,0},{3,1},{4,6},{5,7},{6,4},{7,5},{8,10},{9,11},{10,... | collective-permute-start | bytes 196616 | tf_op jit(solution)/shard_map/ppermute | solution.py:509
  17.7 3.4 %shard_map.84 = (f32[4,64,128]{2,1,0:T(8,128)S(1)}, bf16[4,32,256]{2,1,0:T(8,128)(2,1)S(1)}, bf16[4,32,256]{2,1,0:T(8,128)(2,1)S(1)}) custom-call(s32[2]{0:T(128)S(1)} %pad_add_fusion.1.side_ref, bf16[4,4,64,256]{3,2,1,0:T(8,128)(2,1)S(1)} %get-tuple-element.60.refs_0_, s32[1,4096]{1,0:T(1,128)S(1)} %bitcast.12, bf16[8,128,512]{2,1,0:T(8,128)(2,1)S(1)} %copy-done.1, ...), custom_call_target="tpu_custom_call" | custom-call | flops 1140850 | bytes 983 | tf_op jit(solution)/shard_map/pallas_call | solution.py:246
  21.1 0.5 collective-permute-start.5
  21.6 3.5 %collective-permute-done.6.refs_3_ = bf16[4,32,256]{2,1,0:T(8,128)(2,1)S(1)} collective-permute-done((bf16[4,32,256]{2,1,0:T(8,128)(2,1)S(1)}, bf16[4,32,256]{2,1,0:T(8,128)(2,1)S(1)}, u32[]{:S(2)}, u32[]{:S(2)}) %collective-permute-start.6) | collective-permute-done | bytes 65568 | tf_op jit(solution)/shard_map/ppermute | solution.py:509
  25.2 1.6 %collective-permute-done.4.refs_1_ = bf16[4,32,256]{2,1,0:T(8,128)(2,1)S(1)} collective-permute-done((bf16[4,32,256]{2,1,0:T(8,128)(2,1)S(1)}, bf16[4,32,256]{2,1,0:T(8,128)(2,1)S(1)}, u32[]{:S(2)}, u32[]{:S(2)}) %collective-permute-start.4) | collective-permute-done | bytes 65568 | tf_op jit(solution)/shard_map/ppermute | solution.py:509
  26.8 0.1 shard_map.85
  26.8 0.1 collective-permute-start.9
  26.9 1.8 %collective-permute-start.12 = (bf16[128,1024]{1,0:T(8,128)(2,1)S(1)}, bf16[128,1024]{1,0:T(8,128)(2,1)S(1)}, u32[]{:S(2)}, u32[]{:S(2)}) collective-permute-start(bf16[128,1024]{1,0:T(8,128)(2,1)S(1)} %get-tuple-element.77.refs_0_.refs_4_.refs_6_), channel_id=1, source_target_pairs={{0,2},{1,3},{2,0},{3,1},{4,6},{5,7},{6,4},{7,5},{8,10},{9,11},{10,... | collective-permute-start | bytes 786440 | tf_op jit(solution)/shard_map/ppermute | solution.py:509
  28.7 1.6 %collective-permute-start.17 = (bf16[128,1024]{1,0:T(8,128)(2,1)S(1)}, bf16[128,1024]{1,0:T(8,128)(2,1)S(1)}, u32[]{:S(2)}, u32[]{:S(2)}) collective-permute-start(bf16[128,1024]{1,0:T(8,128)(2,1)S(1)} %get-tuple-element.71.mine_ref), channel_id=1, source_target_pairs={{0,8},{4,12},{8,0},{12,4},{16,24},{20,28},{24,16},{28,20},{1,9},{5... | collective-permute-start | bytes 786440 | tf_op jit(solution)/shard_map/ppermute | solution.py:509
  30.3 1.5 %shard_map.86 = (f32[3,4,32,128]{3,2,1,0:T(8,128)S(1)}, bf16[32,256]{1,0:T(8,128)(2,1)S(1)}) custom-call(bf16[4,32,256]{2,1,0:T(8,128)(2,1)S(1)} %get-tuple-element.62.refs_0_, bf16[4,32,256]{2,1,0:T(8,128)(2,1)S(1)} %collective-permute-done.4.refs_1_, bf16[4,32,256]{2,1,0:T(8,128)(2,1)S(1)} %collective-permute-done.5.refs_2_, ...), custom_call_target="tpu_custom_call" | custom-call | flops 75497 | bytes 3145 | tf_op jit(solution)/shard_map/pallas_call | solution.py:309
  31.8 0.1 collective-permute-start.11
  31.9 0.6 collective-permute-start.10
  32.5 3.3 %collective-permute-done.12.refs_5_.refs_7_ = bf16[128,1024]{1,0:T(8,128)(2,1)S(1)} collective-permute-done((bf16[128,1024]{1,0:T(8,128)(2,1)S(1)}, bf16[128,1024]{1,0:T(8,128)(2,1)S(1)}, u32[]{:S(2)}, u32[]{:S(2)}) %collective-permute-start.12) | collective-permute-done | bytes 262176 | tf_op jit(solution)/shard_map/ppermute | solution.py:509
  35.8 0.2 collective-permute-done.10.other_ref
  36.0 1.1 %collective-permute-done.17.other_ref = bf16[128,1024]{1,0:T(8,128)(2,1)S(1)} collective-permute-done((bf16[128,1024]{1,0:T(8,128)(2,1)S(1)}, bf16[128,1024]{1,0:T(8,128)(2,1)S(1)}, u32[]{:S(2)}, u32[]{:S(2)}) %collective-permute-start.17) | collective-permute-done | bytes 262176 | tf_op jit(solution)/shard_map/ppermute | solution.py:509
  37.2 0.3 shard_map.88
  37.5 0.7 %collective-permute-start.18 = (bf16[128,1024]{1,0:T(8,128)(2,1)S(1)}, bf16[128,1024]{1,0:T(8,128)(2,1)S(1)}, u32[]{:S(2)}, u32[]{:S(2)}) collective-permute-start(bf16[128,1024]{1,0:T(8,128)(2,1)S(1)} %shard_map.90), channel_id=1, source_target_pairs={{0,2},{1,3},{2,0},{3,1},{4,6},{5,7},{6,4},{7,5},{8,10},{9,11},{10,... | collective-permute-start | bytes 786440 | tf_op jit(solution)/shard_map/ppermute | solution.py:509
  38.2 2.6 %collective-permute-start.22 = (bf16[128,512]{1,0:T(8,128)(2,1)S(1)}, bf16[128,512]{1,0:T(8,128)(2,1)S(1)}, u32[]{:S(2)}, u32[]{:S(2)}) collective-permute-start(bf16[128,512]{1,0:T(8,128)(2,1)S(1)} %get-tuple-element.92.mine_ref), channel_id=1, source_target_pairs={{0,16},{4,20},{8,24},{12,28},{16,0},{20,4},{24,8},{28,12},{1,17},{... | collective-permute-start | bytes 393224 | tf_op jit(solution)/shard_map/ppermute | solution.py:509
  40.8 2.3 %collective-permute-start.14 = (bf16[32,256]{1,0:T(8,128)(2,1)S(1)}, bf16[32,256]{1,0:T(8,128)(2,1)S(1)}, u32[]{:S(2)}, u32[]{:S(2)}) collective-permute-start(bf16[32,256]{1,0:T(8,128)(2,1)S(1)} %get-tuple-element.85.refs_1_.refs_3_), channel_id=1, source_target_pairs={{0,6},{1,7},{2,4},{3,5},{4,2},{5,3},{6,0},{7,1},{8,14},{9,15},{10,... | collective-permute-start | bytes 49160 | tf_op jit(solution)/shard_map/ppermute | solution.py:522
  43.1 0.5 collective-permute-start.15
  43.6 0.6 collective-permute-start.16
  44.3 2.7 %collective-permute-done.14.refs_0_ = bf16[32,256]{1,0:T(8,128)(2,1)S(1)} collective-permute-done((bf16[32,256]{1,0:T(8,128)(2,1)S(1)}, bf16[32,256]{1,0:T(8,128)(2,1)S(1)}, u32[]{:S(2)}, u32[]{:S(2)}) %collective-permute-start.14) | collective-permute-done | bytes 16416 | tf_op jit(solution)/shard_map/ppermute | solution.py:522
  47.0 0.0 collective-permute-done.15.refs_1_
  47.1 0.3 collective-permute-done.16.refs_2_
  47.4 0.6 shard_map.91
  48.1 1.1 %collective-permute-start.23 = (bf16[128,1280]{1,0:T(8,128)(2,1)S(1)}, bf16[128,1280]{1,0:T(8,128)(2,1)S(1)}, u32[]{:S(2)}, u32[]{:S(2)}) collective-permute-start(bf16[128,1280]{1,0:T(8,128)(2,1)S(1)} %shard_map.96), channel_id=1, source_target_pairs={{0,2},{1,3},{2,0},{3,1},{4,6},{5,7},{6,4},{7,5},{8,10},{9,11},{10,... | collective-permute-start | bytes 983048 | tf_op jit(solution)/shard_map/ppermute | solution.py:509
  49.2 0.1 collective-permute-start.20
  49.3 1.6 %collective-permute-start.19 = (bf16[32,256]{1,0:T(8,128)(2,1)S(1)}, bf16[32,256]{1,0:T(8,128)(2,1)S(1)}, u32[]{:S(2)}, u32[]{:S(2)}) collective-permute-start(bf16[32,256]{1,0:T(8,128)(2,1)S(1)} %get-tuple-element.86.refs_1_.refs_0_.refs_2_), channel_id=1, source_target_pairs={{0,8},{4,12},{8,0},{12,4},{16,24},{20,28},{24,16},{28,20},{1,9},{5... | collective-permute-start | bytes 49160 | tf_op jit(solution)/shard_map/ppermute | solution.py:509
  50.9 2.2 %all-gather = bf16[256,1024]{1,0:T(8,128)(2,1)S(1)} all-gather(bf16[128,1024]{1,0:T(8,128)(2,1)S(1)} %shard_map.93), channel_id=2, replica_groups={{0,1},{2,3},{4,5},{6,7},{8,9},{10,11},{12,13},{14,15},{16,17},{18,19},{..., dimensions={0}, use_global_device_ids=true | all-gather | bytes 786432 | tf_op jit(solution)/shard_map/all_gather | solution.py:515
  53.1 0.6 shard_map.94
  53.7 2.6 %collective-permute-start.21 = (bf16[32,256]{1,0:T(8,128)(2,1)S(1)}, bf16[32,256]{1,0:T(8,128)(2,1)S(1)}, u32[]{:S(2)}, u32[]{:S(2)}) collective-permute-start(bf16[32,256]{1,0:T(8,128)(2,1)S(1)} %get-tuple-element.87._.refs_0_), channel_id=1, source_target_pairs={{0,16},{4,20},{8,24},{12,28},{16,0},{20,4},{24,8},{28,12},{1,17},{... | collective-permute-start | bytes 49160 | tf_op jit(solution)/shard_map/ppermute | solution.py:509
  56.3 0.4 collective-permute-done.23.tail_ref
  56.7 2.3 %all-gather.1 = bf16[256,1280]{1,0:T(8,128)(2,1)S(1)} all-gather(bf16[128,1280]{1,0:T(8,128)(2,1)S(1)} %shard_map.97), channel_id=3, replica_groups={{0,1},{2,3},{4,5},{6,7},{8,9},{10,11},{12,13},{14,15},{16,17},{18,19},{..., dimensions={0}, use_global_device_ids=true | all-gather | bytes 983040 | tf_op jit(solution)/shard_map/all_gather | solution.py:515
  59.0 1.1 %shard_map.98 = bf16[4,32,256]{2,1,0:T(8,128)(2,1)S(1)} custom-call(bf16[32,256]{1,0:T(8,128)(2,1)S(1)} %get-tuple-element.87._.refs_0_, bf16[32,256]{1,0:T(8,128)(2,1)S(1)} %collective-permute-done.21.refs_1_, f32[4,32,128]{2,1,0:T(8,128)S(1)} %get-tuple-element.88.refs_2_, f32[4,32,128]{2,1,0:T(8,128)S(1)} %get-tuple-element.89.refs_3_, ...), custom_call_target="tpu_custom_call" | custom-call | flops 67108 | bytes 4194 | tf_op jit(solution)/shard_map/pallas_call | solution.py:477
  60.1 5.9 %all-gather.2 = bf16[16,32,256]{2,1,0:T(8,128)(2,1)S(1)} all-gather(bf16[4,32,256]{2,1,0:T(8,128)(2,1)S(1)} %shard_map.98), channel_id=4, replica_groups=mesh['leaf'=8,'rhs'=4] {'rhs'}, dimensions={0}, use_global_device_ids=true | all-gather | bytes 327680 | tf_op jit(solution)/shard_map/all_gather | solution.py:618
  66.0 1.0 %shard_map.99 = f32[8,64,128]{2,1,0:T(8,128)} custom-call(f32[4,64,128]{2,1,0:T(8,128)S(1)} %get-tuple-element.54.far_ref, f32[4,64,128]{2,1,0:T(8,128)S(1)} %get-tuple-element.61.own_ref, bf16[4,4,32,256]{3,2,1,0:T(8,128)(2,1)S(1)} %bitcast.10, bf16[8,128,256]{2,1,0:T(8,128)(2,1)S(1)} %copy-done.3), custom_call_target="tpu_custom_call" | custom-call | flops 33554 | bytes 524 | tf_op jit(solution)/shard_map/pallas_call | solution.py:500
  (39 shorter events, 0.3 us)
Async XLA Ops:
  0.0 11.6 %copy-start.2 = (bf16[8,128,256]{2,1,0:T(8,128)(2,1)S(1)}, bf16[8,128,256]{2,1,0:T(8,128)(2,1)}, u32[]{:S(2)}) copy-start(bf16[8,128,256]{2,1,0:T(8,128)(2,1)} %refs_3_.1) | copy-start | bytes 1572868
  0.0 6.6 %collective-permute-start = (bf16[64,1024]{1,0:T(8,128)(2,1)}, bf16[64,1024]{1,0:T(8,128)(2,1)S(1)}, u32[]{:S(2)}, u32[]{:S(2)}) collective-permute-start(bf16[64,1024]{1,0:T(8,128)(2,1)} %refs_0_.1), channel_id=1, source_target_pairs={{0,2},{1,3},{2,0},{3,1},{4,6},{5,7},{6,4},{7,5},{8,10},{9,11},{10,... | collective-permute-start | bytes 393224 | tf_op jit(solution)/shard_map/ppermute | solution.py:509
  2.9 3.7 %collective-permute-start.1 = (bf16[64,1024]{1,0:T(8,128)(2,1)}, bf16[64,1024]{1,0:T(8,128)(2,1)S(1)}, u32[]{:S(2)}, u32[]{:S(2)}) collective-permute-start(bf16[64,1024]{1,0:T(8,128)(2,1)} %refs_0_.1), channel_id=1, source_target_pairs={{0,1},{1,0},{2,3},{3,2},{4,5},{5,4},{6,7},{7,6},{8,9},{9,8},{10,11... | collective-permute-start | bytes 393224 | tf_op jit(solution)/shard_map/ppermute | solution.py:509
  2.9 8.6 %copy-start.6 = (bf16[64,1024]{1,0:T(8,128)(2,1)S(1)}, bf16[64,1024]{1,0:T(8,128)(2,1)}, u32[]{:S(2)}) copy-start(bf16[64,1024]{1,0:T(8,128)(2,1)} %refs_0_.1) | copy-start | bytes 393220
  6.6 1.3 %collective-permute-start.2 = (bf16[64,1024]{1,0:T(8,128)(2,1)S(1)}, bf16[64,1024]{1,0:T(8,128)(2,1)S(1)}, u32[]{:S(2)}, u32[]{:S(2)}) collective-permute-start(bf16[64,1024]{1,0:T(8,128)(2,1)S(1)} %collective-permute-done.refs_1_), channel_id=1, source_target_pairs={{0,1},{1,0},{2,3},{3,2},{4,5},{5,4},{6,7},{7,6},{8,9},{9,8},{10,11... | collective-permute-start | bytes 393224 | tf_op jit(solution)/shard_map/ppermute | solution.py:509
  8.0 9.7 %collective-permute-start.3 = (bf16[4,128,1024]{2,1,0:T(8,128)(2,1)}, bf16[4,128,1024]{2,1,0:T(8,128)(2,1)S(1)}, u32[]{:S(2)}, u32[]{:S(2)}) collective-permute-start(bf16[4,128,1024]{2,1,0:T(8,128)(2,1)} %get-tuple-element.57.refs_4_.own_ref.refs_15_), channel_id=1, source_target_pairs={{0,1},{1,0},{2,3},{3,2},{4,5},{5,4},{6,7},{7,6},{8,9},{9,8},{10,11... | collective-permute-start | bytes 3145736 | tf_op jit(solution)/shard_map/ppermute | solution.py:509
  8.1 18.7 %collective-permute-start.7 = (bf16[3,128,768]{2,1,0:T(8,128)(2,1)}, bf16[3,128,768]{2,1,0:T(8,128)(2,1)S(1)}, u32[]{:S(2)}, u32[]{:S(2)}) collective-permute-start(bf16[3,128,768]{2,1,0:T(8,128)(2,1)} %get-tuple-element.50), channel_id=1, source_target_pairs={{0,2},{1,3},{2,0},{3,1},{4,6},{5,7},{6,4},{7,5},{8,10},{9,11},{10,... | collective-permute-start | bytes 1769480 | tf_op jit(solution)/shard_map/ppermute | solution.py:509
  9.9 1.7 %copy-start.7 = (s32[4096]{0:T(1024)S(1)}, s32[4096]{0:T(1024)}, u32[]{:S(2)}) copy-start(s32[4096]{0:T(1024)} %param.9) | copy-start | bytes 49156
  9.9 11.7 %collective-permute-start.8 = (bf16[128,1024]{1,0:T(8,128)(2,1)}, bf16[128,1024]{1,0:T(8,128)(2,1)S(1)}, u32[]{:S(2)}, u32[]{:S(2)}) collective-permute-start(bf16[128,1024]{1,0:T(8,128)(2,1)} %get-tuple-element.68.mine_ref), channel_id=1, source_target_pairs={{0,4},{4,0},{8,12},{12,8},{16,20},{20,16},{24,28},{28,24},{1,5},{5... | collective-permute-start | bytes 786440 | tf_op jit(solution)/shard_map/ppermute | solution.py:509
  11.6 1.2 %copy-start.1 = (bf16[8,128,512]{2,1,0:T(8,128)(2,1)S(1)}, bf16[8,128,512]{2,1,0:T(8,128)(2,1)}, u32[]{:S(2)}) copy-start(bf16[8,128,512]{2,1,0:T(8,128)(2,1)} %refs_2_.1) | copy-start | bytes 3145732
  16.2 8.9 %collective-permute-start.6 = (bf16[4,32,256]{2,1,0:T(8,128)(2,1)S(1)}, bf16[4,32,256]{2,1,0:T(8,128)(2,1)S(1)}, u32[]{:S(2)}, u32[]{:S(2)}) collective-permute-start(bf16[4,32,256]{2,1,0:T(8,128)(2,1)S(1)} %get-tuple-element.65), channel_id=1, source_target_pairs={{0,3},{1,2},{2,1},{3,0},{4,7},{5,6},{6,5},{7,4},{8,11},{9,10},{10,... | collective-permute-start | bytes 196616 | tf_op jit(solution)/shard_map/ppermute | solution.py:509
  16.3 10.4 %collective-permute-start.4 = (bf16[4,32,256]{2,1,0:T(8,128)(2,1)S(1)}, bf16[4,32,256]{2,1,0:T(8,128)(2,1)S(1)}, u32[]{:S(2)}, u32[]{:S(2)}) collective-permute-start(bf16[4,32,256]{2,1,0:T(8,128)(2,1)S(1)} %get-tuple-element.58), channel_id=1, source_target_pairs={{0,2},{1,3},{2,0},{3,1},{4,6},{5,7},{6,4},{7,5},{8,10},{9,11},{10,... | collective-permute-start | bytes 196616 | tf_op jit(solution)/shard_map/ppermute | solution.py:509
  17.7 9.1 %copy-start.4 = (bf16[128,1024]{1,0:T(8,128)(2,1)S(1)}, bf16[128,1024]{1,0:T(8,128)(2,1)}, u32[]{:S(2)}) copy-start(bf16[128,1024]{1,0:T(8,128)(2,1)} %get-tuple-element.68.mine_ref) | copy-start | bytes 786436
  17.7 9.1 %copy-start.5 = (bf16[128,768]{1,0:T(8,128)(2,1)S(1)}, bf16[128,768]{1,0:T(8,128)(2,1)}, u32[]{:S(2)}) copy-start(bf16[128,768]{1,0:T(8,128)(2,1)} %get-tuple-element.70.refs_0_) | copy-start | bytes 589828
  17.7 12.6 %copy-start = (bf16[4,128,1024]{2,1,0:T(8,128)(2,1)S(1)}, bf16[4,128,1024]{2,1,0:T(8,128)(2,1)}, u32[]{:S(2)}) copy-start(bf16[4,128,1024]{2,1,0:T(8,128)(2,1)} %get-tuple-element.57.refs_4_.own_ref.refs_15_) | copy-start | bytes 3145732
  21.1 5.7 %collective-permute-start.5 = (bf16[4,32,256]{2,1,0:T(8,128)(2,1)S(1)}, bf16[4,32,256]{2,1,0:T(8,128)(2,1)S(1)}, u32[]{:S(2)}, u32[]{:S(2)}) collective-permute-start(bf16[4,32,256]{2,1,0:T(8,128)(2,1)S(1)} %get-tuple-element.64), channel_id=1, source_target_pairs={{0,1},{1,0},{2,3},{3,2},{4,5},{5,4},{6,7},{7,6},{8,9},{9,8},{10,11... | collective-permute-start | bytes 196616 | tf_op jit(solution)/shard_map/ppermute | solution.py:509
  26.8 3.5 %collective-permute-start.9 = (bf16[3,128,768]{2,1,0:T(8,128)(2,1)S(1)}, bf16[3,128,768]{2,1,0:T(8,128)(2,1)S(1)}, u32[]{:S(2)}, u32[]{:S(2)}) collective-permute-start(bf16[3,128,768]{2,1,0:T(8,128)(2,1)S(1)} %collective-permute-done.7.refs_5_), channel_id=1, source_target_pairs={{0,1},{1,0},{2,3},{3,2},{4,5},{5,4},{6,7},{7,6},{8,9},{9,8},{10,11... | collective-permute-start | bytes 1769480 | tf_op jit(solution)/shard_map/ppermute | solution.py:509
  26.9 8.9 %collective-permute-start.12 = (bf16[128,1024]{1,0:T(8,128)(2,1)S(1)}, bf16[128,1024]{1,0:T(8,128)(2,1)S(1)}, u32[]{:S(2)}, u32[]{:S(2)}) collective-permute-start(bf16[128,1024]{1,0:T(8,128)(2,1)S(1)} %get-tuple-element.77.refs_0_.refs_4_.refs_6_), channel_id=1, source_target_pairs={{0,2},{1,3},{2,0},{3,1},{4,6},{5,7},{6,4},{7,5},{8,10},{9,11},{10,... | collective-permute-start | bytes 786440 | tf_op jit(solution)/shard_map/ppermute | solution.py:509
  28.7 8.4 %collective-permute-start.17 = (bf16[128,1024]{1,0:T(8,128)(2,1)S(1)}, bf16[128,1024]{1,0:T(8,128)(2,1)S(1)}, u32[]{:S(2)}, u32[]{:S(2)}) collective-permute-start(bf16[128,1024]{1,0:T(8,128)(2,1)S(1)} %get-tuple-element.71.mine_ref), channel_id=1, source_target_pairs={{0,8},{4,12},{8,0},{12,4},{16,24},{20,28},{24,16},{28,20},{1,9},{5... | collective-permute-start | bytes 786440 | tf_op jit(solution)/shard_map/ppermute | solution.py:509
  31.8 5.3 %collective-permute-start.11 = (bf16[128,1024]{1,0:T(8,128)(2,1)S(1)}, bf16[128,1024]{1,0:T(8,128)(2,1)S(1)}, u32[]{:S(2)}, u32[]{:S(2)}) collective-permute-start(bf16[128,1024]{1,0:T(8,128)(2,1)S(1)} %shard_map.87), channel_id=1, source_target_pairs={{0,1},{1,0},{2,3},{3,2},{4,5},{5,4},{6,7},{7,6},{8,9},{9,8},{10,11... | collective-permute-start | bytes 786440 | tf_op jit(solution)/shard_map/ppermute | solution.py:509
  31.9 4.1 %collective-permute-start.10 = (bf16[32,256]{1,0:T(8,128)(2,1)S(1)}, bf16[32,256]{1,0:T(8,128)(2,1)S(1)}, u32[]{:S(2)}, u32[]{:S(2)}) collective-permute-start(bf16[32,256]{1,0:T(8,128)(2,1)S(1)} %get-tuple-element.73.refs_1_.mine_ref), channel_id=1, source_target_pairs={{0,2},{1,3},{2,0},{3,1},{4,6},{5,7},{6,4},{7,5},{8,10},{9,11},{10,... | collective-permute-start | bytes 49160 | tf_op jit(solution)/shard_map/ppermute | solution.py:509
  36.0 4.8 %collective-permute-start.13 = (bf16[128,1024]{1,0:T(8,128)(2,1)S(1)}, bf16[128,1024]{1,0:T(8,128)(2,1)S(1)}, u32[]{:S(2)}, u32[]{:S(2)}) collective-permute-start(bf16[128,1024]{1,0:T(8,128)(2,1)S(1)} %collective-permute-done.12.refs_5_.refs_7_), channel_id=1, source_target_pairs={{0,1},{1,0},{2,3},{3,2},{4,5},{5,4},{6,7},{7,6},{8,9},{9,8},{10,11... | collective-permute-start | bytes 786440 | tf_op jit(solution)/shard_map/ppermute | solution.py:509
  37.5 9.9 %collective-permute-start.18 = (bf16[128,1024]{1,0:T(8,128)(2,1)S(1)}, bf16[128,1024]{1,0:T(8,128)(2,1)S(1)}, u32[]{:S(2)}, u32[]{:S(2)}) collective-permute-start(bf16[128,1024]{1,0:T(8,128)(2,1)S(1)} %shard_map.90), channel_id=1, source_target_pairs={{0,2},{1,3},{2,0},{3,1},{4,6},{5,7},{6,4},{7,5},{8,10},{9,11},{10,... | collective-permute-start | bytes 786440 | tf_op jit(solution)/shard_map/ppermute | solution.py:509
  38.2 9.8 %collective-permute-start.22 = (bf16[128,512]{1,0:T(8,128)(2,1)S(1)}, bf16[128,512]{1,0:T(8,128)(2,1)S(1)}, u32[]{:S(2)}, u32[]{:S(2)}) collective-permute-start(bf16[128,512]{1,0:T(8,128)(2,1)S(1)} %get-tuple-element.92.mine_ref), channel_id=1, source_target_pairs={{0,16},{4,20},{8,24},{12,28},{16,0},{20,4},{24,8},{28,12},{1,17},{... | collective-permute-start | bytes 393224 | tf_op jit(solution)/shard_map/ppermute | solution.py:509
  40.8 6.2 %collective-permute-start.14 = (bf16[32,256]{1,0:T(8,128)(2,1)S(1)}, bf16[32,256]{1,0:T(8,128)(2,1)S(1)}, u32[]{:S(2)}, u32[]{:S(2)}) collective-permute-start(bf16[32,256]{1,0:T(8,128)(2,1)S(1)} %get-tuple-element.85.refs_1_.refs_3_), channel_id=1, source_target_pairs={{0,6},{1,7},{2,4},{3,5},{4,2},{5,3},{6,0},{7,1},{8,14},{9,15},{10,... | collective-permute-start | bytes 49160 | tf_op jit(solution)/shard_map/ppermute | solution.py:522
  43.1 3.9 %collective-permute-start.15 = (bf16[32,256]{1,0:T(8,128)(2,1)S(1)}, bf16[32,256]{1,0:T(8,128)(2,1)S(1)}, u32[]{:S(2)}, u32[]{:S(2)}) collective-permute-start(bf16[32,256]{1,0:T(8,128)(2,1)S(1)} %get-tuple-element.85.refs_1_.refs_3_), channel_id=1, source_target_pairs={{0,4},{4,0},{8,12},{12,8},{16,20},{20,16},{24,28},{28,24},{1,5},{5... | collective-permute-start | bytes 49160 | tf_op jit(solution)/shard_map/ppermute | solution.py:509
  43.6 3.7 %collective-permute-start.16 = (bf16[32,256]{1,0:T(8,128)(2,1)S(1)}, bf16[32,256]{1,0:T(8,128)(2,1)S(1)}, u32[]{:S(2)}, u32[]{:S(2)}) collective-permute-start(bf16[32,256]{1,0:T(8,128)(2,1)S(1)} %get-tuple-element.85.refs_1_.refs_3_), channel_id=1, source_target_pairs={{0,2},{1,3},{2,0},{3,1},{4,6},{5,7},{6,4},{7,5},{8,10},{9,11},{10,... | collective-permute-start | bytes 49160 | tf_op jit(solution)/shard_map/ppermute | solution.py:509
  48.1 8.6 %collective-permute-start.23 = (bf16[128,1280]{1,0:T(8,128)(2,1)S(1)}, bf16[128,1280]{1,0:T(8,128)(2,1)S(1)}, u32[]{:S(2)}, u32[]{:S(2)}) collective-permute-start(bf16[128,1280]{1,0:T(8,128)(2,1)S(1)} %shard_map.96), channel_id=1, source_target_pairs={{0,2},{1,3},{2,0},{3,1},{4,6},{5,7},{6,4},{7,5},{8,10},{9,11},{10,... | collective-permute-start | bytes 983048 | tf_op jit(solution)/shard_map/ppermute | solution.py:509
  49.2 3.9 %collective-permute-start.20 = (bf16[128,1024]{1,0:T(8,128)(2,1)S(1)}, bf16[128,1024]{1,0:T(8,128)(2,1)S(1)}, u32[]{:S(2)}, u32[]{:S(2)}) collective-permute-start(bf16[128,1024]{1,0:T(8,128)(2,1)S(1)} %shard_map.92), channel_id=1, source_target_pairs={{0,1},{1,0},{2,3},{3,2},{4,5},{5,4},{6,7},{7,6},{8,9},{9,8},{10,11... | collective-permute-start | bytes 786440 | tf_op jit(solution)/shard_map/ppermute | solution.py:509
  49.3 3.9 %collective-permute-start.19 = (bf16[32,256]{1,0:T(8,128)(2,1)S(1)}, bf16[32,256]{1,0:T(8,128)(2,1)S(1)}, u32[]{:S(2)}, u32[]{:S(2)}) collective-permute-start(bf16[32,256]{1,0:T(8,128)(2,1)S(1)} %get-tuple-element.86.refs_1_.refs_0_.refs_2_), channel_id=1, source_target_pairs={{0,8},{4,12},{8,0},{12,4},{16,24},{20,28},{24,16},{28,20},{1,9},{5... | collective-permute-start | bytes 49160 | tf_op jit(solution)/shard_map/ppermute | solution.py:509
  53.7 5.3 %collective-permute-start.21 = (bf16[32,256]{1,0:T(8,128)(2,1)S(1)}, bf16[32,256]{1,0:T(8,128)(2,1)S(1)}, u32[]{:S(2)}, u32[]{:S(2)}) collective-permute-start(bf16[32,256]{1,0:T(8,128)(2,1)S(1)} %get-tuple-element.87._.refs_0_), channel_id=1, source_target_pairs={{0,16},{4,20},{8,24},{12,28},{16,0},{20,4},{24,8},{28,12},{1,17},{... | collective-permute-start | bytes 49160 | tf_op jit(solution)/shard_map/ppermute | solution.py:509
  59.0 7.0 %copy-start.3 = (bf16[8,128,256]{2,1,0:T(8,128)(2,1)S(1)}, bf16[8,128,256]{2,1,0:T(8,128)(2,1)}, u32[]{:S(2)}) copy-start(bf16[8,128,256]{2,1,0:T(8,128)(2,1)} %coupling_ref.1) | copy-start | bytes 1572868

commit v10 on v9

--- a/solution.py
+++ b/solution.py
@@ -557,8 +557,8 @@
     )
     points = [across, beside, swap(after(across, beside), "rhs", 1)]
     half_far = swap(send, "rhs", CORES)
-    keep_near = swap(after(keep, points), "rhs", 1)
-    carrier = after(carrier, points)
+    keep_near = swap(after(keep, points[:2]), "rhs", 1)
+    carrier = after(carrier, points[:2])
     points = [right_side, *points]
 
     leaves = (point_order, leaf_inverse, leaf_basis)

time: 67.2 us -> 65.8 us (0.979)
  waiting for transfers between devices: 15.3 us -> 13.8 us
    ppermute x23, waiting for transfers between devices: 12.5 us -> 11.1 us  [swap(): lax.ppermute(block, axis, [(i, i ^ bit) for i in range(lax.axis_size(axis...]
  transfers between devices with their start and end apart: 24 -> 24, of which waited for: 10 -> 9; matrix products, arithmetic and copies ran while one was open for 0% -> 0% of each run, Pallas kernels for 19% -> 20%
where the time goes in v10:
time: 65.8 us; the launch traced here: 65.6 us
  starting transfers between devices  24.8 us (38%)
  Pallas kernels  15.1 us (23%)
  waiting for transfers between devices  13.8 us (21%)
  blocking collectives  10.4 us (16%)
  local copies, waits for them, and re-layouts  1.25 us (2%)
    ppermute x23, starting transfers between devices, swap(): lax.ppermute(block, axis, [(i, i ^ bit) for i in range(lax.axis_size(axis...  22.4 us
    ppermute x23, waiting for transfers between devices, swap(): lax.ppermute(block, axis, [(i, i ^ bit) for i in range(lax.axis_size(axis...  11.1 us
    pallas_call x2, Pallas kernels, leaf_up(): pl.pallas_call(functools.partial(leaf_kernel, len(points)), grid_spec=plt...  6.82 us
    all_gather x1, blocking collectives, body(): incoming = lax.all_gather(shares, 'rhs', axis=0)  5.9 us
    all_gather x2, blocking collectives, gather_cores(): return lax.all_gather(block, 'rhs', axis_index_groups=cores)  4.46 us
    pallas_call x1, Pallas kernels, pack(): pl.pallas_call(functools.partial(pack_kernel, per_dev), in_specs=[pl.Bloc...  2.99 us
    ppermute x1, waiting for transfers between devices, far_swap(): lax.ppermute(block, ('leaf', 'rhs'), [(i, i ^ flip) for i in range(count)])  2.73 us
    ppermute x1, starting transfers between devices, far_swap(): lax.ppermute(block, ('leaf', 'rhs'), [(i, i ^ flip) for i in range(count)])  2.34 us
  transfers between devices with their start and end apart: 24, of which 9 were waited for; matrix products, arithmetic and copies ran while one was open for 0% of the time, Pallas kernels for 20%

profile of v10, /device:TPU:0, one launch (start us, length us, event | category | flops | bytes accessed | tf_op | source)
XLA Modules:
  0.0 65.6 jit_solution(4593290728634285813)
XLA Ops:
  0.0 2.9 %collective-permute-start = (bf16[64,1024]{1,0:T(8,128)(2,1)}, bf16[64,1024]{1,0:T(8,128)(2,1)S(1)}, u32[]{:S(2)}, u32[]{:S(2)}) collective-permute-start(bf16[64,1024]{1,0:T(8,128)(2,1)} %refs_0_.1), channel_id=1, source_target_pairs={{0,2},{1,3},{2,0},{3,1},{4,6},{5,7},{6,4},{7,5},{8,10},{9,11},{10,... | collective-permute-start | bytes 393224 | tf_op jit(solution)/shard_map/ppermute | solution.py:509
  2.9 3.0 %shard_map.82 = (bf16[3,128,768]{2,1,0:T(8,128)(2,1)}, bf16[128,768]{1,0:T(8,128)(2,1)}, bf16[4,128,1024]{2,1,0:T(8,128)(2,1)}, bf16[128,1024]{1,0:T(8,128)(2,1)}) custom-call(bf16[8,128,512]{2,1,0:T(8,128)(2,1)} %inverse.1, bf16[8,128,256]{2,1,0:T(8,128)(2,1)} %basis.1, bf16[8,128,256]{2,1,0:T(8,128)(2,1)} %coupling.1), custom_call_target="tpu_custom_call" | custom-call | bytes 4194 | tf_op jit(solution)/shard_map/pallas_call | solution.py:93
  5.9 0.7 %collective-permute-done.refs_1_ = bf16[64,1024]{1,0:T(8,128)(2,1)S(1)} collective-permute-done((bf16[64,1024]{1,0:T(8,128)(2,1)}, bf16[64,1024]{1,0:T(8,128)(2,1)S(1)}, u32[]{:S(2)}, u32[]{:S(2)}) %collective-permute-start) | collective-permute-done | bytes 131104 | tf_op jit(solution)/shard_map/ppermute | solution.py:509
  6.7 1.7 %collective-permute-start.7 = (bf16[3,128,768]{2,1,0:T(8,128)(2,1)}, bf16[3,128,768]{2,1,0:T(8,128)(2,1)S(1)}, u32[]{:S(2)}, u32[]{:S(2)}) collective-permute-start(bf16[3,128,768]{2,1,0:T(8,128)(2,1)} %get-tuple-element.50), channel_id=1, source_target_pairs={{0,2},{1,3},{2,0},{3,1},{4,6},{5,7},{6,4},{7,5},{8,10},{9,11},{10,... | collective-permute-start | bytes 1769480 | tf_op jit(solution)/shard_map/ppermute | solution.py:509
  8.4 0.2 collective-permute-start.2
  8.6 1.5 %collective-permute-start.8 = (bf16[128,1024]{1,0:T(8,128)(2,1)}, bf16[128,1024]{1,0:T(8,128)(2,1)S(1)}, u32[]{:S(2)}, u32[]{:S(2)}) collective-permute-start(bf16[128,1024]{1,0:T(8,128)(2,1)} %get-tuple-element.68.mine_ref), channel_id=1, source_target_pairs={{0,4},{4,0},{8,12},{12,8},{16,20},{20,16},{24,28},{28,24},{1,5},{5... | collective-permute-start | bytes 786440 | tf_op jit(solution)/shard_map/ppermute | solution.py:509
  10.1 0.1 pad_add_fusion.side_ref
  10.2 0.1 pad_add_fusion.1.side_ref
  10.3 0.0 copy-start.1
  10.3 1.2 %copy-done.1 = bf16[8,128,512]{2,1,0:T(8,128)(2,1)S(1)} copy-done((bf16[8,128,512]{2,1,0:T(8,128)(2,1)S(1)}, bf16[8,128,512]{2,1,0:T(8,128)(2,1)}, u32[]{:S(2)}) %copy-start.1) | copy-done | bytes 1048600
  11.5 3.4 %shard_map.83 = (f32[4,64,128]{2,1,0:T(8,128)S(1)}, bf16[4,32,256]{2,1,0:T(8,128)(2,1)S(1)}, bf16[4,32,256]{2,1,0:T(8,128)(2,1)S(1)}, bf16[4,4,64,256]{3,2,1,0:T(8,128)(2,1)S(1)}) custom-call(s32[2]{0:T(128)S(1)} %pad_add_fusion.side_ref, bf16[64,1024]{1,0:T(8,128)(2,1)S(1)} %copy-done.6, bf16[64,1024]{1,0:T(8,128)(2,1)S(1)} %collective-permute-done.refs_1_, ...), custom_call_target="tpu_custom_call" | custom-call | flops 1140850 | bytes 983 | tf_op jit(solution)/shard_map/pallas_call | solution.py:246
  15.0 0.7 %collective-permute-start.6 = (bf16[4,32,256]{2,1,0:T(8,128)(2,1)S(1)}, bf16[4,32,256]{2,1,0:T(8,128)(2,1)S(1)}, u32[]{:S(2)}, u32[]{:S(2)}) collective-permute-start(bf16[4,32,256]{2,1,0:T(8,128)(2,1)S(1)} %get-tuple-element.65), channel_id=1, source_target_pairs={{0,3},{1,2},{2,1},{3,0},{4,7},{5,6},{6,5},{7,4},{8,11},{9,10},{10,... | collective-permute-start | bytes 196616 | tf_op jit(solution)/shard_map/ppermute | solution.py:509
  15.7 1.0 %collective-permute-start.4 = (bf16[4,32,256]{2,1,0:T(8,128)(2,1)S(1)}, bf16[4,32,256]{2,1,0:T(8,128)(2,1)S(1)}, u32[]{:S(2)}, u32[]{:S(2)}) collective-permute-start(bf16[4,32,256]{2,1,0:T(8,128)(2,1)S(1)} %get-tuple-element.58), channel_id=1, source_target_pairs={{0,2},{1,3},{2,0},{3,1},{4,6},{5,7},{6,4},{7,5},{8,10},{9,11},{10,... | collective-permute-start | bytes 196616 | tf_op jit(solution)/shard_map/ppermute | solution.py:509
  16.7 3.4 %shard_map.84 = (f32[4,64,128]{2,1,0:T(8,128)S(1)}, bf16[4,32,256]{2,1,0:T(8,128)(2,1)S(1)}, bf16[4,32,256]{2,1,0:T(8,128)(2,1)S(1)}) custom-call(s32[2]{0:T(128)S(1)} %pad_add_fusion.1.side_ref, bf16[4,4,64,256]{3,2,1,0:T(8,128)(2,1)S(1)} %get-tuple-element.60.refs_0_, s32[1,4096]{1,0:T(1,128)S(1)} %bitcast.12, bf16[8,128,512]{2,1,0:T(8,128)(2,1)S(1)} %copy-done.1, ...), custom_call_target="tpu_custom_call" | custom-call | flops 1140850 | bytes 983 | tf_op jit(solution)/shard_map/pallas_call | solution.py:246
  20.1 0.3 collective-permute-start.5
  20.4 3.3 %collective-permute-done.6.refs_3_ = bf16[4,32,256]{2,1,0:T(8,128)(2,1)S(1)} collective-permute-done((bf16[4,32,256]{2,1,0:T(8,128)(2,1)S(1)}, bf16[4,32,256]{2,1,0:T(8,128)(2,1)S(1)}, u32[]{:S(2)}, u32[]{:S(2)}) %collective-permute-start.6) | collective-permute-done | bytes 65568 | tf_op jit(solution)/shard_map/ppermute | solution.py:509
  23.7 1.8 %collective-permute-done.4.refs_1_ = bf16[4,32,256]{2,1,0:T(8,128)(2,1)S(1)} collective-permute-done((bf16[4,32,256]{2,1,0:T(8,128)(2,1)S(1)}, bf16[4,32,256]{2,1,0:T(8,128)(2,1)S(1)}, u32[]{:S(2)}, u32[]{:S(2)}) %collective-permute-start.4) | collective-permute-done | bytes 65568 | tf_op jit(solution)/shard_map/ppermute | solution.py:509
  25.4 0.1 shard_map.85
  25.5 0.1 collective-permute-start.9
  25.6 1.8 %collective-permute-start.12 = (bf16[128,1024]{1,0:T(8,128)(2,1)S(1)}, bf16[128,1024]{1,0:T(8,128)(2,1)S(1)}, u32[]{:S(2)}, u32[]{:S(2)}) collective-permute-start(bf16[128,1024]{1,0:T(8,128)(2,1)S(1)} %get-tuple-element.77.refs_0_.refs_4_.refs_6_), channel_id=1, source_target_pairs={{0,2},{1,3},{2,0},{3,1},{4,6},{5,7},{6,4},{7,5},{8,10},{9,11},{10,... | collective-permute-start | bytes 786440 | tf_op jit(solution)/shard_map/ppermute | solution.py:509
  27.4 1.6 %collective-permute-start.17 = (bf16[128,1024]{1,0:T(8,128)(2,1)S(1)}, bf16[128,1024]{1,0:T(8,128)(2,1)S(1)}, u32[]{:S(2)}, u32[]{:S(2)}) collective-permute-start(bf16[128,1024]{1,0:T(8,128)(2,1)S(1)} %get-tuple-element.71.mine_ref), channel_id=1, source_target_pairs={{0,8},{4,12},{8,0},{12,4},{16,24},{20,28},{24,16},{28,20},{1,9},{5... | collective-permute-start | bytes 786440 | tf_op jit(solution)/shard_map/ppermute | solution.py:509
  29.0 1.5 %shard_map.86 = (f32[3,4,32,128]{3,2,1,0:T(8,128)S(1)}, bf16[32,256]{1,0:T(8,128)(2,1)S(1)}) custom-call(bf16[4,32,256]{2,1,0:T(8,128)(2,1)S(1)} %get-tuple-element.62.refs_0_, bf16[4,32,256]{2,1,0:T(8,128)(2,1)S(1)} %collective-permute-done.4.refs_1_, bf16[4,32,256]{2,1,0:T(8,128)(2,1)S(1)} %collective-permute-done.5.refs_2_, ...), custom_call_target="tpu_custom_call" | custom-call | flops 75497 | bytes 3145 | tf_op jit(solution)/shard_map/pallas_call | solution.py:309
  30.5 0.1 collective-permute-start.11
  30.6 0.6 collective-permute-start.10
  31.2 3.3 %collective-permute-done.12.refs_5_.refs_7_ = bf16[128,1024]{1,0:T(8,128)(2,1)S(1)} collective-permute-done((bf16[128,1024]{1,0:T(8,128)(2,1)S(1)}, bf16[128,1024]{1,0:T(8,128)(2,1)S(1)}, u32[]{:S(2)}, u32[]{:S(2)}) %collective-permute-start.12) | collective-permute-done | bytes 262176 | tf_op jit(solution)/shard_map/ppermute | solution.py:509
  34.5 0.2 collective-permute-done.10.other_ref
  34.7 1.1 %collective-permute-done.17.other_ref = bf16[128,1024]{1,0:T(8,128)(2,1)S(1)} collective-permute-done((bf16[128,1024]{1,0:T(8,128)(2,1)S(1)}, bf16[128,1024]{1,0:T(8,128)(2,1)S(1)}, u32[]{:S(2)}, u32[]{:S(2)}) %collective-permute-start.17) | collective-permute-done | bytes 262176 | tf_op jit(solution)/shard_map/ppermute | solution.py:509
  35.8 0.3 shard_map.88
  36.1 0.7 %collective-permute-start.18 = (bf16[128,1024]{1,0:T(8,128)(2,1)S(1)}, bf16[128,1024]{1,0:T(8,128)(2,1)S(1)}, u32[]{:S(2)}, u32[]{:S(2)}) collective-permute-start(bf16[128,1024]{1,0:T(8,128)(2,1)S(1)} %shard_map.90), channel_id=1, source_target_pairs={{0,2},{1,3},{2,0},{3,1},{4,6},{5,7},{6,4},{7,5},{8,10},{9,11},{10,... | collective-permute-start | bytes 786440 | tf_op jit(solution)/shard_map/ppermute | solution.py:509
  36.9 2.6 %collective-permute-start.22 = (bf16[128,512]{1,0:T(8,128)(2,1)S(1)}, bf16[128,512]{1,0:T(8,128)(2,1)S(1)}, u32[]{:S(2)}, u32[]{:S(2)}) collective-permute-start(bf16[128,512]{1,0:T(8,128)(2,1)S(1)} %get-tuple-element.92.mine_ref), channel_id=1, source_target_pairs={{0,16},{4,20},{8,24},{12,28},{16,0},{20,4},{24,8},{28,12},{1,17},{... | collective-permute-start | bytes 393224 | tf_op jit(solution)/shard_map/ppermute | solution.py:509
  39.4 2.3 %collective-permute-start.14 = (bf16[32,256]{1,0:T(8,128)(2,1)S(1)}, bf16[32,256]{1,0:T(8,128)(2,1)S(1)}, u32[]{:S(2)}, u32[]{:S(2)}) collective-permute-start(bf16[32,256]{1,0:T(8,128)(2,1)S(1)} %get-tuple-element.85.refs_1_.refs_3_), channel_id=1, source_target_pairs={{0,6},{1,7},{2,4},{3,5},{4,2},{5,3},{6,0},{7,1},{8,14},{9,15},{10,... | collective-permute-start | bytes 49160 | tf_op jit(solution)/shard_map/ppermute | solution.py:522
  41.8 0.5 collective-permute-start.15
  42.3 0.6 collective-permute-start.16
  42.9 2.7 %collective-permute-done.14.refs_0_ = bf16[32,256]{1,0:T(8,128)(2,1)S(1)} collective-permute-done((bf16[32,256]{1,0:T(8,128)(2,1)S(1)}, bf16[32,256]{1,0:T(8,128)(2,1)S(1)}, u32[]{:S(2)}, u32[]{:S(2)}) %collective-permute-start.14) | collective-permute-done | bytes 16416 | tf_op jit(solution)/shard_map/ppermute | solution.py:522
  45.7 0.0 collective-permute-done.15.refs_1_
  45.7 0.3 collective-permute-done.16.refs_2_
  46.0 0.6 shard_map.91
  46.7 1.1 %collective-permute-start.23 = (bf16[128,1280]{1,0:T(8,128)(2,1)S(1)}, bf16[128,1280]{1,0:T(8,128)(2,1)S(1)}, u32[]{:S(2)}, u32[]{:S(2)}) collective-permute-start(bf16[128,1280]{1,0:T(8,128)(2,1)S(1)} %shard_map.96), channel_id=1, source_target_pairs={{0,2},{1,3},{2,0},{3,1},{4,6},{5,7},{6,4},{7,5},{8,10},{9,11},{10,... | collective-permute-start | bytes 983048 | tf_op jit(solution)/shard_map/ppermute | solution.py:509
  47.8 0.1 collective-permute-start.20
  47.9 1.6 %collective-permute-start.19 = (bf16[32,256]{1,0:T(8,128)(2,1)S(1)}, bf16[32,256]{1,0:T(8,128)(2,1)S(1)}, u32[]{:S(2)}, u32[]{:S(2)}) collective-permute-start(bf16[32,256]{1,0:T(8,128)(2,1)S(1)} %get-tuple-element.86.refs_1_.refs_0_.refs_2_), channel_id=1, source_target_pairs={{0,8},{4,12},{8,0},{12,4},{16,24},{20,28},{24,16},{28,20},{1,9},{5... | collective-permute-start | bytes 49160 | tf_op jit(solution)/shard_map/ppermute | solution.py:509
  49.6 2.2 %all-gather = bf16[256,1024]{1,0:T(8,128)(2,1)S(1)} all-gather(bf16[128,1024]{1,0:T(8,128)(2,1)S(1)} %shard_map.93), channel_id=2, replica_groups={{0,1},{2,3},{4,5},{6,7},{8,9},{10,11},{12,13},{14,15},{16,17},{18,19},{..., dimensions={0}, use_global_device_ids=true | all-gather | bytes 786432 | tf_op jit(solution)/shard_map/all_gather | solution.py:515
  51.8 0.6 shard_map.94
  52.3 2.6 %collective-permute-start.21 = (bf16[32,256]{1,0:T(8,128)(2,1)S(1)}, bf16[32,256]{1,0:T(8,128)(2,1)S(1)}, u32[]{:S(2)}, u32[]{:S(2)}) collective-permute-start(bf16[32,256]{1,0:T(8,128)(2,1)S(1)} %get-tuple-element.87._.refs_0_), channel_id=1, source_target_pairs={{0,16},{4,20},{8,24},{12,28},{16,0},{20,4},{24,8},{28,12},{1,17},{... | collective-permute-start | bytes 49160 | tf_op jit(solution)/shard_map/ppermute | solution.py:509
  55.0 0.4 collective-permute-done.23.tail_ref
  55.4 2.3 %all-gather.1 = bf16[256,1280]{1,0:T(8,128)(2,1)S(1)} all-gather(bf16[128,1280]{1,0:T(8,128)(2,1)S(1)} %shard_map.97), channel_id=3, replica_groups={{0,1},{2,3},{4,5},{6,7},{8,9},{10,11},{12,13},{14,15},{16,17},{18,19},{..., dimensions={0}, use_global_device_ids=true | all-gather | bytes 983040 | tf_op jit(solution)/shard_map/all_gather | solution.py:515
  57.6 1.1 %shard_map.98 = bf16[4,32,256]{2,1,0:T(8,128)(2,1)S(1)} custom-call(bf16[32,256]{1,0:T(8,128)(2,1)S(1)} %get-tuple-element.87._.refs_0_, bf16[32,256]{1,0:T(8,128)(2,1)S(1)} %collective-permute-done.21.refs_1_, f32[4,32,128]{2,1,0:T(8,128)S(1)} %get-tuple-element.88.refs_2_, f32[4,32,128]{2,1,0:T(8,128)S(1)} %get-tuple-element.89.refs_3_, ...), custom_call_target="tpu_custom_call" | custom-call | flops 67108 | bytes 4194 | tf_op jit(solution)/shard_map/pallas_call | solution.py:477
  58.7 5.9 %all-gather.2 = bf16[16,32,256]{2,1,0:T(8,128)(2,1)S(1)} all-gather(bf16[4,32,256]{2,1,0:T(8,128)(2,1)S(1)} %shard_map.98), channel_id=4, replica_groups=mesh['leaf'=8,'rhs'=4] {'rhs'}, dimensions={0}, use_global_device_ids=true | all-gather | bytes 327680 | tf_op jit(solution)/shard_map/all_gather | solution.py:618
  64.6 1.0 %shard_map.99 = f32[8,64,128]{2,1,0:T(8,128)} custom-call(f32[4,64,128]{2,1,0:T(8,128)S(1)} %get-tuple-element.54.far_ref, f32[4,64,128]{2,1,0:T(8,128)S(1)} %get-tuple-element.61.own_ref, bf16[4,4,32,256]{3,2,1,0:T(8,128)(2,1)S(1)} %bitcast.10, bf16[8,128,256]{2,1,0:T(8,128)(2,1)S(1)} %copy-done.3), custom_call_target="tpu_custom_call" | custom-call | flops 33554 | bytes 524 | tf_op jit(solution)/shard_map/pallas_call | solution.py:500
  (39 shorter events, 0.3 us)
Async XLA Ops:
  0.0 10.3 %copy-start.2 = (bf16[8,128,256]{2,1,0:T(8,128)(2,1)S(1)}, bf16[8,128,256]{2,1,0:T(8,128)(2,1)}, u32[]{:S(2)}) copy-start(bf16[8,128,256]{2,1,0:T(8,128)(2,1)} %refs_3_.1) | copy-start | bytes 1572868
  0.0 6.6 %collective-permute-start = (bf16[64,1024]{1,0:T(8,128)(2,1)}, bf16[64,1024]{1,0:T(8,128)(2,1)S(1)}, u32[]{:S(2)}, u32[]{:S(2)}) collective-permute-start(bf16[64,1024]{1,0:T(8,128)(2,1)} %refs_0_.1), channel_id=1, source_target_pairs={{0,2},{1,3},{2,0},{3,1},{4,6},{5,7},{6,4},{7,5},{8,10},{9,11},{10,... | collective-permute-start | bytes 393224 | tf_op jit(solution)/shard_map/ppermute | solution.py:509
  2.9 3.7 %collective-permute-start.1 = (bf16[64,1024]{1,0:T(8,128)(2,1)}, bf16[64,1024]{1,0:T(8,128)(2,1)S(1)}, u32[]{:S(2)}, u32[]{:S(2)}) collective-permute-start(bf16[64,1024]{1,0:T(8,128)(2,1)} %refs_0_.1), channel_id=1, source_target_pairs={{0,1},{1,0},{2,3},{3,2},{4,5},{5,4},{6,7},{7,6},{8,9},{9,8},{10,11... | collective-permute-start | bytes 393224 | tf_op jit(solution)/shard_map/ppermute | solution.py:509
  2.9 7.4 %copy-start.6 = (bf16[64,1024]{1,0:T(8,128)(2,1)S(1)}, bf16[64,1024]{1,0:T(8,128)(2,1)}, u32[]{:S(2)}) copy-start(bf16[64,1024]{1,0:T(8,128)(2,1)} %refs_0_.1) | copy-start | bytes 393220
  6.6 10.0 %collective-permute-start.3 = (bf16[4,128,1024]{2,1,0:T(8,128)(2,1)}, bf16[4,128,1024]{2,1,0:T(8,128)(2,1)S(1)}, u32[]{:S(2)}, u32[]{:S(2)}) collective-permute-start(bf16[4,128,1024]{2,1,0:T(8,128)(2,1)} %get-tuple-element.57.refs_4_.own_ref.refs_15_), channel_id=1, source_target_pairs={{0,1},{1,0},{2,3},{3,2},{4,5},{5,4},{6,7},{7,6},{8,9},{9,8},{10,11... | collective-permute-start | bytes 3145736 | tf_op jit(solution)/shard_map/ppermute | solution.py:509
  6.7 18.8 %collective-permute-start.7 = (bf16[3,128,768]{2,1,0:T(8,128)(2,1)}, bf16[3,128,768]{2,1,0:T(8,128)(2,1)S(1)}, u32[]{:S(2)}, u32[]{:S(2)}) collective-permute-start(bf16[3,128,768]{2,1,0:T(8,128)(2,1)} %get-tuple-element.50), channel_id=1, source_target_pairs={{0,2},{1,3},{2,0},{3,1},{4,6},{5,7},{6,4},{7,5},{8,10},{9,11},{10,... | collective-permute-start | bytes 1769480 | tf_op jit(solution)/shard_map/ppermute | solution.py:509
  8.4 1.9 %copy-start.7 = (s32[4096]{0:T(1024)S(1)}, s32[4096]{0:T(1024)}, u32[]{:S(2)}) copy-start(s32[4096]{0:T(1024)} %param.9) | copy-start | bytes 49156
  8.4 1.9 %collective-permute-start.2 = (bf16[64,1024]{1,0:T(8,128)(2,1)S(1)}, bf16[64,1024]{1,0:T(8,128)(2,1)S(1)}, u32[]{:S(2)}, u32[]{:S(2)}) collective-permute-start(bf16[64,1024]{1,0:T(8,128)(2,1)S(1)} %collective-permute-done.refs_1_), channel_id=1, source_target_pairs={{0,1},{1,0},{2,3},{3,2},{4,5},{5,4},{6,7},{7,6},{8,9},{9,8},{10,11... | collective-permute-start | bytes 393224 | tf_op jit(solution)/shard_map/ppermute | solution.py:509
  8.6 11.8 %collective-permute-start.8 = (bf16[128,1024]{1,0:T(8,128)(2,1)}, bf16[128,1024]{1,0:T(8,128)(2,1)S(1)}, u32[]{:S(2)}, u32[]{:S(2)}) collective-permute-start(bf16[128,1024]{1,0:T(8,128)(2,1)} %get-tuple-element.68.mine_ref), channel_id=1, source_target_pairs={{0,4},{4,0},{8,12},{12,8},{16,20},{20,16},{24,28},{28,24},{1,5},{5... | collective-permute-start | bytes 786440 | tf_op jit(solution)/shard_map/ppermute | solution.py:509
  10.3 1.2 %copy-start.1 = (bf16[8,128,512]{2,1,0:T(8,128)(2,1)S(1)}, bf16[8,128,512]{2,1,0:T(8,128)(2,1)}, u32[]{:S(2)}) copy-start(bf16[8,128,512]{2,1,0:T(8,128)(2,1)} %refs_2_.1) | copy-start | bytes 3145732
  15.0 8.7 %collective-permute-start.6 = (bf16[4,32,256]{2,1,0:T(8,128)(2,1)S(1)}, bf16[4,32,256]{2,1,0:T(8,128)(2,1)S(1)}, u32[]{:S(2)}, u32[]{:S(2)}) collective-permute-start(bf16[4,32,256]{2,1,0:T(8,128)(2,1)S(1)} %get-tuple-element.65), channel_id=1, source_target_pairs={{0,3},{1,2},{2,1},{3,0},{4,7},{5,6},{6,5},{7,4},{8,11},{9,10},{10,... | collective-permute-start | bytes 196616 | tf_op jit(solution)/shard_map/ppermute | solution.py:509
  15.7 9.7 %collective-permute-start.4 = (bf16[4,32,256]{2,1,0:T(8,128)(2,1)S(1)}, bf16[4,32,256]{2,1,0:T(8,128)(2,1)S(1)}, u32[]{:S(2)}, u32[]{:S(2)}) collective-permute-start(bf16[4,32,256]{2,1,0:T(8,128)(2,1)S(1)} %get-tuple-element.58), channel_id=1, source_target_pairs={{0,2},{1,3},{2,0},{3,1},{4,6},{5,7},{6,4},{7,5},{8,10},{9,11},{10,... | collective-permute-start | bytes 196616 | tf_op jit(solution)/shard_map/ppermute | solution.py:509
  16.7 8.8 %copy-start.4 = (bf16[128,1024]{1,0:T(8,128)(2,1)S(1)}, bf16[128,1024]{1,0:T(8,128)(2,1)}, u32[]{:S(2)}) copy-start(bf16[128,1024]{1,0:T(8,128)(2,1)} %get-tuple-element.68.mine_ref) | copy-start | bytes 786436
  16.7 8.8 %copy-start.5 = (bf16[128,768]{1,0:T(8,128)(2,1)S(1)}, bf16[128,768]{1,0:T(8,128)(2,1)}, u32[]{:S(2)}) copy-start(bf16[128,768]{1,0:T(8,128)(2,1)} %get-tuple-element.70.refs_0_) | copy-start | bytes 589828
  16.7 12.3 %copy-start = (bf16[4,128,1024]{2,1,0:T(8,128)(2,1)S(1)}, bf16[4,128,1024]{2,1,0:T(8,128)(2,1)}, u32[]{:S(2)}) copy-start(bf16[4,128,1024]{2,1,0:T(8,128)(2,1)} %get-tuple-element.57.refs_4_.own_ref.refs_15_) | copy-start | bytes 3145732
  20.1 5.4 %collective-permute-start.5 = (bf16[4,32,256]{2,1,0:T(8,128)(2,1)S(1)}, bf16[4,32,256]{2,1,0:T(8,128)(2,1)S(1)}, u32[]{:S(2)}, u32[]{:S(2)}) collective-permute-start(bf16[4,32,256]{2,1,0:T(8,128)(2,1)S(1)} %get-tuple-element.64), channel_id=1, source_target_pairs={{0,1},{1,0},{2,3},{3,2},{4,5},{5,4},{6,7},{7,6},{8,9},{9,8},{10,11... | collective-permute-start | bytes 196616 | tf_op jit(solution)/shard_map/ppermute | solution.py:509
  25.5 3.5 %collective-permute-start.9 = (bf16[3,128,768]{2,1,0:T(8,128)(2,1)S(1)}, bf16[3,128,768]{2,1,0:T(8,128)(2,1)S(1)}, u32[]{:S(2)}, u32[]{:S(2)}) collective-permute-start(bf16[3,128,768]{2,1,0:T(8,128)(2,1)S(1)} %collective-permute-done.7.refs_5_), channel_id=1, source_target_pairs={{0,1},{1,0},{2,3},{3,2},{4,5},{5,4},{6,7},{7,6},{8,9},{9,8},{10,11... | collective-permute-start | bytes 1769480 | tf_op jit(solution)/shard_map/ppermute | solution.py:509
  25.6 8.9 %collective-permute-start.12 = (bf16[128,1024]{1,0:T(8,128)(2,1)S(1)}, bf16[128,1024]{1,0:T(8,128)(2,1)S(1)}, u32[]{:S(2)}, u32[]{:S(2)}) collective-permute-start(bf16[128,1024]{1,0:T(8,128)(2,1)S(1)} %get-tuple-element.77.refs_0_.refs_4_.refs_6_), channel_id=1, source_target_pairs={{0,2},{1,3},{2,0},{3,1},{4,6},{5,7},{6,4},{7,5},{8,10},{9,11},{10,... | collective-permute-start | bytes 786440 | tf_op jit(solution)/shard_map/ppermute | solution.py:509
  27.4 8.4 %collective-permute-start.17 = (bf16[128,1024]{1,0:T(8,128)(2,1)S(1)}, bf16[128,1024]{1,0:T(8,128)(2,1)S(1)}, u32[]{:S(2)}, u32[]{:S(2)}) collective-permute-start(bf16[128,1024]{1,0:T(8,128)(2,1)S(1)} %get-tuple-element.71.mine_ref), channel_id=1, source_target_pairs={{0,8},{4,12},{8,0},{12,4},{16,24},{20,28},{24,16},{28,20},{1,9},{5... | collective-permute-start | bytes 786440 | tf_op jit(solution)/shard_map/ppermute | solution.py:509
  30.5 5.3 %collective-permute-start.11 = (bf16[128,1024]{1,0:T(8,128)(2,1)S(1)}, bf16[128,1024]{1,0:T(8,128)(2,1)S(1)}, u32[]{:S(2)}, u32[]{:S(2)}) collective-permute-start(bf16[128,1024]{1,0:T(8,128)(2,1)S(1)} %shard_map.87), channel_id=1, source_target_pairs={{0,1},{1,0},{2,3},{3,2},{4,5},{5,4},{6,7},{7,6},{8,9},{9,8},{10,11... | collective-permute-start | bytes 786440 | tf_op jit(solution)/shard_map/ppermute | solution.py:509
  30.6 4.1 %collective-permute-start.10 = (bf16[32,256]{1,0:T(8,128)(2,1)S(1)}, bf16[32,256]{1,0:T(8,128)(2,1)S(1)}, u32[]{:S(2)}, u32[]{:S(2)}) collective-permute-start(bf16[32,256]{1,0:T(8,128)(2,1)S(1)} %get-tuple-element.73.refs_1_.mine_ref), channel_id=1, source_target_pairs={{0,2},{1,3},{2,0},{3,1},{4,6},{5,7},{6,4},{7,5},{8,10},{9,11},{10,... | collective-permute-start | bytes 49160 | tf_op jit(solution)/shard_map/ppermute | solution.py:509
  34.7 4.8 %collective-permute-start.13 = (bf16[128,1024]{1,0:T(8,128)(2,1)S(1)}, bf16[128,1024]{1,0:T(8,128)(2,1)S(1)}, u32[]{:S(2)}, u32[]{:S(2)}) collective-permute-start(bf16[128,1024]{1,0:T(8,128)(2,1)S(1)} %collective-permute-done.12.refs_5_.refs_7_), channel_id=1, source_target_pairs={{0,1},{1,0},{2,3},{3,2},{4,5},{5,4},{6,7},{7,6},{8,9},{9,8},{10,11... | collective-permute-start | bytes 786440 | tf_op jit(solution)/shard_map/ppermute | solution.py:509
  36.1 9.9 %collective-permute-start.18 = (bf16[128,1024]{1,0:T(8,128)(2,1)S(1)}, bf16[128,1024]{1,0:T(8,128)(2,1)S(1)}, u32[]{:S(2)}, u32[]{:S(2)}) collective-permute-start(bf16[128,1024]{1,0:T(8,128)(2,1)S(1)} %shard_map.90), channel_id=1, source_target_pairs={{0,2},{1,3},{2,0},{3,1},{4,6},{5,7},{6,4},{7,5},{8,10},{9,11},{10,... | collective-permute-start | bytes 786440 | tf_op jit(solution)/shard_map/ppermute | solution.py:509
  36.9 9.8 %collective-permute-start.22 = (bf16[128,512]{1,0:T(8,128)(2,1)S(1)}, bf16[128,512]{1,0:T(8,128)(2,1)S(1)}, u32[]{:S(2)}, u32[]{:S(2)}) collective-permute-start(bf16[128,512]{1,0:T(8,128)(2,1)S(1)} %get-tuple-element.92.mine_ref), channel_id=1, source_target_pairs={{0,16},{4,20},{8,24},{12,28},{16,0},{20,4},{24,8},{28,12},{1,17},{... | collective-permute-start | bytes 393224 | tf_op jit(solution)/shard_map/ppermute | solution.py:509
  39.4 6.2 %collective-permute-start.14 = (bf16[32,256]{1,0:T(8,128)(2,1)S(1)}, bf16[32,256]{1,0:T(8,128)(2,1)S(1)}, u32[]{:S(2)}, u32[]{:S(2)}) collective-permute-start(bf16[32,256]{1,0:T(8,128)(2,1)S(1)} %get-tuple-element.85.refs_1_.refs_3_), channel_id=1, source_target_pairs={{0,6},{1,7},{2,4},{3,5},{4,2},{5,3},{6,0},{7,1},{8,14},{9,15},{10,... | collective-permute-start | bytes 49160 | tf_op jit(solution)/shard_map/ppermute | solution.py:522
  41.8 3.9 %collective-permute-start.15 = (bf16[32,256]{1,0:T(8,128)(2,1)S(1)}, bf16[32,256]{1,0:T(8,128)(2,1)S(1)}, u32[]{:S(2)}, u32[]{:S(2)}) collective-permute-start(bf16[32,256]{1,0:T(8,128)(2,1)S(1)} %get-tuple-element.85.refs_1_.refs_3_), channel_id=1, source_target_pairs={{0,4},{4,0},{8,12},{12,8},{16,20},{20,16},{24,28},{28,24},{1,5},{5... | collective-permute-start | bytes 49160 | tf_op jit(solution)/shard_map/ppermute | solution.py:509
  42.3 3.7 %collective-permute-start.16 = (bf16[32,256]{1,0:T(8,128)(2,1)S(1)}, bf16[32,256]{1,0:T(8,128)(2,1)S(1)}, u32[]{:S(2)}, u32[]{:S(2)}) collective-permute-start(bf16[32,256]{1,0:T(8,128)(2,1)S(1)} %get-tuple-element.85.refs_1_.refs_3_), channel_id=1, source_target_pairs={{0,2},{1,3},{2,0},{3,1},{4,6},{5,7},{6,4},{7,5},{8,10},{9,11},{10,... | collective-permute-start | bytes 49160 | tf_op jit(solution)/shard_map/ppermute | solution.py:509
  46.7 8.6 %collective-permute-start.23 = (bf16[128,1280]{1,0:T(8,128)(2,1)S(1)}, bf16[128,1280]{1,0:T(8,128)(2,1)S(1)}, u32[]{:S(2)}, u32[]{:S(2)}) collective-permute-start(bf16[128,1280]{1,0:T(8,128)(2,1)S(1)} %shard_map.96), channel_id=1, source_target_pairs={{0,2},{1,3},{2,0},{3,1},{4,6},{5,7},{6,4},{7,5},{8,10},{9,11},{10,... | collective-permute-start | bytes 983048 | tf_op jit(solution)/shard_map/ppermute | solution.py:509
  47.8 3.9 %collective-permute-start.20 = (bf16[128,1024]{1,0:T(8,128)(2,1)S(1)}, bf16[128,1024]{1,0:T(8,128)(2,1)S(1)}, u32[]{:S(2)}, u32[]{:S(2)}) collective-permute-start(bf16[128,1024]{1,0:T(8,128)(2,1)S(1)} %shard_map.92), channel_id=1, source_target_pairs={{0,1},{1,0},{2,3},{3,2},{4,5},{5,4},{6,7},{7,6},{8,9},{9,8},{10,11... | collective-permute-start | bytes 786440 | tf_op jit(solution)/shard_map/ppermute | solution.py:509
  47.9 3.9 %collective-permute-start.19 = (bf16[32,256]{1,0:T(8,128)(2,1)S(1)}, bf16[32,256]{1,0:T(8,128)(2,1)S(1)}, u32[]{:S(2)}, u32[]{:S(2)}) collective-permute-start(bf16[32,256]{1,0:T(8,128)(2,1)S(1)} %get-tuple-element.86.refs_1_.refs_0_.refs_2_), channel_id=1, source_target_pairs={{0,8},{4,12},{8,0},{12,4},{16,24},{20,28},{24,16},{28,20},{1,9},{5... | collective-permute-start | bytes 49160 | tf_op jit(solution)/shard_map/ppermute | solution.py:509
  52.3 5.3 %collective-permute-start.21 = (bf16[32,256]{1,0:T(8,128)(2,1)S(1)}, bf16[32,256]{1,0:T(8,128)(2,1)S(1)}, u32[]{:S(2)}, u32[]{:S(2)}) collective-permute-start(bf16[32,256]{1,0:T(8,128)(2,1)S(1)} %get-tuple-element.87._.refs_0_), channel_id=1, source_target_pairs={{0,16},{4,20},{8,24},{12,28},{16,0},{20,4},{24,8},{28,12},{1,17},{... | collective-permute-start | bytes 49160 | tf_op jit(solution)/shard_map/ppermute | solution.py:509
  57.6 7.0 %copy-start.3 = (bf16[8,128,256]{2,1,0:T(8,128)(2,1)S(1)}, bf16[8,128,256]{2,1,0:T(8,128)(2,1)}, u32[]{:S(2)}) copy-start(bf16[8,128,256]{2,1,0:T(8,128)(2,1)} %coupling_ref.1) | copy-start | bytes 1572868
